TPU v7x, 32 devices: a whole 2x2x4 slice. The times are simulated.
32 devices in a mesh: rows: 32 (over z, y, x, core).
Axes of the slice: x: 2, y: 2, z: 4, core: 2. Of those that a mesh axis runs over, the one named last changes fastest.
Arguments:
- features: bfloat16 [131072, 256], P('rows'), may hold values from -6 to 6
- tile_cols: int32 [1024, 6], P('rows'), may hold values from 0 to 1023, as said below
- tile_masks: int32 [1024, 6, 128, 128], P('rows'), may hold values from 0 to 1, as said below
- degree: int32 [131072], P('rows'), may hold values from 1 to 768, as said below
- weight: bfloat16 [512, 256], replicated, may hold values from -0.25 to 0.25
Outputs:
- embedding: bfloat16 [131072, 256], P('rows')
Inputs may be any that keep to these rules, and one draw needn't show every extreme that they name: `tile_cols`: each row block has exactly 2 tiles whose column block lies on the device that holds the row block (column block c lies on device c // 32); its other 4 tiles name column blocks of other devices. Over the row blocks of one device, at most 10 tiles name column blocks of any one other device, and exactly 10 for some other device; they name at most 5 distinct column blocks of any one other device, and exactly 5 for some. `tile_masks`: every item has at least one neighbour in the first tile of its row block. degree of item r * 128 + a is the number of ones in tile_masks[r, t, a, :] over all t; on every device some item reaches the most.
All inputs are finite; a program needn't handle non-finite values.
Results may differ from a plain program's by a relative error of at most 0.0027.
Values may be sent and summed in bfloat16 or wider, within the bound.
No kernel may reach another device: no remote copies, remote signals or barrier semaphores. Data moves between devices by JAX's collectives and lax.ppermute only.
A program may use at most 192 MiB of HBM per device.

v0:
```python
import jax
import jax.numpy as jnp
from jax import lax
from jax.sharding import PartitionSpec as P

REM_PB = 4


def request_table(owners, ranks, within, asking, peers, capacity):
    target = jnp.where(asking, owners, peers)
    table = jnp.zeros((peers, capacity), jnp.int32)
    return table.at[target, ranks].set(within, mode="drop")


def on_device(features, tile_cols, tile_masks, degree, weight):
    blocks_here, per_block = tile_cols.shape
    tile = tile_masks.shape[2]
    width = features.shape[1]
    peers = lax.axis_size("rows")
    myself = lax.axis_index("rows")
    distinct_most = max(2, (REM_PB * blocks_here + peers - 2) // (peers - 1))
    local_blocks = features.reshape(blocks_here, tile, width)
    columns = tile_cols.reshape(-1)
    owners = columns // blocks_here
    within = columns % blocks_here
    remote = owners != myself
    positions = jnp.arange(columns.shape[0], dtype=jnp.int32)
    earlier = positions[None, :] < positions[:, None]
    same_owner = (owners[:, None] == owners[None, :]) & earlier
    capacity = 2 * distinct_most
    ranks = jnp.sum(same_owner & remote[None, :], axis=1)
    requests = request_table(owners, ranks, within, remote, peers, capacity)
    received = lax.all_to_all(
        local_blocks[lax.all_to_all(requests, "rows", split_axis=0, concat_axis=0, tiled=True)],
        "rows",
        split_axis=0,
        concat_axis=0,
        tiled=True,
    )
    table = jnp.concatenate([local_blocks, received.reshape(-1, tile, width)], axis=0)
    slots = jnp.where(remote, blocks_here + owners * capacity + ranks, within)
    picked = table[slots].reshape(blocks_here, per_block, tile, width)
    sums = jnp.einsum(
        "rtij,rtjd->rid",
        tile_masks.astype(jnp.bfloat16),
        picked,
        preferred_element_type=jnp.float32,
    )
    mean = (sums.reshape(-1, width) / degree.astype(jnp.float32)[:, None]).astype(jnp.bfloat16)
    joined = jnp.concatenate([features, mean], axis=1)
    hidden = jnp.maximum(jnp.dot(joined, weight, preferred_element_type=jnp.float32), 0.0)
    scale = lax.rsqrt(jnp.sum(hidden * hidden, axis=1, keepdims=True) + 1e-06)
    return (hidden * scale).astype(jnp.bfloat16)


def solution(mesh):
    in_specs = (P("rows", None), P("rows", None), P("rows", None, None, None), P("rows"), P())
    out_specs = P("rows", None)
    return jax.shard_map(
        on_device, mesh=mesh, in_specs=in_specs, out_specs=out_specs, check_vma=False
    )
```

profile of v0, /device:TPU:0, one launch (start us, length us, event | category | flops | bytes accessed | tf_op | source)
XLA Modules:
  0.0 562.1 jit_solution(6063558246471832006)
XLA Ops:
  0.0 0.0 copy-start
  0.0 0.0 copy-start.1
  0.0 0.9 copy.15
  0.9 0.1 reshape.264
  1.0 0.1 reshape.263
  1.2 0.2 convert_reduce_fusion
  1.4 10.5 %scatter_fusion = s32[32,10]{0,1:T(8,128)S(1)} fusion(s32[32,10]{0,1:T(8,128)S(1)} %broadcast.276, s32[192]{0:T(256)S(1)} %bitcast.27, s32[192]{0:T(256)S(1)} %and_select_fusion.2), kind=kCustom, calls=%fused_computation.2 | custom fusion | bytes 3840 | tf_op jit(solution)/shard_map/scatter | solution.py:12
  11.9 0.1 copy.17
  12.0 14.2 %all_to_all.17 = s32[32,1,10]{2,1,0:T(1,128)S(1)} all-to-all(s32[32,1,10]{2,1,0:T(1,128)S(1)} %copy.17), channel_id=1, replica_groups=mesh['rows'=32] {'rows'}, dimensions={0} | all-to-all | bytes 2560 | tf_op jit(solution)/shard_map/all_to_all | solution.py:34
  26.2 0.1 reshape.270
  26.4 0.0 copy-done.1
  26.4 11.0 %gather_fusion = bf16[320,128,256]{2,1,0:T(8,128)(2,1)} fusion(bf16[32,128,256]{2,1,0:T(8,128)(2,1)S(1)} %bitcast.22, s32[1024]{0:T(1024)S(1)} %pad_clamp_fusion.1), kind=kCustom, calls=%fused_computation | custom fusion | bytes 41944320 | tf_op jit(solution)/shard_map/gather | solution.py:34
  37.3 0.0 copy-start.2
  37.3 4.1 all-to-all-start.1
  41.4 0.0 copy-done.2
  41.5 467.0 %all-to-all-done.1 = bf16[32,10,128,256]{3,2,1,0:T(8,128)(2,1)} async-done(((bf16[32,10,128,256]{3,2,1,0:T(8,128)(2,1)}), bf16[32,10,128,256]{3,2,1,0:T(8,128)(2,1)}, u32[]{:S(2)}, u32[]{:S(2)}) %all-to-all-start.1) | async-done | bytes 20971552 | tf_op jit(solution)/shard_map/all_to_all | solution.py:33
  508.5 18.5 %pad_maximum_fusion = bf16[352,128,256]{2,1,0:T(8,128)(2,1)} fusion(bf16[320,128,256]{2,1,0:T(8,128)(2,1)} %bitcast.6, bf16[32,128,256]{2,1,0:T(8,128)(2,1)S(1)} %bitcast.23), kind=kLoop, calls=%fused_computation.3 | loop fusion | flops 11534336 | bytes 46137344 | tf_op jit(solution)/shard_map/concatenate | solution.py:40
  527.0 15.8 %gather_fusion.1 = bf16[192,128,256]{2,1,0:T(8,128)(2,1)} fusion(bf16[352,128,256]{2,1,0:T(8,128)(2,1)} %pad_maximum_fusion, s32[1024]{0:T(1024)S(1)} %pad_clamp_fusion), kind=kCustom, calls=%fused_computation.1 | custom fusion | bytes 25166592 | tf_op jit(solution)/shard_map/gather | solution.py:42
  542.7 12.3 %fusion = f32[32,256,128,1]{1,2,3,0:T(8,128)} fusion(bf16[32,6,128,256]{3,2,1,0:T(8,128)(2,1)} %bitcast.26, s32[32,6,128,128]{3,2,1,0:T(8,128)} %param.7), kind=kOutput, calls=%fused_computation.4 | convolution fusion | flops 1613758464 | bytes 29360128 | tf_op jit(solution)/shard_map/rtij,rtjd->rid/dot_general | solution.py:43
  555.0 2.6 fusion.5
  557.6 0.0 copy-done
  557.7 1.6 multiply_reduce_fusion
  559.3 0.4 multiply_convert_fusion
  559.7 2.5 copy.18
  (10 shorter events, 0.1 us)
Async XLA Ops:
  0.0 557.6 %copy-start = (bf16[512,256]{1,0:T(8,128)(2,1)S(1)}, bf16[512,256]{1,0:T(8,128)(2,1)}, u32[]{:S(2)}) copy-start(bf16[512,256]{1,0:T(8,128)(2,1)} %param.9) | copy-start | bytes 786436
  0.0 26.4 %copy-start.1 = (bf16[4096,256]{1,0:T(8,128)(2,1)S(1)}, bf16[4096,256]{1,0:T(8,128)(2,1)}, u32[]{:S(2)}) copy-start(bf16[4096,256]{1,0:T(8,128)(2,1)} %param.5) | copy-start | bytes 6291460
  37.3 4.1 copy-start.2
  37.3 471.2 %all-to-all-start.1 = ((bf16[32,10,128,256]{3,2,1,0:T(8,128)(2,1)}), bf16[32,10,128,256]{3,2,1,0:T(8,128)(2,1)}, u32[]{:S(2)}, u32[]{:S(2)}) async-start(bf16[32,10,128,256]{3,2,1,0:T(8,128)(2,1)} %bitcast.25), calls=%async_computation.1 | async-start | bytes 41943040 | tf_op jit(solution)/shard_map/all_to_all | solution.py:33
where the time goes:
time: 563 us; the launch traced here: 562 us
  waiting for transfers between devices  467 us (83%)
  local copies, waits for them, and re-layouts  41 us (7%)
  other arithmetic  21.7 us (4%)
  blocking collectives  14.2 us (3%)
  matrix products  13.9 us (2%)
    all_to_all x1, waiting for transfers between devices, on_device(): lax.all_to_all(local_blocks[lax.all_to_all(requests, 'rows', split_axis=0...  467 us
    concatenate x1, other arithmetic, on_device(): jnp.concatenate([local_blocks, received.reshape(-1, tile, width)], axis=0)  18.5 us
    gather x1, local copies, waits for them, and re-layouts, on_device(): picked = table[slots].reshape(blocks_here, per_block, tile, width)  15.8 us
    all_to_all x1, blocking collectives, on_device(): lax.all_to_all(requests, 'rows', split_axis=0, concat_axis=0, tiled=True)  14.2 us
    dot_general x1, matrix products, on_device(): jnp.einsum('rtij,rtjd->rid', tile_masks.astype(jnp.bfloat16), picked, pre...  12.3 us
  transfers between devices with their start and end apart: 1, of which 1 were waited for; matrix products, arithmetic and copies ran while one was open for 0% of the time, Pallas kernels for 0%

commit v1 on v0

v1 whole, which is shorter than its diff:
```python
import functools

import jax
import jax.numpy as jnp
from jax import lax
from jax.experimental import pallas as pl
from jax.experimental.pallas import tpu as pltpu
from jax.sharding import PartitionSpec as P

REM_PB = 4
PLANES = 4


def arrival_order(planes):
    order = []
    for z in range(planes):
        mine = [(0, 0)]
        for step in range(1, planes):
            if z + step < planes:
                mine.append((step, -1))
            if z - step >= 0:
                mine.append((step, 1))
        order.append(mine)
    return order


def pick_row(table, z):
    return jnp.sum(jnp.where(jnp.arange(table.shape[0])[:, None] == z, table, 0), axis=0)


def choose_kernel(which, ids, *refs, sources, outputs, capacity):
    froms, tos, sems = refs[:sources], refs[sources : sources + outputs], refs[-1]
    for j, source in enumerate(froms):

        @pl.when(which[0] == j)
        def _():
            copies = []
            for o, out in enumerate(tos):
                for s in range(capacity):
                    n = o * capacity + s
                    copies.append(pltpu.make_async_copy(source.at[ids[n]], out.at[s], sems.at[n]))
            for copy in copies:
                copy.start()
            for copy in copies:
                copy.wait()


def choose(which, ids, froms, outputs, capacity):
    block = froms[0].shape[1:]
    moved = outputs * capacity * block[0] * block[1] * 2
    return pl.pallas_call(
        functools.partial(choose_kernel, sources=len(froms), outputs=outputs, capacity=capacity),
        grid_spec=pltpu.PrefetchScalarGridSpec(
            num_scalar_prefetch=2,
            grid=(1,),
            in_specs=[pl.BlockSpec(memory_space=pl.ANY)] * len(froms),
            out_specs=[pl.BlockSpec(memory_space=pl.ANY)] * outputs,
            scratch_shapes=[pltpu.SemaphoreType.DMA((outputs * capacity,))],
        ),
        out_shape=[jax.ShapeDtypeStruct((capacity,) + block, froms[0].dtype)] * outputs,
        cost_estimate=pl.CostEstimate(flops=0, bytes_accessed=2 * moved, transcendentals=0),
        name="choose_blocks",
    )(which, ids, *froms)


def layer_kernel(slots, *refs, pieces, starts, per_block):
    froms = refs[:pieces]
    masks, degree, weight, out, table, sems = refs[pieces:]
    row = pl.program_id(0)
    tile, width = table.shape[1:]

    @pl.when(row == 0)
    def _():
        copies = [
            pltpu.make_async_copy(piece, table.at[pl.ds(at, piece.shape[0])], sems.at[n])
            for n, (piece, at) in enumerate(zip(froms, starts))
        ]
        for copy in copies:
            copy.start()
        for copy in copies:
            copy.wait()

    sums = jnp.zeros((tile, width), jnp.float32)
    for t in range(per_block):
        mask = masks[0, t].astype(jnp.float32).astype(jnp.bfloat16)
        picked = table[slots[row * per_block + t]]
        sums = sums + jnp.dot(mask, picked, preferred_element_type=jnp.float32)
    count = jnp.broadcast_to(degree[pl.ds(row, 1), :].astype(jnp.float32), (tile, tile)).T
    count = jnp.concatenate([count] * (width // tile), axis=1)
    mean = (sums / count).astype(jnp.bfloat16)
    hidden = jnp.dot(table[row], weight[:width], preferred_element_type=jnp.float32)
    hidden = hidden + jnp.dot(mean, weight[width:], preferred_element_type=jnp.float32)
    hidden = jnp.maximum(hidden, 0.0)
    scale = lax.rsqrt(jnp.sum(hidden * hidden, axis=1, keepdims=True) + 1e-06)
    out[...] = (hidden * scale).astype(jnp.bfloat16)


def layer(slots, froms, starts, blocks_in_table, tile_masks, degree, weight):
    rows, per_block, tile, _ = tile_masks.shape
    width = weight.shape[0] // 2
    out_width = weight.shape[1]
    return pl.pallas_call(
        functools.partial(layer_kernel, pieces=len(froms), starts=starts, per_block=per_block),
        grid_spec=pltpu.PrefetchScalarGridSpec(
            num_scalar_prefetch=1,
            grid=(rows,),
            in_specs=[pl.BlockSpec(memory_space=pl.ANY)] * len(froms)
            + [
                pl.BlockSpec((1, per_block, tile, tile), lambda r, s: (r, 0, 0, 0)),
                pl.BlockSpec((rows, tile), lambda r, s: (0, 0)),
                pl.BlockSpec((2 * width, out_width), lambda r, s: (0, 0)),
            ],
            out_specs=pl.BlockSpec((tile, out_width), lambda r, s: (r, 0)),
            scratch_shapes=[
                pltpu.VMEM((blocks_in_table, tile, width), jnp.bfloat16),
                pltpu.SemaphoreType.DMA((len(froms),)),
            ],
        ),
        out_shape=jax.ShapeDtypeStruct((rows * tile, out_width), jnp.bfloat16),
        compiler_params=pltpu.CompilerParams(vmem_limit_bytes=40 * 1024 * 1024),
        cost_estimate=pl.CostEstimate(
            flops=2 * rows * tile * (per_block * tile + 2 * width) * width,
            bytes_accessed=rows * per_block * tile * tile * 4 + blocks_in_table * tile * width * 2,
            transcendentals=rows * tile,
        ),
        name="sage_layer",
    )(slots, *froms, tile_masks, degree, weight)


def on_device(features, tile_cols, tile_masks, degree, weight):
    blocks_here, per_block = tile_cols.shape
    tile = tile_masks.shape[2]
    width = features.shape[1]
    peers = lax.axis_size("rows")
    planes = PLANES if peers % PLANES == 0 else 1
    plane = peers // planes
    myself = lax.axis_index("rows")
    z, p = myself // plane, myself % plane
    capacity = max(2, (REM_PB * blocks_here + peers - 2) // (peers - 1))
    order = arrival_order(planes)
    local = features.reshape(blocks_here, tile, width)

    arrived = {(0, 0): local}
    for step in range(1, planes):
        for way in (-1, 1):
            held = arrived[(step - 1, way)] if step > 1 else local
            pairs = [
                (a * plane + q, (a + way) * plane + q)
                for a in range(planes)
                if 0 <= a + way < planes and 0 <= a - way * (step - 1) < planes
                for q in range(plane)
            ]
            arrived[(step, way)] = lax.ppermute(held, "rows", pairs)

    columns = tile_cols.reshape(-1)
    all_columns = lax.all_gather(columns, "rows")
    partners = p ^ jnp.arange(plane, dtype=jnp.int32)
    asked = all_columns[z * plane + partners]
    plane_at = jnp.array(
        [[a - way * step for step, way in order[a]] for a in range(planes)], jnp.int32
    )
    sources = pick_row(plane_at, z)
    line = sources * plane + p
    blocks = jnp.arange(blocks_here, dtype=jnp.int32)
    wanted = (line[:, None] * blocks_here + blocks[None, :]).reshape(-1)
    need = jnp.any(asked[:, :, None] == wanted[None, None, :], axis=1)
    need = need.reshape(plane, planes, blocks_here).astype(jnp.int32)
    below = blocks[:, None] > blocks[None, :]
    place = jnp.sum(jnp.where(below, need[:, :, None, :], 0), axis=3)
    seat = jnp.arange(capacity, dtype=jnp.int32)
    chosen = jnp.sum(
        jnp.where(
            (need[:, :, None, :] == 1) & (place[:, :, None, :] == seat[:, None]), blocks, 0
        ),
        axis=3,
    )

    owners, within = columns // blocks_here, columns % blocks_here
    positions = jnp.arange(columns.shape[0], dtype=jnp.int32)
    same = columns[:, None] == columns[None, :]
    first = ~jnp.any(same & (positions[None, :] < positions[:, None]), axis=1)
    ahead = (owners[:, None] == owners[None, :]) & (columns[None, :] < columns[:, None])
    ranks = jnp.sum(ahead & first[None, :], axis=1, dtype=jnp.int32)
    stage_at = jnp.array(
        [
            [[a - way * step for step, way in order[a]].index(b) for b in range(planes)]
            for a in range(planes)
        ],
        jnp.int32,
    )
    stages = pick_row(stage_at, z)
    their_plane = owners // plane
    stage = jnp.sum(
        jnp.where(their_plane[:, None] == jnp.arange(planes), stages[None, :], 0), axis=1
    )
    partner = (owners % plane) ^ p
    slots = jnp.where(
        owners == myself,
        within,
        blocks_here + (stage * plane + partner) * capacity + ranks,
    )

    froms, starts = [local], [0]
    for k in range(planes):
        kinds = sorted(set(order[a][k] for a in range(planes)))
        which_at = jnp.array([[kinds.index(order[a][k])] for a in range(planes)], jnp.int32)
        skip = 1 if k == 0 else 0
        ids = chosen[skip:, k, :].reshape(-1)
        picked = choose(
            pick_row(which_at, z), ids, [arrived[kind] for kind in kinds], plane - skip, capacity
        )
        for m in range(skip, plane):
            part = picked[m - skip]
            if m > 0:
                pairs = [
                    (a * plane + q, a * plane + (q ^ m)) for a in range(planes) for q in range(plane)
                ]
                part = lax.ppermute(part, "rows", pairs)
            froms.append(part)
            starts.append(blocks_here + (k * plane + m) * capacity)

    return layer(
        slots,
        froms,
        tuple(starts),
        blocks_here + peers * capacity,
        tile_masks,
        degree.reshape(blocks_here, tile),
        weight,
    )


def solution(mesh):
    in_specs = (P("rows", None), P("rows", None), P("rows", None, None, None), P("rows"), P())
    out_specs = P("rows", None)
    return jax.shard_map(
        on_device, mesh=mesh, in_specs=in_specs, out_specs=out_specs, check_vma=False
    )
```

time: 563 us -> 601 us (1.067)
  Pallas kernels: 0 us -> 349 us
  waiting for transfers between devices: 467 us -> 120 us
  blocking collectives: 14.2 us -> 73.8 us
  starting transfers between devices: 4.11 us -> 35.4 us
  local copies, waits for them, and re-layouts: 41 us -> 14.3 us
  other arithmetic: 21.7 us -> 4.8 us
  matrix products: 13.9 us -> 0 us
    all_to_all x1 -> x0, waiting for transfers between devices: 467 us -> none  [on_device(): lax.all_to_all(local_blocks[lax.all_to_all(requests, 'rows', split_axis=0...]
    pallas_call x0 -> x5, Pallas kernels: none -> 349 us  [the longest x4 318 us: choose(): pl.pallas_call(functools.partial(choose_kernel, sources=len(froms), outpu...]
    ppermute x0 -> x34, waiting for transfers between devices: none -> 120 us  [the longest x28 74.2 us: on_device(): part = lax.ppermute(part, 'rows', pairs)]
    all_gather x0 -> x1, blocking collectives: none -> 73.8 us  [on_device(): all_columns = lax.all_gather(columns, 'rows')]
    ppermute x0 -> x34, starting transfers between devices: none -> 35.4 us  [the longest x28 22.3 us: on_device(): part = lax.ppermute(part, 'rows', pairs)]
    gather x2 -> x1, local copies, waits for them, and re-layouts: 26.7 us -> 0.56 us  [on_device(): asked = all_columns[z * plane + partners]]
    concatenate x2 -> x0, other arithmetic: 18.5 us -> none  [the longest x1 18.5 us: on_device(): jnp.concatenate([local_blocks, received.reshape(-1, tile, width)], axis=0)]
    all_to_all x1 -> x0, blocking collectives: 14.2 us -> none  [on_device(): lax.all_to_all(requests, 'rows', split_axis=0, concat_axis=0, tiled=True)]
  transfers between devices with their start and end apart: 1 -> 34, of which waited for: 1 -> 10; matrix products, arithmetic and copies ran while one was open for 0% -> 2% of each run, Pallas kernels for 0% -> 53%
where the time goes in v1:
time: 601 us; the launch traced here: 598 us
  Pallas kernels  349 us (58%)
  waiting for transfers between devices  120 us (20%)
  blocking collectives  73.8 us (12%)
  starting transfers between devices  35.4 us (6%)
  local copies, waits for them, and re-layouts  14.3 us (2%)
    pallas_call x4, Pallas kernels, choose(): pl.pallas_call(functools.partial(choose_kernel, sources=len(froms), outpu...  318 us
    ppermute x28, waiting for transfers between devices, on_device(): part = lax.ppermute(part, 'rows', pairs)  74.2 us
    all_gather x1, blocking collectives, on_device(): all_columns = lax.all_gather(columns, 'rows')  73.8 us
    ppermute x6, waiting for transfers between devices, on_device(): arrived[step, way] = lax.ppermute(held, 'rows', pairs)  46 us
    pallas_call x1, Pallas kernels, layer(): pl.pallas_call(functools.partial(layer_kernel, pieces=len(froms), starts=...  30.6 us
    ppermute x28, starting transfers between devices, on_device(): part = lax.ppermute(part, 'rows', pairs)  22.3 us
    ppermute x6, starting transfers between devices, on_device(): arrived[step, way] = lax.ppermute(held, 'rows', pairs)  13.1 us
  transfers between devices with their start and end apart: 34, of which 10 were waited for; matrix products, arithmetic and copies ran while one was open for 2% of the time, Pallas kernels for 53%

profile of v1, /device:TPU:0, one launch (start us, length us, event | category | flops | bytes accessed | tf_op | source)
XLA Modules:
  0.0 597.7 jit_solution(3866938784550866983)
XLA Ops:
  0.0 5.2 collective-permute-start.8
  5.2 1.3 collective-permute-start.7
  6.5 43.8 %collective-permute-done.8.refs_1_.refs_0_ = bf16[32,128,256]{2,1,0:T(8,128)(2,1)S(1)} collective-permute-done((bf16[32,128,256]{2,1,0:T(8,128)(2,1)}, bf16[32,128,256]{2,1,0:T(8,128)(2,1)S(1)}, u32[]{:S(2)}, u32[]{:S(2)}) %collective-permute-start.8) | collective-permute-done | bytes 2097184 | tf_op jit(solution)/shard_map/ppermute | solution.py:153
  50.2 2.0 collective-permute-start.17
  52.2 2.2 collective-permute-done.7.refs_0_
  54.5 1.3 collective-permute-start.16
  55.8 0.8 select_reduce_fusion.3
  56.8 0.8 copy.18
  57.6 73.8 %all-gather = s32[32,1,192]{2,1,0:T(1,128)S(1)} all-gather(s32[1,1,192]{2,1,0:T(1,128)S(1)} %reshape.178), channel_id=1, replica_groups=mesh['rows'=32] {'rows'}, dimensions={0}, use_global_device_ids=true | all-gather | bytes 25344 | tf_op jit(solution)/shard_map/all_gather | solution.py:156
  132.4 2.1 collective-permute-start.26
  134.5 1.3 collective-permute-start.25
  137.0 0.7 reshape_squeeze.12.ids
  137.7 71.6 %choose_blocks.4 = (bf16[5,128,256]{2,1,0:T(8,128)(2,1)}, bf16[5,128,256]{2,1,0:T(8,128)(2,1)}, bf16[5,128,256]{2,1,0:T(8,128)(2,1)}, bf16[5,128,256]{2,1,0:T(8,...) custom-call(s32[1]{0:T(128)} %constant.97.which, ...), custom_call_target="tpu_custom_call" | custom-call | bytes 4587520 | tf_op jit(solution)/shard_map/choose_blocks/pallas_call | solution.py:51
  209.7 1.5 collective-permute-start.2
  211.2 9.2 %collective-permute-done.1.refs_2_ = bf16[5,128,256]{2,1,0:T(8,128)(2,1)S(1)} collective-permute-done((bf16[5,128,256]{2,1,0:T(8,128)(2,1)}, bf16[5,128,256]{2,1,0:T(8,128)(2,1)S(1)}, u32[]{:S(2)}, u32[]{:S(2)}) %collective-permute-start.1) | collective-permute-done | bytes 327712 | tf_op jit(solution)/shard_map/ppermute | solution.py:218
  220.4 5.5 collective-permute-done.2.refs_3_
  226.0 3.1 collective-permute-start.6
  229.7 0.7 select_reduce_fusion.7
  230.4 82.2 %choose_blocks.5 = (bf16[5,128,256]{2,1,0:T(8,128)(2,1)}, bf16[5,128,256]{2,1,0:T(8,128)(2,1)}, bf16[5,128,256]{2,1,0:T(8,128)(2,1)}, bf16[5,128,256]{2,1,0:T(8,...) custom-call(s32[1]{0:T(128)} %bitcast.2.which, ...), custom_call_target="tpu_custom_call" | custom-call | bytes 5242880 | tf_op jit(solution)/shard_map/choose_blocks/pallas_call | solution.py:51
  313.3 1.4 collective-permute-start.11
  314.7 8.9 %collective-permute-done.10.refs_10_ = bf16[5,128,256]{2,1,0:T(8,128)(2,1)S(1)} collective-permute-done((bf16[5,128,256]{2,1,0:T(8,128)(2,1)}, bf16[5,128,256]{2,1,0:T(8,128)(2,1)S(1)}, u32[]{:S(2)}, u32[]{:S(2)}) %collective-permute-start.10) | collective-permute-done | bytes 327712 | tf_op jit(solution)/shard_map/ppermute | solution.py:218
  323.6 6.1 %collective-permute-done.11.refs_11_ = bf16[5,128,256]{2,1,0:T(8,128)(2,1)S(1)} collective-permute-done((bf16[5,128,256]{2,1,0:T(8,128)(2,1)}, bf16[5,128,256]{2,1,0:T(8,128)(2,1)S(1)}, u32[]{:S(2)}, u32[]{:S(2)}) %collective-permute-start.11) | collective-permute-done | bytes 327712 | tf_op jit(solution)/shard_map/ppermute | solution.py:218
  330.7 0.7 select_reduce_fusion.6
  331.3 82.2 %choose_blocks.6 = (bf16[5,128,256]{2,1,0:T(8,128)(2,1)}, bf16[5,128,256]{2,1,0:T(8,128)(2,1)}, bf16[5,128,256]{2,1,0:T(8,128)(2,1)}, bf16[5,128,256]{2,1,0:T(8,...) custom-call(s32[1]{0:T(128)} %bitcast.3.which, ...), custom_call_target="tpu_custom_call" | custom-call | bytes 5242880 | tf_op jit(solution)/shard_map/choose_blocks/pallas_call | solution.py:51
  413.6 2.7 collective-permute-start.15
  416.6 1.6 collective-permute-start.20
  419.2 0.7 select_reduce_fusion.5
  419.9 82.4 %choose_blocks.7 = (bf16[5,128,256]{2,1,0:T(8,128)(2,1)}, bf16[5,128,256]{2,1,0:T(8,128)(2,1)}, bf16[5,128,256]{2,1,0:T(8,128)(2,1)}, bf16[5,128,256]{2,1,0:T(8,...) custom-call(s32[1]{0:T(128)} %bitcast.4.which, ...), custom_call_target="tpu_custom_call" | custom-call | bytes 5242880 | tf_op jit(solution)/shard_map/choose_blocks/pallas_call | solution.py:51
  502.2 1.8 collective-permute-start.22
  504.4 2.3 collective-permute-start.24
  507.5 18.7 %collective-permute-done.22.refs_21_ = bf16[5,128,256]{2,1,0:T(8,128)(2,1)S(1)} collective-permute-done((bf16[5,128,256]{2,1,0:T(8,128)(2,1)}, bf16[5,128,256]{2,1,0:T(8,128)(2,1)S(1)}, u32[]{:S(2)}, u32[]{:S(2)}) %collective-permute-start.22) | collective-permute-done | bytes 327712 | tf_op jit(solution)/shard_map/ppermute | solution.py:218
  526.2 0.9 collective-permute-start.29
  527.2 1.5 collective-permute-start.30
  528.7 2.6 collective-permute-start.32
  531.7 4.1 collective-permute-done.29.refs_27_
  535.8 15.2 %collective-permute-done.30.refs_28_ = bf16[5,128,256]{2,1,0:T(8,128)(2,1)S(1)} collective-permute-done((bf16[5,128,256]{2,1,0:T(8,128)(2,1)}, bf16[5,128,256]{2,1,0:T(8,128)(2,1)S(1)}, u32[]{:S(2)}, u32[]{:S(2)}) %collective-permute-start.30) | collective-permute-done | bytes 327712 | tf_op jit(solution)/shard_map/ppermute | solution.py:218
  551.1 6.3 %collective-permute-done.31.refs_29_ = bf16[5,128,256]{2,1,0:T(8,128)(2,1)S(1)} collective-permute-done((bf16[5,128,256]{2,1,0:T(8,128)(2,1)}, bf16[5,128,256]{2,1,0:T(8,128)(2,1)S(1)}, u32[]{:S(2)}, u32[]{:S(2)}) %collective-permute-start.31) | collective-permute-done | bytes 327712 | tf_op jit(solution)/shard_map/ppermute | solution.py:218
  557.4 1.0 copy-done.2
  558.4 1.0 copy-done.4
  559.4 1.0 copy-done.6
  560.4 1.0 copy-done.7
  561.3 1.0 copy-done.9
  562.3 1.0 copy-done.11
  563.3 1.0 copy-done.13
  564.2 1.0 copy-done.14
  565.2 1.0 copy-done.15
  566.2 0.9 copy-done.16
  567.1 30.6 %sage_layer.1 = bf16[4096,256]{1,0:T(8,128)(2,1)} custom-call(s32[192]{0:T(256)S(1)} %compare_select_fusion.1.slots, bf16[32,128,256]{2,1,0:T(8,128)(2,1)S(1)} %bitcast.21, bf16[5,128,256]{2,1,0:T(8,128)(2,1)S(1)} %collective-permute-done.refs_1_, bf16[5,128,256]{2,1,0:T(8,128)(2,1)S(1)} %collective-permute-done.1.refs_2_, ...), custom_call_target="tpu_custom_call" | custom-call | flops 2684354560 | bytes 25165824 | tf_op jit(solution)/shard_map/sage_layer/pallas_call | solution.py:102
  (110 shorter events, 8.1 us)
Async XLA Ops:
  0.0 229.7 %copy-start.21 = (s32[4,1]{0,1:T(1,128)S(1)}, s32[4,1]{0,1:T(1,128)}, u32[]{:S(2)}) copy-start(s32[4,1]{0,1:T(1,128)} %constant.93.clone) | copy-start | bytes 52
  0.0 50.2 %collective-permute-start.8 = (bf16[32,128,256]{2,1,0:T(8,128)(2,1)}, bf16[32,128,256]{2,1,0:T(8,128)(2,1)S(1)}, u32[]{:S(2)}, u32[]{:S(2)}) collective-permute-start(bf16[32,128,256]{2,1,0:T(8,128)(2,1)} %bitcast.18), channel_id=1, source_target_pairs={{0,8},{1,9},{2,10},{3,11},{4,12},{5,13},{6,14},{7,15},{8,16},{9,17... | collective-permute-start | bytes 6291464 | tf_op jit(solution)/shard_map/ppermute | solution.py:153
  5.2 49.3 %collective-permute-start.7 = (bf16[32,128,256]{2,1,0:T(8,128)(2,1)}, bf16[32,128,256]{2,1,0:T(8,128)(2,1)}, u32[]{:S(2)}, u32[]{:S(2)}) collective-permute-start(bf16[32,128,256]{2,1,0:T(8,128)(2,1)} %bitcast.19), channel_id=1, source_target_pairs={{8,0},{9,1},{10,2},{11,3},{12,4},{13,5},{14,6},{15,7},{16,8},{17,9... | collective-permute-start | bytes 6291464 | tf_op jit(solution)/shard_map/ppermute | solution.py:153
  50.2 170.2 %copy-start.18 = (bf16[32,128,256]{2,1,0:T(8,128)(2,1)}, bf16[32,128,256]{2,1,0:T(8,128)(2,1)S(1)}, u32[]{:S(2)}) copy-start(bf16[32,128,256]{2,1,0:T(8,128)(2,1)S(1)} %collective-permute-done.8.refs_1_.refs_0_) | copy-start | bytes 6291460
  50.2 82.1 %collective-permute-start.17 = (bf16[32,128,256]{2,1,0:T(8,128)(2,1)S(1)}, bf16[32,128,256]{2,1,0:T(8,128)(2,1)}, u32[]{:S(2)}, u32[]{:S(2)}) collective-permute-start(bf16[32,128,256]{2,1,0:T(8,128)(2,1)S(1)} %collective-permute-done.8.refs_1_.refs_0_), channel_id=1, source_target_pairs={{8,16},{9,17},{10,18},{11,19},{12,20},{13,21},{14,22},{15,23},{16,... | collective-permute-start | bytes 6291464 | tf_op jit(solution)/shard_map/ppermute | solution.py:153
  54.5 80.0 %collective-permute-start.16 = (bf16[32,128,256]{2,1,0:T(8,128)(2,1)}, bf16[32,128,256]{2,1,0:T(8,128)(2,1)}, u32[]{:S(2)}, u32[]{:S(2)}) collective-permute-start(bf16[32,128,256]{2,1,0:T(8,128)(2,1)} %collective-permute-done.7.refs_0_), channel_id=1, source_target_pairs={{8,0},{9,1},{10,2},{11,3},{12,4},{13,5},{14,6},{15,7},{16,8},{17,9... | collective-permute-start | bytes 6291464 | tf_op jit(solution)/shard_map/ppermute | solution.py:153
  132.4 284.2 %collective-permute-start.26 = (bf16[32,128,256]{2,1,0:T(8,128)(2,1)}, bf16[32,128,256]{2,1,0:T(8,128)(2,1)}, u32[]{:S(2)}, u32[]{:S(2)}) collective-permute-start(bf16[32,128,256]{2,1,0:T(8,128)(2,1)} %collective-permute-done.17.refs_2_.refs_1_), channel_id=1, source_target_pairs={{16,24},{17,25},{18,26},{19,27},{20,28},{21,29},{22,30},{23,31}} | collective-permute-start | bytes 6291464 | tf_op jit(solution)/shard_map/ppermute | solution.py:153
  134.5 283.7 %collective-permute-start.25 = (bf16[32,128,256]{2,1,0:T(8,128)(2,1)}, bf16[32,128,256]{2,1,0:T(8,128)(2,1)}, u32[]{:S(2)}, u32[]{:S(2)}) collective-permute-start(bf16[32,128,256]{2,1,0:T(8,128)(2,1)} %collective-permute-done.16.refs_1_.refs_0_), channel_id=1, source_target_pairs={{8,0},{9,1},{10,2},{11,3},{12,4},{13,5},{14,6},{15,7}} | collective-permute-start | bytes 6291464 | tf_op jit(solution)/shard_map/ppermute | solution.py:153
  209.3 1.9 collective-permute-start
  209.7 10.8 %collective-permute-start.1 = (bf16[5,128,256]{2,1,0:T(8,128)(2,1)}, bf16[5,128,256]{2,1,0:T(8,128)(2,1)S(1)}, u32[]{:S(2)}, u32[]{:S(2)}) collective-permute-start(bf16[5,128,256]{2,1,0:T(8,128)(2,1)} %get-tuple-element.37), channel_id=1, source_target_pairs={{0,2},{1,3},{2,0},{3,1},{4,6},{5,7},{6,4},{7,5},{8,10},{9,11},{10,... | collective-permute-start | bytes 983048 | tf_op jit(solution)/shard_map/ppermute | solution.py:218
  209.7 16.3 %collective-permute-start.2 = (bf16[5,128,256]{2,1,0:T(8,128)(2,1)}, bf16[5,128,256]{2,1,0:T(8,128)(2,1)S(1)}, u32[]{:S(2)}, u32[]{:S(2)}) collective-permute-start(bf16[5,128,256]{2,1,0:T(8,128)(2,1)} %get-tuple-element.38), channel_id=1, source_target_pairs={{0,3},{1,2},{2,1},{3,0},{4,7},{5,6},{6,5},{7,4},{8,11},{9,10},{10,... | collective-permute-start | bytes 983048 | tf_op jit(solution)/shard_map/ppermute | solution.py:218
  211.2 14.7 %collective-permute-start.3 = (bf16[5,128,256]{2,1,0:T(8,128)(2,1)}, bf16[5,128,256]{2,1,0:T(8,128)(2,1)S(1)}, u32[]{:S(2)}, u32[]{:S(2)}) collective-permute-start(bf16[5,128,256]{2,1,0:T(8,128)(2,1)} %get-tuple-element.39), channel_id=1, source_target_pairs={{0,4},{1,5},{2,6},{3,7},{4,0},{5,1},{6,2},{7,3},{8,12},{9,13},{10,... | collective-permute-start | bytes 983048 | tf_op jit(solution)/shard_map/ppermute | solution.py:218
  220.4 92.3 %collective-permute-start.4 = (bf16[5,128,256]{2,1,0:T(8,128)(2,1)}, bf16[5,128,256]{2,1,0:T(8,128)(2,1)S(1)}, u32[]{:S(2)}, u32[]{:S(2)}) collective-permute-start(bf16[5,128,256]{2,1,0:T(8,128)(2,1)} %get-tuple-element.40), channel_id=1, source_target_pairs={{0,5},{1,4},{2,7},{3,6},{4,1},{5,0},{6,3},{7,2},{8,13},{9,12},{10,... | collective-permute-start | bytes 983048 | tf_op jit(solution)/shard_map/ppermute | solution.py:218
  225.9 86.8 %collective-permute-start.5 = (bf16[5,128,256]{2,1,0:T(8,128)(2,1)}, bf16[5,128,256]{2,1,0:T(8,128)(2,1)S(1)}, u32[]{:S(2)}, u32[]{:S(2)}) collective-permute-start(bf16[5,128,256]{2,1,0:T(8,128)(2,1)} %get-tuple-element.41), channel_id=1, source_target_pairs={{0,6},{1,7},{2,4},{3,5},{4,2},{5,3},{6,0},{7,1},{8,14},{9,15},{10,... | collective-permute-start | bytes 983048 | tf_op jit(solution)/shard_map/ppermute | solution.py:218
  226.0 87.3 %collective-permute-start.6 = (bf16[5,128,256]{2,1,0:T(8,128)(2,1)}, bf16[5,128,256]{2,1,0:T(8,128)(2,1)S(1)}, u32[]{:S(2)}, u32[]{:S(2)}) collective-permute-start(bf16[5,128,256]{2,1,0:T(8,128)(2,1)} %get-tuple-element.42), channel_id=1, source_target_pairs={{0,7},{1,6},{2,5},{3,4},{4,3},{5,2},{6,1},{7,0},{8,15},{9,14},{10,... | collective-permute-start | bytes 983048 | tf_op jit(solution)/shard_map/ppermute | solution.py:218
  230.4 100.2 %copy-start.20 = (s32[4,1]{0,1:T(1,128)S(1)}, s32[4,1]{0,1:T(1,128)}, u32[]{:S(2)}) copy-start(s32[4,1]{0,1:T(1,128)} %constant.94.clone) | copy-start | bytes 52
  312.7 100.8 %copy-start.1 = (bf16[5,128,256]{2,1,0:T(8,128)(2,1)}, bf16[5,128,256]{2,1,0:T(8,128)(2,1)S(1)}, u32[]{:S(2)}) copy-start(bf16[5,128,256]{2,1,0:T(8,128)(2,1)S(1)} %collective-permute-done.4.refs_5_) | copy-start | bytes 983044
  312.7 2.0 collective-permute-start.9
  312.8 100.7 %copy-start.3 = (bf16[5,128,256]{2,1,0:T(8,128)(2,1)}, bf16[5,128,256]{2,1,0:T(8,128)(2,1)S(1)}, u32[]{:S(2)}) copy-start(bf16[5,128,256]{2,1,0:T(8,128)(2,1)S(1)} %collective-permute-done.5.refs_6_) | copy-start | bytes 983044
  312.8 10.8 %collective-permute-start.10 = (bf16[5,128,256]{2,1,0:T(8,128)(2,1)}, bf16[5,128,256]{2,1,0:T(8,128)(2,1)S(1)}, u32[]{:S(2)}, u32[]{:S(2)}) collective-permute-start(bf16[5,128,256]{2,1,0:T(8,128)(2,1)} %get-tuple-element.45), channel_id=1, source_target_pairs={{0,2},{1,3},{2,0},{3,1},{4,6},{5,7},{6,4},{7,5},{8,10},{9,11},{10,... | collective-permute-start | bytes 983048 | tf_op jit(solution)/shard_map/ppermute | solution.py:218
  313.3 100.2 %copy-start.5 = (bf16[5,128,256]{2,1,0:T(8,128)(2,1)}, bf16[5,128,256]{2,1,0:T(8,128)(2,1)S(1)}, u32[]{:S(2)}) copy-start(bf16[5,128,256]{2,1,0:T(8,128)(2,1)S(1)} %collective-permute-done.6.refs_7_) | copy-start | bytes 983044
  313.3 16.4 %collective-permute-start.11 = (bf16[5,128,256]{2,1,0:T(8,128)(2,1)}, bf16[5,128,256]{2,1,0:T(8,128)(2,1)S(1)}, u32[]{:S(2)}, u32[]{:S(2)}) collective-permute-start(bf16[5,128,256]{2,1,0:T(8,128)(2,1)} %get-tuple-element.46), channel_id=1, source_target_pairs={{0,3},{1,2},{2,1},{3,0},{4,7},{5,6},{6,5},{7,4},{8,11},{9,10},{10,... | collective-permute-start | bytes 983048 | tf_op jit(solution)/shard_map/ppermute | solution.py:218
  314.7 98.9 %copy-start.8 = (bf16[5,128,256]{2,1,0:T(8,128)(2,1)}, bf16[5,128,256]{2,1,0:T(8,128)(2,1)S(1)}, u32[]{:S(2)}) copy-start(bf16[5,128,256]{2,1,0:T(8,128)(2,1)S(1)} %collective-permute-done.9.refs_9_) | copy-start | bytes 983044
  314.7 98.9 %collective-permute-start.12 = (bf16[5,128,256]{2,1,0:T(8,128)(2,1)}, bf16[5,128,256]{2,1,0:T(8,128)(2,1)}, u32[]{:S(2)}, u32[]{:S(2)}) collective-permute-start(bf16[5,128,256]{2,1,0:T(8,128)(2,1)} %get-tuple-element.47), channel_id=1, source_target_pairs={{0,4},{1,5},{2,6},{3,7},{4,0},{5,1},{6,2},{7,3},{8,12},{9,13},{10,... | collective-permute-start | bytes 983048 | tf_op jit(solution)/shard_map/ppermute | solution.py:218
  323.6 90.0 %copy-start.10 = (bf16[5,128,256]{2,1,0:T(8,128)(2,1)}, bf16[5,128,256]{2,1,0:T(8,128)(2,1)S(1)}, u32[]{:S(2)}) copy-start(bf16[5,128,256]{2,1,0:T(8,128)(2,1)S(1)} %collective-permute-done.10.refs_10_) | copy-start | bytes 983044
  323.6 92.7 %collective-permute-start.13 = (bf16[5,128,256]{2,1,0:T(8,128)(2,1)}, bf16[5,128,256]{2,1,0:T(8,128)(2,1)}, u32[]{:S(2)}, u32[]{:S(2)}) collective-permute-start(bf16[5,128,256]{2,1,0:T(8,128)(2,1)} %get-tuple-element.48), channel_id=1, source_target_pairs={{0,5},{1,4},{2,7},{3,6},{4,1},{5,0},{6,3},{7,2},{8,13},{9,12},{10,... | collective-permute-start | bytes 983048 | tf_op jit(solution)/shard_map/ppermute | solution.py:218
  329.7 83.9 %copy-start.12 = (bf16[5,128,256]{2,1,0:T(8,128)(2,1)}, bf16[5,128,256]{2,1,0:T(8,128)(2,1)S(1)}, u32[]{:S(2)}) copy-start(bf16[5,128,256]{2,1,0:T(8,128)(2,1)S(1)} %collective-permute-done.11.refs_11_) | copy-start | bytes 983044
  329.7 86.7 %collective-permute-start.14 = (bf16[5,128,256]{2,1,0:T(8,128)(2,1)}, bf16[5,128,256]{2,1,0:T(8,128)(2,1)}, u32[]{:S(2)}, u32[]{:S(2)}) collective-permute-start(bf16[5,128,256]{2,1,0:T(8,128)(2,1)} %get-tuple-element.49), channel_id=1, source_target_pairs={{0,6},{1,7},{2,4},{3,5},{4,2},{5,3},{6,0},{7,1},{8,14},{9,15},{10,... | collective-permute-start | bytes 983048 | tf_op jit(solution)/shard_map/ppermute | solution.py:218
  331.3 87.9 %copy-start.19 = (s32[4,1]{0,1:T(1,128)S(1)}, s32[4,1]{0,1:T(1,128)}, u32[]{:S(2)}) copy-start(s32[4,1]{0,1:T(1,128)} %constant.95.clone) | copy-start | bytes 52
  413.6 88.6 %collective-permute-start.15 = (bf16[5,128,256]{2,1,0:T(8,128)(2,1)}, bf16[5,128,256]{2,1,0:T(8,128)(2,1)}, u32[]{:S(2)}, u32[]{:S(2)}) collective-permute-start(bf16[5,128,256]{2,1,0:T(8,128)(2,1)} %get-tuple-element.50), channel_id=1, source_target_pairs={{0,7},{1,6},{2,5},{3,4},{4,3},{5,2},{6,1},{7,0},{8,15},{9,14},{10,... | collective-permute-start | bytes 983048 | tf_op jit(solution)/shard_map/ppermute | solution.py:218
  416.3 87.7 %collective-permute-start.18 = (bf16[5,128,256]{2,1,0:T(8,128)(2,1)}, bf16[5,128,256]{2,1,0:T(8,128)(2,1)}, u32[]{:S(2)}, u32[]{:S(2)}) collective-permute-start(bf16[5,128,256]{2,1,0:T(8,128)(2,1)} %get-tuple-element.52), channel_id=1, source_target_pairs={{0,1},{1,0},{2,3},{3,2},{4,5},{5,4},{6,7},{7,6},{8,9},{9,8},{10,11... | collective-permute-start | bytes 983048 | tf_op jit(solution)/shard_map/ppermute | solution.py:218
  416.4 88.0 %collective-permute-start.19 = (bf16[5,128,256]{2,1,0:T(8,128)(2,1)}, bf16[5,128,256]{2,1,0:T(8,128)(2,1)}, u32[]{:S(2)}, u32[]{:S(2)}) collective-permute-start(bf16[5,128,256]{2,1,0:T(8,128)(2,1)} %get-tuple-element.53), channel_id=1, source_target_pairs={{0,2},{1,3},{2,0},{3,1},{4,6},{5,7},{6,4},{7,5},{8,10},{9,11},{10,... | collective-permute-start | bytes 983048 | tf_op jit(solution)/shard_map/ppermute | solution.py:218
  416.6 90.1 %collective-permute-start.20 = (bf16[5,128,256]{2,1,0:T(8,128)(2,1)}, bf16[5,128,256]{2,1,0:T(8,128)(2,1)}, u32[]{:S(2)}, u32[]{:S(2)}) collective-permute-start(bf16[5,128,256]{2,1,0:T(8,128)(2,1)} %get-tuple-element.54), channel_id=1, source_target_pairs={{0,3},{1,2},{2,1},{3,0},{4,7},{5,6},{6,5},{7,4},{8,11},{9,10},{10,... | collective-permute-start | bytes 983048 | tf_op jit(solution)/shard_map/ppermute | solution.py:218
  418.2 88.9 %collective-permute-start.21 = (bf16[5,128,256]{2,1,0:T(8,128)(2,1)}, bf16[5,128,256]{2,1,0:T(8,128)(2,1)}, u32[]{:S(2)}, u32[]{:S(2)}) collective-permute-start(bf16[5,128,256]{2,1,0:T(8,128)(2,1)} %get-tuple-element.55), channel_id=1, source_target_pairs={{0,4},{1,5},{2,6},{3,7},{4,0},{5,1},{6,2},{7,3},{8,12},{9,13},{10,... | collective-permute-start | bytes 983048 | tf_op jit(solution)/shard_map/ppermute | solution.py:218
  419.9 137.5 %copy-start = (bf16[4096,256]{1,0:T(8,128)(2,1)S(1)}, bf16[4096,256]{1,0:T(8,128)(2,1)}, u32[]{:S(2)}) copy-start(bf16[4096,256]{1,0:T(8,128)(2,1)} %param.11) | copy-start | bytes 6291460
  419.9 137.6 %copy-start.17 = (s32[4096]{0:T(1024)S(1)}, s32[4096]{0:T(1024)}, u32[]{:S(2)}) copy-start(s32[4096]{0:T(1024)} %param.14) | copy-start | bytes 49156
  502.2 24.0 %collective-permute-start.22 = (bf16[5,128,256]{2,1,0:T(8,128)(2,1)}, bf16[5,128,256]{2,1,0:T(8,128)(2,1)S(1)}, u32[]{:S(2)}, u32[]{:S(2)}) collective-permute-start(bf16[5,128,256]{2,1,0:T(8,128)(2,1)} %get-tuple-element.56), channel_id=1, source_target_pairs={{0,5},{1,4},{2,7},{3,6},{4,1},{5,0},{6,3},{7,2},{8,13},{9,12},{10,... | collective-permute-start | bytes 983048 | tf_op jit(solution)/shard_map/ppermute | solution.py:218
  504.0 23.1 %collective-permute-start.23 = (bf16[5,128,256]{2,1,0:T(8,128)(2,1)}, bf16[5,128,256]{2,1,0:T(8,128)(2,1)S(1)}, u32[]{:S(2)}, u32[]{:S(2)}) collective-permute-start(bf16[5,128,256]{2,1,0:T(8,128)(2,1)} %get-tuple-element.57), channel_id=1, source_target_pairs={{0,6},{1,7},{2,4},{3,5},{4,2},{5,3},{6,0},{7,1},{8,14},{9,15},{10,... | collective-permute-start | bytes 983048 | tf_op jit(solution)/shard_map/ppermute | solution.py:218
  504.4 24.3 %collective-permute-start.24 = (bf16[5,128,256]{2,1,0:T(8,128)(2,1)}, bf16[5,128,256]{2,1,0:T(8,128)(2,1)S(1)}, u32[]{:S(2)}, u32[]{:S(2)}) collective-permute-start(bf16[5,128,256]{2,1,0:T(8,128)(2,1)} %get-tuple-element.58), channel_id=1, source_target_pairs={{0,7},{1,6},{2,5},{3,4},{4,3},{5,2},{6,1},{7,0},{8,15},{9,14},{10,... | collective-permute-start | bytes 983048 | tf_op jit(solution)/shard_map/ppermute | solution.py:218
  506.7 22.0 %collective-permute-start.27 = (bf16[5,128,256]{2,1,0:T(8,128)(2,1)}, bf16[5,128,256]{2,1,0:T(8,128)(2,1)S(1)}, u32[]{:S(2)}, u32[]{:S(2)}) collective-permute-start(bf16[5,128,256]{2,1,0:T(8,128)(2,1)} %get-tuple-element.60), channel_id=1, source_target_pairs={{0,1},{1,0},{2,3},{3,2},{4,5},{5,4},{6,7},{7,6},{8,9},{9,8},{10,11... | collective-permute-start | bytes 983048 | tf_op jit(solution)/shard_map/ppermute | solution.py:218
  507.1 24.3 %collective-permute-start.28 = (bf16[5,128,256]{2,1,0:T(8,128)(2,1)}, bf16[5,128,256]{2,1,0:T(8,128)(2,1)S(1)}, u32[]{:S(2)}, u32[]{:S(2)}) collective-permute-start(bf16[5,128,256]{2,1,0:T(8,128)(2,1)} %get-tuple-element.61), channel_id=1, source_target_pairs={{0,2},{1,3},{2,0},{3,1},{4,6},{5,7},{6,4},{7,5},{8,10},{9,11},{10,... | collective-permute-start | bytes 983048 | tf_op jit(solution)/shard_map/ppermute | solution.py:218
  526.2 9.6 %collective-permute-start.29 = (bf16[5,128,256]{2,1,0:T(8,128)(2,1)}, bf16[5,128,256]{2,1,0:T(8,128)(2,1)S(1)}, u32[]{:S(2)}, u32[]{:S(2)}) collective-permute-start(bf16[5,128,256]{2,1,0:T(8,128)(2,1)} %get-tuple-element.62), channel_id=1, source_target_pairs={{0,3},{1,2},{2,1},{3,0},{4,7},{5,6},{6,5},{7,4},{8,11},{9,10},{10,... | collective-permute-start | bytes 983048 | tf_op jit(solution)/shard_map/ppermute | solution.py:218
  527.2 23.9 %collective-permute-start.30 = (bf16[5,128,256]{2,1,0:T(8,128)(2,1)}, bf16[5,128,256]{2,1,0:T(8,128)(2,1)S(1)}, u32[]{:S(2)}, u32[]{:S(2)}) collective-permute-start(bf16[5,128,256]{2,1,0:T(8,128)(2,1)} %get-tuple-element.63), channel_id=1, source_target_pairs={{0,4},{1,5},{2,6},{3,7},{4,0},{5,1},{6,2},{7,3},{8,12},{9,13},{10,... | collective-permute-start | bytes 983048 | tf_op jit(solution)/shard_map/ppermute | solution.py:218
  528.7 28.7 %collective-permute-start.31 = (bf16[5,128,256]{2,1,0:T(8,128)(2,1)}, bf16[5,128,256]{2,1,0:T(8,128)(2,1)S(1)}, u32[]{:S(2)}, u32[]{:S(2)}) collective-permute-start(bf16[5,128,256]{2,1,0:T(8,128)(2,1)} %get-tuple-element.64), channel_id=1, source_target_pairs={{0,5},{1,4},{2,7},{3,6},{4,1},{5,0},{6,3},{7,2},{8,13},{9,12},{10,... | collective-permute-start | bytes 983048 | tf_op jit(solution)/shard_map/ppermute | solution.py:218
  528.7 28.7 %collective-permute-start.32 = (bf16[5,128,256]{2,1,0:T(8,128)(2,1)}, bf16[5,128,256]{2,1,0:T(8,128)(2,1)S(1)}, u32[]{:S(2)}, u32[]{:S(2)}) collective-permute-start(bf16[5,128,256]{2,1,0:T(8,128)(2,1)} %get-tuple-element.65), channel_id=1, source_target_pairs={{0,6},{1,7},{2,4},{3,5},{4,2},{5,3},{6,0},{7,1},{8,14},{9,15},{10,... | collective-permute-start | bytes 983048 | tf_op jit(solution)/shard_map/ppermute | solution.py:218
  531.3 26.1 %collective-permute-start.33 = (bf16[5,128,256]{2,1,0:T(8,128)(2,1)}, bf16[5,128,256]{2,1,0:T(8,128)(2,1)S(1)}, u32[]{:S(2)}, u32[]{:S(2)}) collective-permute-start(bf16[5,128,256]{2,1,0:T(8,128)(2,1)} %get-tuple-element.66), channel_id=1, source_target_pairs={{0,7},{1,6},{2,5},{3,4},{4,3},{5,2},{6,1},{7,0},{8,15},{9,14},{10,... | collective-permute-start | bytes 983048 | tf_op jit(solution)/shard_map/ppermute | solution.py:218
  557.4 1.0 copy-start.2
  558.4 1.0 copy-start.4
  (8 other events, 7.8 us)

commit v2 on v1

v2 whole, which is shorter than its diff:
```python
import functools

import jax
import jax.numpy as jnp
from jax import lax
from jax.experimental import pallas as pl
from jax.experimental.pallas import tpu as pltpu
from jax.sharding import PartitionSpec as P

REM_PB = 4
PLANES = 4


def arrival_order(planes):
    order = []
    for z in range(planes):
        mine = [(0, 0)]
        for step in range(1, planes):
            if z + step < planes:
                mine.append((step, -1))
            if z - step >= 0:
                mine.append((step, 1))
        order.append(mine)
    return order


def pick_row(table, z):
    return jnp.sum(jnp.where(jnp.arange(table.shape[0])[:, None] == z, table, 0), axis=0)


def choose_kernel(which, ids, *refs, sources):
    froms, out, sem = refs[:sources], refs[sources], refs[-1]
    count = out.shape[0]
    for j, source in enumerate(froms):

        @pl.when(which[0] == j)
        def _():
            copies = [
                pltpu.make_async_copy(source.at[ids[n]], out.at[n], sem.at[n]) for n in range(count)
            ]
            for copy in copies:
                copy.start()
            for copy in copies:
                copy.wait()


def choose(which, ids, froms):
    block = froms[0].shape[1:]
    count = ids.shape[0]
    moved = count * block[0] * block[1] * 2
    return pl.pallas_call(
        functools.partial(choose_kernel, sources=len(froms)),
        grid_spec=pltpu.PrefetchScalarGridSpec(
            num_scalar_prefetch=2,
            grid=(1,),
            in_specs=[pl.BlockSpec(memory_space=pltpu.HBM)] * len(froms),
            out_specs=pl.BlockSpec((count,) + block, lambda i, w, s: (0, 0, 0)),
            scratch_shapes=[pltpu.SemaphoreType.DMA((count,))],
        ),
        out_shape=jax.ShapeDtypeStruct((count,) + block, froms[0].dtype),
        compiler_params=pltpu.CompilerParams(vmem_limit_bytes=32 * 1024 * 1024),
        cost_estimate=pl.CostEstimate(flops=0, bytes_accessed=2 * moved, transcendentals=0),
        name="choose_blocks",
    )(which, ids, *froms)


def layer_kernel(slots, *refs, pieces, starts):
    froms = refs[:pieces]
    masks, degree, weight, out, table, means, sems = refs[pieces:]
    step = pl.program_id(0)
    rows, per_block = masks.shape[:2]
    tile, width = table.shape[1:]

    @pl.when(step == 0)
    def _():
        copies = [
            pltpu.make_async_copy(piece, table.at[pl.ds(at, piece.shape[0])], sems.at[n])
            for n, (piece, at) in enumerate(zip(froms, starts))
        ]
        for copy in copies:
            copy.start()
        for copy in copies:
            copy.wait()

    for r in range(rows):
        row = step * rows + r
        mask = jnp.concatenate(
            [masks[r, t].astype(jnp.float32).astype(jnp.bfloat16) for t in range(per_block)], axis=1
        )
        picked = jnp.concatenate(
            [table[slots[row * per_block + t]] for t in range(per_block)], axis=0
        )
        sums = jnp.dot(mask, picked, preferred_element_type=jnp.float32)
        count = jnp.broadcast_to(degree[pl.ds(row, 1), :].astype(jnp.float32), (tile, tile)).T
        count = jnp.concatenate([count] * (width // tile), axis=1)
        means[pl.ds(r * tile, tile), :] = (sums / count).astype(jnp.bfloat16)
    own = table[pl.ds(step * rows, rows)].reshape(rows * tile, width)
    hidden = jnp.dot(own, weight[:width], preferred_element_type=jnp.float32)
    hidden = hidden + jnp.dot(means[...], weight[width:], preferred_element_type=jnp.float32)
    hidden = jnp.maximum(hidden, 0.0)
    scale = lax.rsqrt(jnp.sum(hidden * hidden, axis=1, keepdims=True) + 1e-06)
    out[...] = (hidden * scale).astype(jnp.bfloat16)


def layer(slots, froms, starts, blocks_in_table, tile_masks, degree, weight):
    blocks_here, per_block, tile, _ = tile_masks.shape
    width = weight.shape[0] // 2
    out_width = weight.shape[1]
    rows = 4 if blocks_here % 4 == 0 else 1
    return pl.pallas_call(
        functools.partial(layer_kernel, pieces=len(froms), starts=starts),
        grid_spec=pltpu.PrefetchScalarGridSpec(
            num_scalar_prefetch=1,
            grid=(blocks_here // rows,),
            in_specs=[pl.BlockSpec(memory_space=pltpu.HBM)] * len(froms)
            + [
                pl.BlockSpec((rows, per_block, tile, tile), lambda r, s: (r, 0, 0, 0)),
                pl.BlockSpec((blocks_here, tile), lambda r, s: (0, 0)),
                pl.BlockSpec((2 * width, out_width), lambda r, s: (0, 0)),
            ],
            out_specs=pl.BlockSpec((rows * tile, out_width), lambda r, s: (r, 0)),
            scratch_shapes=[
                pltpu.VMEM((blocks_in_table, tile, width), jnp.bfloat16),
                pltpu.VMEM((rows * tile, width), jnp.bfloat16),
                pltpu.SemaphoreType.DMA((len(froms),)),
            ],
        ),
        out_shape=jax.ShapeDtypeStruct((blocks_here * tile, out_width), jnp.bfloat16),
        compiler_params=pltpu.CompilerParams(vmem_limit_bytes=48 * 1024 * 1024),
        cost_estimate=pl.CostEstimate(
            flops=2 * blocks_here * tile * (per_block * tile + 2 * width) * width,
            bytes_accessed=blocks_here * per_block * tile * tile * 4 + blocks_in_table * tile * width * 2,
            transcendentals=blocks_here * tile,
        ),
        name="sage_layer",
    )(slots, *froms, tile_masks, degree, weight)


def on_device(features, tile_cols, tile_masks, degree, weight):
    blocks_here, per_block = tile_cols.shape
    tile = tile_masks.shape[2]
    width = features.shape[1]
    peers = lax.axis_size("rows")
    planes = PLANES if peers % PLANES == 0 else 1
    plane = peers // planes
    myself = lax.axis_index("rows")
    z, p = myself // plane, myself % plane
    capacity = max(2, (REM_PB * blocks_here + peers - 2) // (peers - 1))
    order = arrival_order(planes)

    columns = tile_cols.reshape(-1)
    shifted = [columns]
    for m in range(1, plane):
        pairs = [
            (a * plane + q, a * plane + (q ^ m)) for a in range(planes) for q in range(plane)
        ]
        shifted.append(lax.ppermute(columns, "rows", pairs))
    features, asked = lax.optimization_barrier((features, jnp.stack(shifted)))
    local = features.reshape(blocks_here, tile, width)

    arrived = {(0, 0): local}
    for step in range(1, planes):
        for way in (-1, 1):
            held = arrived[(step - 1, way)] if step > 1 else local
            pairs = [
                (a * plane + q, (a + way) * plane + q)
                for a in range(planes)
                if 0 <= a + way < planes and 0 <= a - way * (step - 1) < planes
                for q in range(plane)
            ]
            arrived[(step, way)] = lax.ppermute(held, "rows", pairs)

    plane_at = jnp.array(
        [[a - way * step for step, way in order[a]] for a in range(planes)], jnp.int32
    )
    sources = pick_row(plane_at, z)
    line = sources * plane + p
    blocks = jnp.arange(blocks_here, dtype=jnp.int32)
    wanted = (line[:, None] * blocks_here + blocks[None, :]).reshape(-1)
    need = jnp.any(asked[:, :, None] == wanted[None, None, :], axis=1)
    need = need.reshape(plane, planes, blocks_here).astype(jnp.int32)
    below = blocks[:, None] > blocks[None, :]
    place = jnp.sum(jnp.where(below, need[:, :, None, :], 0), axis=3)
    seat = jnp.arange(capacity, dtype=jnp.int32)
    chosen = jnp.sum(
        jnp.where(
            (need[:, :, None, :] == 1) & (place[:, :, None, :] == seat[:, None]), blocks, 0
        ),
        axis=3,
    )

    owners, within = columns // blocks_here, columns % blocks_here
    positions = jnp.arange(columns.shape[0], dtype=jnp.int32)
    same = columns[:, None] == columns[None, :]
    first = ~jnp.any(same & (positions[None, :] < positions[:, None]), axis=1)
    ahead = (owners[:, None] == owners[None, :]) & (columns[None, :] < columns[:, None])
    ranks = jnp.sum(ahead & first[None, :], axis=1, dtype=jnp.int32)
    stage_at = jnp.array(
        [
            [[a - way * step for step, way in order[a]].index(b) for b in range(planes)]
            for a in range(planes)
        ],
        jnp.int32,
    )
    stages = pick_row(stage_at, z)
    their_plane = owners // plane
    stage = jnp.sum(
        jnp.where(their_plane[:, None] == jnp.arange(planes), stages[None, :], 0), axis=1
    )
    slots = jnp.where(
        owners == myself,
        within,
        blocks_here + (stage * plane + owners % plane) * capacity + ranks,
    )

    others = jnp.arange(plane, dtype=jnp.int32)
    swap = (others[:, None] ^ p) == others[None, :]
    chosen = jnp.sum(jnp.where(swap[:, :, None, None], chosen[None], 0), axis=1)
    groups = [[a * plane + q for q in range(plane)] for a in range(planes)]
    froms, starts = [local], [0]
    for k in range(planes):
        kinds = sorted(set(order[a][k] for a in range(planes)))
        which_at = jnp.array([[kinds.index(order[a][k])] for a in range(planes)], jnp.int32)
        ids = chosen[:, k, :].reshape(-1)
        picked = choose(pick_row(which_at, z), ids, [arrived[kind] for kind in kinds])
        froms.append(
            lax.all_to_all(
                picked, "rows", split_axis=0, concat_axis=0, axis_index_groups=groups, tiled=True
            )
        )
        starts.append(blocks_here + k * plane * capacity)

    return layer(
        slots,
        froms,
        tuple(starts),
        blocks_here + peers * capacity,
        tile_masks,
        degree.reshape(blocks_here, tile),
        weight,
    )


def solution(mesh):
    in_specs = (P("rows", None), P("rows", None), P("rows", None, None, None), P("rows"), P())
    out_specs = P("rows", None)
    return jax.shard_map(
        on_device, mesh=mesh, in_specs=in_specs, out_specs=out_specs, check_vma=False
    )
```

time: 601 us -> 265 us (0.44)
  Pallas kernels: 349 us -> 29.4 us
  blocking collectives: 73.8 us -> 0 us
  waiting for transfers between devices: 120 us -> 180 us
    pallas_call x4, Pallas kernels: 318 us -> 15.1 us  [choose(): pl.pallas_call(functools.partial(choose_kernel, sources=len(froms)), grid...]
    ppermute x6, waiting for transfers between devices: 46 us -> 145 us  [on_device(): arrived[step, way] = lax.ppermute(held, 'rows', pairs)]
    all_gather x1 -> x0, blocking collectives: 73.8 us -> none  [on_device(): all_columns = lax.all_gather(columns, 'rows')]
    ppermute x28 -> x7, waiting for transfers between devices: 74.2 us -> 3.5 us  [on_device(): shifted.append(lax.ppermute(columns, 'rows', pairs))]
    all_to_all x0 -> x4, waiting for transfers between devices: none -> 31.7 us  [on_device(): lax.all_to_all(picked, 'rows', split_axis=0, concat_axis=0, axis_index_gr...]
    all_to_all x0 -> x4, starting transfers between devices: none -> 17.3 us  [on_device(): lax.all_to_all(picked, 'rows', split_axis=0, concat_axis=0, axis_index_gr...]
    pallas_call x1, Pallas kernels: 30.6 us -> 14.4 us  [layer(): pl.pallas_call(functools.partial(layer_kernel, pieces=len(froms), starts=...]
    ppermute x28 -> x7, starting transfers between devices: 22.3 us -> 7.68 us  [on_device(): shifted.append(lax.ppermute(columns, 'rows', pairs))]
  transfers between devices with their start and end apart: 34 -> 17, of which waited for: 10 -> 7; matrix products, arithmetic and copies ran while one was open for 2% -> 2% of each run, Pallas kernels for 53% -> 4%
where the time goes in v2:
time: 265 us; the launch traced here: 264 us
  waiting for transfers between devices  180 us (68%)
  starting transfers between devices  37.7 us (14%)
  Pallas kernels  29.4 us (11%)
  local copies, waits for them, and re-layouts  11.1 us (4%)
  other arithmetic  5.14 us (2%)
    ppermute x6, waiting for transfers between devices, on_device(): arrived[step, way] = lax.ppermute(held, 'rows', pairs)  145 us
    all_to_all x4, waiting for transfers between devices, on_device(): lax.all_to_all(picked, 'rows', split_axis=0, concat_axis=0, axis_index_gr...  31.7 us
    all_to_all x4, starting transfers between devices, on_device(): lax.all_to_all(picked, 'rows', split_axis=0, concat_axis=0, axis_index_gr...  17.3 us
    pallas_call x4, Pallas kernels, choose(): pl.pallas_call(functools.partial(choose_kernel, sources=len(froms)), grid...  15.1 us
    pallas_call x1, Pallas kernels, layer(): pl.pallas_call(functools.partial(layer_kernel, pieces=len(froms), starts=...  14.4 us
    ppermute x6, starting transfers between devices, on_device(): arrived[step, way] = lax.ppermute(held, 'rows', pairs)  12.7 us
    unnamed x23, local copies, waits for them, and re-layouts  10.1 us
    ppermute x7, starting transfers between devices, on_device(): shifted.append(lax.ppermute(columns, 'rows', pairs))  7.68 us
  transfers between devices with their start and end apart: 17, of which 7 were waited for; matrix products, arithmetic and copies ran while one was open for 2% of the time, Pallas kernels for 4%

profile of v2, /device:TPU:0, one launch (start us, length us, event | category | flops | bytes accessed | tf_op | source)
XLA Modules:
  0.0 263.5 jit_solution(4680563811462696995)
XLA Ops:
  0.0 0.8 copy.14
  0.8 0.1 reshape.171
  0.9 2.5 collective-permute-start.4
  3.3 0.6 collective-permute-start.3
  4.0 1.4 collective-permute-start.2
  5.3 0.3 collective-permute-start.1
  5.7 0.2 collective-permute-start
  5.9 0.8 select_reduce_fusion.4
  6.8 2.5 collective-permute-start.5
  9.3 0.2 collective-permute-start.6
  9.5 0.1 reshape.172
  9.7 1.5 collective-permute-done.5
  11.3 2.0 collective-permute-done.6
  13.2 0.3 compare_reduce_fusion
  13.6 0.6 select_reduce_fusion
  14.3 0.4 select_reduce_fusion.2
  14.7 0.4 select_reduce_fusion.1
  15.3 1.6 copy-done.4
  16.9 4.5 %choose_blocks.4 = bf16[40,128,256]{2,1,0:T(8,128)(2,1)S(1)} custom-call(s32[1]{0:T(128)} %constant.95.which, s32[40]{0:T(128)S(1)} %reshape_squeeze.12.ids, bf16[32,128,256]{2,1,0:T(8,128)(2,1)S(1)} %bitcast.22), custom_call_target="tpu_custom_call" | custom-call | bytes 5242880 | tf_op jit(solution)/shard_map/choose_blocks/pallas_call | solution.py:51
  21.4 1.5 copy-done.2
  22.9 3.8 %all-to-all-start = ((bf16[40,128,256]{2,1,0:T(8,128)(2,1)}), bf16[40,128,256]{2,1,0:T(8,128)(2,1)S(1)}, u32[]{:S(2)}, u32[]{:S(2)}) async-start(bf16[40,128,256]{2,1,0:T(8,128)(2,1)} %copy-done.2), calls=%async_computation | async-start | bytes 5242880 | tf_op jit(solution)/shard_map/all_to_all | solution.py:227
  26.6 4.9 %collective-permute-start.8 = (bf16[32,128,256]{2,1,0:T(8,128)(2,1)}, bf16[32,128,256]{2,1,0:T(8,128)(2,1)}, u32[]{:S(2)}, u32[]{:S(2)}) collective-permute-start(bf16[32,128,256]{2,1,0:T(8,128)(2,1)} %bitcast.20), channel_id=1, source_target_pairs={{0,8},{1,9},{2,10},{3,11},{4,12},{5,13},{6,14},{7,15},{8,16},{9,17... | collective-permute-start | bytes 6291464 | tf_op jit(solution)/shard_map/ppermute | solution.py:171
  31.5 1.3 collective-permute-start.7
  32.8 0.6 select_reduce_fusion.8
  33.6 42.3 %collective-permute-done.8.refs_1_.refs_0_ = bf16[32,128,256]{2,1,0:T(8,128)(2,1)} collective-permute-done((bf16[32,128,256]{2,1,0:T(8,128)(2,1)}, bf16[32,128,256]{2,1,0:T(8,128)(2,1)}, u32[]{:S(2)}, u32[]{:S(2)}) %collective-permute-start.8) | collective-permute-done | bytes 2097184 | tf_op jit(solution)/shard_map/ppermute | solution.py:171
  75.9 5.5 %collective-permute-done.7.refs_0_ = bf16[32,128,256]{2,1,0:T(8,128)(2,1)} collective-permute-done((bf16[32,128,256]{2,1,0:T(8,128)(2,1)}, bf16[32,128,256]{2,1,0:T(8,128)(2,1)}, u32[]{:S(2)}, u32[]{:S(2)}) %collective-permute-start.7) | collective-permute-done | bytes 2097184 | tf_op jit(solution)/shard_map/ppermute | solution.py:171
  81.3 3.4 %choose_blocks.5 = bf16[40,128,256]{2,1,0:T(8,128)(2,1)S(1)} custom-call(s32[1]{0:T(128)} %bitcast.8.which, s32[40]{0:T(128)S(1)} %reshape_squeeze.13.ids, bf16[32,128,256]{2,1,0:T(8,128)(2,1)} %collective-permute-done.7.refs_0_, bf16[32,128,256]{2,1,0:T(8,128)(2,1)} %collective-permute-done.8.refs_1_.refs_0_), custom_call_target="tpu_custom_call" | custom-call | bytes 5242880 | tf_op jit(solution)/shard_map/choose_blocks/pallas_call | solution.py:51
  84.8 1.5 copy-done.1
  86.3 4.5 %all-to-all-start.1 = ((bf16[40,128,256]{2,1,0:T(8,128)(2,1)}), bf16[40,128,256]{2,1,0:T(8,128)(2,1)}, u32[]{:S(2)}, u32[]{:S(2)}) async-start(bf16[40,128,256]{2,1,0:T(8,128)(2,1)} %copy-done.1), calls=%async_computation.1 | async-start | bytes 5242880 | tf_op jit(solution)/shard_map/all_to_all | solution.py:227
  90.8 2.0 collective-permute-start.10
  92.8 1.3 collective-permute-start.9
  94.1 0.6 select_reduce_fusion.7
  94.9 48.9 %collective-permute-done.9.refs_1_.refs_0_ = bf16[32,128,256]{2,1,0:T(8,128)(2,1)} collective-permute-done((bf16[32,128,256]{2,1,0:T(8,128)(2,1)}, bf16[32,128,256]{2,1,0:T(8,128)(2,1)}, u32[]{:S(2)}, u32[]{:S(2)}) %collective-permute-start.9) | collective-permute-done | bytes 2097184 | tf_op jit(solution)/shard_map/ppermute | solution.py:171
  143.8 3.3 %choose_blocks.6 = bf16[40,128,256]{2,1,0:T(8,128)(2,1)S(1)} custom-call(s32[1]{0:T(128)} %bitcast.9.which, s32[40]{0:T(128)S(1)} %reshape_squeeze.14.ids, bf16[32,128,256]{2,1,0:T(8,128)(2,1)} %collective-permute-done.8.refs_1_.refs_0_, bf16[32,128,256]{2,1,0:T(8,128)(2,1)} %collective-permute-done.9.refs_1_.refs_0_, ...), custom_call_target="tpu_custom_call" | custom-call | bytes 5242880 | tf_op jit(solution)/shard_map/choose_blocks/pallas_call | solution.py:51
  147.1 1.5 copy-done
  148.6 4.5 %all-to-all-start.2 = ((bf16[40,128,256]{2,1,0:T(8,128)(2,1)}), bf16[40,128,256]{2,1,0:T(8,128)(2,1)}, u32[]{:S(2)}, u32[]{:S(2)}) async-start(bf16[40,128,256]{2,1,0:T(8,128)(2,1)} %copy-done), calls=%async_computation.2 | async-start | bytes 5242880 | tf_op jit(solution)/shard_map/all_to_all | solution.py:227
  153.1 2.0 collective-permute-start.12
  155.1 1.3 collective-permute-start.11
  156.4 0.6 select_reduce_fusion.6
  157.2 48.0 %collective-permute-done.11.refs_2_ = bf16[32,128,256]{2,1,0:T(8,128)(2,1)} collective-permute-done((bf16[32,128,256]{2,1,0:T(8,128)(2,1)}, bf16[32,128,256]{2,1,0:T(8,128)(2,1)}, u32[]{:S(2)}, u32[]{:S(2)}) %collective-permute-start.11) | collective-permute-done | bytes 2097184 | tf_op jit(solution)/shard_map/ppermute | solution.py:171
  205.2 3.9 %choose_blocks.7 = bf16[40,128,256]{2,1,0:T(8,128)(2,1)S(1)} custom-call(s32[1]{0:T(128)} %bitcast.10.which, s32[40]{0:T(128)S(1)} %reshape_squeeze.15.ids, bf16[32,128,256]{2,1,0:T(8,128)(2,1)} %collective-permute-done.9.refs_1_.refs_0_, bf16[32,128,256]{2,1,0:T(8,128)(2,1)} %collective-permute-done.10.refs_2_.refs_1_, ...), custom_call_target="tpu_custom_call" | custom-call | bytes 5242880 | tf_op jit(solution)/shard_map/choose_blocks/pallas_call | solution.py:51
  209.2 1.6 copy-done.3
  210.8 4.5 %all-to-all-start.3 = ((bf16[40,128,256]{2,1,0:T(8,128)(2,1)}), bf16[40,128,256]{2,1,0:T(8,128)(2,1)}, u32[]{:S(2)}, u32[]{:S(2)}) async-start(bf16[40,128,256]{2,1,0:T(8,128)(2,1)} %copy-done.3), calls=%async_computation.3 | async-start | bytes 5242880 | tf_op jit(solution)/shard_map/all_to_all | solution.py:227
  215.3 0.2 fusion.1
  215.6 0.2 convert_reduce_fusion
  215.8 31.7 %all-to-all-done.3.refs_4_ = bf16[40,128,256]{2,1,0:T(8,128)(2,1)} async-done(((bf16[40,128,256]{2,1,0:T(8,128)(2,1)}), bf16[40,128,256]{2,1,0:T(8,128)(2,1)}, u32[]{:S(2)}, u32[]{:S(2)}) %all-to-all-start.3) | async-done | bytes 2621472 | tf_op jit(solution)/shard_map/all_to_all | solution.py:227
  247.6 1.6 copy-done.5
  249.2 14.4 %sage_layer.1 = bf16[4096,256]{1,0:T(8,128)(2,1)} custom-call(s32[192]{0:T(256)S(1)} %compare_select_fusion.slots, bf16[32,128,256]{2,1,0:T(8,128)(2,1)S(1)} %bitcast.23, bf16[40,128,256]{2,1,0:T(8,128)(2,1)S(1)} %all-to-all-done.refs_1_, bf16[40,128,256]{2,1,0:T(8,128)(2,1)} %all-to-all-done.1.refs_2_, bf16[40,128,256]{2,1,0:T(8,128)(2,1)} %all-to-all-done.2.refs_3_, ...), custom_call_target="tpu_custom_call" | custom-call | flops 2684354560 | bytes 25165824 | tf_op jit(solution)/shard_map/sage_layer/pallas_call | solution.py:110
  (52 shorter events, 1.2 us)
Async XLA Ops:
  0.9 5.9 %collective-permute-start.4 = (s32[192]{0:T(256)S(1)}, s32[192]{0:T(256)S(1)}, u32[]{:S(2)}, u32[]{:S(2)}) collective-permute-start(s32[192]{0:T(256)S(1)} %reshape.171), channel_id=1, source_target_pairs={{0,5},{1,4},{2,7},{3,6},{4,1},{5,0},{6,3},{7,2},{8,13},{9,12},{10,... | collective-permute-start | bytes 2312 | tf_op jit(solution)/shard_map/ppermute | solution.py:157
  3.3 6.0 %collective-permute-start.3 = (s32[192]{0:T(256)S(1)}, s32[192]{0:T(256)S(1)}, u32[]{:S(2)}, u32[]{:S(2)}) collective-permute-start(s32[192]{0:T(256)S(1)} %reshape.171), channel_id=1, source_target_pairs={{0,4},{1,5},{2,6},{3,7},{4,0},{5,1},{6,2},{7,3},{8,12},{9,13},{10,... | collective-permute-start | bytes 2312 | tf_op jit(solution)/shard_map/ppermute | solution.py:157
  4.0 5.7 %collective-permute-start.2 = (s32[192]{0:T(256)S(1)}, s32[192]{0:T(256)S(1)}, u32[]{:S(2)}, u32[]{:S(2)}) collective-permute-start(s32[192]{0:T(256)S(1)} %reshape.171), channel_id=1, source_target_pairs={{0,3},{1,2},{2,1},{3,0},{4,7},{5,6},{6,5},{7,4},{8,11},{9,10},{10,... | collective-permute-start | bytes 2312 | tf_op jit(solution)/shard_map/ppermute | solution.py:157
  5.3 4.4 %collective-permute-start.1 = (s32[192]{0:T(256)S(1)}, s32[192]{0:T(256)S(1)}, u32[]{:S(2)}, u32[]{:S(2)}) collective-permute-start(s32[192]{0:T(256)S(1)} %reshape.171), channel_id=1, source_target_pairs={{0,2},{1,3},{2,0},{3,1},{4,6},{5,7},{6,4},{7,5},{8,10},{9,11},{10,... | collective-permute-start | bytes 2312 | tf_op jit(solution)/shard_map/ppermute | solution.py:157
  5.7 4.1 %collective-permute-start = (s32[192]{0:T(256)S(1)}, s32[192]{0:T(256)S(1)}, u32[]{:S(2)}, u32[]{:S(2)}) collective-permute-start(s32[192]{0:T(256)S(1)} %reshape.171), channel_id=1, source_target_pairs={{0,1},{1,0},{2,3},{3,2},{4,5},{5,4},{6,7},{7,6},{8,9},{9,8},{10,11... | collective-permute-start | bytes 2312 | tf_op jit(solution)/shard_map/ppermute | solution.py:157
  6.8 4.5 %collective-permute-start.5 = (s32[192]{0:T(256)S(1)}, s32[192]{0:T(256)S(1)}, u32[]{:S(2)}, u32[]{:S(2)}) collective-permute-start(s32[192]{0:T(256)S(1)} %reshape.171), channel_id=1, source_target_pairs={{0,6},{1,7},{2,4},{3,5},{4,2},{5,3},{6,0},{7,1},{8,14},{9,15},{10,... | collective-permute-start | bytes 2312 | tf_op jit(solution)/shard_map/ppermute | solution.py:157
  9.3 3.9 %collective-permute-start.6 = (s32[192]{0:T(256)S(1)}, s32[192]{0:T(256)S(1)}, u32[]{:S(2)}, u32[]{:S(2)}) collective-permute-start(s32[192]{0:T(256)S(1)} %reshape.171), channel_id=1, source_target_pairs={{0,7},{1,6},{2,5},{3,4},{4,3},{5,2},{6,1},{7,0},{8,15},{9,14},{10,... | collective-permute-start | bytes 2312 | tf_op jit(solution)/shard_map/ppermute | solution.py:157
  15.3 1.6 copy-start.4
  21.4 1.5 copy-start.2
  22.9 9.9 %copy-start.10 = (s32[4,1]{0,1:T(1,128)S(1)}, s32[4,1]{0,1:T(1,128)}, u32[]{:S(2)}) copy-start(s32[4,1]{0,1:T(1,128)} %constant.91.clone) | copy-start | bytes 52
  22.9 63.4 %all-to-all-start = ((bf16[40,128,256]{2,1,0:T(8,128)(2,1)}), bf16[40,128,256]{2,1,0:T(8,128)(2,1)S(1)}, u32[]{:S(2)}, u32[]{:S(2)}) async-start(bf16[40,128,256]{2,1,0:T(8,128)(2,1)} %copy-done.2), calls=%async_computation | async-start | bytes 5242880 | tf_op jit(solution)/shard_map/all_to_all | solution.py:227
  26.6 49.2 %collective-permute-start.8 = (bf16[32,128,256]{2,1,0:T(8,128)(2,1)}, bf16[32,128,256]{2,1,0:T(8,128)(2,1)}, u32[]{:S(2)}, u32[]{:S(2)}) collective-permute-start(bf16[32,128,256]{2,1,0:T(8,128)(2,1)} %bitcast.20), channel_id=1, source_target_pairs={{0,8},{1,9},{2,10},{3,11},{4,12},{5,13},{6,14},{7,15},{8,16},{9,17... | collective-permute-start | bytes 6291464 | tf_op jit(solution)/shard_map/ppermute | solution.py:171
  31.5 49.8 %collective-permute-start.7 = (bf16[32,128,256]{2,1,0:T(8,128)(2,1)}, bf16[32,128,256]{2,1,0:T(8,128)(2,1)}, u32[]{:S(2)}, u32[]{:S(2)}) collective-permute-start(bf16[32,128,256]{2,1,0:T(8,128)(2,1)} %bitcast.21), channel_id=1, source_target_pairs={{8,0},{9,1},{10,2},{11,3},{12,4},{13,5},{14,6},{15,7},{16,8},{17,9... | collective-permute-start | bytes 6291464 | tf_op jit(solution)/shard_map/ppermute | solution.py:171
  84.8 1.5 copy-start.1
  86.3 7.8 %copy-start.9 = (s32[4,1]{0,1:T(1,128)S(1)}, s32[4,1]{0,1:T(1,128)}, u32[]{:S(2)}) copy-start(s32[4,1]{0,1:T(1,128)} %constant.92.clone) | copy-start | bytes 52
  86.3 62.3 %all-to-all-start.1 = ((bf16[40,128,256]{2,1,0:T(8,128)(2,1)}), bf16[40,128,256]{2,1,0:T(8,128)(2,1)}, u32[]{:S(2)}, u32[]{:S(2)}) async-start(bf16[40,128,256]{2,1,0:T(8,128)(2,1)} %copy-done.1), calls=%async_computation.1 | async-start | bytes 5242880 | tf_op jit(solution)/shard_map/all_to_all | solution.py:227
  90.8 4.1 %collective-permute-start.10 = (bf16[32,128,256]{2,1,0:T(8,128)(2,1)}, bf16[32,128,256]{2,1,0:T(8,128)(2,1)}, u32[]{:S(2)}, u32[]{:S(2)}) collective-permute-start(bf16[32,128,256]{2,1,0:T(8,128)(2,1)} %collective-permute-done.8.refs_1_.refs_0_), channel_id=1, source_target_pairs={{8,16},{9,17},{10,18},{11,19},{12,20},{13,21},{14,22},{15,23},{16,... | collective-permute-start | bytes 6291464 | tf_op jit(solution)/shard_map/ppermute | solution.py:171
  92.8 51.0 %collective-permute-start.9 = (bf16[32,128,256]{2,1,0:T(8,128)(2,1)}, bf16[32,128,256]{2,1,0:T(8,128)(2,1)}, u32[]{:S(2)}, u32[]{:S(2)}) collective-permute-start(bf16[32,128,256]{2,1,0:T(8,128)(2,1)} %collective-permute-done.7.refs_0_), channel_id=1, source_target_pairs={{8,0},{9,1},{10,2},{11,3},{12,4},{13,5},{14,6},{15,7},{16,8},{17,9... | collective-permute-start | bytes 6291464 | tf_op jit(solution)/shard_map/ppermute | solution.py:171
  147.1 1.5 copy-start
  148.6 7.8 %copy-start.8 = (s32[4,1]{0,1:T(1,128)S(1)}, s32[4,1]{0,1:T(1,128)}, u32[]{:S(2)}) copy-start(s32[4,1]{0,1:T(1,128)} %constant.93.clone) | copy-start | bytes 52
  148.6 62.1 %all-to-all-start.2 = ((bf16[40,128,256]{2,1,0:T(8,128)(2,1)}), bf16[40,128,256]{2,1,0:T(8,128)(2,1)}, u32[]{:S(2)}, u32[]{:S(2)}) async-start(bf16[40,128,256]{2,1,0:T(8,128)(2,1)} %copy-done), calls=%async_computation.2 | async-start | bytes 5242880 | tf_op jit(solution)/shard_map/all_to_all | solution.py:227
  153.1 4.1 %collective-permute-start.12 = (bf16[32,128,256]{2,1,0:T(8,128)(2,1)}, bf16[32,128,256]{2,1,0:T(8,128)(2,1)}, u32[]{:S(2)}, u32[]{:S(2)}) collective-permute-start(bf16[32,128,256]{2,1,0:T(8,128)(2,1)} %collective-permute-done.10.refs_2_.refs_1_), channel_id=1, source_target_pairs={{16,24},{17,25},{18,26},{19,27},{20,28},{21,29},{22,30},{23,31}} | collective-permute-start | bytes 6291464 | tf_op jit(solution)/shard_map/ppermute | solution.py:171
  155.1 50.1 %collective-permute-start.11 = (bf16[32,128,256]{2,1,0:T(8,128)(2,1)}, bf16[32,128,256]{2,1,0:T(8,128)(2,1)}, u32[]{:S(2)}, u32[]{:S(2)}) collective-permute-start(bf16[32,128,256]{2,1,0:T(8,128)(2,1)} %collective-permute-done.9.refs_1_.refs_0_), channel_id=1, source_target_pairs={{8,0},{9,1},{10,2},{11,3},{12,4},{13,5},{14,6},{15,7}} | collective-permute-start | bytes 6291464 | tf_op jit(solution)/shard_map/ppermute | solution.py:171
  209.2 1.6 copy-start.3
  210.7 36.8 %copy-start.6 = (bf16[512,256]{1,0:T(8,128)(2,1)S(1)}, bf16[512,256]{1,0:T(8,128)(2,1)}, u32[]{:S(2)}) copy-start(bf16[512,256]{1,0:T(8,128)(2,1)} %refs_7_.1) | copy-start | bytes 786436
  210.7 36.8 %copy-start.7 = (s32[4096]{0:T(1024)S(1)}, s32[4096]{0:T(1024)}, u32[]{:S(2)}) copy-start(s32[4096]{0:T(1024)} %param.14) | copy-start | bytes 49156
  210.8 36.8 %all-to-all-start.3 = ((bf16[40,128,256]{2,1,0:T(8,128)(2,1)}), bf16[40,128,256]{2,1,0:T(8,128)(2,1)}, u32[]{:S(2)}, u32[]{:S(2)}) async-start(bf16[40,128,256]{2,1,0:T(8,128)(2,1)} %copy-done.3), calls=%async_computation.3 | async-start | bytes 5242880 | tf_op jit(solution)/shard_map/all_to_all | solution.py:227
  247.6 1.6 copy-start.5

commit v3 on v2

--- a/solution.py
+++ b/solution.py
@@ -9,6 +9,8 @@
 
 REM_PB = 4
 PLANES = 4
+HALVES = 2
+CHOOSE_WEIGHT = 200
 
 
 def arrival_order(planes):
@@ -28,40 +30,59 @@
     return jnp.sum(jnp.where(jnp.arange(table.shape[0])[:, None] == z, table, 0), axis=0)
 
 
-def choose_kernel(which, ids, *refs, sources):
-    froms, out, sem = refs[:sources], refs[sources], refs[-1]
+def choose_kernel(which, ids, *refs, kinds, parts):
+    froms, out, held, in_sems, out_sems = refs[: kinds * parts], *refs[kinds * parts :]
     count = out.shape[0]
-    for j, source in enumerate(froms):
+    tall = out.shape[1] // parts
+
+    def arrival(source, n, h):
+        here = held.at[n, pl.ds(h * tall, tall)]
+        return pltpu.make_async_copy(source.at[ids[n]], here, in_sems.at[n, h])
+
+    for j in range(kinds):
 
         @pl.when(which[0] == j)
         def _():
-            copies = [
-                pltpu.make_async_copy(source.at[ids[n]], out.at[n], sem.at[n]) for n in range(count)
-            ]
-            for copy in copies:
-                copy.start()
-            for copy in copies:
-                copy.wait()
+            for n in range(count):
+                for h in range(parts):
+                    arrival(froms[j * parts + h], n, h).start()
+
+    leaving = []
+    for n in range(count):
+        for h in range(parts):
+            arrival(froms[h], n, h).wait()
+        leaving.append(pltpu.make_async_copy(held.at[n], out.at[n], out_sems.at[n]))
+        leaving[-1].start()
+    for copy in leaving:
+        copy.wait()
 
 
 def choose(which, ids, froms):
-    block = froms[0].shape[1:]
+    parts = len(froms[0])
+    _, tall, width = froms[0][0].shape
+    block = (parts * tall, width)
     count = ids.shape[0]
     moved = count * block[0] * block[1] * 2
     return pl.pallas_call(
-        functools.partial(choose_kernel, sources=len(froms)),
+        functools.partial(choose_kernel, kinds=len(froms), parts=parts),
         grid_spec=pltpu.PrefetchScalarGridSpec(
             num_scalar_prefetch=2,
             grid=(1,),
-            in_specs=[pl.BlockSpec(memory_space=pltpu.HBM)] * len(froms),
-            out_specs=pl.BlockSpec((count,) + block, lambda i, w, s: (0, 0, 0)),
-            scratch_shapes=[pltpu.SemaphoreType.DMA((count,))],
-        ),
-        out_shape=jax.ShapeDtypeStruct((count,) + block, froms[0].dtype),
+            in_specs=[pl.BlockSpec(memory_space=pltpu.HBM)] * (parts * len(froms)),
+            out_specs=pl.BlockSpec(memory_space=pltpu.HBM),
+            scratch_shapes=[
+                pltpu.VMEM((count,) + block, froms[0][0].dtype),
+                pltpu.SemaphoreType.DMA((count, parts)),
+                pltpu.SemaphoreType.DMA((count,)),
+            ],
+        ),
+        out_shape=jax.ShapeDtypeStruct((count,) + block, froms[0][0].dtype),
         compiler_params=pltpu.CompilerParams(vmem_limit_bytes=32 * 1024 * 1024),
-        cost_estimate=pl.CostEstimate(flops=0, bytes_accessed=2 * moved, transcendentals=0),
+        cost_estimate=pl.CostEstimate(
+            flops=0, bytes_accessed=CHOOSE_WEIGHT * moved, transcendentals=0
+        ),
         name="choose_blocks",
-    )(which, ids, *froms)
+    )(which, ids, *[part for source in froms for part in source])
 
 
 def layer_kernel(slots, *refs, pieces, starts):
@@ -74,8 +95,12 @@
     @pl.when(step == 0)
     def _():
         copies = [
-            pltpu.make_async_copy(piece, table.at[pl.ds(at, piece.shape[0])], sems.at[n])
-            for n, (piece, at) in enumerate(zip(froms, starts))
+            pltpu.make_async_copy(
+                piece,
+                table.at[pl.ds(at, piece.shape[0]), pl.ds(top, piece.shape[1])],
+                sems.at[n],
+            )
+            for n, (piece, (at, top)) in enumerate(zip(froms, starts))
         ]
         for copy in copies:
             copy.start()
@@ -148,27 +173,34 @@
     capacity = max(2, (REM_PB * blocks_here + peers - 2) // (peers - 1))
     order = arrival_order(planes)
 
+    local = features.reshape(blocks_here, tile, width)
+    groups = [[a * plane + q for q in range(plane)] for a in range(planes)]
+
     columns = tile_cols.reshape(-1)
-    shifted = [columns]
-    for m in range(1, plane):
-        pairs = [
-            (a * plane + q, a * plane + (q ^ m)) for a in range(planes) for q in range(plane)
-        ]
-        shifted.append(lax.ppermute(columns, "rows", pairs))
-    features, asked = lax.optimization_barrier((features, jnp.stack(shifted)))
-    local = features.reshape(blocks_here, tile, width)
-
-    arrived = {(0, 0): local}
+    asked = lax.all_to_all(
+        jnp.broadcast_to(columns, (plane,) + columns.shape),
+        "rows",
+        split_axis=0,
+        concat_axis=0,
+        axis_index_groups=groups,
+        tiled=True,
+    )
+
+    tall = tile // HALVES
+    held = [local[:, :tall], local[:, tall:]]
+    held[1], asked = lax.optimization_barrier((held[1], asked))
+    arrived = [{} for _ in range(HALVES)]
     for step in range(1, planes):
-        for way in (-1, 1):
-            held = arrived[(step - 1, way)] if step > 1 else local
-            pairs = [
-                (a * plane + q, (a + way) * plane + q)
-                for a in range(planes)
-                if 0 <= a + way < planes and 0 <= a - way * (step - 1) < planes
-                for q in range(plane)
-            ]
-            arrived[(step, way)] = lax.ppermute(held, "rows", pairs)
+        for h in range(HALVES):
+            for way in (-1, 1):
+                pairs = [
+                    (a * plane + q, (a + way) * plane + q)
+                    for a in range(planes)
+                    if 0 <= a + way < planes and 0 <= a - way * (step - 1) < planes
+                    for q in range(plane)
+                ]
+                source = held[h] if step == 1 else arrived[h][step - 1, way]
+                arrived[h][step, way] = lax.ppermute(source, "rows", pairs)
 
     plane_at = jnp.array(
         [[a - way * step for step, way in order[a]] for a in range(planes)], jnp.int32
@@ -213,22 +245,26 @@
         blocks_here + (stage * plane + owners % plane) * capacity + ranks,
     )
 
-    others = jnp.arange(plane, dtype=jnp.int32)
-    swap = (others[:, None] ^ p) == others[None, :]
-    chosen = jnp.sum(jnp.where(swap[:, :, None, None], chosen[None], 0), axis=1)
-    groups = [[a * plane + q for q in range(plane)] for a in range(planes)]
-    froms, starts = [local], [0]
+    froms, starts = [local], [(0, 0)]
     for k in range(planes):
         kinds = sorted(set(order[a][k] for a in range(planes)))
         which_at = jnp.array([[kinds.index(order[a][k])] for a in range(planes)], jnp.int32)
+        which = pick_row(which_at, z)
         ids = chosen[:, k, :].reshape(-1)
-        picked = choose(pick_row(which_at, z), ids, [arrived[kind] for kind in kinds])
-        froms.append(
-            lax.all_to_all(
-                picked, "rows", split_axis=0, concat_axis=0, axis_index_groups=groups, tiled=True
+        if k == 0:
+            lots = [(0, [[local]])]
+        elif k < planes - 1:
+            lots = [(0, [[arrived[h][kind] for h in range(HALVES)] for kind in kinds])]
+        else:
+            lots = [(h * tall, [[arrived[h][kind]] for kind in kinds]) for h in range(HALVES)]
+        for top, sources_k in lots:
+            picked = choose(which, ids, sources_k)
+            froms.append(
+                lax.all_to_all(
+                    picked, "rows", split_axis=0, concat_axis=0, axis_index_groups=groups, tiled=True
+                )
             )
-        )
-        starts.append(blocks_here + k * plane * capacity)
+            starts.append((blocks_here + k * plane * capacity, top))
 
     return layer(
         slots,

time: 265 us -> 283 us (1.068)
  Pallas kernels: 29.4 us -> 46.3 us
  waiting for transfers between devices: 180 us -> 167 us
  starting transfers between devices: 37.7 us -> 48.5 us
  local copies, waits for them, and re-layouts: 11.1 us -> 14.5 us
    ppermute x13 -> x12, waiting for transfers between devices: 148 us -> 127 us  [on_device(): arrived[h][step, way] = lax.ppermute(source, 'rows', pairs)]
    pallas_call x4 -> x5, Pallas kernels: 15.1 us -> 31.8 us  [choose(): pl.pallas_call(functools.partial(choose_kernel, kinds=len(froms), parts=p...]
    all_to_all x4 -> x5, waiting for transfers between devices: 31.7 us -> 39.8 us  [on_device(): lax.all_to_all(picked, 'rows', split_axis=0, concat_axis=0, axis_index_gr...]
    all_to_all x0 -> x1, starting transfers between devices: none -> 5.17 us  [on_device(): lax.all_to_all(jnp.broadcast_to(columns, (plane,) + columns.shape), 'rows...]
    all_to_all x4 -> x5, starting transfers between devices: 17.3 us -> 21.8 us  [on_device(): lax.all_to_all(picked, 'rows', split_axis=0, concat_axis=0, axis_index_gr...]
    slice x0 -> x1, local copies, waits for them, and re-layouts: none -> 3.2 us  [on_device(): held = [local[:, :tall], local[:, tall:]]]
    ppermute x13 -> x12, starting transfers between devices: 20.4 us -> 21.6 us  [on_device(): arrived[h][step, way] = lax.ppermute(source, 'rows', pairs)]
    unnamed x23 -> x28, local copies, waits for them, and re-layouts: 10.1 us -> 9.75 us
  transfers between devices with their start and end apart: 17 -> 18, of which waited for: 7 -> 11; matrix products, arithmetic and copies ran while one was open for 2% -> 3% of each run, Pallas kernels for 4% -> 8%
where the time goes in v3:
time: 283 us; the launch traced here: 282 us
  waiting for transfers between devices  167 us (59%)
  starting transfers between devices  48.5 us (17%)
  Pallas kernels  46.3 us (16%)
  local copies, waits for them, and re-layouts  14.5 us (5%)
  other arithmetic  4.79 us (2%)
    ppermute x12, waiting for transfers between devices, on_device(): arrived[h][step, way] = lax.ppermute(source, 'rows', pairs)  127 us
    all_to_all x5, waiting for transfers between devices, on_device(): lax.all_to_all(picked, 'rows', split_axis=0, concat_axis=0, axis_index_gr...  39.8 us
    pallas_call x5, Pallas kernels, choose(): pl.pallas_call(functools.partial(choose_kernel, kinds=len(froms), parts=p...  31.8 us
    all_to_all x5, starting transfers between devices, on_device(): lax.all_to_all(picked, 'rows', split_axis=0, concat_axis=0, axis_index_gr...  21.8 us
    ppermute x12, starting transfers between devices, on_device(): arrived[h][step, way] = lax.ppermute(source, 'rows', pairs)  21.6 us
    pallas_call x1, Pallas kernels, layer(): pl.pallas_call(functools.partial(layer_kernel, pieces=len(froms), starts=...  14.6 us
    unnamed x28, local copies, waits for them, and re-layouts  9.75 us
  transfers between devices with their start and end apart: 18, of which 11 were waited for; matrix products, arithmetic and copies ran while one was open for 3% of the time, Pallas kernels for 8%

profile of v3, /device:TPU:0, one launch (start us, length us, event | category | flops | bytes accessed | tf_op | source)
XLA Modules:
  0.0 281.6 jit_solution(10739181852111072038)
XLA Ops:
  0.0 0.9 copy.20
  1.6 5.2 %all-to-all-start = ((s32[8,1,192]{2,1,0:T(1,128)}), s32[8,1,192]{2,1,0:T(1,128)S(1)}, u32[]{:S(2)}, u32[]{:S(2)}) async-start(s32[8,1,192]{2,1,0:T(1,128)} %broadcast_in_dim.89), calls=%async_computation | async-start | bytes 16384 | tf_op jit(solution)/shard_map/all_to_all | solution.py:180
  6.8 0.8 select_reduce_fusion.3
  7.7 3.2 %fusion.4 = (bf16[32,64,256]{2,1,0:T(8,128)(2,1)}, bf16[32,64,256]{2,1,0:T(8,128)(2,1)}) fusion(bf16[32,128,256]{2,1,0:T(8,128)(2,1)} %bitcast.16), kind=kLoop, calls=%fused_computation.39 | loop fusion | bytes 4194304 | tf_op jit(solution)/shard_map/slice | solution.py:190
  11.9 0.6 select_reduce_fusion
  13.2 8.3 %choose_blocks.5 = bf16[40,128,256]{2,1,0:T(8,128)(2,1)S(1)} custom-call(s32[1]{0:T(128)} %constant.95.which, s32[40]{0:T(128)S(1)} %reshape_squeeze.12.ids, bf16[32,128,256]{2,1,0:T(8,128)(2,1)S(1)} %bitcast.17), custom_call_target="tpu_custom_call" | custom-call | bytes 524288000 | tf_op jit(solution)/shard_map/choose_blocks/pallas_call | solution.py:66
  21.4 1.5 copy-done.3
  22.9 4.5 %all-to-all-start.1 = ((bf16[40,128,256]{2,1,0:T(8,128)(2,1)}), bf16[40,128,256]{2,1,0:T(8,128)(2,1)}, u32[]{:S(2)}, u32[]{:S(2)}) async-start(bf16[40,128,256]{2,1,0:T(8,128)(2,1)} %copy-done.3), calls=%async_computation.1 | async-start | bytes 5242880 | tf_op jit(solution)/shard_map/all_to_all | solution.py:263
  27.5 3.6 %collective-permute-start.2 = (bf16[32,64,256]{2,1,0:T(8,128)(2,1)}, bf16[32,64,256]{2,1,0:T(8,128)(2,1)S(1)}, u32[]{:S(2)}, u32[]{:S(2)}) collective-permute-start(bf16[32,64,256]{2,1,0:T(8,128)(2,1)} %get-tuple-element.13), channel_id=1, source_target_pairs={{0,8},{1,9},{2,10},{3,11},{4,12},{5,13},{6,14},{7,15},{8,16},{9,17... | collective-permute-start | bytes 3145736 | tf_op jit(solution)/shard_map/ppermute | solution.py:203
  31.0 1.3 collective-permute-start
  32.3 5.6 %collective-permute-start.3 = (bf16[32,64,256]{2,1,0:T(8,128)(2,1)}, bf16[32,64,256]{2,1,0:T(8,128)(2,1)}, u32[]{:S(2)}, u32[]{:S(2)}) collective-permute-start(bf16[32,64,256]{2,1,0:T(8,128)(2,1)} %get-tuple-element.8), channel_id=1, source_target_pairs={{0,8},{1,9},{2,10},{3,11},{4,12},{5,13},{6,14},{7,15},{8,16},{9,17... | collective-permute-start | bytes 3145736 | tf_op jit(solution)/shard_map/ppermute | solution.py:203
  37.9 1.3 collective-permute-start.1
  39.2 0.7 select_reduce_fusion.7
  40.1 14.7 %collective-permute-done.2.refs_2_.refs_0_ = bf16[32,64,256]{2,1,0:T(8,128)(2,1)S(1)} collective-permute-done((bf16[32,64,256]{2,1,0:T(8,128)(2,1)}, bf16[32,64,256]{2,1,0:T(8,128)(2,1)S(1)}, u32[]{:S(2)}, u32[]{:S(2)}) %collective-permute-start.2) | collective-permute-done | bytes 1048608 | tf_op jit(solution)/shard_map/ppermute | solution.py:203
  54.8 4.5 %collective-permute-done.refs_0_ = bf16[32,64,256]{2,1,0:T(8,128)(2,1)} collective-permute-done((bf16[32,64,256]{2,1,0:T(8,128)(2,1)}, bf16[32,64,256]{2,1,0:T(8,128)(2,1)}, u32[]{:S(2)}, u32[]{:S(2)}) %collective-permute-start) | collective-permute-done | bytes 1048608 | tf_op jit(solution)/shard_map/ppermute | solution.py:203
  59.3 17.4 %collective-permute-done.3.refs_3_.refs_1_ = bf16[32,64,256]{2,1,0:T(8,128)(2,1)} collective-permute-done((bf16[32,64,256]{2,1,0:T(8,128)(2,1)}, bf16[32,64,256]{2,1,0:T(8,128)(2,1)}, u32[]{:S(2)}, u32[]{:S(2)}) %collective-permute-start.3) | collective-permute-done | bytes 1048608 | tf_op jit(solution)/shard_map/ppermute | solution.py:203
  76.7 4.2 %collective-permute-done.1.refs_1_ = bf16[32,64,256]{2,1,0:T(8,128)(2,1)} collective-permute-done((bf16[32,64,256]{2,1,0:T(8,128)(2,1)}, bf16[32,64,256]{2,1,0:T(8,128)(2,1)}, u32[]{:S(2)}, u32[]{:S(2)}) %collective-permute-start.1) | collective-permute-done | bytes 1048608 | tf_op jit(solution)/shard_map/ppermute | solution.py:203
  80.9 6.8 %choose_blocks.6 = bf16[40,128,256]{2,1,0:T(8,128)(2,1)S(1)} custom-call(s32[1]{0:T(128)} %bitcast.1.which, s32[40]{0:T(128)S(1)} %reshape_squeeze.13.ids, bf16[32,64,256]{2,1,0:T(8,128)(2,1)} %collective-permute-done.refs_0_, bf16[32,64,256]{2,1,0:T(8,128)(2,1)} %collective-permute-done.1.refs_1_, ...), custom_call_target="tpu_custom_call" | custom-call | bytes 524288000 | tf_op jit(solution)/shard_map/choose_blocks/pallas_call | solution.py:66
  87.7 1.5 copy-done.2
  89.2 4.5 %all-to-all-start.2 = ((bf16[40,128,256]{2,1,0:T(8,128)(2,1)}), bf16[40,128,256]{2,1,0:T(8,128)(2,1)}, u32[]{:S(2)}, u32[]{:S(2)}) async-start(bf16[40,128,256]{2,1,0:T(8,128)(2,1)} %copy-done.2), calls=%async_computation.2 | async-start | bytes 5242880 | tf_op jit(solution)/shard_map/all_to_all | solution.py:263
  93.7 1.6 collective-permute-start.6
  95.4 1.3 collective-permute-start.4
  96.7 0.7 collective-permute-start.9
  97.4 27.6 %collective-permute-done.4.refs_2_.refs_0_ = bf16[32,64,256]{2,1,0:T(8,128)(2,1)} collective-permute-done((bf16[32,64,256]{2,1,0:T(8,128)(2,1)}, bf16[32,64,256]{2,1,0:T(8,128)(2,1)}, u32[]{:S(2)}, u32[]{:S(2)}) %collective-permute-start.4) | collective-permute-done | bytes 1048608 | tf_op jit(solution)/shard_map/ppermute | solution.py:203
  125.0 1.3 collective-permute-start.8
  126.3 1.7 collective-permute-start.7
  128.0 1.3 collective-permute-start.5
  129.3 0.7 select_reduce_fusion.5
  130.2 23.1 %collective-permute-done.8.refs_2_ = bf16[32,64,256]{2,1,0:T(8,128)(2,1)} collective-permute-done((bf16[32,64,256]{2,1,0:T(8,128)(2,1)}, bf16[32,64,256]{2,1,0:T(8,128)(2,1)}, u32[]{:S(2)}, u32[]{:S(2)}) %collective-permute-start.8) | collective-permute-done | bytes 1048608 | tf_op jit(solution)/shard_map/ppermute | solution.py:203
  153.3 4.5 %choose_blocks.8 = bf16[40,64,256]{2,1,0:T(8,128)(2,1)S(1)} custom-call(s32[1]{0:T(128)} %bitcast.3.which, s32[40]{0:T(128)S(1)} %reshape_squeeze.15.ids, bf16[32,64,256]{2,1,0:T(8,128)(2,1)} %collective-permute-done.4.refs_2_.refs_0_, bf16[32,64,256]{2,1,0:T(8,128)(2,1)} %collective-permute-done.6.refs_4_.refs_1_, ...), custom_call_target="tpu_custom_call" | custom-call | bytes 262144000 | tf_op jit(solution)/shard_map/choose_blocks/pallas_call | solution.py:66
  157.8 1.0 copy-done.4
  158.8 3.9 %all-to-all-start.4 = ((bf16[40,64,256]{2,1,0:T(8,128)(2,1)}), bf16[40,64,256]{2,1,0:T(8,128)(2,1)S(1)}, u32[]{:S(2)}, u32[]{:S(2)}) async-start(bf16[40,64,256]{2,1,0:T(8,128)(2,1)} %copy-done.4), calls=%async_computation.4 | async-start | bytes 2621440 | tf_op jit(solution)/shard_map/all_to_all | solution.py:263
  162.7 0.7 collective-permute-start.11
  163.5 10.8 %collective-permute-done.5.refs_3_.refs_0_ = bf16[32,64,256]{2,1,0:T(8,128)(2,1)} collective-permute-done((bf16[32,64,256]{2,1,0:T(8,128)(2,1)}, bf16[32,64,256]{2,1,0:T(8,128)(2,1)}, u32[]{:S(2)}, u32[]{:S(2)}) %collective-permute-start.5) | collective-permute-done | bytes 1048608 | tf_op jit(solution)/shard_map/ppermute | solution.py:203
  174.3 1.3 collective-permute-start.10
  175.6 24.5 %collective-permute-done.10.refs_2_ = bf16[32,64,256]{2,1,0:T(8,128)(2,1)S(1)} collective-permute-done((bf16[32,64,256]{2,1,0:T(8,128)(2,1)}, bf16[32,64,256]{2,1,0:T(8,128)(2,1)S(1)}, u32[]{:S(2)}, u32[]{:S(2)}) %collective-permute-start.10) | collective-permute-done | bytes 1048608 | tf_op jit(solution)/shard_map/ppermute | solution.py:203
  200.1 5.6 %choose_blocks.9 = bf16[40,64,256]{2,1,0:T(8,128)(2,1)S(1)} custom-call(s32[1]{0:T(128)} %bitcast.3.which, s32[40]{0:T(128)S(1)} %reshape_squeeze.15.ids, bf16[32,64,256]{2,1,0:T(8,128)(2,1)} %collective-permute-done.5.refs_3_.refs_0_, bf16[32,64,256]{2,1,0:T(8,128)(2,1)} %collective-permute-done.7.refs_5_.refs_1_, ...), custom_call_target="tpu_custom_call" | custom-call | bytes 262144000 | tf_op jit(solution)/shard_map/choose_blocks/pallas_call | solution.py:66
  205.7 1.1 copy-done.5
  206.8 4.4 %all-to-all-start.5 = ((bf16[40,64,256]{2,1,0:T(8,128)(2,1)}), bf16[40,64,256]{2,1,0:T(8,128)(2,1)}, u32[]{:S(2)}, u32[]{:S(2)}) async-start(bf16[40,64,256]{2,1,0:T(8,128)(2,1)} %copy-done.5), calls=%async_computation.5 | async-start | bytes 2621440 | tf_op jit(solution)/shard_map/all_to_all | solution.py:263
  211.2 0.6 select_reduce_fusion.6
  212.0 1.2 copy-done.7
  213.2 6.5 %choose_blocks.7 = bf16[40,128,256]{2,1,0:T(8,128)(2,1)S(1)} custom-call(s32[1]{0:T(128)} %bitcast.2.which, s32[40]{0:T(128)S(1)} %reshape_squeeze.14.ids, bf16[32,64,256]{2,1,0:T(8,128)(2,1)S(1)} %copy-done.7, bf16[32,64,256]{2,1,0:T(8,128)(2,1)} %collective-permute-done.3.refs_3_.refs_1_, bf16[32,64,256]{2,1,0:T(8,128)(2,1)} %collective-permute-done.4.refs_2_.refs_0_, ...), custom_call_target="tpu_custom_call" | custom-call | bytes 524288000 | tf_op jit(solution)/shard_map/choose_blocks/pallas_call | solution.py:66
  219.8 1.5 copy-done.1
  221.3 8.1 %all-to-all-done.5.refs_5_ = bf16[40,64,256]{2,1,0:T(8,128)(2,1)} async-done(((bf16[40,64,256]{2,1,0:T(8,128)(2,1)}), bf16[40,64,256]{2,1,0:T(8,128)(2,1)}, u32[]{:S(2)}, u32[]{:S(2)}) %all-to-all-start.5) | async-done | bytes 1310752 | tf_op jit(solution)/shard_map/all_to_all | solution.py:263
  229.4 4.4 %all-to-all-start.3 = ((bf16[40,128,256]{2,1,0:T(8,128)(2,1)}), bf16[40,128,256]{2,1,0:T(8,128)(2,1)}, u32[]{:S(2)}, u32[]{:S(2)}) async-start(bf16[40,128,256]{2,1,0:T(8,128)(2,1)} %copy-done.1), calls=%async_computation.3 | async-start | bytes 5242880 | tf_op jit(solution)/shard_map/all_to_all | solution.py:263
  234.4 31.7 %all-to-all-done.3.refs_3_ = bf16[40,128,256]{2,1,0:T(8,128)(2,1)} async-done(((bf16[40,128,256]{2,1,0:T(8,128)(2,1)}), bf16[40,128,256]{2,1,0:T(8,128)(2,1)}, u32[]{:S(2)}, u32[]{:S(2)}) %all-to-all-start.3) | async-done | bytes 2621472 | tf_op jit(solution)/shard_map/all_to_all | solution.py:263
  266.1 0.9 copy-done.8
  267.1 14.6 %sage_layer.1 = bf16[4096,256]{1,0:T(8,128)(2,1)} custom-call(s32[192]{0:T(256)S(1)} %compare_select_fusion.slots, bf16[32,128,256]{2,1,0:T(8,128)(2,1)S(1)} %bitcast.18, bf16[40,128,256]{2,1,0:T(8,128)(2,1)} %all-to-all-done.1.refs_1_, bf16[40,128,256]{2,1,0:T(8,128)(2,1)} %all-to-all-done.2.refs_2_, bf16[40,128,256]{2,1,0:T(8,128)(2,1)} %all-to-all-done.3.refs_3_, ...), custom_call_target="tpu_custom_call" | custom-call | flops 2684354560 | bytes 25165824 | tf_op jit(solution)/shard_map/sage_layer/pallas_call | solution.py:135
  (57 shorter events, 3.5 us)
Async XLA Ops:
  0.0 13.2 %copy-start = (bf16[4096,256]{1,0:T(8,128)(2,1)S(1)}, bf16[4096,256]{1,0:T(8,128)(2,1)}, u32[]{:S(2)}) copy-start(bf16[4096,256]{1,0:T(8,128)(2,1)} %param.11) | copy-start | bytes 6291460
  1.6 9.9 %all-to-all-start = ((s32[8,1,192]{2,1,0:T(1,128)}), s32[8,1,192]{2,1,0:T(1,128)S(1)}, u32[]{:S(2)}, u32[]{:S(2)}) async-start(s32[8,1,192]{2,1,0:T(1,128)} %broadcast_in_dim.89), calls=%async_computation | async-start | bytes 16384 | tf_op jit(solution)/shard_map/all_to_all | solution.py:180
  21.4 1.5 copy-start.3
  22.9 16.3 %copy-start.12 = (s32[4,1]{0,1:T(1,128)S(1)}, s32[4,1]{0,1:T(1,128)}, u32[]{:S(2)}) copy-start(s32[4,1]{0,1:T(1,128)} %constant.91.clone) | copy-start | bytes 52
  22.9 66.2 %all-to-all-start.1 = ((bf16[40,128,256]{2,1,0:T(8,128)(2,1)}), bf16[40,128,256]{2,1,0:T(8,128)(2,1)}, u32[]{:S(2)}, u32[]{:S(2)}) async-start(bf16[40,128,256]{2,1,0:T(8,128)(2,1)} %copy-done.3), calls=%async_computation.1 | async-start | bytes 5242880 | tf_op jit(solution)/shard_map/all_to_all | solution.py:263
  27.5 27.3 %collective-permute-start.2 = (bf16[32,64,256]{2,1,0:T(8,128)(2,1)}, bf16[32,64,256]{2,1,0:T(8,128)(2,1)S(1)}, u32[]{:S(2)}, u32[]{:S(2)}) collective-permute-start(bf16[32,64,256]{2,1,0:T(8,128)(2,1)} %get-tuple-element.13), channel_id=1, source_target_pairs={{0,8},{1,9},{2,10},{3,11},{4,12},{5,13},{6,14},{7,15},{8,16},{9,17... | collective-permute-start | bytes 3145736 | tf_op jit(solution)/shard_map/ppermute | solution.py:203
  31.0 28.2 %collective-permute-start = (bf16[32,64,256]{2,1,0:T(8,128)(2,1)}, bf16[32,64,256]{2,1,0:T(8,128)(2,1)}, u32[]{:S(2)}, u32[]{:S(2)}) collective-permute-start(bf16[32,64,256]{2,1,0:T(8,128)(2,1)} %get-tuple-element.13), channel_id=1, source_target_pairs={{8,0},{9,1},{10,2},{11,3},{12,4},{13,5},{14,6},{15,7},{16,8},{17,9... | collective-permute-start | bytes 3145736 | tf_op jit(solution)/shard_map/ppermute | solution.py:203
  32.3 44.3 %collective-permute-start.3 = (bf16[32,64,256]{2,1,0:T(8,128)(2,1)}, bf16[32,64,256]{2,1,0:T(8,128)(2,1)}, u32[]{:S(2)}, u32[]{:S(2)}) collective-permute-start(bf16[32,64,256]{2,1,0:T(8,128)(2,1)} %get-tuple-element.8), channel_id=1, source_target_pairs={{0,8},{1,9},{2,10},{3,11},{4,12},{5,13},{6,14},{7,15},{8,16},{9,17... | collective-permute-start | bytes 3145736 | tf_op jit(solution)/shard_map/ppermute | solution.py:203
  37.9 43.0 %collective-permute-start.1 = (bf16[32,64,256]{2,1,0:T(8,128)(2,1)}, bf16[32,64,256]{2,1,0:T(8,128)(2,1)}, u32[]{:S(2)}, u32[]{:S(2)}) collective-permute-start(bf16[32,64,256]{2,1,0:T(8,128)(2,1)} %get-tuple-element.8), channel_id=1, source_target_pairs={{8,0},{9,1},{10,2},{11,3},{12,4},{13,5},{14,6},{15,7},{16,8},{17,9... | collective-permute-start | bytes 3145736 | tf_op jit(solution)/shard_map/ppermute | solution.py:203
  54.8 39.0 %copy-start.6 = (bf16[32,64,256]{2,1,0:T(8,128)(2,1)}, bf16[32,64,256]{2,1,0:T(8,128)(2,1)S(1)}, u32[]{:S(2)}) copy-start(bf16[32,64,256]{2,1,0:T(8,128)(2,1)S(1)} %collective-permute-done.2.refs_2_.refs_0_) | copy-start | bytes 3145732
  87.7 1.5 copy-start.2
  89.2 40.1 %copy-start.11 = (s32[4,1]{0,1:T(1,128)S(1)}, s32[4,1]{0,1:T(1,128)}, u32[]{:S(2)}) copy-start(s32[4,1]{0,1:T(1,128)} %constant.93.clone) | copy-start | bytes 52
  89.2 69.7 %all-to-all-start.2 = ((bf16[40,128,256]{2,1,0:T(8,128)(2,1)}), bf16[40,128,256]{2,1,0:T(8,128)(2,1)}, u32[]{:S(2)}, u32[]{:S(2)}) async-start(bf16[40,128,256]{2,1,0:T(8,128)(2,1)} %copy-done.2), calls=%async_computation.2 | async-start | bytes 5242880 | tf_op jit(solution)/shard_map/all_to_all | solution.py:263
  93.7 2.9 %collective-permute-start.6 = (bf16[32,64,256]{2,1,0:T(8,128)(2,1)S(1)}, bf16[32,64,256]{2,1,0:T(8,128)(2,1)}, u32[]{:S(2)}, u32[]{:S(2)}) collective-permute-start(bf16[32,64,256]{2,1,0:T(8,128)(2,1)S(1)} %collective-permute-done.2.refs_2_.refs_0_), channel_id=1, source_target_pairs={{8,16},{9,17},{10,18},{11,19},{12,20},{13,21},{14,22},{15,23},{16,... | collective-permute-start | bytes 3145736 | tf_op jit(solution)/shard_map/ppermute | solution.py:203
  95.4 29.6 %collective-permute-start.4 = (bf16[32,64,256]{2,1,0:T(8,128)(2,1)}, bf16[32,64,256]{2,1,0:T(8,128)(2,1)}, u32[]{:S(2)}, u32[]{:S(2)}) collective-permute-start(bf16[32,64,256]{2,1,0:T(8,128)(2,1)} %collective-permute-done.refs_0_), channel_id=1, source_target_pairs={{8,0},{9,1},{10,2},{11,3},{12,4},{13,5},{14,6},{15,7},{16,8},{17,9... | collective-permute-start | bytes 3145736 | tf_op jit(solution)/shard_map/ppermute | solution.py:203
  96.7 33.5 %collective-permute-start.9 = (bf16[32,64,256]{2,1,0:T(8,128)(2,1)}, bf16[32,64,256]{2,1,0:T(8,128)(2,1)S(1)}, u32[]{:S(2)}, u32[]{:S(2)}) collective-permute-start(bf16[32,64,256]{2,1,0:T(8,128)(2,1)} %collective-permute-done.6.refs_4_.refs_1_), channel_id=1, source_target_pairs={{16,24},{17,25},{18,26},{19,27},{20,28},{21,29},{22,30},{23,31}} | collective-permute-start | bytes 3145736 | tf_op jit(solution)/shard_map/ppermute | solution.py:203
  125.0 28.3 %collective-permute-start.8 = (bf16[32,64,256]{2,1,0:T(8,128)(2,1)}, bf16[32,64,256]{2,1,0:T(8,128)(2,1)}, u32[]{:S(2)}, u32[]{:S(2)}) collective-permute-start(bf16[32,64,256]{2,1,0:T(8,128)(2,1)} %collective-permute-done.4.refs_2_.refs_0_), channel_id=1, source_target_pairs={{8,0},{9,1},{10,2},{11,3},{12,4},{13,5},{14,6},{15,7}} | collective-permute-start | bytes 3145736 | tf_op jit(solution)/shard_map/ppermute | solution.py:203
  126.3 36.5 %collective-permute-start.7 = (bf16[32,64,256]{2,1,0:T(8,128)(2,1)}, bf16[32,64,256]{2,1,0:T(8,128)(2,1)}, u32[]{:S(2)}, u32[]{:S(2)}) collective-permute-start(bf16[32,64,256]{2,1,0:T(8,128)(2,1)} %collective-permute-done.3.refs_3_.refs_1_), channel_id=1, source_target_pairs={{8,16},{9,17},{10,18},{11,19},{12,20},{13,21},{14,22},{15,23},{16,... | collective-permute-start | bytes 3145736 | tf_op jit(solution)/shard_map/ppermute | solution.py:203
  128.0 46.3 %collective-permute-start.5 = (bf16[32,64,256]{2,1,0:T(8,128)(2,1)}, bf16[32,64,256]{2,1,0:T(8,128)(2,1)}, u32[]{:S(2)}, u32[]{:S(2)}) collective-permute-start(bf16[32,64,256]{2,1,0:T(8,128)(2,1)} %collective-permute-done.1.refs_1_), channel_id=1, source_target_pairs={{8,0},{9,1},{10,2},{11,3},{12,4},{13,5},{14,6},{15,7},{16,8},{17,9... | collective-permute-start | bytes 3145736 | tf_op jit(solution)/shard_map/ppermute | solution.py:203
  157.8 1.1 copy-start.4
  158.8 47.9 %all-to-all-start.4 = ((bf16[40,64,256]{2,1,0:T(8,128)(2,1)}), bf16[40,64,256]{2,1,0:T(8,128)(2,1)S(1)}, u32[]{:S(2)}, u32[]{:S(2)}) async-start(bf16[40,64,256]{2,1,0:T(8,128)(2,1)} %copy-done.4), calls=%async_computation.4 | async-start | bytes 2621440 | tf_op jit(solution)/shard_map/all_to_all | solution.py:263
  162.7 12.8 %collective-permute-start.11 = (bf16[32,64,256]{2,1,0:T(8,128)(2,1)}, bf16[32,64,256]{2,1,0:T(8,128)(2,1)S(1)}, u32[]{:S(2)}, u32[]{:S(2)}) collective-permute-start(bf16[32,64,256]{2,1,0:T(8,128)(2,1)} %collective-permute-done.7.refs_5_.refs_1_), channel_id=1, source_target_pairs={{16,24},{17,25},{18,26},{19,27},{20,28},{21,29},{22,30},{23,31}} | collective-permute-start | bytes 3145736 | tf_op jit(solution)/shard_map/ppermute | solution.py:203
  174.3 25.8 %collective-permute-start.10 = (bf16[32,64,256]{2,1,0:T(8,128)(2,1)}, bf16[32,64,256]{2,1,0:T(8,128)(2,1)S(1)}, u32[]{:S(2)}, u32[]{:S(2)}) collective-permute-start(bf16[32,64,256]{2,1,0:T(8,128)(2,1)} %collective-permute-done.5.refs_3_.refs_0_), channel_id=1, source_target_pairs={{8,0},{9,1},{10,2},{11,3},{12,4},{13,5},{14,6},{15,7}} | collective-permute-start | bytes 3145736 | tf_op jit(solution)/shard_map/ppermute | solution.py:203
  205.7 1.1 copy-start.5
  206.8 4.4 %copy-start.10 = (s32[4,1]{0,1:T(1,128)S(1)}, s32[4,1]{0,1:T(1,128)}, u32[]{:S(2)}) copy-start(s32[4,1]{0,1:T(1,128)} %constant.92.clone) | copy-start | bytes 52
  206.8 22.6 %all-to-all-start.5 = ((bf16[40,64,256]{2,1,0:T(8,128)(2,1)}), bf16[40,64,256]{2,1,0:T(8,128)(2,1)}, u32[]{:S(2)}, u32[]{:S(2)}) async-start(bf16[40,64,256]{2,1,0:T(8,128)(2,1)} %copy-done.5), calls=%async_computation.5 | async-start | bytes 2621440 | tf_op jit(solution)/shard_map/all_to_all | solution.py:263
  212.0 1.2 copy-start.7
  219.8 1.6 copy-start.1
  221.3 44.8 %copy-start.9 = (s32[4096]{0:T(1024)S(1)}, s32[4096]{0:T(1024)}, u32[]{:S(2)}) copy-start(s32[4096]{0:T(1024)} %param.14) | copy-start | bytes 49156
  229.4 36.7 %all-to-all-start.3 = ((bf16[40,128,256]{2,1,0:T(8,128)(2,1)}), bf16[40,128,256]{2,1,0:T(8,128)(2,1)}, u32[]{:S(2)}, u32[]{:S(2)}) async-start(bf16[40,128,256]{2,1,0:T(8,128)(2,1)} %copy-done.1), calls=%async_computation.3 | async-start | bytes 5242880 | tf_op jit(solution)/shard_map/all_to_all | solution.py:263
  266.1 1.0 copy-start.8

commit v4 on v3

v4 whole, which is shorter than its diff:
```python
import functools

import jax
import jax.numpy as jnp
from jax import lax
from jax.experimental import pallas as pl
from jax.experimental.pallas import tpu as pltpu
from jax.sharding import PartitionSpec as P

REM_PB = 4
PLANES = 4
CHUNKS = 4
VMEM_LIMIT = 60 * 1024 * 1024


def choose_kernel(ids, blocks, out, held, in_sem, out_sem):
    count = out.shape[0]
    for n in range(count):
        pltpu.make_async_copy(blocks.at[ids[n]], held.at[n], in_sem).start()
    pltpu.make_async_copy(out, held, in_sem).wait()
    leaving = pltpu.make_async_copy(held, out, out_sem)
    leaving.start()
    leaving.wait()


def choose(ids, blocks):
    out = (ids.shape[0],) + blocks.shape[1:]
    moved = out[0] * out[1] * out[2] * 2
    return pl.pallas_call(
        choose_kernel,
        grid_spec=pltpu.PrefetchScalarGridSpec(
            num_scalar_prefetch=1,
            grid=(1,),
            in_specs=[pl.BlockSpec(memory_space=pltpu.HBM)],
            out_specs=pl.BlockSpec(memory_space=pltpu.HBM),
            scratch_shapes=[
                pltpu.VMEM(out, blocks.dtype),
                pltpu.SemaphoreType.DMA,
                pltpu.SemaphoreType.DMA,
            ],
        ),
        out_shape=jax.ShapeDtypeStruct(out, blocks.dtype),
        compiler_params=pltpu.CompilerParams(vmem_limit_bytes=VMEM_LIMIT),
        cost_estimate=pl.CostEstimate(flops=0, bytes_accessed=4 * moved, transcendentals=0),
        name="choose_blocks",
    )(ids, blocks)


def layer_kernel(slots, *refs, pieces, starts):
    froms = refs[:pieces]
    masks, degree, weight, out, table, means, sems = refs[pieces:]
    step = pl.program_id(0)
    rows, per_block = masks.shape[:2]
    tile, width = table.shape[1:]

    @pl.when(step == 0)
    def _():
        copies = [
            pltpu.make_async_copy(
                piece,
                table.at[pl.ds(at, piece.shape[0]), pl.ds(top, piece.shape[1])],
                sems.at[n],
            )
            for n, (piece, (at, top)) in enumerate(zip(froms, starts))
        ]
        for copy in copies:
            copy.start()
        for copy in copies:
            copy.wait()

    for r in range(rows):
        row = step * rows + r
        mask = jnp.concatenate(
            [masks[r, t].astype(jnp.float32).astype(jnp.bfloat16) for t in range(per_block)], axis=1
        )
        picked = jnp.concatenate(
            [table[slots[row * per_block + t]] for t in range(per_block)], axis=0
        )
        sums = jnp.dot(mask, picked, preferred_element_type=jnp.float32)
        count = jnp.broadcast_to(degree[pl.ds(row, 1), :].astype(jnp.float32), (tile, tile)).T
        count = jnp.concatenate([count] * (width // tile), axis=1)
        means[pl.ds(r * tile, tile), :] = (sums / count).astype(jnp.bfloat16)
    own = table[pl.ds(step * rows, rows)].reshape(rows * tile, width)
    hidden = jnp.dot(own, weight[:width], preferred_element_type=jnp.float32)
    hidden = hidden + jnp.dot(means[...], weight[width:], preferred_element_type=jnp.float32)
    hidden = jnp.maximum(hidden, 0.0)
    scale = lax.rsqrt(jnp.sum(hidden * hidden, axis=1, keepdims=True) + 1e-06)
    out[...] = (hidden * scale).astype(jnp.bfloat16)


def layer(slots, froms, starts, blocks_in_table, tile_masks, degree, weight):
    blocks_here, per_block, tile, _ = tile_masks.shape
    width = weight.shape[0] // 2
    out_width = weight.shape[1]
    rows = 4 if blocks_here % 4 == 0 else 1
    return pl.pallas_call(
        functools.partial(layer_kernel, pieces=len(froms), starts=starts),
        grid_spec=pltpu.PrefetchScalarGridSpec(
            num_scalar_prefetch=1,
            grid=(blocks_here // rows,),
            in_specs=[pl.BlockSpec(memory_space=pltpu.HBM)] * len(froms)
            + [
                pl.BlockSpec((rows, per_block, tile, tile), lambda r, s: (r, 0, 0, 0)),
                pl.BlockSpec((blocks_here, tile), lambda r, s: (0, 0)),
                pl.BlockSpec((2 * width, out_width), lambda r, s: (0, 0)),
            ],
            out_specs=pl.BlockSpec((rows * tile, out_width), lambda r, s: (r, 0)),
            scratch_shapes=[
                pltpu.VMEM((blocks_in_table, tile, width), jnp.bfloat16),
                pltpu.VMEM((rows * tile, width), jnp.bfloat16),
                pltpu.SemaphoreType.DMA((len(froms),)),
            ],
        ),
        out_shape=jax.ShapeDtypeStruct((blocks_here * tile, out_width), jnp.bfloat16),
        compiler_params=pltpu.CompilerParams(vmem_limit_bytes=VMEM_LIMIT),
        cost_estimate=pl.CostEstimate(
            flops=2 * blocks_here * tile * (per_block * tile + 2 * width) * width,
            bytes_accessed=blocks_here * per_block * tile * tile * 4 + blocks_in_table * tile * width * 2,
            transcendentals=blocks_here * tile,
        ),
        name="sage_layer",
    )(slots, *froms, tile_masks, degree, weight)


def on_device(features, tile_cols, tile_masks, degree, weight):
    blocks_here, per_block = tile_cols.shape
    tile = tile_masks.shape[2]
    width = features.shape[1]
    peers = lax.axis_size("rows")
    planes = PLANES if peers % PLANES == 0 else 1
    plane = peers // planes
    myself = lax.axis_index("rows")
    p = myself % plane
    capacity = max(2, (REM_PB * blocks_here + peers - 2) // (peers - 1))
    local = features.reshape(blocks_here, tile, width)
    groups = [[a * plane + q for q in range(plane)] for a in range(planes)]
    lines = [[a * plane + q for a in range(planes)] for q in range(plane)]

    tall = tile // CHUNKS
    spread = [
        lax.all_gather(
            local[:, c * tall : (c + 1) * tall], "rows", axis_index_groups=lines, tiled=True
        )
        for c in range(CHUNKS)
    ]

    columns = tile_cols.reshape(-1)
    asked = lax.all_to_all(
        jnp.broadcast_to(columns, (plane,) + columns.shape),
        "rows",
        split_axis=0,
        concat_axis=0,
        axis_index_groups=groups,
        tiled=True,
    )
    blocks = jnp.arange(blocks_here, dtype=jnp.int32)
    line = jnp.arange(planes, dtype=jnp.int32) * plane + p
    wanted = (line[:, None] * blocks_here + blocks[None, :]).reshape(-1)
    need = jnp.any(asked[:, :, None] == wanted[None, None, :], axis=1)
    need = need.reshape(plane, planes, blocks_here).astype(jnp.int32)
    below = blocks[:, None] > blocks[None, :]
    place = jnp.sum(jnp.where(below, need[:, :, None, :], 0), axis=3)
    seat = jnp.arange(capacity, dtype=jnp.int32)
    taken = (need[:, :, None, :] == 1) & (place[:, :, None, :] == seat[:, None])
    chosen = jnp.sum(jnp.where(taken, blocks, 0), axis=3)
    ids = (chosen + jnp.arange(planes, dtype=jnp.int32)[:, None] * blocks_here).reshape(-1)

    owners, within = columns // blocks_here, columns % blocks_here
    positions = jnp.arange(columns.shape[0], dtype=jnp.int32)
    same = columns[:, None] == columns[None, :]
    first = ~jnp.any(same & (positions[None, :] < positions[:, None]), axis=1)
    ahead = (owners[:, None] == owners[None, :]) & (columns[None, :] < columns[:, None])
    ranks = jnp.sum(ahead & first[None, :], axis=1, dtype=jnp.int32)
    place_of = (owners % plane) * planes + owners // plane
    slots = jnp.where(owners == myself, within, blocks_here + place_of * capacity + ranks)

    froms, starts = [local], [(0, 0)]
    for c in range(CHUNKS):
        froms.append(
            lax.all_to_all(
                choose(ids, spread[c]),
                "rows",
                split_axis=0,
                concat_axis=0,
                axis_index_groups=groups,
                tiled=True,
            )
        )
        starts.append((blocks_here, c * tall))

    return layer(
        slots,
        froms,
        tuple(starts),
        blocks_here + peers * capacity,
        tile_masks,
        degree.reshape(blocks_here, tile),
        weight,
    )


def solution(mesh):
    in_specs = (P("rows", None), P("rows", None), P("rows", None, None, None), P("rows"), P())
    out_specs = P("rows", None)
    return jax.shard_map(
        on_device, mesh=mesh, in_specs=in_specs, out_specs=out_specs, check_vma=False
    )
```

time: 283 us -> 263 us (0.929)
  starting transfers between devices: 48.5 us -> 21.6 us
  waiting for transfers between devices: 167 us -> 185 us
  Pallas kernels: 46.3 us -> 32.6 us
  between operations: 0.33 us -> 13.3 us
  local copies, waits for them, and re-layouts: 14.5 us -> 6.2 us
    all_gather x0 -> x4, waiting for transfers between devices: none -> 148 us  [on_device(): lax.all_gather(local[:, c * tall:(c + 1) * tall], 'rows', axis_index_grou...]
    ppermute x12 -> x0, waiting for transfers between devices: 127 us -> none  [on_device(): arrived[h][step, way] = lax.ppermute(source, 'rows', pairs)]
    ppermute x12 -> x0, starting transfers between devices: 21.6 us -> none  [on_device(): arrived[h][step, way] = lax.ppermute(source, 'rows', pairs)]
    pallas_call x5 -> x4, Pallas kernels: 31.8 us -> 16.9 us  [choose(): pl.pallas_call(choose_kernel, grid_spec=pltpu.PrefetchScalarGridSpec(num_...]
    all_to_all x5 -> x4, waiting for transfers between devices: 39.8 us -> 31.3 us  [on_device(): lax.all_to_all(choose(ids, spread[c]), 'rows', split_axis=0, concat_axis=...]
    unnamed x28 -> x8, local copies, waits for them, and re-layouts: 9.75 us -> 1.63 us
    all_to_all x5 -> x4, starting transfers between devices: 21.8 us -> 16.4 us  [on_device(): lax.all_to_all(choose(ids, spread[c]), 'rows', split_axis=0, concat_axis=...]
    all_to_all x1, waiting for transfers between devices: 0.53 us -> 4.53 us  [on_device(): lax.all_to_all(jnp.broadcast_to(columns, (plane,) + columns.shape), 'rows...]
  transfers between devices with their start and end apart: 18 -> 9, of which waited for: 11 -> 6; matrix products, arithmetic and copies ran while one was open for 3% -> 2% of each run, Pallas kernels for 8% -> 6%
where the time goes in v4:
time: 263 us; the launch traced here: 262 us
  waiting for transfers between devices  185 us (70%)
  Pallas kernels  32.6 us (12%)
  starting transfers between devices  21.6 us (8%)
  between operations  13.3 us (5%)
  local copies, waits for them, and re-layouts  6.2 us (2%)
    all_gather x4, waiting for transfers between devices, on_device(): lax.all_gather(local[:, c * tall:(c + 1) * tall], 'rows', axis_index_grou...  148 us
    all_to_all x4, waiting for transfers between devices, on_device(): lax.all_to_all(choose(ids, spread[c]), 'rows', split_axis=0, concat_axis=...  31.3 us
    pallas_call x4, Pallas kernels, choose(): pl.pallas_call(choose_kernel, grid_spec=pltpu.PrefetchScalarGridSpec(num_...  16.9 us
    all_to_all x4, starting transfers between devices, on_device(): lax.all_to_all(choose(ids, spread[c]), 'rows', split_axis=0, concat_axis=...  16.4 us
    pallas_call x1, Pallas kernels, layer(): pl.pallas_call(functools.partial(layer_kernel, pieces=len(froms), starts=...  15.7 us
  transfers between devices with their start and end apart: 9, of which 6 were waited for; matrix products, arithmetic and copies ran while one was open for 2% of the time, Pallas kernels for 6%

profile of v4, /device:TPU:0, one launch (start us, length us, event | category | flops | bytes accessed | tf_op | source)
XLA Modules:
  0.0 261.5 jit_solution(7573438932750801553)
XLA Ops:
  6.5 0.0 all-gather.5.cloned.1.call-start
  6.5 2.9 %fusion.5 = (bf16[32,32,256]{2,1,0:T(8,128)(2,1)}, bf16[32,32,256]{2,1,0:T(8,128)(2,1)}, bf16[32,32,256]{2,1,0:T(8,128)(2,1)}, bf16[32,32,256]{2,1,0:T(8,128)(2,1)}) fusion(bf16[32,128,256]{2,1,0:T(8,128)(2,1)} %bitcast.5), kind=kLoop, calls=%fused_computation.31 | loop fusion | bytes 4194304 | tf_op jit(solution)/shard_map/slice | solution.py:142
  9.4 0.0 all-gather.5.cloned.1.call-update
  9.4 0.0 all-gather.7.cloned.1.call-start
  9.5 0.7 all-gather.7.cloned.1.call-update
  10.2 0.0 copy-done.2
  10.2 0.1 copy.12
  10.3 0.1 reshape.124
  10.4 0.6 broadcast_in_dim.26
  11.0 5.2 %all-to-all-start = ((s32[8,1,192]{2,1,0:T(1,128)}), s32[8,1,192]{2,1,0:T(1,128)S(1)}, u32[]{:S(2)}, u32[]{:S(2)}) async-start(s32[8,1,192]{2,1,0:T(1,128)} %broadcast_in_dim.26), calls=%async_computation | async-start | bytes 16384 | tf_op jit(solution)/shard_map/all_to_all | solution.py:148
  16.2 0.1 iota_add_fusion
  16.3 0.1 add.87
  16.4 4.5 %all-to-all-done = s32[8,1,192]{2,1,0:T(1,128)S(1)} async-done(((s32[8,1,192]{2,1,0:T(1,128)}), s32[8,1,192]{2,1,0:T(1,128)S(1)}, u32[]{:S(2)}, u32[]{:S(2)}) %all-to-all-start) | async-done | bytes 6176 | tf_op jit(solution)/shard_map/all_to_all | solution.py:148
  20.9 0.3 compare_reduce_fusion
  21.2 0.1 reshape.127
  21.3 0.6 select_reduce_fusion
  21.9 0.4 select_reduce_fusion.1
  22.4 0.1 broadcast_add_fusion
  22.4 0.1 copy.15
  22.5 0.7 add.90.ids
  23.2 35.0 %all-gather.5.cloned.1.call-done.blocks = bf16[128,32,256]{2,1,0:T(8,128)(2,1)} async-done(((bf16[32,32,256]{2,1,0:T(8,128)(2,1)}), bf16[128,32,256]{2,1,0:T(8,128)(2,1)}) %all-gather.5.cloned.1.call-update) | async-done | bytes 2097168 | tf_op jit(solution)/shard_map/all_gather | solution.py:141
  58.2 4.1 %choose_blocks.4 = bf16[160,32,256]{2,1,0:T(8,128)(2,1)} custom-call(s32[160]{0:T(256)} %add.90.ids, bf16[128,32,256]{2,1,0:T(8,128)(2,1)} %all-gather.5.cloned.1.call-done.blocks), custom_call_target="tpu_custom_call" | custom-call | bytes 10485760 | tf_op jit(solution)/shard_map/choose_blocks/pallas_call | solution.py:29
  62.4 3.7 %all-to-all-start.1 = ((bf16[160,32,256]{2,1,0:T(8,128)(2,1)}), bf16[160,32,256]{2,1,0:T(8,128)(2,1)S(1)}, u32[]{:S(2)}, u32[]{:S(2)}) async-start(bf16[160,32,256]{2,1,0:T(8,128)(2,1)} %choose_blocks.4), calls=%async_computation.1 | async-start | bytes 5242880 | tf_op jit(solution)/shard_map/all_to_all | solution.py:180
  66.1 0.0 all-gather.9.cloned.1.call-start
  66.1 0.7 all-gather.9.cloned.1.call-update
  66.8 37.6 %all-gather.7.cloned.1.call-done.blocks = bf16[128,32,256]{2,1,0:T(8,128)(2,1)} async-done(((bf16[32,32,256]{2,1,0:T(8,128)(2,1)}), bf16[128,32,256]{2,1,0:T(8,128)(2,1)}) %all-gather.7.cloned.1.call-update) | async-done | bytes 2097168 | tf_op jit(solution)/shard_map/all_gather | solution.py:141
  104.4 4.3 %choose_blocks.5 = bf16[160,32,256]{2,1,0:T(8,128)(2,1)} custom-call(s32[160]{0:T(256)} %add.90.ids, bf16[128,32,256]{2,1,0:T(8,128)(2,1)} %all-gather.7.cloned.1.call-done.blocks), custom_call_target="tpu_custom_call" | custom-call | bytes 10485760 | tf_op jit(solution)/shard_map/choose_blocks/pallas_call | solution.py:29
  108.7 0.0 all-to-all-done.1.refs_1_
  108.7 0.0 copy-start
  108.7 4.4 %all-to-all-start.2 = ((bf16[160,32,256]{2,1,0:T(8,128)(2,1)}), bf16[160,32,256]{2,1,0:T(8,128)(2,1)}, u32[]{:S(2)}, u32[]{:S(2)}) async-start(bf16[160,32,256]{2,1,0:T(8,128)(2,1)} %choose_blocks.5), calls=%async_computation.2 | async-start | bytes 5242880 | tf_op jit(solution)/shard_map/all_to_all | solution.py:180
  113.2 0.0 all-gather.11.cloned.1.call-start
  113.2 0.0 copy-done
  113.2 0.5 all-gather.11.cloned.1.call-update
  113.7 36.9 %all-gather.9.cloned.1.call-done.blocks = bf16[128,32,256]{2,1,0:T(8,128)(2,1)} async-done(((bf16[32,32,256]{2,1,0:T(8,128)(2,1)}), bf16[128,32,256]{2,1,0:T(8,128)(2,1)}) %all-gather.9.cloned.1.call-update) | async-done | bytes 2097168 | tf_op jit(solution)/shard_map/all_gather | solution.py:141
  150.7 4.2 %choose_blocks.6 = bf16[160,32,256]{2,1,0:T(8,128)(2,1)} custom-call(s32[160]{0:T(256)} %add.90.ids, bf16[128,32,256]{2,1,0:T(8,128)(2,1)} %all-gather.9.cloned.1.call-done.blocks), custom_call_target="tpu_custom_call" | custom-call | bytes 10485760 | tf_op jit(solution)/shard_map/choose_blocks/pallas_call | solution.py:29
  154.9 0.0 all-to-all-done.2.refs_2_
  154.9 3.8 %all-to-all-start.3 = ((bf16[160,32,256]{2,1,0:T(8,128)(2,1)}), bf16[160,32,256]{2,1,0:T(8,128)(2,1)S(1)}, u32[]{:S(2)}, u32[]{:S(2)}) async-start(bf16[160,32,256]{2,1,0:T(8,128)(2,1)} %choose_blocks.6), calls=%async_computation.3 | async-start | bytes 5242880 | tf_op jit(solution)/shard_map/all_to_all | solution.py:180
  158.7 38.1 %all-gather.11.cloned.1.call-done.blocks = bf16[128,32,256]{2,1,0:T(8,128)(2,1)} async-done(((bf16[32,32,256]{2,1,0:T(8,128)(2,1)}), bf16[128,32,256]{2,1,0:T(8,128)(2,1)}) %all-gather.11.cloned.1.call-update) | async-done | bytes 2097168 | tf_op jit(solution)/shard_map/all_gather | solution.py:141
  196.8 4.2 %choose_blocks.7 = bf16[160,32,256]{2,1,0:T(8,128)(2,1)} custom-call(s32[160]{0:T(256)} %add.90.ids, bf16[128,32,256]{2,1,0:T(8,128)(2,1)} %all-gather.11.cloned.1.call-done.blocks), custom_call_target="tpu_custom_call" | custom-call | bytes 10485760 | tf_op jit(solution)/shard_map/choose_blocks/pallas_call | solution.py:29
  201.0 0.0 all-to-all-done.3.refs_3_
  201.0 0.0 copy-start.1
  201.1 1.5 copy-done.1
  202.6 4.4 %all-to-all-start.4 = ((bf16[160,32,256]{2,1,0:T(8,128)(2,1)}), bf16[160,32,256]{2,1,0:T(8,128)(2,1)}, u32[]{:S(2)}, u32[]{:S(2)}) async-start(bf16[160,32,256]{2,1,0:T(8,128)(2,1)} %choose_blocks.7), calls=%async_computation.4 | async-start | bytes 5242880 | tf_op jit(solution)/shard_map/all_to_all | solution.py:180
  207.0 0.2 fusion.1
  207.2 0.2 convert_reduce_fusion
  207.4 0.6 compare_select_fusion.slots
  208.0 31.3 %all-to-all-done.4.refs_4_ = bf16[160,32,256]{2,1,0:T(8,128)(2,1)} async-done(((bf16[160,32,256]{2,1,0:T(8,128)(2,1)}), bf16[160,32,256]{2,1,0:T(8,128)(2,1)}, u32[]{:S(2)}, u32[]{:S(2)}) %all-to-all-start.4) | async-done | bytes 2621472 | tf_op jit(solution)/shard_map/all_to_all | solution.py:180
  239.3 15.7 %sage_layer.1 = bf16[4096,256]{1,0:T(8,128)(2,1)} custom-call(s32[192]{0:T(256)} %compare_select_fusion.slots, bf16[32,128,256]{2,1,0:T(8,128)(2,1)} %bitcast.6, bf16[160,32,256]{2,1,0:T(8,128)(2,1)} %copy-done, bf16[160,32,256]{2,1,0:T(8,128)(2,1)} %all-to-all-done.2.refs_2_, bf16[160,32,256]{2,1,0:T(8,128)(2,1)} %copy-done.1, ...), custom_call_target="tpu_custom_call" | custom-call | flops 2684354560 | bytes 25165824 | tf_op jit(solution)/shard_map/sage_layer/pallas_call | solution.py:96
  (11 shorter events, 0.1 us)
Async XLA Ops:
  6.5 51.7 %all-gather.5.cloned.1.call-start = ((), (), s32[]{:S(2)}) async-start(), calls=%async_computation.5 | async-start | bytes 2621440 | tf_op jit(solution)/shard_map/all_gather | solution.py:141
  6.5 3.7 %copy-start.2 = (s32[32,6]{0,1:T(8,128)S(1)}, s32[32,6]{0,1:T(8,128)}, u32[]{:S(2)}) copy-start(s32[32,6]{0,1:T(8,128)} %param.6) | copy-start | bytes 2308
  9.4 95.0 %all-gather.7.cloned.1.call-start = ((), (), s32[]{:S(2)}) async-start(), calls=%async_computation.6 | async-start | bytes 2621440 | tf_op jit(solution)/shard_map/all_gather | solution.py:141
  11.0 9.9 %all-to-all-start = ((s32[8,1,192]{2,1,0:T(1,128)}), s32[8,1,192]{2,1,0:T(1,128)S(1)}, u32[]{:S(2)}, u32[]{:S(2)}) async-start(s32[8,1,192]{2,1,0:T(1,128)} %broadcast_in_dim.26), calls=%async_computation | async-start | bytes 16384 | tf_op jit(solution)/shard_map/all_to_all | solution.py:148
  62.4 46.3 %all-to-all-start.1 = ((bf16[160,32,256]{2,1,0:T(8,128)(2,1)}), bf16[160,32,256]{2,1,0:T(8,128)(2,1)S(1)}, u32[]{:S(2)}, u32[]{:S(2)}) async-start(bf16[160,32,256]{2,1,0:T(8,128)(2,1)} %choose_blocks.4), calls=%async_computation.1 | async-start | bytes 5242880 | tf_op jit(solution)/shard_map/all_to_all | solution.py:180
  66.1 84.6 %all-gather.9.cloned.1.call-start = ((), (), s32[]{:S(2)}) async-start(), calls=%async_computation.7 | async-start | bytes 2621440 | tf_op jit(solution)/shard_map/all_gather | solution.py:141
  108.7 4.5 %copy-start = (bf16[160,32,256]{2,1,0:T(8,128)(2,1)}, bf16[160,32,256]{2,1,0:T(8,128)(2,1)S(1)}, u32[]{:S(2)}) copy-start(bf16[160,32,256]{2,1,0:T(8,128)(2,1)S(1)} %all-to-all-done.1.refs_1_) | copy-start | bytes 7864324
  108.7 46.2 %all-to-all-start.2 = ((bf16[160,32,256]{2,1,0:T(8,128)(2,1)}), bf16[160,32,256]{2,1,0:T(8,128)(2,1)}, u32[]{:S(2)}, u32[]{:S(2)}) async-start(bf16[160,32,256]{2,1,0:T(8,128)(2,1)} %choose_blocks.5), calls=%async_computation.2 | async-start | bytes 5242880 | tf_op jit(solution)/shard_map/all_to_all | solution.py:180
  113.2 83.6 %all-gather.11.cloned.1.call-start = ((), (), s32[]{:S(2)}) async-start(), calls=%async_computation.8 | async-start | bytes 2621440 | tf_op jit(solution)/shard_map/all_gather | solution.py:141
  154.9 46.1 %all-to-all-start.3 = ((bf16[160,32,256]{2,1,0:T(8,128)(2,1)}), bf16[160,32,256]{2,1,0:T(8,128)(2,1)S(1)}, u32[]{:S(2)}, u32[]{:S(2)}) async-start(bf16[160,32,256]{2,1,0:T(8,128)(2,1)} %choose_blocks.6), calls=%async_computation.3 | async-start | bytes 5242880 | tf_op jit(solution)/shard_map/all_to_all | solution.py:180
  201.0 1.5 copy-start.1
  202.6 36.7 %all-to-all-start.4 = ((bf16[160,32,256]{2,1,0:T(8,128)(2,1)}), bf16[160,32,256]{2,1,0:T(8,128)(2,1)}, u32[]{:S(2)}, u32[]{:S(2)}) async-start(bf16[160,32,256]{2,1,0:T(8,128)(2,1)} %choose_blocks.7), calls=%async_computation.4 | async-start | bytes 5242880 | tf_op jit(solution)/shard_map/all_to_all | solution.py:180
Sparse Core Ops, SparseCore 0:
  9.6 48.6 all-gather.4
  59.8 44.5 all-gather.6
  106.0 44.6 all-gather.8
  152.1 44.6 all-gather.10

commit v5 on v4

--- a/solution.py
+++ b/solution.py
@@ -9,41 +9,66 @@
 
 REM_PB = 4
 PLANES = 4
-CHUNKS = 4
+CHUNKS = 1
+
 VMEM_LIMIT = 60 * 1024 * 1024
 
 
-def choose_kernel(ids, blocks, out, held, in_sem, out_sem):
-    count = out.shape[0]
-    for n in range(count):
-        pltpu.make_async_copy(blocks.at[ids[n]], held.at[n], in_sem).start()
+def arrival_order(planes):
+    order = []
+    for z in range(planes):
+        mine = [(0, 0)]
+        for step in range(1, planes):
+            if z + step < planes:
+                mine.append((step, -1))
+            if z - step >= 0:
+                mine.append((step, 1))
+        order.append(mine)
+    return order
+
+
+def pick_row(table, z):
+    return jnp.sum(jnp.where(jnp.arange(table.shape[0])[:, None] == z, table, 0), axis=0)
+
+
+def choose_kernel(which, ids, *refs, top):
+    *froms, out, held, in_sem, out_sem = refs
+    count, tall = out.shape[:2]
+    for j, source in enumerate(froms):
+
+        @pl.when(which[0] == j)
+        def _():
+            for n in range(count):
+                block = source.at[ids[n], pl.ds(top, tall)]
+                pltpu.make_async_copy(block, held.at[n], in_sem).start()
+
     pltpu.make_async_copy(out, held, in_sem).wait()
     leaving = pltpu.make_async_copy(held, out, out_sem)
     leaving.start()
     leaving.wait()
 
 
-def choose(ids, blocks):
-    out = (ids.shape[0],) + blocks.shape[1:]
+def choose(which, ids, froms, tall, top=0):
+    out = (ids.shape[0], tall, froms[0].shape[2])
     moved = out[0] * out[1] * out[2] * 2
     return pl.pallas_call(
-        choose_kernel,
+        functools.partial(choose_kernel, top=top),
         grid_spec=pltpu.PrefetchScalarGridSpec(
-            num_scalar_prefetch=1,
+            num_scalar_prefetch=2,
             grid=(1,),
-            in_specs=[pl.BlockSpec(memory_space=pltpu.HBM)],
+            in_specs=[pl.BlockSpec(memory_space=pltpu.HBM)] * len(froms),
             out_specs=pl.BlockSpec(memory_space=pltpu.HBM),
             scratch_shapes=[
-                pltpu.VMEM(out, blocks.dtype),
+                pltpu.VMEM(out, froms[0].dtype),
                 pltpu.SemaphoreType.DMA,
                 pltpu.SemaphoreType.DMA,
             ],
         ),
-        out_shape=jax.ShapeDtypeStruct(out, blocks.dtype),
+        out_shape=jax.ShapeDtypeStruct(out, froms[0].dtype),
         compiler_params=pltpu.CompilerParams(vmem_limit_bytes=VMEM_LIMIT),
-        cost_estimate=pl.CostEstimate(flops=0, bytes_accessed=4 * moved, transcendentals=0),
+        cost_estimate=pl.CostEstimate(flops=0, bytes_accessed=2 * moved, transcendentals=0),
         name="choose_blocks",
-    )(ids, blocks)
+    )(which, ids, *froms)
 
 
 def layer_kernel(slots, *refs, pieces, starts):
@@ -130,19 +155,25 @@
     planes = PLANES if peers % PLANES == 0 else 1
     plane = peers // planes
     myself = lax.axis_index("rows")
-    p = myself % plane
+    z, p = myself // plane, myself % plane
     capacity = max(2, (REM_PB * blocks_here + peers - 2) // (peers - 1))
     local = features.reshape(blocks_here, tile, width)
     groups = [[a * plane + q for q in range(plane)] for a in range(planes)]
-    lines = [[a * plane + q for a in range(planes)] for q in range(plane)]
+    order = arrival_order(planes)
 
     tall = tile // CHUNKS
-    spread = [
-        lax.all_gather(
-            local[:, c * tall : (c + 1) * tall], "rows", axis_index_groups=lines, tiled=True
-        )
-        for c in range(CHUNKS)
-    ]
+    arrived = [{} for _ in range(CHUNKS)]
+    for step in range(1, planes):
+        for c in range(CHUNKS):
+            for way in (-1, 1):
+                pairs = [
+                    (a * plane + q, (a + way) * plane + q)
+                    for a in range(planes)
+                    if 0 <= a + way < planes and 0 <= a - way * (step - 1) < planes
+                    for q in range(plane)
+                ]
+                held = local[:, c * tall : (c + 1) * tall] if step == 1 else arrived[c][step - 1, way]
+                arrived[c][step, way] = lax.ppermute(held, "rows", pairs)
 
     columns = tile_cols.reshape(-1)
     asked = lax.all_to_all(
@@ -154,7 +185,10 @@
         tiled=True,
     )
     blocks = jnp.arange(blocks_here, dtype=jnp.int32)
-    line = jnp.arange(planes, dtype=jnp.int32) * plane + p
+    plane_at = jnp.array(
+        [[a - way * step for step, way in order[a]] for a in range(planes)], jnp.int32
+    )
+    line = pick_row(plane_at, z) * plane + p
     wanted = (line[:, None] * blocks_here + blocks[None, :]).reshape(-1)
     need = jnp.any(asked[:, :, None] == wanted[None, None, :], axis=1)
     need = need.reshape(plane, planes, blocks_here).astype(jnp.int32)
@@ -163,7 +197,6 @@
     seat = jnp.arange(capacity, dtype=jnp.int32)
     taken = (need[:, :, None, :] == 1) & (place[:, :, None, :] == seat[:, None])
     chosen = jnp.sum(jnp.where(taken, blocks, 0), axis=3)
-    ids = (chosen + jnp.arange(planes, dtype=jnp.int32)[:, None] * blocks_here).reshape(-1)
 
     owners, within = columns // blocks_here, columns % blocks_here
     positions = jnp.arange(columns.shape[0], dtype=jnp.int32)
@@ -171,22 +204,39 @@
     first = ~jnp.any(same & (positions[None, :] < positions[:, None]), axis=1)
     ahead = (owners[:, None] == owners[None, :]) & (columns[None, :] < columns[:, None])
     ranks = jnp.sum(ahead & first[None, :], axis=1, dtype=jnp.int32)
-    place_of = (owners % plane) * planes + owners // plane
-    slots = jnp.where(owners == myself, within, blocks_here + place_of * capacity + ranks)
+    stage_at = jnp.array(
+        [
+            [[a - way * step for step, way in order[a]].index(b) for b in range(planes)]
+            for a in range(planes)
+        ],
+        jnp.int32,
+    )
+    stages = pick_row(stage_at, z)
+    their_plane = owners // plane
+    stage = jnp.sum(
+        jnp.where(their_plane[:, None] == jnp.arange(planes), stages[None, :], 0), axis=1
+    )
+    place_of = (stage * plane + owners % plane) * capacity
+    slots = jnp.where(owners == myself, within, blocks_here + place_of + ranks)
 
     froms, starts = [local], [(0, 0)]
-    for c in range(CHUNKS):
-        froms.append(
-            lax.all_to_all(
-                choose(ids, spread[c]),
-                "rows",
-                split_axis=0,
-                concat_axis=0,
-                axis_index_groups=groups,
-                tiled=True,
+    for k in range(planes):
+        kinds = sorted(set(order[a][k] for a in range(planes)))
+        which_at = jnp.array([[kinds.index(order[a][k])] for a in range(planes)], jnp.int32)
+        which = pick_row(which_at, z)
+        for c in range(CHUNKS):
+            ids = chosen[:, k, :].reshape(-1)
+            if k == 0:
+                picked = choose(which, ids, [local], tall, c * tall)
+            else:
+                picked = choose(which, ids, [arrived[c][kind] for kind in kinds], tall)
+            used = jnp.any(taken[:, k], axis=2).reshape(-1)
+            picked = jnp.where(used[:, None, None], picked, 0)
+            received = lax.all_to_all(
+                picked, "rows", split_axis=0, concat_axis=0, axis_index_groups=groups, tiled=True
             )
-        )
-        starts.append((blocks_here, c * tall))
+            froms.append(received)
+            starts.append((blocks_here + k * plane * capacity, c * tall))
 
     return layer(
         slots,

time: 263 us -> 215 us (0.82)
  waiting for transfers between devices: 185 us -> 117 us
  other arithmetic: 2.49 us -> 19.7 us
  between operations: 13.3 us -> 0.21 us
  starting transfers between devices: 21.6 us -> 34.1 us
    all_gather x4 -> x0, waiting for transfers between devices: 148 us -> none  [on_device(): lax.all_gather(local[:, c * tall:(c + 1) * tall], 'rows', axis_index_grou...]
    ppermute x0 -> x6, waiting for transfers between devices: none -> 82.4 us  [on_device(): arrived[c][step, way] = lax.ppermute(held, 'rows', pairs)]
    ppermute x0 -> x6, starting transfers between devices: none -> 14.1 us  [on_device(): arrived[c][step, way] = lax.ppermute(held, 'rows', pairs)]
    select_n x2 -> x6, other arithmetic: 0.58 us -> 14.6 us  [the longest x4 14 us: on_device(): picked = jnp.where(used[:, None, None], picked, 0)]
    reduce_sum x0 -> x5, other arithmetic: none -> 2.77 us  [the longest x4 2.69 us: pick_row(): jnp.sum(jnp.where(jnp.arange(table.shape[0])[:, None] == z, table, 0), ax...]
  transfers between devices with their start and end apart: 9 -> 11, of which waited for: 6 -> 6; matrix products, arithmetic and copies ran while one was open for 2% -> 12% of each run, Pallas kernels for 6% -> 9%
where the time goes in v5:
time: 215 us; the launch traced here: 214 us
  waiting for transfers between devices  117 us (54%)
  Pallas kernels  34.4 us (16%)
  starting transfers between devices  34.1 us (16%)
  other arithmetic  19.7 us (9%)
  local copies, waits for them, and re-layouts  8.32 us (4%)
    ppermute x6, waiting for transfers between devices, on_device(): arrived[c][step, way] = lax.ppermute(held, 'rows', pairs)  82.4 us
    all_to_all x4, waiting for transfers between devices, on_device(): lax.all_to_all(picked, 'rows', split_axis=0, concat_axis=0, axis_index_gr...  31.2 us
    pallas_call x4, Pallas kernels, choose(): pl.pallas_call(functools.partial(choose_kernel, top=top), grid_spec=pltpu...  18.7 us
    all_to_all x4, starting transfers between devices, on_device(): lax.all_to_all(picked, 'rows', split_axis=0, concat_axis=0, axis_index_gr...  16.3 us
    pallas_call x1, Pallas kernels, layer(): pl.pallas_call(functools.partial(layer_kernel, pieces=len(froms), starts=...  15.7 us
    ppermute x6, starting transfers between devices, on_device(): arrived[c][step, way] = lax.ppermute(held, 'rows', pairs)  14.1 us
    select_n x4, other arithmetic, on_device(): picked = jnp.where(used[:, None, None], picked, 0)  14 us
  transfers between devices with their start and end apart: 11, of which 6 were waited for; matrix products, arithmetic and copies ran while one was open for 12% of the time, Pallas kernels for 9%

profile of v5, /device:TPU:0, one launch (start us, length us, event | category | flops | bytes accessed | tf_op | source)
XLA Modules:
  0.0 214.0 jit_solution(17479347025444786946)
XLA Ops:
  0.0 6.2 %collective-permute-start.1 = (bf16[32,128,256]{2,1,0:T(8,128)(2,1)}, bf16[32,128,256]{2,1,0:T(8,128)(2,1)}, u32[]{:S(2)}, u32[]{:S(2)}) collective-permute-start(bf16[32,128,256]{2,1,0:T(8,128)(2,1)} %bitcast.16), channel_id=1, source_target_pairs={{0,8},{1,9},{2,10},{3,11},{4,12},{5,13},{6,14},{7,15},{8,16},{9,17... | collective-permute-start | bytes 6291464 | tf_op jit(solution)/shard_map/ppermute | solution.py:176
  6.2 1.3 collective-permute-start
  7.5 0.8 copy.24
  8.3 0.1 reshape.155
  8.4 0.6 broadcast_in_dim.126
  9.0 3.7 %all-to-all-start = ((s32[8,1,192]{2,1,0:T(1,128)}), s32[8,1,192]{2,1,0:T(1,128)S(1)}, u32[]{:S(2)}, u32[]{:S(2)}) async-start(s32[8,1,192]{2,1,0:T(1,128)} %broadcast_in_dim.126), calls=%async_computation | async-start | bytes 16384 | tf_op jit(solution)/shard_map/all_to_all | solution.py:179
  12.7 0.8 select_reduce_fusion.3
  13.7 3.7 %all-to-all-done = s32[8,1,192]{2,1,0:T(1,128)S(1)} async-done(((s32[8,1,192]{2,1,0:T(1,128)}), s32[8,1,192]{2,1,0:T(1,128)S(1)}, u32[]{:S(2)}, u32[]{:S(2)}) %all-to-all-start) | async-done | bytes 6176 | tf_op jit(solution)/shard_map/all_to_all | solution.py:179
  17.4 0.3 compare_reduce_fusion
  17.8 0.6 select_reduce_fusion
  18.5 0.4 select_reduce_fusion.1
  18.9 0.4 slice_reduce_fusion
  19.4 0.1 copy.27
  19.6 0.6 reshape_squeeze.12.ids
  20.2 4.2 %choose_blocks.4 = bf16[40,128,256]{2,1,0:T(8,128)(2,1)} custom-call(s32[1]{0:T(128)} %constant.97.which, s32[40]{0:T(128)} %reshape_squeeze.12.ids, bf16[32,128,256]{2,1,0:T(8,128)(2,1)} %bitcast.18), custom_call_target="tpu_custom_call" | custom-call | bytes 5242880 | tf_op jit(solution)/shard_map/choose_blocks/pallas_call | solution.py:54
  24.4 3.5 %broadcast_select_fusion.3 = bf16[40,128,256]{2,1,0:T(8,128)(2,1)} fusion(bf16[40,128,256]{2,1,0:T(8,128)(2,1)} %choose_blocks.4, pred[40]{0:T(512)(128)(4,1)S(1)} %broadcast_in_dim.130), kind=kLoop, calls=%fused_computation.3 | loop fusion | flops 1310720 | bytes 5242920 | tf_op jit(solution)/shard_map/jit(_where)/select_n | solution.py:234
  27.9 3.8 %all-to-all-start.1 = ((bf16[40,128,256]{2,1,0:T(8,128)(2,1)}), bf16[40,128,256]{2,1,0:T(8,128)(2,1)S(1)}, u32[]{:S(2)}, u32[]{:S(2)}) async-start(bf16[40,128,256]{2,1,0:T(8,128)(2,1)} %broadcast_select_fusion.3), calls=%async_computation.1 | async-start | bytes 5242880 | tf_op jit(solution)/shard_map/all_to_all | solution.py:235
  31.7 0.6 select_reduce_fusion.7
  32.3 0.1 copy.29
  32.6 0.6 reshape_squeeze.13.ids
  33.2 16.9 %collective-permute-done.1.refs_1_.refs_0_ = bf16[32,128,256]{2,1,0:T(8,128)(2,1)} collective-permute-done((bf16[32,128,256]{2,1,0:T(8,128)(2,1)}, bf16[32,128,256]{2,1,0:T(8,128)(2,1)}, u32[]{:S(2)}, u32[]{:S(2)}) %collective-permute-start.1) | collective-permute-done | bytes 2097184 | tf_op jit(solution)/shard_map/ppermute | solution.py:176
  50.1 2.0 collective-permute-start.3
  52.2 3.4 %collective-permute-done.refs_0_ = bf16[32,128,256]{2,1,0:T(8,128)(2,1)} collective-permute-done((bf16[32,128,256]{2,1,0:T(8,128)(2,1)}, bf16[32,128,256]{2,1,0:T(8,128)(2,1)}, u32[]{:S(2)}, u32[]{:S(2)}) %collective-permute-start) | collective-permute-done | bytes 2097184 | tf_op jit(solution)/shard_map/ppermute | solution.py:176
  55.5 1.3 collective-permute-start.2
  56.8 4.6 %choose_blocks.5 = bf16[40,128,256]{2,1,0:T(8,128)(2,1)} custom-call(s32[1]{0:T(128)} %bitcast.1.which, s32[40]{0:T(128)} %reshape_squeeze.13.ids, bf16[32,128,256]{2,1,0:T(8,128)(2,1)} %collective-permute-done.refs_0_, bf16[32,128,256]{2,1,0:T(8,128)(2,1)} %collective-permute-done.1.refs_1_.refs_0_), custom_call_target="tpu_custom_call" | custom-call | bytes 5242880 | tf_op jit(solution)/shard_map/choose_blocks/pallas_call | solution.py:54
  61.5 3.6 %broadcast_select_fusion.2 = bf16[40,128,256]{2,1,0:T(8,128)(2,1)} fusion(bf16[40,128,256]{2,1,0:T(8,128)(2,1)} %choose_blocks.5, pred[40]{0:T(512)(128)(4,1)S(1)} %broadcast_in_dim.136), kind=kLoop, calls=%fused_computation.2 | loop fusion | flops 1310720 | bytes 5242920 | tf_op jit(solution)/shard_map/jit(_where)/select_n | solution.py:234
  65.0 1.5 copy-done
  66.6 4.4 %all-to-all-start.2 = ((bf16[40,128,256]{2,1,0:T(8,128)(2,1)}), bf16[40,128,256]{2,1,0:T(8,128)(2,1)}, u32[]{:S(2)}, u32[]{:S(2)}) async-start(bf16[40,128,256]{2,1,0:T(8,128)(2,1)} %broadcast_select_fusion.2), calls=%async_computation.2 | async-start | bytes 5242880 | tf_op jit(solution)/shard_map/all_to_all | solution.py:235
  71.0 0.6 select_reduce_fusion.6
  71.9 0.6 reshape_squeeze.14.ids
  72.5 2.0 collective-permute-start.5
  74.5 29.6 %collective-permute-done.2.refs_1_.refs_0_ = bf16[32,128,256]{2,1,0:T(8,128)(2,1)} collective-permute-done((bf16[32,128,256]{2,1,0:T(8,128)(2,1)}, bf16[32,128,256]{2,1,0:T(8,128)(2,1)}, u32[]{:S(2)}, u32[]{:S(2)}) %collective-permute-start.2) | collective-permute-done | bytes 2097184 | tf_op jit(solution)/shard_map/ppermute | solution.py:176
  104.1 1.3 collective-permute-start.4
  105.4 5.1 %choose_blocks.6 = bf16[40,128,256]{2,1,0:T(8,128)(2,1)} custom-call(s32[1]{0:T(128)} %bitcast.2.which, s32[40]{0:T(128)} %reshape_squeeze.14.ids, bf16[32,128,256]{2,1,0:T(8,128)(2,1)} %collective-permute-done.1.refs_1_.refs_0_, bf16[32,128,256]{2,1,0:T(8,128)(2,1)} %collective-permute-done.2.refs_1_.refs_0_, ...), custom_call_target="tpu_custom_call" | custom-call | bytes 5242880 | tf_op jit(solution)/shard_map/choose_blocks/pallas_call | solution.py:54
  110.6 3.5 %broadcast_select_fusion.1 = bf16[40,128,256]{2,1,0:T(8,128)(2,1)} fusion(bf16[40,128,256]{2,1,0:T(8,128)(2,1)} %choose_blocks.6, pred[40]{0:T(512)(128)(4,1)S(1)} %broadcast_in_dim.138), kind=kLoop, calls=%fused_computation.1 | loop fusion | flops 1310720 | bytes 5242920 | tf_op jit(solution)/shard_map/jit(_where)/select_n | solution.py:234
  114.1 3.8 %all-to-all-start.3 = ((bf16[40,128,256]{2,1,0:T(8,128)(2,1)}), bf16[40,128,256]{2,1,0:T(8,128)(2,1)S(1)}, u32[]{:S(2)}, u32[]{:S(2)}) async-start(bf16[40,128,256]{2,1,0:T(8,128)(2,1)} %broadcast_select_fusion.1), calls=%async_computation.3 | async-start | bytes 5242880 | tf_op jit(solution)/shard_map/all_to_all | solution.py:235
  117.8 0.6 select_reduce_fusion.5
  118.7 0.7 reshape_squeeze.15.ids
  119.4 32.4 %collective-permute-done.4.refs_2_ = bf16[32,128,256]{2,1,0:T(8,128)(2,1)} collective-permute-done((bf16[32,128,256]{2,1,0:T(8,128)(2,1)}, bf16[32,128,256]{2,1,0:T(8,128)(2,1)}, u32[]{:S(2)}, u32[]{:S(2)}) %collective-permute-start.4) | collective-permute-done | bytes 2097184 | tf_op jit(solution)/shard_map/ppermute | solution.py:176
  151.8 4.7 %choose_blocks.7 = bf16[40,128,256]{2,1,0:T(8,128)(2,1)} custom-call(s32[1]{0:T(128)} %bitcast.3.which, s32[40]{0:T(128)} %reshape_squeeze.15.ids, bf16[32,128,256]{2,1,0:T(8,128)(2,1)} %collective-permute-done.2.refs_1_.refs_0_, bf16[32,128,256]{2,1,0:T(8,128)(2,1)} %collective-permute-done.3.refs_2_.refs_1_, ...), custom_call_target="tpu_custom_call" | custom-call | bytes 5242880 | tf_op jit(solution)/shard_map/choose_blocks/pallas_call | solution.py:54
  156.6 3.5 %broadcast_select_fusion = bf16[40,128,256]{2,1,0:T(8,128)(2,1)} fusion(bf16[40,128,256]{2,1,0:T(8,128)(2,1)} %choose_blocks.7, pred[40]{0:T(512)(128)(4,1)S(1)} %broadcast_in_dim.140), kind=kLoop, calls=%fused_computation | loop fusion | flops 1310720 | bytes 5242920 | tf_op jit(solution)/shard_map/jit(_where)/select_n | solution.py:234
  160.1 1.6 copy-done.1
  161.6 4.4 %all-to-all-start.4 = ((bf16[40,128,256]{2,1,0:T(8,128)(2,1)}), bf16[40,128,256]{2,1,0:T(8,128)(2,1)}, u32[]{:S(2)}, u32[]{:S(2)}) async-start(bf16[40,128,256]{2,1,0:T(8,128)(2,1)} %broadcast_select_fusion), calls=%async_computation.4 | async-start | bytes 5242880 | tf_op jit(solution)/shard_map/all_to_all | solution.py:235
  166.0 0.2 fusion.1
  166.3 0.2 convert_reduce_fusion
  166.5 0.6 compare_select_fusion.slots
  167.1 31.2 %all-to-all-done.4.refs_4_ = bf16[40,128,256]{2,1,0:T(8,128)(2,1)} async-done(((bf16[40,128,256]{2,1,0:T(8,128)(2,1)}), bf16[40,128,256]{2,1,0:T(8,128)(2,1)}, u32[]{:S(2)}, u32[]{:S(2)}) %all-to-all-start.4) | async-done | bytes 2621472 | tf_op jit(solution)/shard_map/all_to_all | solution.py:235
  198.3 15.7 %sage_layer.1 = bf16[4096,256]{1,0:T(8,128)(2,1)} custom-call(s32[192]{0:T(256)} %compare_select_fusion.slots, bf16[32,128,256]{2,1,0:T(8,128)(2,1)} %bitcast.19, bf16[40,128,256]{2,1,0:T(8,128)(2,1)} %copy-done, bf16[40,128,256]{2,1,0:T(8,128)(2,1)} %all-to-all-done.2.refs_2_, bf16[40,128,256]{2,1,0:T(8,128)(2,1)} %copy-done.1, ...), custom_call_target="tpu_custom_call" | custom-call | flops 2684354560 | bytes 25165824 | tf_op jit(solution)/shard_map/sage_layer/pallas_call | solution.py:121
  (39 shorter events, 1.3 us)
Async XLA Ops:
  0.0 50.1 %collective-permute-start.1 = (bf16[32,128,256]{2,1,0:T(8,128)(2,1)}, bf16[32,128,256]{2,1,0:T(8,128)(2,1)}, u32[]{:S(2)}, u32[]{:S(2)}) collective-permute-start(bf16[32,128,256]{2,1,0:T(8,128)(2,1)} %bitcast.16), channel_id=1, source_target_pairs={{0,8},{1,9},{2,10},{3,11},{4,12},{5,13},{6,14},{7,15},{8,16},{9,17... | collective-permute-start | bytes 6291464 | tf_op jit(solution)/shard_map/ppermute | solution.py:176
  6.2 49.3 %collective-permute-start = (bf16[32,128,256]{2,1,0:T(8,128)(2,1)}, bf16[32,128,256]{2,1,0:T(8,128)(2,1)}, u32[]{:S(2)}, u32[]{:S(2)}) collective-permute-start(bf16[32,128,256]{2,1,0:T(8,128)(2,1)} %bitcast.17), channel_id=1, source_target_pairs={{8,0},{9,1},{10,2},{11,3},{12,4},{13,5},{14,6},{15,7},{16,8},{17,9... | collective-permute-start | bytes 6291464 | tf_op jit(solution)/shard_map/ppermute | solution.py:176
  9.0 8.4 %all-to-all-start = ((s32[8,1,192]{2,1,0:T(1,128)}), s32[8,1,192]{2,1,0:T(1,128)S(1)}, u32[]{:S(2)}, u32[]{:S(2)}) async-start(s32[8,1,192]{2,1,0:T(1,128)} %broadcast_in_dim.126), calls=%async_computation | async-start | bytes 16384 | tf_op jit(solution)/shard_map/all_to_all | solution.py:179
  27.9 3.8 %copy-start.4 = (s32[4,1]{0,1:T(1,128)S(1)}, s32[4,1]{0,1:T(1,128)}, u32[]{:S(2)}) copy-start(s32[4,1]{0,1:T(1,128)} %constant.93.clone) | copy-start | bytes 52
  27.9 37.1 %all-to-all-start.1 = ((bf16[40,128,256]{2,1,0:T(8,128)(2,1)}), bf16[40,128,256]{2,1,0:T(8,128)(2,1)S(1)}, u32[]{:S(2)}, u32[]{:S(2)}) async-start(bf16[40,128,256]{2,1,0:T(8,128)(2,1)} %broadcast_select_fusion.3), calls=%async_computation.1 | async-start | bytes 5242880 | tf_op jit(solution)/shard_map/all_to_all | solution.py:235
  50.1 22.4 %collective-permute-start.3 = (bf16[32,128,256]{2,1,0:T(8,128)(2,1)}, bf16[32,128,256]{2,1,0:T(8,128)(2,1)}, u32[]{:S(2)}, u32[]{:S(2)}) collective-permute-start(bf16[32,128,256]{2,1,0:T(8,128)(2,1)} %collective-permute-done.1.refs_1_.refs_0_), channel_id=1, source_target_pairs={{8,16},{9,17},{10,18},{11,19},{12,20},{13,21},{14,22},{15,23},{16,... | collective-permute-start | bytes 6291464 | tf_op jit(solution)/shard_map/ppermute | solution.py:176
  55.5 48.6 %collective-permute-start.2 = (bf16[32,128,256]{2,1,0:T(8,128)(2,1)}, bf16[32,128,256]{2,1,0:T(8,128)(2,1)}, u32[]{:S(2)}, u32[]{:S(2)}) collective-permute-start(bf16[32,128,256]{2,1,0:T(8,128)(2,1)} %collective-permute-done.refs_0_), channel_id=1, source_target_pairs={{8,0},{9,1},{10,2},{11,3},{12,4},{13,5},{14,6},{15,7},{16,8},{17,9... | collective-permute-start | bytes 6291464 | tf_op jit(solution)/shard_map/ppermute | solution.py:176
  65.0 5.9 %copy-start.3 = (s32[4,1]{0,1:T(1,128)S(1)}, s32[4,1]{0,1:T(1,128)}, u32[]{:S(2)}) copy-start(s32[4,1]{0,1:T(1,128)} %constant.94.clone) | copy-start | bytes 52
  65.0 1.5 copy-start
  66.6 47.5 %all-to-all-start.2 = ((bf16[40,128,256]{2,1,0:T(8,128)(2,1)}), bf16[40,128,256]{2,1,0:T(8,128)(2,1)}, u32[]{:S(2)}, u32[]{:S(2)}) async-start(bf16[40,128,256]{2,1,0:T(8,128)(2,1)} %broadcast_select_fusion.2), calls=%async_computation.2 | async-start | bytes 5242880 | tf_op jit(solution)/shard_map/all_to_all | solution.py:235
  72.5 46.9 %collective-permute-start.5 = (bf16[32,128,256]{2,1,0:T(8,128)(2,1)}, bf16[32,128,256]{2,1,0:T(8,128)(2,1)}, u32[]{:S(2)}, u32[]{:S(2)}) collective-permute-start(bf16[32,128,256]{2,1,0:T(8,128)(2,1)} %collective-permute-done.3.refs_2_.refs_1_), channel_id=1, source_target_pairs={{16,24},{17,25},{18,26},{19,27},{20,28},{21,29},{22,30},{23,31}} | collective-permute-start | bytes 6291464 | tf_op jit(solution)/shard_map/ppermute | solution.py:176
  104.1 47.7 %collective-permute-start.4 = (bf16[32,128,256]{2,1,0:T(8,128)(2,1)}, bf16[32,128,256]{2,1,0:T(8,128)(2,1)}, u32[]{:S(2)}, u32[]{:S(2)}) collective-permute-start(bf16[32,128,256]{2,1,0:T(8,128)(2,1)} %collective-permute-done.2.refs_1_.refs_0_), channel_id=1, source_target_pairs={{8,0},{9,1},{10,2},{11,3},{12,4},{13,5},{14,6},{15,7}} | collective-permute-start | bytes 6291464 | tf_op jit(solution)/shard_map/ppermute | solution.py:176
  114.1 3.8 %copy-start.2 = (s32[4,1]{0,1:T(1,128)S(1)}, s32[4,1]{0,1:T(1,128)}, u32[]{:S(2)}) copy-start(s32[4,1]{0,1:T(1,128)} %constant.95.clone) | copy-start | bytes 52
  114.1 46.0 %all-to-all-start.3 = ((bf16[40,128,256]{2,1,0:T(8,128)(2,1)}), bf16[40,128,256]{2,1,0:T(8,128)(2,1)S(1)}, u32[]{:S(2)}, u32[]{:S(2)}) async-start(bf16[40,128,256]{2,1,0:T(8,128)(2,1)} %broadcast_select_fusion.1), calls=%async_computation.3 | async-start | bytes 5242880 | tf_op jit(solution)/shard_map/all_to_all | solution.py:235
  160.1 1.6 copy-start.1
  161.6 36.7 %all-to-all-start.4 = ((bf16[40,128,256]{2,1,0:T(8,128)(2,1)}), bf16[40,128,256]{2,1,0:T(8,128)(2,1)}, u32[]{:S(2)}, u32[]{:S(2)}) async-start(bf16[40,128,256]{2,1,0:T(8,128)(2,1)} %broadcast_select_fusion), calls=%async_computation.4 | async-start | bytes 5242880 | tf_op jit(solution)/shard_map/all_to_all | solution.py:235

commit v6 on v5

v6 whole, which is shorter than its diff:
```python
import functools

import jax
import jax.numpy as jnp
from jax import lax
from jax.experimental import pallas as pl
from jax.experimental.pallas import tpu as pltpu
from jax.sharding import PartitionSpec as P

REM_PB = 4
PLANES = 4
LAST = 1

VMEM_LIMIT = 60 * 1024 * 1024


def arrival_order(planes):
    order = []
    for z in range(planes):
        mine = [(0, 0)]
        for step in range(1, planes):
            if z + step < planes:
                mine.append((step, -1))
            if z - step >= 0:
                mine.append((step, 1))
        order.append(mine)
    return order


def pick_row(table, z):
    return jnp.sum(jnp.where(jnp.arange(table.shape[0])[:, None] == z, table, 0), axis=0)


def choose_kernel(ids, *refs):
    *froms, out, held, in_sem, out_sem = refs
    count = out.shape[0]
    tall = froms[0].shape[1]
    for n in range(count):
        for h, source in enumerate(froms):
            pltpu.make_async_copy(source.at[ids[n]], held.at[n, pl.ds(h * tall, tall)], in_sem).start()
    pltpu.make_async_copy(out, held, in_sem).wait()
    leaving = pltpu.make_async_copy(held, out, out_sem)
    leaving.start()
    leaving.wait()


def choose(ids, froms):
    out = (ids.shape[0], len(froms) * froms[0].shape[1], froms[0].shape[2])
    moved = out[0] * out[1] * out[2] * 2
    return pl.pallas_call(
        choose_kernel,
        grid_spec=pltpu.PrefetchScalarGridSpec(
            num_scalar_prefetch=1,
            grid=(1,),
            in_specs=[pl.BlockSpec(memory_space=pltpu.HBM)] * len(froms),
            out_specs=pl.BlockSpec(memory_space=pltpu.HBM),
            scratch_shapes=[
                pltpu.VMEM(out, froms[0].dtype),
                pltpu.SemaphoreType.DMA,
                pltpu.SemaphoreType.DMA,
            ],
        ),
        out_shape=jax.ShapeDtypeStruct(out, froms[0].dtype),
        compiler_params=pltpu.CompilerParams(vmem_limit_bytes=VMEM_LIMIT),
        cost_estimate=pl.CostEstimate(flops=0, bytes_accessed=2 * moved, transcendentals=0),
        name="choose_blocks",
    )(ids, *froms)


def early_kernel(slots, late, counts, *refs, pieces, starts):
    froms = refs[:pieces]
    masks, sums, left, table, sems = refs[pieces:]
    step = pl.program_id(0)
    rows, per_block = masks.shape[:2]
    tile, width = table.shape[1:]
    spare = left.shape[2] // tile

    @pl.when(step == 0)
    def _():
        copies = [
            pltpu.make_async_copy(piece, table.at[pl.ds(at, piece.shape[0])], sems.at[n])
            for n, (piece, at) in enumerate(zip(froms, starts))
        ]
        for copy in copies:
            copy.start()
        table[table.shape[0] - 1] = jnp.zeros((tile, width), table.dtype)
        for copy in copies:
            copy.wait()

    for r in range(rows):
        row = step * rows + r
        mask = jnp.concatenate(
            [masks[r, t].astype(jnp.float32).astype(jnp.bfloat16) for t in range(per_block)], axis=1
        )
        picked = jnp.concatenate(
            [table[slots[row * per_block + t]] for t in range(per_block)], axis=0
        )
        sums[pl.ds(r * tile, tile), :] = jnp.dot(mask, picked, preferred_element_type=jnp.float32)
        for t in range(spare):
            kept = masks[r, late[row * spare + t]].astype(jnp.float32)
            kept = jnp.where(t < counts[row], kept, 0.0).astype(jnp.bfloat16)
            left[r, :, t * tile : (t + 1) * tile] = kept


def early(slots, late, counts, froms, starts, blocks_in_table, tile_masks, width):
    blocks_here, per_block, tile, _ = tile_masks.shape
    spare = late.shape[0] // blocks_here
    rows = 4 if blocks_here % 4 == 0 else 1
    return pl.pallas_call(
        functools.partial(early_kernel, pieces=len(froms), starts=starts),
        grid_spec=pltpu.PrefetchScalarGridSpec(
            num_scalar_prefetch=3,
            grid=(blocks_here // rows,),
            in_specs=[pl.BlockSpec(memory_space=pltpu.HBM)] * len(froms)
            + [pl.BlockSpec((rows, per_block, tile, tile), lambda r, *_: (r, 0, 0, 0))],
            out_specs=[
                pl.BlockSpec((rows * tile, width), lambda r, *_: (r, 0)),
                pl.BlockSpec((rows, tile, spare * tile), lambda r, *_: (r, 0, 0)),
            ],
            scratch_shapes=[
                pltpu.VMEM((blocks_in_table, tile, width), jnp.bfloat16),
                pltpu.SemaphoreType.DMA((len(froms),)),
            ],
        ),
        out_shape=[
            jax.ShapeDtypeStruct((blocks_here * tile, width), jnp.float32),
            jax.ShapeDtypeStruct((blocks_here, tile, spare * tile), jnp.bfloat16),
        ],
        compiler_params=pltpu.CompilerParams(vmem_limit_bytes=VMEM_LIMIT),
        cost_estimate=pl.CostEstimate(
            flops=2 * blocks_here * tile * per_block * tile * width,
            bytes_accessed=blocks_here * per_block * tile * tile * 6 + blocks_in_table * tile * width * 2,
            transcendentals=0,
        ),
        name="early_sums",
    )(slots, late, counts, *froms, tile_masks)


def layer_kernel(slots, counts, *refs, pieces, starts):
    froms = refs[:pieces]
    sums, left, features, degree, weight, out, table, totals, means, sems = refs[pieces:]
    step = pl.program_id(0)
    rows, tile = left.shape[:2]
    width = table.shape[2]
    spare = left.shape[2] // tile

    @pl.when(step == 0)
    def _():
        copies = [
            pltpu.make_async_copy(piece, table.at[:, pl.ds(top, piece.shape[1])], sems.at[n])
            for n, (piece, top) in enumerate(zip(froms, starts))
        ]
        for copy in copies:
            copy.start()
        for copy in copies:
            copy.wait()

    for r in range(rows):
        row = step * rows + r
        here = pl.ds(r * tile, tile)

        def add(base, first, count):
            picked = jnp.concatenate(
                [table[slots[row * spare + t]] for t in range(first, first + count)], axis=0
            )
            mask = left[r, :, first * tile : (first + count) * tile]
            totals[here, :] = base[here, :] + jnp.dot(mask, picked, preferred_element_type=jnp.float32)

        pair = min(2, spare)
        add(sums, 0, pair)
        for first in range(pair, spare, pair):
            pl.when(counts[row] > first)(functools.partial(add, totals, first, min(pair, spare - first)))
        count = jnp.broadcast_to(degree[pl.ds(row, 1), :].astype(jnp.float32), (tile, tile)).T
        count = jnp.concatenate([count] * (width // tile), axis=1)
        means[here, :] = (totals[here, :] / count).astype(jnp.bfloat16)
    hidden = jnp.dot(features[...], weight[:width], preferred_element_type=jnp.float32)
    hidden = hidden + jnp.dot(means[...], weight[width:], preferred_element_type=jnp.float32)
    hidden = jnp.maximum(hidden, 0.0)
    scale = lax.rsqrt(jnp.sum(hidden * hidden, axis=1, keepdims=True) + 1e-06)
    out[...] = (hidden * scale).astype(jnp.bfloat16)


def layer(slots, counts, froms, starts, sums, left, features, degree, weight):
    blocks_here, tile, across = left.shape
    width = features.shape[1]
    out_width = weight.shape[1]
    rows = 4 if blocks_here % 4 == 0 else 1
    items = (rows * tile, width)
    return pl.pallas_call(
        functools.partial(layer_kernel, pieces=len(froms), starts=starts),
        grid_spec=pltpu.PrefetchScalarGridSpec(
            num_scalar_prefetch=2,
            grid=(blocks_here // rows,),
            in_specs=[pl.BlockSpec(memory_space=pltpu.HBM)] * len(froms)
            + [
                pl.BlockSpec(items, lambda r, *_: (r, 0)),
                pl.BlockSpec((rows, tile, across), lambda r, *_: (r, 0, 0)),
                pl.BlockSpec(items, lambda r, *_: (r, 0)),
                pl.BlockSpec((blocks_here, tile), lambda r, *_: (0, 0)),
                pl.BlockSpec((2 * width, out_width), lambda r, *_: (0, 0)),
            ],
            out_specs=pl.BlockSpec((rows * tile, out_width), lambda r, *_: (r, 0)),
            scratch_shapes=[
                pltpu.VMEM((froms[0].shape[0], tile, width), jnp.bfloat16),
                pltpu.VMEM(items, jnp.float32),
                pltpu.VMEM(items, jnp.bfloat16),
                pltpu.SemaphoreType.DMA((len(froms),)),
            ],
        ),
        out_shape=jax.ShapeDtypeStruct((blocks_here * tile, out_width), jnp.bfloat16),
        compiler_params=pltpu.CompilerParams(vmem_limit_bytes=VMEM_LIMIT),
        cost_estimate=pl.CostEstimate(
            flops=2 * blocks_here * tile * (across + 2 * width) * out_width,
            bytes_accessed=blocks_here * tile * (4 * width + 2 * across + 2 * width + 2 * out_width),
            transcendentals=blocks_here * tile,
        ),
        name="sage_layer",
    )(slots, counts, *froms, sums, left, features, degree, weight)


def on_device(features, tile_cols, tile_masks, degree, weight):
    blocks_here, per_block = tile_cols.shape
    tile = tile_masks.shape[2]
    width = features.shape[1]
    peers = lax.axis_size("rows")
    planes = PLANES if peers % PLANES == 0 else 1
    plane = peers // planes
    myself = lax.axis_index("rows")
    z, p = myself // plane, myself % plane
    capacity = max(2, (REM_PB * blocks_here + peers - 2) // (peers - 1))
    local = features.reshape(blocks_here, tile, width)
    groups = [[a * plane + q for q in range(plane)] for a in range(planes)]
    order = arrival_order(planes)

    columns = tile_cols.reshape(-1)
    asked = lax.all_to_all(
        jnp.broadcast_to(columns, (plane,) + columns.shape),
        "rows",
        split_axis=0,
        concat_axis=0,
        axis_index_groups=groups,
        tiled=True,
    )
    blocks = jnp.arange(blocks_here, dtype=jnp.int32)
    plane_at = jnp.array(
        [[a - way * step for step, way in order[a]] for a in range(planes)], jnp.int32
    )
    line = pick_row(plane_at, z) * plane + p
    wanted = (line[:, None] * blocks_here + blocks[None, :]).reshape(-1)
    need = jnp.any(asked[:, :, None] == wanted[None, None, :], axis=1)
    need = need.reshape(plane, planes, blocks_here).astype(jnp.int32)
    below = blocks[:, None] > blocks[None, :]
    place = jnp.sum(jnp.where(below, need[:, :, None, :], 0), axis=3)
    seat = jnp.arange(capacity, dtype=jnp.int32)
    taken = (need[:, :, None, :] == 1) & (place[:, :, None, :] == seat[:, None])
    chosen = jnp.sum(jnp.where(taken, blocks, 0), axis=3)

    owners, within = columns // blocks_here, columns % blocks_here
    positions = jnp.arange(columns.shape[0], dtype=jnp.int32)
    same = columns[:, None] == columns[None, :]
    first = ~jnp.any(same & (positions[None, :] < positions[:, None]), axis=1)
    ahead = (owners[:, None] == owners[None, :]) & (columns[None, :] < columns[:, None])
    ranks = jnp.sum(ahead & first[None, :], axis=1, dtype=jnp.int32)
    stage_at = jnp.array(
        [
            [[a - way * step for step, way in order[a]].index(b) for b in range(planes)]
            for a in range(planes)
        ],
        jnp.int32,
    )
    stages = pick_row(stage_at, z)
    their_plane = owners // plane
    stage = jnp.sum(
        jnp.where(their_plane[:, None] == jnp.arange(planes), stages[None, :], 0), axis=1
    )
    seats = (owners % plane) * capacity + ranks
    here = planes - 1 if planes > 1 else 1
    nothing = blocks_here + here * plane * capacity
    slots = blocks_here + stage * plane * capacity + seats
    slots = jnp.where(owners == myself, within, jnp.where(stage < here, slots, nothing))

    last = ((stage >= here) & (owners != myself)).reshape(blocks_here, per_block)
    counts = jnp.sum(last, axis=1, dtype=jnp.int32)
    order_in = jnp.cumsum(last, axis=1) - 1
    spots = jnp.arange(REM_PB, dtype=jnp.int32)
    chair = last[:, None, :] & (order_in[:, None, :] == spots[:, None])
    late = jnp.sum(jnp.where(chair, jnp.arange(per_block, dtype=jnp.int32), 0), axis=2, dtype=jnp.int32)
    late_slots = jnp.sum(
        jnp.where(chair, seats.reshape(blocks_here, 1, per_block), 0), axis=2, dtype=jnp.int32
    )

    arrived = {(0, -1): local, (0, 1): local}
    froms, starts, sums = [local], [0], None
    picked = received = None
    for k in range(planes):
        finish = k == planes - 1 and k > 0
        kinds = sorted(set(order[a][k] for a in range(planes)))
        which_at = jnp.array([[kinds.index(order[a][k])] for a in range(planes)], jnp.int32)
        which = pick_row(which_at, z)[0]
        if k > 0:
            pairs = {
                way: [
                    (a * plane + q, (a + way) * plane + q)
                    for a in range(planes)
                    if 0 <= a + way < planes and 0 <= a - way * (k - 1) < planes
                    for q in range(plane)
                ]
                for way in (-1, 1)
            }
        if finish:
            through = jnp.where(z < planes // 2, arrived[k - 1, -1], arrived[k - 1, 1])
            tall = tile // LAST
            cut = [through[:, c * tall : (c + 1) * tall] for c in range(LAST)]
            ended = [lax.ppermute(part, "rows", pairs[-1] + pairs[1]) for part in cut]
            outer = (z == 0) | (z == planes - 1)
            lots = []
            for c in range(LAST):
                end, _ = lax.optimization_barrier((ended[c], picked))
                lots.append([jnp.where(outer, end, cut[c])])
        elif k > 0:
            for way in (-1, 1):
                arrived[k, way] = lax.ppermute(arrived[k - 1, way], "rows", pairs[way])
            arrived[k, -1], arrived[k, 1], _ = lax.optimization_barrier(
                (arrived[k, -1], arrived[k, 1], picked)
            )
            source = arrived[kinds[0]]
            for j, kind in enumerate(kinds):
                if j > 0:
                    source = jnp.where(which == j, arrived[kind], source)
            lots = [[source]]
        else:
            lots = [[local]]
        ids = chosen[:, k, :].reshape(-1)
        parts = []
        for sources in lots:
            if received is not None:
                ids, _ = lax.optimization_barrier((ids, received))
            picked = choose(ids, sources)
            received = lax.all_to_all(
                picked, "rows", split_axis=0, concat_axis=0, axis_index_groups=groups, tiled=True
            )
            parts.append(received)
        if k < here:
            froms += parts
            starts.append(blocks_here + k * plane * capacity)

    sums, left = early(
        slots, late.reshape(-1), counts, froms, tuple(starts), nothing + 1, tile_masks, width
    )
    tops = tuple(c * (tile // len(parts)) for c in range(len(parts)))
    return layer(
        late_slots.reshape(-1),
        counts,
        parts,
        tops,
        sums,
        left,
        features,
        degree.reshape(blocks_here, tile),
        weight,
    )


def solution(mesh):
    in_specs = (P("rows", None), P("rows", None), P("rows", None, None, None), P("rows"), P())
    out_specs = P("rows", None)
    return jax.shard_map(
        on_device, mesh=mesh, in_specs=in_specs, out_specs=out_specs, check_vma=False
    )
```

time: 215 us -> 218 us (1.014)
  Pallas kernels: 34.4 us -> 46.6 us
  waiting for transfers between devices: 117 us -> 113 us
  starting transfers between devices: 34.1 us -> 30.7 us
  other arithmetic: 19.7 us -> 16.3 us
    all_to_all x4, waiting for transfers between devices: 31.2 us -> 12.8 us  [on_device(): lax.all_to_all(picked, 'rows', split_axis=0, concat_axis=0, axis_index_gr...]
    ppermute x6 -> x5, waiting for transfers between devices: 82.4 us -> 96 us  [the longest x4 58.1 us: on_device(): arrived[k, way] = lax.ppermute(arrived[k - 1, way], 'rows', pairs[way])]
    pallas_call x4 -> x5, Pallas kernels: 18.7 us -> 32.1 us  [the longest x4 16.5 us: choose(): pl.pallas_call(choose_kernel, grid_spec=pltpu.PrefetchScalarGridSpec(num_...]
    select_n x5 -> x4, other arithmetic: 14.6 us -> 11.4 us  [the longest x1 4.55 us: on_device(): through = jnp.where(z < planes // 2, arrived[k - 1, -1], arrived[k - 1, 1])]
    ppermute x6 -> x5, starting transfers between devices: 14.1 us -> 12.1 us  [the longest x4 10.8 us: on_device(): arrived[k, way] = lax.ppermute(arrived[k - 1, way], 'rows', pairs[way])]
  transfers between devices with their start and end apart: 11 -> 10, of which waited for: 6 -> 6; matrix products, arithmetic and copies ran while one was open for 12% -> 10% of each run, Pallas kernels for 9% -> 13%
where the time goes in v6:
time: 218 us; the launch traced here: 216 us
  waiting for transfers between devices  113 us (52%)
  Pallas kernels  46.6 us (21%)
  starting transfers between devices  30.7 us (14%)
  other arithmetic  16.3 us (7%)
  local copies, waits for them, and re-layouts  7.84 us (4%)
    ppermute x4, waiting for transfers between devices, on_device(): arrived[k, way] = lax.ppermute(arrived[k - 1, way], 'rows', pairs[way])  58.1 us
    ppermute x1, waiting for transfers between devices, on_device(): ended = [lax.ppermute(part, 'rows', pairs[-1] + pairs[1]) for part in cut]  37.8 us
    pallas_call x4, Pallas kernels, choose(): pl.pallas_call(choose_kernel, grid_spec=pltpu.PrefetchScalarGridSpec(num_...  16.5 us
    pallas_call x1, Pallas kernels, early(): pl.pallas_call(functools.partial(early_kernel, pieces=len(froms), starts=...  15.6 us
    all_to_all x4, starting transfers between devices, on_device(): lax.all_to_all(picked, 'rows', split_axis=0, concat_axis=0, axis_index_gr...  14.8 us
    pallas_call x1, Pallas kernels, layer(): pl.pallas_call(functools.partial(layer_kernel, pieces=len(froms), starts=...  14.5 us
    all_to_all x4, waiting for transfers between devices, on_device(): lax.all_to_all(picked, 'rows', split_axis=0, concat_axis=0, axis_index_gr...  12.8 us
    ppermute x4, starting transfers between devices, on_device(): arrived[k, way] = lax.ppermute(arrived[k - 1, way], 'rows', pairs[way])  10.8 us
  transfers between devices with their start and end apart: 10, of which 6 were waited for; matrix products, arithmetic and copies ran while one was open for 10% of the time, Pallas kernels for 13%

profile of v6, /device:TPU:0, one launch (start us, length us, event | category | flops | bytes accessed | tf_op | source)
XLA Modules:
  0.0 216.1 jit_solution(14481063100544839081)
XLA Ops:
  0.0 6.2 %collective-permute-start.1 = (bf16[32,128,256]{2,1,0:T(8,128)(2,1)}, bf16[32,128,256]{2,1,0:T(8,128)(2,1)}, u32[]{:S(2)}, u32[]{:S(2)}) collective-permute-start(bf16[32,128,256]{2,1,0:T(8,128)(2,1)} %bitcast.13), channel_id=1, source_target_pairs={{0,8},{1,9},{2,10},{3,11},{4,12},{5,13},{6,14},{7,15},{8,16},{9,17... | collective-permute-start | bytes 6291464 | tf_op jit(solution)/shard_map/ppermute | solution.py:322
  6.2 1.3 collective-permute-start
  7.5 0.8 copy.34
  8.3 0.1 reshape.208
  8.4 0.6 broadcast_in_dim.109
  9.0 3.7 %all-to-all-start = ((s32[8,1,192]{2,1,0:T(1,128)}), s32[8,1,192]{2,1,0:T(1,128)S(1)}, u32[]{:S(2)}, u32[]{:S(2)}) async-start(s32[8,1,192]{2,1,0:T(1,128)} %broadcast_in_dim.109), calls=%async_computation | async-start | bytes 16384 | tf_op jit(solution)/shard_map/all_to_all | solution.py:236
  12.7 0.8 select_reduce_fusion.5
  13.7 3.7 %all-to-all-done = s32[8,1,192]{2,1,0:T(1,128)S(1)} async-done(((s32[8,1,192]{2,1,0:T(1,128)}), s32[8,1,192]{2,1,0:T(1,128)S(1)}, u32[]{:S(2)}, u32[]{:S(2)}) %all-to-all-start) | async-done | bytes 6176 | tf_op jit(solution)/shard_map/all_to_all | solution.py:236
  17.4 0.3 compare_reduce_fusion
  17.8 0.6 select_reduce_fusion
  18.5 0.4 select_reduce_fusion.1
  19.0 0.6 reshape_squeeze.15.ids
  19.6 4.2 %choose_blocks.4 = bf16[40,128,256]{2,1,0:T(8,128)(2,1)} custom-call(s32[40]{0:T(128)} %reshape_squeeze.15.ids, bf16[32,128,256]{2,1,0:T(8,128)(2,1)} %bitcast.15), custom_call_target="tpu_custom_call" | custom-call | bytes 5242880 | tf_op jit(solution)/shard_map/choose_blocks/pallas_call | solution.py:50
  23.8 3.6 %all-to-all-start.1 = ((bf16[40,128,256]{2,1,0:T(8,128)(2,1)}), bf16[40,128,256]{2,1,0:T(8,128)(2,1)S(1)}, u32[]{:S(2)}, u32[]{:S(2)}) async-start(bf16[40,128,256]{2,1,0:T(8,128)(2,1)} %choose_blocks.4), calls=%async_computation.1 | async-start | bytes 5242880 | tf_op jit(solution)/shard_map/all_to_all | solution.py:339
  27.5 22.7 %collective-permute-done.1 = bf16[32,128,256]{2,1,0:T(8,128)(2,1)} collective-permute-done((bf16[32,128,256]{2,1,0:T(8,128)(2,1)}, bf16[32,128,256]{2,1,0:T(8,128)(2,1)}, u32[]{:S(2)}, u32[]{:S(2)}) %collective-permute-start.1) | collective-permute-done | bytes 2097184 | tf_op jit(solution)/shard_map/ppermute | solution.py:322
  50.1 5.4 %collective-permute-done = bf16[32,128,256]{2,1,0:T(8,128)(2,1)} collective-permute-done((bf16[32,128,256]{2,1,0:T(8,128)(2,1)}, bf16[32,128,256]{2,1,0:T(8,128)(2,1)}, u32[]{:S(2)}, u32[]{:S(2)}) %collective-permute-start) | collective-permute-done | bytes 2097184 | tf_op jit(solution)/shard_map/ppermute | solution.py:322
  55.5 1.3 collective-permute-start.2
  56.8 2.0 collective-permute-start.3
  58.8 0.6 fusion.12
  60.2 0.7 reshape_squeeze.14.ids
  60.9 3.1 %broadcast_select_fusion.2.refs_0_ = bf16[32,128,256]{2,1,0:T(8,128)(2,1)} fusion(bf16[32,128,256]{2,1,0:T(8,128)(2,1)} %collective-permute-done.1, bf16[32,128,256]{2,1,0:T(8,128)(2,1)} %collective-permute-done, pred[]{:T(512)S(6)} %eq.159), kind=kLoop, calls=%fused_computation.3 | loop fusion | flops 1048576 | bytes 6291457 | tf_op jit(solution)/shard_map/jit(_where)/select_n | solution.py:329
  64.0 4.1 %choose_blocks.5 = bf16[40,128,256]{2,1,0:T(8,128)(2,1)} custom-call(s32[40]{0:T(128)} %reshape_squeeze.14.ids, bf16[32,128,256]{2,1,0:T(8,128)(2,1)} %broadcast_select_fusion.2.refs_0_), custom_call_target="tpu_custom_call" | custom-call | bytes 5242880 | tf_op jit(solution)/shard_map/choose_blocks/pallas_call | solution.py:50
  68.2 3.7 %all-to-all-start.2 = ((bf16[40,128,256]{2,1,0:T(8,128)(2,1)}), bf16[40,128,256]{2,1,0:T(8,128)(2,1)S(1)}, u32[]{:S(2)}, u32[]{:S(2)}) async-start(bf16[40,128,256]{2,1,0:T(8,128)(2,1)} %choose_blocks.5), calls=%async_computation.2 | async-start | bytes 5242880 | tf_op jit(solution)/shard_map/all_to_all | solution.py:339
  71.9 0.6 fusion.13
  73.8 30.1 %collective-permute-done.2 = bf16[32,128,256]{2,1,0:T(8,128)(2,1)} collective-permute-done((bf16[32,128,256]{2,1,0:T(8,128)(2,1)}, bf16[32,128,256]{2,1,0:T(8,128)(2,1)}, u32[]{:S(2)}, u32[]{:S(2)}) %collective-permute-start.2) | collective-permute-done | bytes 2097184 | tf_op jit(solution)/shard_map/ppermute | solution.py:322
  103.9 4.5 %broadcast_select_fusion = (bf16[32,128,256]{2,1,0:T(8,128)(2,1)}, bf16[32,128,256]{2,1,0:T(8,128)(2,1)}) fusion(bf16[32,128,256]{2,1,0:T(8,128)(2,1)} %collective-permute-done.2, bf16[32,128,256]{2,1,0:T(8,128)(2,1)} %collective-permute-done.3, pred[]{:T(512)S(6)} %lt.58, bf16[32,128,256]{2,1,0:T(8,128)(2,1)} %collective-permute-done.1, pred[]{:T(512)S(6)} %eq.161, ...), kind=kLoop, calls=%fused_computation.1 | loop fusion | flops 3145728 | bytes 10485763 | tf_op jit(solution)/shard_map/jit(_where)/select_n | solution.py:311
  108.5 1.3 collective-permute-start.4
  109.8 0.6 reshape_squeeze.13.ids
  110.4 4.1 %choose_blocks.6 = bf16[40,128,256]{2,1,0:T(8,128)(2,1)} custom-call(s32[40]{0:T(128)} %reshape_squeeze.13.ids, bf16[32,128,256]{2,1,0:T(8,128)(2,1)} %get-tuple-element.34.refs_0_), custom_call_target="tpu_custom_call" | custom-call | bytes 5242880 | tf_op jit(solution)/shard_map/choose_blocks/pallas_call | solution.py:50
  114.5 3.7 %all-to-all-start.3 = ((bf16[40,128,256]{2,1,0:T(8,128)(2,1)}), bf16[40,128,256]{2,1,0:T(8,128)(2,1)S(1)}, u32[]{:S(2)}, u32[]{:S(2)}) async-start(bf16[40,128,256]{2,1,0:T(8,128)(2,1)} %choose_blocks.6), calls=%async_computation.3 | async-start | bytes 5242880 | tf_op jit(solution)/shard_map/all_to_all | solution.py:339
  118.4 0.6 reshape_squeeze.12.ids
  118.9 37.8 %collective-permute-done.4 = bf16[32,128,256]{2,1,0:T(8,128)(2,1)} collective-permute-done((bf16[32,128,256]{2,1,0:T(8,128)(2,1)}, bf16[32,128,256]{2,1,0:T(8,128)(2,1)}, u32[]{:S(2)}, u32[]{:S(2)}) %collective-permute-start.4) | collective-permute-done | bytes 2097184 | tf_op jit(solution)/shard_map/ppermute | solution.py:314
  156.7 3.1 %broadcast_select_fusion.1.refs_0_ = bf16[32,128,256]{2,1,0:T(8,128)(2,1)} fusion(bf16[32,128,256]{2,1,0:T(8,128)(2,1)} %collective-permute-done.4, bf16[32,128,256]{2,1,0:T(8,128)(2,1)} %get-tuple-element.33, pred[]{:T(512)S(6)} %or.3), kind=kLoop, calls=%fused_computation.2 | loop fusion | flops 1048576 | bytes 6291457 | tf_op jit(solution)/shard_map/jit(_where)/select_n | solution.py:319
  159.9 4.1 %choose_blocks.7 = bf16[40,128,256]{2,1,0:T(8,128)(2,1)} custom-call(s32[40]{0:T(128)} %reshape_squeeze.12.ids, bf16[32,128,256]{2,1,0:T(8,128)(2,1)} %broadcast_select_fusion.1.refs_0_), custom_call_target="tpu_custom_call" | custom-call | bytes 5242880 | tf_op jit(solution)/shard_map/choose_blocks/pallas_call | solution.py:50
  164.0 3.7 %all-to-all-start.4 = ((bf16[40,128,256]{2,1,0:T(8,128)(2,1)}), bf16[40,128,256]{2,1,0:T(8,128)(2,1)S(1)}, u32[]{:S(2)}, u32[]{:S(2)}) async-start(bf16[40,128,256]{2,1,0:T(8,128)(2,1)} %choose_blocks.7), calls=%async_computation.4 | async-start | bytes 5242880 | tf_op jit(solution)/shard_map/all_to_all | solution.py:339
  167.7 0.2 fusion.1
  168.0 0.1 ge.10
  168.2 0.2 convert_reduce_fusion
  168.4 0.1 reduce_sum.104
  168.5 0.7 convert_reduce_fusion.1
  169.3 0.2 reduce_window_sum.11
  169.7 0.6 reshape.211.late
  170.4 0.6 reshape.209.slots
  171.0 0.6 compare_select_fusion.1.slots
  171.6 15.6 %early_sums.1 = (f32[4096,256]{1,0:T(8,128)}, bf16[32,128,512]{2,1,0:T(8,128)(2,1)}) custom-call(s32[192]{0:T(256)} %compare_select_fusion.1.slots, s32[128]{0:T(128)} %reshape.211.late, s32[32]{0:T(128)} %get-tuple-element.29.counts, bf16[32,128,256]{2,1,0:T(8,128)(2,1)} %bitcast.16, bf16[40,128,256]{2,1,0:T(8,128)(2,1)} %copy-done.1, ...), custom_call_target="tpu_custom_call" | custom-call | flops 1610612736 | bytes 28901376 | tf_op jit(solution)/shard_map/early_sums/pallas_call | solution.py:109
  187.2 12.8 %all-to-all-done.4.refs_0_ = bf16[40,128,256]{2,1,0:T(8,128)(2,1)S(1)} async-done(((bf16[40,128,256]{2,1,0:T(8,128)(2,1)}), bf16[40,128,256]{2,1,0:T(8,128)(2,1)S(1)}, u32[]{:S(2)}, u32[]{:S(2)}) %all-to-all-start.4) | async-done | bytes 2621472 | tf_op jit(solution)/shard_map/all_to_all | solution.py:339
  200.0 1.6 copy-done
  201.6 14.5 %sage_layer.1 = bf16[4096,256]{1,0:T(8,128)(2,1)} custom-call(s32[128]{0:T(128)} %reshape.209.slots, s32[32]{0:T(128)} %get-tuple-element.29.counts, bf16[40,128,256]{2,1,0:T(8,128)(2,1)} %copy-done, f32[4096,256]{1,0:T(8,128)} %get-tuple-element.23.refs_1_, bf16[32,128,512]{2,1,0:T(8,128)(2,1)} %get-tuple-element.24.refs_2_, bf16[4096,256]{1,0:T(8,128)(2,1)} %refs_3_.1, ...), custom_call_target="tpu_custom_call" | custom-call | flops 2147483648 | bytes 12582912 | tf_op jit(solution)/shard_map/sage_layer/pallas_call | solution.py:189
  (43 shorter events, 1.2 us)
Async XLA Ops:
  0.0 50.1 %collective-permute-start.1 = (bf16[32,128,256]{2,1,0:T(8,128)(2,1)}, bf16[32,128,256]{2,1,0:T(8,128)(2,1)}, u32[]{:S(2)}, u32[]{:S(2)}) collective-permute-start(bf16[32,128,256]{2,1,0:T(8,128)(2,1)} %bitcast.13), channel_id=1, source_target_pairs={{0,8},{1,9},{2,10},{3,11},{4,12},{5,13},{6,14},{7,15},{8,16},{9,17... | collective-permute-start | bytes 6291464 | tf_op jit(solution)/shard_map/ppermute | solution.py:322
  6.2 49.3 %collective-permute-start = (bf16[32,128,256]{2,1,0:T(8,128)(2,1)}, bf16[32,128,256]{2,1,0:T(8,128)(2,1)}, u32[]{:S(2)}, u32[]{:S(2)}) collective-permute-start(bf16[32,128,256]{2,1,0:T(8,128)(2,1)} %bitcast.14), channel_id=1, source_target_pairs={{8,0},{9,1},{10,2},{11,3},{12,4},{13,5},{14,6},{15,7},{16,8},{17,9... | collective-permute-start | bytes 6291464 | tf_op jit(solution)/shard_map/ppermute | solution.py:322
  9.0 8.4 %all-to-all-start = ((s32[8,1,192]{2,1,0:T(1,128)}), s32[8,1,192]{2,1,0:T(1,128)S(1)}, u32[]{:S(2)}, u32[]{:S(2)}) async-start(s32[8,1,192]{2,1,0:T(1,128)} %broadcast_in_dim.109), calls=%async_computation | async-start | bytes 16384 | tf_op jit(solution)/shard_map/all_to_all | solution.py:236
  23.8 35.0 %copy-start.5 = (s32[4,1]{0,1:T(1,128)S(1)}, s32[4,1]{0,1:T(1,128)}, u32[]{:S(2)}) copy-start(s32[4,1]{0,1:T(1,128)} %constant.102.clone) | copy-start | bytes 52
  23.8 40.2 %all-to-all-start.1 = ((bf16[40,128,256]{2,1,0:T(8,128)(2,1)}), bf16[40,128,256]{2,1,0:T(8,128)(2,1)S(1)}, u32[]{:S(2)}, u32[]{:S(2)}) async-start(bf16[40,128,256]{2,1,0:T(8,128)(2,1)} %choose_blocks.4), calls=%async_computation.1 | async-start | bytes 5242880 | tf_op jit(solution)/shard_map/all_to_all | solution.py:339
  55.5 48.4 %collective-permute-start.2 = (bf16[32,128,256]{2,1,0:T(8,128)(2,1)}, bf16[32,128,256]{2,1,0:T(8,128)(2,1)}, u32[]{:S(2)}, u32[]{:S(2)}) collective-permute-start(bf16[32,128,256]{2,1,0:T(8,128)(2,1)} %collective-permute-done), channel_id=1, source_target_pairs={{8,0},{9,1},{10,2},{11,3},{12,4},{13,5},{14,6},{15,7},{16,8},{17,9... | collective-permute-start | bytes 6291464 | tf_op jit(solution)/shard_map/ppermute | solution.py:322
  56.8 47.1 %collective-permute-start.3 = (bf16[32,128,256]{2,1,0:T(8,128)(2,1)}, bf16[32,128,256]{2,1,0:T(8,128)(2,1)}, u32[]{:S(2)}, u32[]{:S(2)}) collective-permute-start(bf16[32,128,256]{2,1,0:T(8,128)(2,1)} %collective-permute-done.1), channel_id=1, source_target_pairs={{8,16},{9,17},{10,18},{11,19},{12,20},{13,21},{14,22},{15,23},{16,... | collective-permute-start | bytes 6291464 | tf_op jit(solution)/shard_map/ppermute | solution.py:322
  64.0 4.1 %copy-start.1 = (bf16[40,128,256]{2,1,0:T(8,128)(2,1)}, bf16[40,128,256]{2,1,0:T(8,128)(2,1)S(1)}, u32[]{:S(2)}) copy-start(bf16[40,128,256]{2,1,0:T(8,128)(2,1)S(1)} %all-to-all-done.1.refs_1_) | copy-start | bytes 7864324
  68.2 3.8 %copy-start.4 = (s32[4,1]{0,1:T(1,128)S(1)}, s32[4,1]{0,1:T(1,128)}, u32[]{:S(2)}) copy-start(s32[4,1]{0,1:T(1,128)} %constant.103.clone) | copy-start | bytes 52
  68.2 42.2 %all-to-all-start.2 = ((bf16[40,128,256]{2,1,0:T(8,128)(2,1)}), bf16[40,128,256]{2,1,0:T(8,128)(2,1)S(1)}, u32[]{:S(2)}, u32[]{:S(2)}) async-start(bf16[40,128,256]{2,1,0:T(8,128)(2,1)} %choose_blocks.5), calls=%async_computation.2 | async-start | bytes 5242880 | tf_op jit(solution)/shard_map/all_to_all | solution.py:339
  108.5 48.3 %collective-permute-start.4 = (bf16[32,128,256]{2,1,0:T(8,128)(2,1)}, bf16[32,128,256]{2,1,0:T(8,128)(2,1)}, u32[]{:S(2)}, u32[]{:S(2)}) collective-permute-start(bf16[32,128,256]{2,1,0:T(8,128)(2,1)} %get-tuple-element.33), channel_id=1, source_target_pairs={{8,0},{9,1},{10,2},{11,3},{12,4},{13,5},{14,6},{15,7},{16,24},{17,... | collective-permute-start | bytes 6291464 | tf_op jit(solution)/shard_map/ppermute | solution.py:314
  110.4 4.1 %copy-start.2 = (bf16[40,128,256]{2,1,0:T(8,128)(2,1)}, bf16[40,128,256]{2,1,0:T(8,128)(2,1)S(1)}, u32[]{:S(2)}) copy-start(bf16[40,128,256]{2,1,0:T(8,128)(2,1)S(1)} %all-to-all-done.2.refs_2_) | copy-start | bytes 7864324
  114.5 45.3 %all-to-all-start.3 = ((bf16[40,128,256]{2,1,0:T(8,128)(2,1)}), bf16[40,128,256]{2,1,0:T(8,128)(2,1)S(1)}, u32[]{:S(2)}, u32[]{:S(2)}) async-start(bf16[40,128,256]{2,1,0:T(8,128)(2,1)} %choose_blocks.6), calls=%async_computation.3 | async-start | bytes 5242880 | tf_op jit(solution)/shard_map/all_to_all | solution.py:339
  159.9 4.1 %copy-start.3 = (bf16[40,128,256]{2,1,0:T(8,128)(2,1)}, bf16[40,128,256]{2,1,0:T(8,128)(2,1)S(1)}, u32[]{:S(2)}) copy-start(bf16[40,128,256]{2,1,0:T(8,128)(2,1)S(1)} %all-to-all-done.3.refs_3_) | copy-start | bytes 7864324
  164.0 36.0 %all-to-all-start.4 = ((bf16[40,128,256]{2,1,0:T(8,128)(2,1)}), bf16[40,128,256]{2,1,0:T(8,128)(2,1)S(1)}, u32[]{:S(2)}, u32[]{:S(2)}) async-start(bf16[40,128,256]{2,1,0:T(8,128)(2,1)} %choose_blocks.7), calls=%async_computation.4 | async-start | bytes 5242880 | tf_op jit(solution)/shard_map/all_to_all | solution.py:339
  200.0 1.6 copy-start

commit v7 on v0

v7 whole, which is shorter than its diff:
```python
import functools

import jax
import jax.numpy as jnp
from jax import lax
from jax.experimental import pallas as pl
from jax.experimental.pallas import tpu as pltpu
from jax.sharding import PartitionSpec as P

REM_PB = 4
PLANES = 4
CHOOSE_FLOPS = 10**10
EARLY_FLOPS = 2 * 10**10

VMEM_LIMIT = 60 * 1024 * 1024


def pick_row(table, z):
    return jnp.sum(jnp.where(jnp.arange(table.shape[0])[:, None] == z, table, 0), axis=0)


def choose_kernel(which, ids, *refs):
    *froms, out, held, in_sem, out_sem = refs
    count = out.shape[0]
    for j, source in enumerate(froms):

        @pl.when(which[0] == j)
        def _():
            for n in range(count):
                pltpu.make_async_copy(source.at[ids[n]], held.at[n], in_sem).start()

    pltpu.make_async_copy(out, held, in_sem).wait()
    leaving = pltpu.make_async_copy(held, out, out_sem)
    leaving.start()
    leaving.wait()


def choose(which, ids, froms):
    out = (ids.shape[0],) + froms[0].shape[1:]
    moved = out[0] * out[1] * out[2] * 2
    return pl.pallas_call(
        choose_kernel,
        grid_spec=pltpu.PrefetchScalarGridSpec(
            num_scalar_prefetch=2,
            grid=(1,),
            in_specs=[pl.BlockSpec(memory_space=pltpu.HBM)] * len(froms),
            out_specs=pl.BlockSpec(memory_space=pltpu.HBM),
            scratch_shapes=[
                pltpu.VMEM(out, froms[0].dtype),
                pltpu.SemaphoreType.DMA,
                pltpu.SemaphoreType.DMA,
            ],
        ),
        out_shape=jax.ShapeDtypeStruct(out, froms[0].dtype),
        compiler_params=pltpu.CompilerParams(vmem_limit_bytes=VMEM_LIMIT),
        cost_estimate=pl.CostEstimate(flops=CHOOSE_FLOPS, bytes_accessed=2 * moved, transcendentals=0),
        name="choose_blocks",
    )(which, ids, *froms)


def fill(pieces, table, sems):
    copies, at = [], 0
    for n, piece in enumerate(pieces):
        here = table.at[pl.ds(at, piece.shape[0])]
        copies.append(pltpu.make_async_copy(piece, here, sems.at[n]))
        at += piece.shape[0]
    for copy in copies:
        copy.start()
    for copy in copies:
        copy.wait()


def early_kernel(slots, late, counts, *refs):
    *froms, masks, degree, sums, left, share, table, sems = refs
    step = pl.program_id(0)
    rows, per_block = masks.shape[:2]
    tile, width = table.shape[1:]
    spare = left.shape[2] // tile

    @pl.when(step == 0)
    def _():
        table[table.shape[0] - 1] = jnp.zeros((tile, width), table.dtype)
        fill(froms, table, sems)

    for r in range(rows):
        row = step * rows + r
        here = pl.ds(r * tile, tile)
        mask = jnp.concatenate(
            [masks[r, t].astype(jnp.float32).astype(jnp.bfloat16) for t in range(per_block)], axis=1
        )
        picked = jnp.concatenate(
            [table[slots[row * per_block + t]] for t in range(per_block)], axis=0
        )
        sums[here, :] = jnp.dot(mask, picked, preferred_element_type=jnp.float32)
        for t in range(spare):
            kept = masks[r, late[row * spare + t]].astype(jnp.float32)
            kept = jnp.where(t < counts[row], kept, 0.0).astype(jnp.bfloat16)
            left[r, :, t * tile : (t + 1) * tile] = kept
        count = degree[pl.ds(row, 1), :].astype(jnp.float32)
        share[here, :] = 1.0 / jnp.broadcast_to(count, (tile, tile)).T


def early(slots, late, counts, froms, tile_masks, degree):
    blocks_here, per_block, tile, _ = tile_masks.shape
    width = froms[0].shape[2]
    spare = late.shape[0] // blocks_here
    rows = 4 if blocks_here % 4 == 0 else 1
    blocks_in_table = sum(piece.shape[0] for piece in froms) + 1
    return pl.pallas_call(
        early_kernel,
        grid_spec=pltpu.PrefetchScalarGridSpec(
            num_scalar_prefetch=3,
            grid=(blocks_here // rows,),
            in_specs=[pl.BlockSpec(memory_space=pl.ANY)] * len(froms)
            + [
                pl.BlockSpec((rows, per_block, tile, tile), lambda r, *_: (r, 0, 0, 0)),
                pl.BlockSpec((blocks_here, tile), lambda r, *_: (0, 0)),
            ],
            out_specs=[
                pl.BlockSpec((rows * tile, width), lambda r, *_: (r, 0)),
                pl.BlockSpec((rows, tile, spare * tile), lambda r, *_: (r, 0, 0)),
                pl.BlockSpec((rows * tile, tile), lambda r, *_: (r, 0)),
            ],
            scratch_shapes=[
                pltpu.VMEM((blocks_in_table, tile, width), jnp.bfloat16),
                pltpu.SemaphoreType.DMA((len(froms),)),
            ],
        ),
        out_shape=[
            jax.ShapeDtypeStruct((blocks_here * tile, width), jnp.float32),
            jax.ShapeDtypeStruct((blocks_here, tile, spare * tile), jnp.bfloat16),
            jax.ShapeDtypeStruct((blocks_here * tile, tile), jnp.float32),
        ],
        compiler_params=pltpu.CompilerParams(vmem_limit_bytes=VMEM_LIMIT),
        cost_estimate=pl.CostEstimate(
            flops=EARLY_FLOPS,
            bytes_accessed=blocks_here * per_block * tile * tile * 6 + blocks_in_table * tile * width * 2,
            transcendentals=0,
        ),
        name="early_sums",
    )(slots, late, counts, *froms, tile_masks, degree)


def layer_kernel(slots, counts, *refs):
    *froms, sums, left, share, features, weight, out, table, totals, sems = refs
    step = pl.program_id(0)
    rows, tile = left.shape[:2]
    width = table.shape[2]
    spare = left.shape[2] // tile
    pair = min(2, spare)
    pl.when(step == 0)(functools.partial(fill, froms, table, sems))

    def added(r, first):
        ends = min(first + pair, spare)
        picked = [table[slots[(step * rows + r) * spare + t]] for t in range(first, ends)]
        mask = left[r, :, first * tile : ends * tile]
        return jnp.dot(mask, jnp.concatenate(picked, axis=0), preferred_element_type=jnp.float32)

    for r in range(rows):
        here = pl.ds(r * tile, tile)
        totals[here, :] = sums[here, :] + added(r, 0)
    for r in range(rows):
        here = pl.ds(r * tile, tile)
        for first in range(pair, spare, pair):

            @pl.when(counts[step * rows + r] > first)
            def _():
                totals[here, :] += added(r, first)

    for r in range(rows):
        here = pl.ds(r * tile, tile)
        part = jnp.concatenate([share[here, :]] * (width // tile), axis=1)
        mean = (totals[here, :] * part).astype(jnp.bfloat16)
        joined = jnp.concatenate([features[here, :], mean], axis=1)
        hidden = jnp.dot(joined, weight[...], preferred_element_type=jnp.float32)
        hidden = jnp.maximum(hidden, 0.0)
        scale = lax.rsqrt(jnp.sum(hidden * hidden, axis=1, keepdims=True) + 1e-06)
        out[here, :] = (hidden * scale).astype(jnp.bfloat16)


def layer(slots, counts, froms, sums, left, share, features, weight):
    blocks_here, tile, across = left.shape
    width = features.shape[1]
    out_width = weight.shape[1]
    rows = 4 if blocks_here % 4 == 0 else 1
    items = rows * tile
    blocks_in_table = sum(piece.shape[0] for piece in froms)
    return pl.pallas_call(
        layer_kernel,
        grid_spec=pltpu.PrefetchScalarGridSpec(
            num_scalar_prefetch=2,
            grid=(blocks_here // rows,),
            in_specs=[pl.BlockSpec(memory_space=pl.ANY)] * len(froms)
            + [
                pl.BlockSpec((items, width), lambda r, *_: (r, 0)),
                pl.BlockSpec((rows, tile, across), lambda r, *_: (r, 0, 0)),
                pl.BlockSpec((items, tile), lambda r, *_: (r, 0)),
                pl.BlockSpec((items, width), lambda r, *_: (r, 0)),
                pl.BlockSpec((2 * width, out_width), lambda r, *_: (0, 0)),
            ],
            out_specs=pl.BlockSpec((items, out_width), lambda r, *_: (r, 0)),
            scratch_shapes=[
                pltpu.VMEM((blocks_in_table, tile, width), jnp.bfloat16),
                pltpu.VMEM((items, width), jnp.float32),
                pltpu.SemaphoreType.DMA((len(froms),)),
            ],
        ),
        out_shape=jax.ShapeDtypeStruct((blocks_here * tile, out_width), jnp.bfloat16),
        compiler_params=pltpu.CompilerParams(vmem_limit_bytes=VMEM_LIMIT),
        cost_estimate=pl.CostEstimate(
            flops=2 * blocks_here * tile * (across + 2 * width) * out_width,
            bytes_accessed=blocks_here * tile * (4 * width + 2 * across + 2 * width + 2 * out_width),
            transcendentals=blocks_here * tile,
        ),
        name="sage_layer",
    )(slots, counts, *froms, sums, left, share, features, weight)


def on_device(features, tile_cols, tile_masks, degree, weight):
    blocks_here, per_block = tile_cols.shape
    tile = tile_masks.shape[2]
    width = features.shape[1]
    peers = lax.axis_size("rows")
    plane = peers // PLANES
    myself = lax.axis_index("rows")
    z, p = myself // plane, myself % plane
    end = (z == 0) | (z == PLANES - 1)
    capacity = max(2, (REM_PB * blocks_here + peers - 2) // (peers - 1))
    seats_all = plane * capacity
    local = features.reshape(blocks_here, tile, width)
    columns = tile_cols.reshape(-1)
    groups = [[a * plane + q for q in range(plane)] for a in range(PLANES)]

    def exchange(x):
        return lax.all_to_all(
            x, "rows", split_axis=0, concat_axis=0, axis_index_groups=groups, tiled=True
        )

    def shift(x, moves):
        pairs = [(a * plane + q, b * plane + q) for a, b in moves for q in range(plane)]
        return lax.ppermute(x, "rows", pairs)

    across = shift(columns, [(0, PLANES - 1), (PLANES - 1, 0)])
    both = jnp.stack([columns, across])
    asked = exchange(jnp.broadcast_to(both[None], (plane,) + both.shape))
    down = [(a, a - 1) for a in range(1, PLANES)]
    up = [(a - 1, a) for a in range(1, PLANES)]
    first, _ = lax.optimization_barrier((local, across))
    from_above, from_below = shift(first, down), shift(first, up)

    rounds = jnp.array([[0, 0, 1, 2], [1, 2, 0, 3], [2, 3, 1, 0], [3, 3, 2, 1]], jnp.int32)
    line = pick_row(rounds, z) * plane + p
    blocks = jnp.arange(blocks_here, dtype=jnp.int32)
    wanted = line[:, None] * blocks_here + blocks[None, :]
    far = end & (jnp.arange(PLANES) == 1)
    asking = jnp.where(far[None, :, None], asked[:, 1, None, :], asked[:, 0, None, :])
    need = jnp.any(asking[:, :, :, None] == wanted[None, :, None, :], axis=2).astype(jnp.int32)
    below = blocks[:, None] > blocks[None, :]
    place = jnp.sum(jnp.where(below, need[:, :, None, :], 0), axis=3)
    seat = jnp.arange(capacity, dtype=jnp.int32)
    taken = (need[:, :, None, :] == 1) & (place[:, :, None, :] == seat[:, None])
    chosen = jnp.sum(jnp.where(taken, blocks, 0), axis=3)
    ids = [chosen[:, k, :].reshape(-1) for k in range(PLANES)]

    owners, within = columns // blocks_here, columns % blocks_here
    positions = jnp.arange(columns.shape[0], dtype=jnp.int32)
    same = columns[:, None] == columns[None, :]
    repeated = jnp.any(same & (positions[None, :] < positions[:, None]), axis=1)
    ahead = (owners[:, None] == owners[None, :]) & (columns[None, :] < columns[:, None])
    ranks = jnp.sum(ahead & ~repeated[None, :], axis=1, dtype=jnp.int32)
    rounds_of = jnp.array([[0, 2, 3, 1], [2, 0, 1, 3], [3, 2, 0, 1], [1, 3, 2, 0]], jnp.int32)
    their_plane = owners // plane
    among = their_plane[:, None] == jnp.arange(PLANES)
    turn = jnp.sum(jnp.where(among, pick_row(rounds_of, z)[None, :], 0), axis=1)
    seats = (owners % plane) * capacity + ranks
    nothing = blocks_here + 3 * seats_all
    final = (turn == 3) | (end & (turn == 1))
    slots = jnp.where(final, nothing, blocks_here + turn * seats_all + seats)
    slots = jnp.where(owners == myself, within, slots)
    seats = jnp.where(turn == 3, seats + seats_all, seats)

    last = final.reshape(blocks_here, per_block)
    counts = jnp.sum(last, axis=1, dtype=jnp.int32)
    order_in = jnp.cumsum(last, axis=1) - 1
    spots = jnp.arange(REM_PB, dtype=jnp.int32)
    chair = last[:, None, :] & (order_in[:, None, :] == spots[:, None])
    late = jnp.sum(jnp.where(chair, jnp.arange(per_block, dtype=jnp.int32), 0), axis=2, dtype=jnp.int32)
    late_slots = jnp.sum(
        jnp.where(chair, seats.reshape(blocks_here, 1, per_block), 0), axis=2, dtype=jnp.int32
    )

    always = jnp.zeros((1,), jnp.int32)
    inner = (~end).astype(jnp.int32)[None]
    picked = choose(always, ids[0], [local])
    got = [exchange(picked)]
    ids[1], _, _ = lax.optimization_barrier((ids[1], picked, from_below))
    picked = choose(inner, ids[1], [local, from_above])
    got.append(exchange(picked))
    second_down = shift(from_above, down[:-1])
    second_up = shift(from_below, up[1:])
    crossed = shift(got[1], [(0, PLANES - 1), (PLANES - 1, 0)])
    ids[2], _ = lax.optimization_barrier((ids[2], picked))
    picked = choose((z > 0).astype(jnp.int32)[None], ids[2], [from_above, from_below])
    got.append(exchange(picked))
    beyond = (z >= PLANES // 2).astype(jnp.int32)[None]
    got.append(exchange(choose(beyond, ids[3], [second_down, second_up])))

    sums, left, share = early(
        slots, late.reshape(-1), counts, [local] + got[:3], tile_masks, degree.reshape(blocks_here, tile)
    )
    return layer(late_slots.reshape(-1), counts, [crossed, got[3]], sums, left, share, features, weight)


def solution(mesh):
    in_specs = (P("rows", None), P("rows", None), P("rows", None, None, None), P("rows"), P())
    out_specs = P("rows", None)
    return jax.shard_map(
        on_device, mesh=mesh, in_specs=in_specs, out_specs=out_specs, check_vma=False
    )
```

time: 563 us -> 245 us (0.44)
  waiting for transfers between devices: 467 us -> 141 us
  Pallas kernels: 0 us -> 47.3 us
  starting transfers between devices: 4.11 us -> 37.7 us
  local copies, waits for them, and re-layouts: 41 us -> 11.2 us
  other arithmetic: 21.7 us -> 4.69 us
  blocking collectives: 14.2 us -> 0 us
  matrix products: 13.9 us -> 0 us
    all_to_all x1 -> x5, waiting for transfers between devices: 467 us -> 38.7 us  [exchange(): lax.all_to_all(x, 'rows', split_axis=0, concat_axis=0, axis_index_groups=...]
    ppermute x0 -> x6, waiting for transfers between devices: none -> 103 us  [shift(): return lax.ppermute(x, 'rows', pairs)]
    pallas_call x0 -> x6, Pallas kernels: none -> 47.3 us  [the longest x4 16.3 us: choose(): pl.pallas_call(choose_kernel, grid_spec=pltpu.PrefetchScalarGridSpec(num_...]
    gather x2 -> x0, local copies, waits for them, and re-layouts: 26.7 us -> none  [the longest x1 15.8 us: on_device(): picked = table[slots].reshape(blocks_here, per_block, tile, width)]
    concatenate x2 -> x0, other arithmetic: 18.5 us -> none  [the longest x1 18.5 us: on_device(): jnp.concatenate([local_blocks, received.reshape(-1, tile, width)], axis=0)]
    ppermute x0 -> x6, starting transfers between devices: none -> 18.3 us  [shift(): return lax.ppermute(x, 'rows', pairs)]
    all_to_all x1 -> x5, starting transfers between devices: 4.11 us -> 19.4 us  [exchange(): lax.all_to_all(x, 'rows', split_axis=0, concat_axis=0, axis_index_groups=...]
    all_to_all x1 -> x0, blocking collectives: 14.2 us -> none  [on_device(): lax.all_to_all(requests, 'rows', split_axis=0, concat_axis=0, tiled=True)]
  transfers between devices with their start and end apart: 1 -> 11, of which waited for: 1 -> 7; matrix products, arithmetic and copies ran while one was open for 0% -> 4% of each run, Pallas kernels for 0% -> 13%
where the time goes in v7:
time: 245 us; the launch traced here: 242 us
  waiting for transfers between devices  141 us (58%)
  Pallas kernels  47.3 us (19%)
  starting transfers between devices  37.7 us (15%)
  local copies, waits for them, and re-layouts  11.2 us (5%)
  other arithmetic  4.69 us (2%)
    ppermute x6, waiting for transfers between devices, shift(): return lax.ppermute(x, 'rows', pairs)  103 us
    all_to_all x5, waiting for transfers between devices, exchange(): lax.all_to_all(x, 'rows', split_axis=0, concat_axis=0, axis_index_groups=...  38.7 us
    all_to_all x5, starting transfers between devices, exchange(): lax.all_to_all(x, 'rows', split_axis=0, concat_axis=0, axis_index_groups=...  19.4 us
    ppermute x6, starting transfers between devices, shift(): return lax.ppermute(x, 'rows', pairs)  18.3 us
    pallas_call x4, Pallas kernels, choose(): pl.pallas_call(choose_kernel, grid_spec=pltpu.PrefetchScalarGridSpec(num_...  16.3 us
    pallas_call x1, Pallas kernels, early(): pl.pallas_call(early_kernel, grid_spec=pltpu.PrefetchScalarGridSpec(num_s...  16.2 us
    pallas_call x1, Pallas kernels, layer(): pl.pallas_call(layer_kernel, grid_spec=pltpu.PrefetchScalarGridSpec(num_s...  14.7 us
    unnamed x8, local copies, waits for them, and re-layouts  5.39 us
  transfers between devices with their start and end apart: 11, of which 7 were waited for; matrix products, arithmetic and copies ran while one was open for 4% of the time, Pallas kernels for 13%

profile of v7, /device:TPU:0, one launch (start us, length us, event | category | flops | bytes accessed | tf_op | source)
XLA Modules:
  0.0 242.4 jit_solution(13379820286138716995)
XLA Ops:
  0.0 0.8 copy.23
  0.8 0.1 reshape.221
  0.9 7.0 %collective-permute-start = (s32[192]{0:T(256)S(1)}, s32[192]{0:T(256)S(1)}, u32[]{:S(2)}, u32[]{:S(2)}) collective-permute-start(s32[192]{0:T(256)S(1)} %reshape.221), channel_id=1, source_target_pairs={{0,24},{1,25},{2,26},{3,27},{4,28},{5,29},{6,30},{7,31},{24,0},{25... | collective-permute-start | bytes 2312 | tf_op jit(solution)/shard_map/ppermute | solution.py:241
  7.9 0.8 select_reduce_fusion.5
  8.9 0.5 collective-permute-done
  9.4 0.6 broadcast_in_dim.153
  10.0 3.9 %all-to-all-start = ((s32[8,2,192]{2,1,0:T(2,128)}), s32[8,2,192]{2,1,0:T(2,128)S(1)}, u32[]{:S(2)}, u32[]{:S(2)}) async-start(s32[8,2,192]{2,1,0:T(2,128)} %broadcast_in_dim.153), calls=%async_computation | async-start | bytes 32768 | tf_op jit(solution)/shard_map/all_to_all | solution.py:235
  13.9 2.7 %collective-permute-start.1 = (bf16[32,128,256]{2,1,0:T(8,128)(2,1)}, bf16[32,128,256]{2,1,0:T(8,128)(2,1)}, u32[]{:S(2)}, u32[]{:S(2)}) collective-permute-start(bf16[32,128,256]{2,1,0:T(8,128)(2,1)} %bitcast.18), channel_id=1, source_target_pairs={{0,8},{1,9},{2,10},{3,11},{4,12},{5,13},{6,14},{7,15},{8,16},{9,17... | collective-permute-start | bytes 6291464 | tf_op jit(solution)/shard_map/ppermute | solution.py:241
  16.6 1.3 collective-permute-start.2
  17.9 0.8 all-to-all-done
  18.8 0.7 compare_reduce_fusion
  19.5 0.6 select_reduce_fusion
  20.2 0.4 select_reduce_fusion.1
  20.7 0.6 reshape_squeeze.13.ids
  21.3 4.1 %choose_blocks.4 = bf16[40,128,256]{2,1,0:T(8,128)(2,1)} custom-call(s32[1]{0:T(128)} %constant.95.clone.1.which, s32[40]{0:T(128)} %reshape_squeeze.13.ids, bf16[32,128,256]{2,1,0:T(8,128)(2,1)} %bitcast.20), custom_call_target="tpu_custom_call" | custom-call | flops 10000000000 | bytes 5242880 | tf_op jit(solution)/shard_map/choose_blocks/pallas_call | solution.py:41
  25.3 3.7 %all-to-all-start.3 = ((bf16[40,128,256]{2,1,0:T(8,128)(2,1)}), bf16[40,128,256]{2,1,0:T(8,128)(2,1)S(1)}, u32[]{:S(2)}, u32[]{:S(2)}) async-start(bf16[40,128,256]{2,1,0:T(8,128)(2,1)} %choose_blocks.4), calls=%async_computation.3 | async-start | bytes 5242880 | tf_op jit(solution)/shard_map/all_to_all | solution.py:235
  29.1 0.7 reshape_squeeze.12.ids
  29.8 31.6 %collective-permute-done.1.refs_1_ = bf16[32,128,256]{2,1,0:T(8,128)(2,1)} collective-permute-done((bf16[32,128,256]{2,1,0:T(8,128)(2,1)}, bf16[32,128,256]{2,1,0:T(8,128)(2,1)}, u32[]{:S(2)}, u32[]{:S(2)}) %collective-permute-start.1) | collective-permute-done | bytes 2097184 | tf_op jit(solution)/shard_map/ppermute | solution.py:241
  61.4 5.5 %collective-permute-done.2.refs_1_.refs_0_ = bf16[32,128,256]{2,1,0:T(8,128)(2,1)} collective-permute-done((bf16[32,128,256]{2,1,0:T(8,128)(2,1)}, bf16[32,128,256]{2,1,0:T(8,128)(2,1)}, u32[]{:S(2)}, u32[]{:S(2)}) %collective-permute-start.2) | collective-permute-done | bytes 2097184 | tf_op jit(solution)/shard_map/ppermute | solution.py:241
  66.8 4.1 %choose_blocks.5 = bf16[40,128,256]{2,1,0:T(8,128)(2,1)} custom-call(s32[1]{0:T(128)} %bitcast.which, s32[40]{0:T(128)} %reshape_squeeze.12.ids, bf16[32,128,256]{2,1,0:T(8,128)(2,1)} %bitcast.21, bf16[32,128,256]{2,1,0:T(8,128)(2,1)} %collective-permute-done.2.refs_1_.refs_0_), custom_call_target="tpu_custom_call" | custom-call | flops 10000000000 | bytes 5242880 | tf_op jit(solution)/shard_map/choose_blocks/pallas_call | solution.py:41
  71.0 1.6 copy-done.1
  72.5 4.4 %all-to-all-start.1 = ((bf16[40,128,256]{2,1,0:T(8,128)(2,1)}), bf16[40,128,256]{2,1,0:T(8,128)(2,1)}, u32[]{:S(2)}, u32[]{:S(2)}) async-start(bf16[40,128,256]{2,1,0:T(8,128)(2,1)} %choose_blocks.5), calls=%async_computation.1 | async-start | bytes 5242880 | tf_op jit(solution)/shard_map/all_to_all | solution.py:235
  77.1 0.7 reshape_squeeze.15.ids
  77.7 1.3 collective-permute-start.4
  79.0 2.0 collective-permute-start.5
  81.0 4.0 %choose_blocks.7 = bf16[40,128,256]{2,1,0:T(8,128)(2,1)} custom-call(s32[1]{0:T(128)} %bitcast.4.which, s32[40]{0:T(128)} %reshape_squeeze.15.ids, bf16[32,128,256]{2,1,0:T(8,128)(2,1)} %collective-permute-done.2.refs_1_.refs_0_, bf16[32,128,256]{2,1,0:T(8,128)(2,1)} %collective-permute-done.1.refs_1_), custom_call_target="tpu_custom_call" | custom-call | flops 10000000000 | bytes 5242880 | tf_op jit(solution)/shard_map/choose_blocks/pallas_call | solution.py:41
  85.0 24.2 %all-to-all-done.1.refs_2_ = bf16[40,128,256]{2,1,0:T(8,128)(2,1)} async-done(((bf16[40,128,256]{2,1,0:T(8,128)(2,1)}), bf16[40,128,256]{2,1,0:T(8,128)(2,1)}, u32[]{:S(2)}, u32[]{:S(2)}) %all-to-all-start.1) | async-done | bytes 2621472 | tf_op jit(solution)/shard_map/all_to_all | solution.py:235
  109.2 3.6 %all-to-all-start.4 = ((bf16[40,128,256]{2,1,0:T(8,128)(2,1)}), bf16[40,128,256]{2,1,0:T(8,128)(2,1)S(1)}, u32[]{:S(2)}, u32[]{:S(2)}) async-start(bf16[40,128,256]{2,1,0:T(8,128)(2,1)} %choose_blocks.7), calls=%async_computation.4 | async-start | bytes 5242880 | tf_op jit(solution)/shard_map/all_to_all | solution.py:235
  113.0 0.1 and.134
  113.1 0.1 eq.159
  113.2 0.2 fusion.1
  113.4 0.2 convert_reduce_fusion
  113.7 0.1 reduce_sum.86
  113.8 0.6 convert_reduce_fusion.1
  114.4 0.2 reduce_window_sum.11
  114.7 0.6 reshape_squeeze.14.ids
  115.3 4.1 %collective-permute-start.3 = (bf16[40,128,256]{2,1,0:T(8,128)(2,1)}, bf16[40,128,256]{2,1,0:T(8,128)(2,1)}, u32[]{:S(2)}, u32[]{:S(2)}) collective-permute-start(bf16[40,128,256]{2,1,0:T(8,128)(2,1)} %all-to-all-done.1.refs_2_), channel_id=1, source_target_pairs={{0,24},{1,25},{2,26},{3,27},{4,28},{5,29},{6,30},{7,31},{24,0},{25... | collective-permute-start | bytes 7864328 | tf_op jit(solution)/shard_map/ppermute | solution.py:241
  119.4 65.0 %collective-permute-done.4.refs_0_ = bf16[32,128,256]{2,1,0:T(8,128)(2,1)} collective-permute-done((bf16[32,128,256]{2,1,0:T(8,128)(2,1)}, bf16[32,128,256]{2,1,0:T(8,128)(2,1)}, u32[]{:S(2)}, u32[]{:S(2)}) %collective-permute-start.4) | collective-permute-done | bytes 2097184 | tf_op jit(solution)/shard_map/ppermute | solution.py:241
  184.4 4.2 %choose_blocks.6 = bf16[40,128,256]{2,1,0:T(8,128)(2,1)} custom-call(s32[1]{0:T(128)} %bitcast.3.which, s32[40]{0:T(128)} %reshape_squeeze.14.ids, bf16[32,128,256]{2,1,0:T(8,128)(2,1)} %collective-permute-done.4.refs_0_, bf16[32,128,256]{2,1,0:T(8,128)(2,1)} %collective-permute-done.5.refs_1_), custom_call_target="tpu_custom_call" | custom-call | flops 10000000000 | bytes 5242880 | tf_op jit(solution)/shard_map/choose_blocks/pallas_call | solution.py:41
  188.6 1.5 copy-done.2
  190.1 3.8 %all-to-all-start.2 = ((bf16[40,128,256]{2,1,0:T(8,128)(2,1)}), bf16[40,128,256]{2,1,0:T(8,128)(2,1)S(1)}, u32[]{:S(2)}, u32[]{:S(2)}) async-start(bf16[40,128,256]{2,1,0:T(8,128)(2,1)} %choose_blocks.6), calls=%async_computation.2 | async-start | bytes 5242880 | tf_op jit(solution)/shard_map/all_to_all | solution.py:235
  194.2 0.6 reshape.225.late
  194.9 0.7 reshape.222.slots
  195.6 0.6 compare_select_fusion.slots
  196.2 16.2 %early_sums.1 = (f32[4096,256]{1,0:T(8,128)}, bf16[32,128,512]{2,1,0:T(8,128)(2,1)}, f32[4096,128]{1,0:T(8,128)}) custom-call(s32[192]{0:T(256)} %compare_select_fusion.slots, s32[128]{0:T(128)} %reshape.225.late, s32[32]{0:T(128)} %get-tuple-element.21.counts, bf16[32,128,256]{2,1,0:T(8,128)(2,1)} %bitcast.22, bf16[40,128,256]{2,1,0:T(8,128)(2,1)} %copy-done.1, ...), custom_call_target="tpu_custom_call" | custom-call | flops 20000000000 | bytes 28901376 | tf_op jit(solution)/shard_map/early_sums/pallas_call | solution.py:109
  212.5 13.6 %all-to-all-done.2.refs_1_ = bf16[40,128,256]{2,1,0:T(8,128)(2,1)S(1)} async-done(((bf16[40,128,256]{2,1,0:T(8,128)(2,1)}), bf16[40,128,256]{2,1,0:T(8,128)(2,1)S(1)}, u32[]{:S(2)}, u32[]{:S(2)}) %all-to-all-start.2) | async-done | bytes 2621472 | tf_op jit(solution)/shard_map/all_to_all | solution.py:235
  226.1 1.6 copy-done
  227.7 14.7 %sage_layer.1 = bf16[4096,256]{1,0:T(8,128)(2,1)} custom-call(s32[128]{0:T(128)} %reshape.222.slots, s32[32]{0:T(128)} %get-tuple-element.21.counts, bf16[40,128,256]{2,1,0:T(8,128)(2,1)} %collective-permute-done.3.refs_0_, bf16[40,128,256]{2,1,0:T(8,128)(2,1)} %copy-done, f32[4096,256]{1,0:T(8,128)} %get-tuple-element.14.refs_2_, ...), custom_call_target="tpu_custom_call" | custom-call | flops 2147483648 | bytes 12582912 | tf_op jit(solution)/shard_map/sage_layer/pallas_call | solution.py:188
  (37 shorter events, 1.2 us)
Async XLA Ops:
  0.9 8.5 %collective-permute-start = (s32[192]{0:T(256)S(1)}, s32[192]{0:T(256)S(1)}, u32[]{:S(2)}, u32[]{:S(2)}) collective-permute-start(s32[192]{0:T(256)S(1)} %reshape.221), channel_id=1, source_target_pairs={{0,24},{1,25},{2,26},{3,27},{4,28},{5,29},{6,30},{7,31},{24,0},{25... | collective-permute-start | bytes 2312 | tf_op jit(solution)/shard_map/ppermute | solution.py:241
  10.0 8.7 %all-to-all-start = ((s32[8,2,192]{2,1,0:T(2,128)}), s32[8,2,192]{2,1,0:T(2,128)S(1)}, u32[]{:S(2)}, u32[]{:S(2)}) async-start(s32[8,2,192]{2,1,0:T(2,128)} %broadcast_in_dim.153), calls=%async_computation | async-start | bytes 32768 | tf_op jit(solution)/shard_map/all_to_all | solution.py:235
  13.9 47.4 %collective-permute-start.1 = (bf16[32,128,256]{2,1,0:T(8,128)(2,1)}, bf16[32,128,256]{2,1,0:T(8,128)(2,1)}, u32[]{:S(2)}, u32[]{:S(2)}) collective-permute-start(bf16[32,128,256]{2,1,0:T(8,128)(2,1)} %bitcast.18), channel_id=1, source_target_pairs={{0,8},{1,9},{2,10},{3,11},{4,12},{5,13},{6,14},{7,15},{8,16},{9,17... | collective-permute-start | bytes 6291464 | tf_op jit(solution)/shard_map/ppermute | solution.py:241
  16.6 50.2 %collective-permute-start.2 = (bf16[32,128,256]{2,1,0:T(8,128)(2,1)}, bf16[32,128,256]{2,1,0:T(8,128)(2,1)}, u32[]{:S(2)}, u32[]{:S(2)}) collective-permute-start(bf16[32,128,256]{2,1,0:T(8,128)(2,1)} %bitcast.19), channel_id=1, source_target_pairs={{8,0},{9,1},{10,2},{11,3},{12,4},{13,5},{14,6},{15,7},{16,8},{17,9... | collective-permute-start | bytes 6291464 | tf_op jit(solution)/shard_map/ppermute | solution.py:241
  25.3 45.6 %all-to-all-start.3 = ((bf16[40,128,256]{2,1,0:T(8,128)(2,1)}), bf16[40,128,256]{2,1,0:T(8,128)(2,1)S(1)}, u32[]{:S(2)}, u32[]{:S(2)}) async-start(bf16[40,128,256]{2,1,0:T(8,128)(2,1)} %choose_blocks.4), calls=%async_computation.3 | async-start | bytes 5242880 | tf_op jit(solution)/shard_map/all_to_all | solution.py:235
  71.0 1.6 copy-start.1
  72.5 36.7 %all-to-all-start.1 = ((bf16[40,128,256]{2,1,0:T(8,128)(2,1)}), bf16[40,128,256]{2,1,0:T(8,128)(2,1)}, u32[]{:S(2)}, u32[]{:S(2)}) async-start(bf16[40,128,256]{2,1,0:T(8,128)(2,1)} %choose_blocks.5), calls=%async_computation.1 | async-start | bytes 5242880 | tf_op jit(solution)/shard_map/all_to_all | solution.py:235
  77.7 106.6 %collective-permute-start.4 = (bf16[32,128,256]{2,1,0:T(8,128)(2,1)}, bf16[32,128,256]{2,1,0:T(8,128)(2,1)}, u32[]{:S(2)}, u32[]{:S(2)}) collective-permute-start(bf16[32,128,256]{2,1,0:T(8,128)(2,1)} %collective-permute-done.2.refs_1_.refs_0_), channel_id=1, source_target_pairs={{8,0},{9,1},{10,2},{11,3},{12,4},{13,5},{14,6},{15,7},{16,8},{17,9... | collective-permute-start | bytes 6291464 | tf_op jit(solution)/shard_map/ppermute | solution.py:241
  79.0 105.3 %collective-permute-start.5 = (bf16[32,128,256]{2,1,0:T(8,128)(2,1)}, bf16[32,128,256]{2,1,0:T(8,128)(2,1)}, u32[]{:S(2)}, u32[]{:S(2)}) collective-permute-start(bf16[32,128,256]{2,1,0:T(8,128)(2,1)} %collective-permute-done.1.refs_1_), channel_id=1, source_target_pairs={{8,16},{9,17},{10,18},{11,19},{12,20},{13,21},{14,22},{15,23},{16,... | collective-permute-start | bytes 6291464 | tf_op jit(solution)/shard_map/ppermute | solution.py:241
  109.2 79.3 %all-to-all-start.4 = ((bf16[40,128,256]{2,1,0:T(8,128)(2,1)}), bf16[40,128,256]{2,1,0:T(8,128)(2,1)S(1)}, u32[]{:S(2)}, u32[]{:S(2)}) async-start(bf16[40,128,256]{2,1,0:T(8,128)(2,1)} %choose_blocks.7), calls=%async_computation.4 | async-start | bytes 5242880 | tf_op jit(solution)/shard_map/all_to_all | solution.py:235
  115.3 110.8 %collective-permute-start.3 = (bf16[40,128,256]{2,1,0:T(8,128)(2,1)}, bf16[40,128,256]{2,1,0:T(8,128)(2,1)}, u32[]{:S(2)}, u32[]{:S(2)}) collective-permute-start(bf16[40,128,256]{2,1,0:T(8,128)(2,1)} %all-to-all-done.1.refs_2_), channel_id=1, source_target_pairs={{0,24},{1,25},{2,26},{3,27},{4,28},{5,29},{6,30},{7,31},{24,0},{25... | collective-permute-start | bytes 7864328 | tf_op jit(solution)/shard_map/ppermute | solution.py:241
  188.6 1.5 copy-start.2
  190.1 36.0 %all-to-all-start.2 = ((bf16[40,128,256]{2,1,0:T(8,128)(2,1)}), bf16[40,128,256]{2,1,0:T(8,128)(2,1)S(1)}, u32[]{:S(2)}, u32[]{:S(2)}) async-start(bf16[40,128,256]{2,1,0:T(8,128)(2,1)} %choose_blocks.6), calls=%async_computation.2 | async-start | bytes 5242880 | tf_op jit(solution)/shard_map/all_to_all | solution.py:235
  226.1 1.6 copy-start

commit v8 on v7

--- a/solution.py
+++ b/solution.py
@@ -9,10 +9,10 @@
 
 REM_PB = 4
 PLANES = 4
-CHOOSE_FLOPS = 10**10
-EARLY_FLOPS = 2 * 10**10
-
-VMEM_LIMIT = 60 * 1024 * 1024
+HEAVY = 3 * 10**10
+LIGHT = 10**10
+
+VMEM_LIMIT = 62 * 1024 * 1024
 
 
 def pick_row(table, z):
@@ -35,7 +35,7 @@
     leaving.wait()
 
 
-def choose(which, ids, froms):
+def choose(which, ids, froms, flops):
     out = (ids.shape[0],) + froms[0].shape[1:]
     moved = out[0] * out[1] * out[2] * 2
     return pl.pallas_call(
@@ -53,9 +53,26 @@
         ),
         out_shape=jax.ShapeDtypeStruct(out, froms[0].dtype),
         compiler_params=pltpu.CompilerParams(vmem_limit_bytes=VMEM_LIMIT),
-        cost_estimate=pl.CostEstimate(flops=CHOOSE_FLOPS, bytes_accessed=2 * moved, transcendentals=0),
+        cost_estimate=pl.CostEstimate(flops=flops, bytes_accessed=2 * moved, transcendentals=0),
         name="choose_blocks",
     )(which, ids, *froms)
+
+
+def either_kernel(second, a, b, out):
+    out[...] = jnp.where(second[0] == 1, b[...], a[...])
+
+
+def either(second, a, b):
+    whole = pl.BlockSpec(a.shape, lambda i, s: (0, 0))
+    return pl.pallas_call(
+        either_kernel,
+        grid_spec=pltpu.PrefetchScalarGridSpec(
+            num_scalar_prefetch=1, grid=(1,), in_specs=[whole, whole], out_specs=whole
+        ),
+        out_shape=jax.ShapeDtypeStruct(a.shape, a.dtype),
+        cost_estimate=pl.CostEstimate(flops=HEAVY, bytes_accessed=0, transcendentals=0),
+        name="either_ids",
+    )(second, a, b)
 
 
 def fill(pieces, table, sems):
@@ -71,7 +88,7 @@
 
 
 def early_kernel(slots, late, counts, *refs):
-    *froms, masks, degree, sums, left, share, table, sems = refs
+    *froms, masks, sums, left, table, sems = refs
     step = pl.program_id(0)
     rows, per_block = masks.shape[:2]
     tile, width = table.shape[1:]
@@ -93,14 +110,11 @@
         )
         sums[here, :] = jnp.dot(mask, picked, preferred_element_type=jnp.float32)
         for t in range(spare):
-            kept = masks[r, late[row * spare + t]].astype(jnp.float32)
-            kept = jnp.where(t < counts[row], kept, 0.0).astype(jnp.bfloat16)
-            left[r, :, t * tile : (t + 1) * tile] = kept
-        count = degree[pl.ds(row, 1), :].astype(jnp.float32)
-        share[here, :] = 1.0 / jnp.broadcast_to(count, (tile, tile)).T
-
-
-def early(slots, late, counts, froms, tile_masks, degree):
+            kept = jnp.where(t < counts[row], masks[r, late[row * spare + t]], 0)
+            left[r, :, t * tile : (t + 1) * tile] = kept.astype(jnp.int8)
+
+
+def early(slots, late, counts, froms, tile_masks):
     blocks_here, per_block, tile, _ = tile_masks.shape
     width = froms[0].shape[2]
     spare = late.shape[0] // blocks_here
@@ -112,14 +126,10 @@
             num_scalar_prefetch=3,
             grid=(blocks_here // rows,),
             in_specs=[pl.BlockSpec(memory_space=pl.ANY)] * len(froms)
-            + [
-                pl.BlockSpec((rows, per_block, tile, tile), lambda r, *_: (r, 0, 0, 0)),
-                pl.BlockSpec((blocks_here, tile), lambda r, *_: (0, 0)),
-            ],
+            + [pl.BlockSpec((rows, per_block, tile, tile), lambda r, *_: (r, 0, 0, 0))],
             out_specs=[
                 pl.BlockSpec((rows * tile, width), lambda r, *_: (r, 0)),
                 pl.BlockSpec((rows, tile, spare * tile), lambda r, *_: (r, 0, 0)),
-                pl.BlockSpec((rows * tile, tile), lambda r, *_: (r, 0)),
             ],
             scratch_shapes=[
                 pltpu.VMEM((blocks_in_table, tile, width), jnp.bfloat16),
@@ -128,21 +138,20 @@
         ),
         out_shape=[
             jax.ShapeDtypeStruct((blocks_here * tile, width), jnp.float32),
-            jax.ShapeDtypeStruct((blocks_here, tile, spare * tile), jnp.bfloat16),
-            jax.ShapeDtypeStruct((blocks_here * tile, tile), jnp.float32),
+            jax.ShapeDtypeStruct((blocks_here, tile, spare * tile), jnp.int8),
         ],
         compiler_params=pltpu.CompilerParams(vmem_limit_bytes=VMEM_LIMIT),
         cost_estimate=pl.CostEstimate(
-            flops=EARLY_FLOPS,
+            flops=2 * LIGHT,
             bytes_accessed=blocks_here * per_block * tile * tile * 6 + blocks_in_table * tile * width * 2,
             transcendentals=0,
         ),
         name="early_sums",
-    )(slots, late, counts, *froms, tile_masks, degree)
+    )(slots, late, counts, *froms, tile_masks)
 
 
 def layer_kernel(slots, counts, *refs):
-    *froms, sums, left, share, features, weight, out, table, totals, sems = refs
+    *froms, sums, left, degree, features, weight, out, table, totals, sems = refs
     step = pl.program_id(0)
     rows, tile = left.shape[:2]
     width = table.shape[2]
@@ -153,7 +162,8 @@
     def added(r, first):
         ends = min(first + pair, spare)
         picked = [table[slots[(step * rows + r) * spare + t]] for t in range(first, ends)]
-        mask = left[r, :, first * tile : ends * tile]
+        mask = left[r, :, first * tile : ends * tile].astype(jnp.int32)
+        mask = mask.astype(jnp.float32).astype(jnp.bfloat16)
         return jnp.dot(mask, jnp.concatenate(picked, axis=0), preferred_element_type=jnp.float32)
 
     for r in range(rows):
@@ -167,9 +177,19 @@
             def _():
                 totals[here, :] += added(r, first)
 
+    across = lax.broadcasted_iota(jnp.int32, (tile, tile), 1)
+    diagonal = lax.broadcasted_iota(jnp.int32, (tile, tile), 0) == across
+    ones = jnp.ones((2 * tile, tile), jnp.bfloat16)
     for r in range(rows):
         here = pl.ds(r * tile, tile)
-        part = jnp.concatenate([share[here, :]] * (width // tile), axis=1)
+        count = degree[pl.ds(step * rows + r, 1), :]
+        small = count & 7
+        halves = [
+            jnp.where(diagonal, part.astype(jnp.float32), 0.0).astype(jnp.bfloat16)
+            for part in (count - small, small)
+        ]
+        count = jnp.dot(jnp.concatenate(halves, axis=1), ones, preferred_element_type=jnp.float32)
+        part = jnp.concatenate([1.0 / count] * (width // tile), axis=1)
         mean = (totals[here, :] * part).astype(jnp.bfloat16)
         joined = jnp.concatenate([features[here, :], mean], axis=1)
         hidden = jnp.dot(joined, weight[...], preferred_element_type=jnp.float32)
@@ -178,11 +198,11 @@
         out[here, :] = (hidden * scale).astype(jnp.bfloat16)
 
 
-def layer(slots, counts, froms, sums, left, share, features, weight):
+def layer(slots, counts, froms, sums, left, degree, features, weight):
     blocks_here, tile, across = left.shape
     width = features.shape[1]
     out_width = weight.shape[1]
-    rows = 4 if blocks_here % 4 == 0 else 1
+    rows = 8 if blocks_here % 8 == 0 else 1
     items = rows * tile
     blocks_in_table = sum(piece.shape[0] for piece in froms)
     return pl.pallas_call(
@@ -194,7 +214,7 @@
             + [
                 pl.BlockSpec((items, width), lambda r, *_: (r, 0)),
                 pl.BlockSpec((rows, tile, across), lambda r, *_: (r, 0, 0)),
-                pl.BlockSpec((items, tile), lambda r, *_: (r, 0)),
+                pl.BlockSpec((blocks_here, tile), lambda r, *_: (0, 0)),
                 pl.BlockSpec((items, width), lambda r, *_: (r, 0)),
                 pl.BlockSpec((2 * width, out_width), lambda r, *_: (0, 0)),
             ],
@@ -209,11 +229,11 @@
         compiler_params=pltpu.CompilerParams(vmem_limit_bytes=VMEM_LIMIT),
         cost_estimate=pl.CostEstimate(
             flops=2 * blocks_here * tile * (across + 2 * width) * out_width,
-            bytes_accessed=blocks_here * tile * (4 * width + 2 * across + 2 * width + 2 * out_width),
+            bytes_accessed=blocks_here * tile * (4 * width + across + 2 * width + 2 * out_width),
             transcendentals=blocks_here * tile,
         ),
         name="sage_layer",
-    )(slots, counts, *froms, sums, left, share, features, weight)
+    )(slots, counts, *froms, sums, left, degree, features, weight)
 
 
 def on_device(features, tile_cols, tile_masks, degree, weight):
@@ -240,27 +260,27 @@
         pairs = [(a * plane + q, b * plane + q) for a, b in moves for q in range(plane)]
         return lax.ppermute(x, "rows", pairs)
 
-    across = shift(columns, [(0, PLANES - 1), (PLANES - 1, 0)])
-    both = jnp.stack([columns, across])
-    asked = exchange(jnp.broadcast_to(both[None], (plane,) + both.shape))
+    asked = exchange(jnp.broadcast_to(columns, (plane,) + columns.shape))
+    across = shift(asked, [(0, PLANES - 1), (PLANES - 1, 0)])
     down = [(a, a - 1) for a in range(1, PLANES)]
     up = [(a - 1, a) for a in range(1, PLANES)]
-    first, _ = lax.optimization_barrier((local, across))
-    from_above, from_below = shift(first, down), shift(first, up)
+    from_above, from_below = shift(local, down), shift(local, up)
 
     rounds = jnp.array([[0, 0, 1, 2], [1, 2, 0, 3], [2, 3, 1, 0], [3, 3, 2, 1]], jnp.int32)
     line = pick_row(rounds, z) * plane + p
     blocks = jnp.arange(blocks_here, dtype=jnp.int32)
     wanted = line[:, None] * blocks_here + blocks[None, :]
-    far = end & (jnp.arange(PLANES) == 1)
-    asking = jnp.where(far[None, :, None], asked[:, 1, None, :], asked[:, 0, None, :])
-    need = jnp.any(asking[:, :, :, None] == wanted[None, :, None, :], axis=2).astype(jnp.int32)
     below = blocks[:, None] > blocks[None, :]
-    place = jnp.sum(jnp.where(below, need[:, :, None, :], 0), axis=3)
     seat = jnp.arange(capacity, dtype=jnp.int32)
-    taken = (need[:, :, None, :] == 1) & (place[:, :, None, :] == seat[:, None])
-    chosen = jnp.sum(jnp.where(taken, blocks, 0), axis=3)
-    ids = [chosen[:, k, :].reshape(-1) for k in range(PLANES)]
+
+    def seated(asking, wanted):
+        need = jnp.any(asking[:, None, :, None] == wanted[None, :, None, :], axis=2).astype(jnp.int32)
+        place = jnp.sum(jnp.where(below, need[:, :, None, :], 0), axis=3)
+        taken = (need[:, :, None, :] == 1) & (place[:, :, None, :] == seat[:, None])
+        return jnp.sum(jnp.where(taken, blocks, 0), axis=3)
+
+    near = seated(asked, wanted)
+    ids = [near[:, k, :].reshape(-1) for k in range(PLANES)]
 
     owners, within = columns // blocks_here, columns % blocks_here
     positions = jnp.arange(columns.shape[0], dtype=jnp.int32)
@@ -291,24 +311,35 @@
 
     always = jnp.zeros((1,), jnp.int32)
     inner = (~end).astype(jnp.int32)[None]
-    picked = choose(always, ids[0], [local])
+    picked = choose(always, ids[0], [local], LIGHT)
     got = [exchange(picked)]
-    ids[1], _, _ = lax.optimization_barrier((ids[1], picked, from_below))
-    picked = choose(inner, ids[1], [local, from_above])
+    across, _, _ = lax.optimization_barrier((across, from_above, from_below))
+    opposite = seated(across, wanted[:1])[:, 0, :]
+    ids[1] = either(end.astype(jnp.int32)[None], near[:, 1, :], opposite).reshape(-1)
+    ids[1], _ = lax.optimization_barrier((ids[1], got[0]))
+    picked = choose(inner, ids[1], [local, from_above], LIGHT)
     got.append(exchange(picked))
     second_down = shift(from_above, down[:-1])
     second_up = shift(from_below, up[1:])
-    crossed = shift(got[1], [(0, PLANES - 1), (PLANES - 1, 0)])
+    leaving, _, _ = lax.optimization_barrier((got[1], second_down, second_up))
+    crossed = shift(leaving, [(0, PLANES - 1), (PLANES - 1, 0)])
     ids[2], _ = lax.optimization_barrier((ids[2], picked))
-    picked = choose((z > 0).astype(jnp.int32)[None], ids[2], [from_above, from_below])
+    picked = choose((z > 0).astype(jnp.int32)[None], ids[2], [from_above, from_below], HEAVY)
     got.append(exchange(picked))
     beyond = (z >= PLANES // 2).astype(jnp.int32)[None]
-    got.append(exchange(choose(beyond, ids[3], [second_down, second_up])))
-
-    sums, left, share = early(
-        slots, late.reshape(-1), counts, [local] + got[:3], tile_masks, degree.reshape(blocks_here, tile)
+    got.append(exchange(choose(beyond, ids[3], [second_down, second_up], LIGHT)))
+
+    sums, left = early(slots, late.reshape(-1), counts, [local] + got[:3], tile_masks)
+    return layer(
+        late_slots.reshape(-1),
+        counts,
+        [crossed, got[3]],
+        sums,
+        left,
+        degree.reshape(blocks_here, tile),
+        features,
+        weight,
     )
-    return layer(late_slots.reshape(-1), counts, [crossed, got[3]], sums, left, share, features, weight)
 
 
 def solution(mesh):

time: 245 us -> 195 us (0.80)
  waiting for transfers between devices: 141 us -> 92.5 us
  starting transfers between devices: 37.7 us -> 40.8 us
  local copies, waits for them, and re-layouts: 11.2 us -> 8.24 us
    ppermute x6, waiting for transfers between devices: 103 us -> 18.9 us  [shift(): return lax.ppermute(x, 'rows', pairs)]
    all_to_all x5, waiting for transfers between devices: 38.7 us -> 73.7 us  [exchange(): lax.all_to_all(x, 'rows', split_axis=0, concat_axis=0, axis_index_groups=...]
    unnamed x8 -> x2, local copies, waits for them, and re-layouts: 5.39 us -> 0.77 us
  transfers between devices with their start and end apart: 11 -> 11, of which waited for: 7 -> 6; matrix products, arithmetic and copies ran while one was open for 4% -> 7% of each run, Pallas kernels for 13% -> 17%
where the time goes in v8:
time: 195 us; the launch traced here: 193 us
  waiting for transfers between devices  92.5 us (47%)
  Pallas kernels  46 us (24%)
  starting transfers between devices  40.8 us (21%)
  local copies, waits for them, and re-layouts  8.24 us (4%)
  other arithmetic  5.35 us (3%)
    all_to_all x5, waiting for transfers between devices, exchange(): lax.all_to_all(x, 'rows', split_axis=0, concat_axis=0, axis_index_groups=...  73.7 us
    all_to_all x5, starting transfers between devices, exchange(): lax.all_to_all(x, 'rows', split_axis=0, concat_axis=0, axis_index_groups=...  21.8 us
    ppermute x6, starting transfers between devices, shift(): return lax.ppermute(x, 'rows', pairs)  19 us
    ppermute x6, waiting for transfers between devices, shift(): return lax.ppermute(x, 'rows', pairs)  18.9 us
    pallas_call x4, Pallas kernels, choose(): pl.pallas_call(choose_kernel, grid_spec=pltpu.PrefetchScalarGridSpec(num_...  16.5 us
    pallas_call x1, Pallas kernels, early(): pl.pallas_call(early_kernel, grid_spec=pltpu.PrefetchScalarGridSpec(num_s...  15 us
    pallas_call x1, Pallas kernels, layer(): pl.pallas_call(layer_kernel, grid_spec=pltpu.PrefetchScalarGridSpec(num_s...  13.2 us
  transfers between devices with their start and end apart: 11, of which 6 were waited for; matrix products, arithmetic and copies ran while one was open for 7% of the time, Pallas kernels for 17%

profile of v8, /device:TPU:0, one launch (start us, length us, event | category | flops | bytes accessed | tf_op | source)
XLA Modules:
  0.0 193.1 jit_solution(6093344688500247851)
XLA Ops:
  0.0 1.3 collective-permute-start.1
  1.3 6.9 %collective-permute-start.2 = (bf16[32,128,256]{2,1,0:T(8,128)(2,1)}, bf16[32,128,256]{2,1,0:T(8,128)(2,1)}, u32[]{:S(2)}, u32[]{:S(2)}) collective-permute-start(bf16[32,128,256]{2,1,0:T(8,128)(2,1)} %bitcast.19), channel_id=1, source_target_pairs={{0,8},{1,9},{2,10},{3,11},{4,12},{5,13},{6,14},{7,15},{8,16},{9,17... | collective-permute-start | bytes 6291464 | tf_op jit(solution)/shard_map/ppermute | solution.py:261
  8.2 0.8 copy.33
  9.1 0.6 broadcast_in_dim.156
  9.7 4.2 %all-to-all-start = ((s32[8,1,192]{2,1,0:T(1,128)}), s32[8,1,192]{2,1,0:T(1,128)S(1)}, u32[]{:S(2)}, u32[]{:S(2)}) async-start(s32[8,1,192]{2,1,0:T(1,128)} %broadcast_in_dim.156), calls=%async_computation | async-start | bytes 16384 | tf_op jit(solution)/shard_map/all_to_all | solution.py:255
  13.9 0.8 select_reduce_fusion.7
  14.7 3.8 %all-to-all-done = s32[8,1,192]{2,1,0:T(1,128)S(1)} async-done(((s32[8,1,192]{2,1,0:T(1,128)}), s32[8,1,192]{2,1,0:T(1,128)S(1)}, u32[]{:S(2)}, u32[]{:S(2)}) %all-to-all-start) | async-done | bytes 6176 | tf_op jit(solution)/shard_map/all_to_all | solution.py:255
  18.5 3.3 %collective-permute-start = (s32[8,192]{1,0:T(8,128)S(1)}, s32[8,192]{1,0:T(8,128)S(1)}, u32[]{:S(2)}, u32[]{:S(2)}) collective-permute-start(s32[8,192]{1,0:T(8,128)S(1)} %bitcast.23), channel_id=1, source_target_pairs={{0,24},{1,25},{2,26},{3,27},{4,28},{5,29},{6,30},{7,31},{24,0},{25... | collective-permute-start | bytes 18440 | tf_op jit(solution)/shard_map/ppermute | solution.py:261
  21.9 0.7 compare_reduce_fusion
  22.6 0.6 select_reduce_fusion
  23.3 0.4 select_reduce_fusion.2
  23.8 0.6 reshape_squeeze.9.ids
  24.4 4.1 %choose_blocks.4 = bf16[40,128,256]{2,1,0:T(8,128)(2,1)} custom-call(s32[1]{0:T(128)} %constant.95.clone.1.which, s32[40]{0:T(128)} %reshape_squeeze.9.ids, bf16[32,128,256]{2,1,0:T(8,128)(2,1)} %bitcast.20), custom_call_target="tpu_custom_call" | custom-call | flops 10000000000 | bytes 5242880 | tf_op jit(solution)/shard_map/choose_blocks/pallas_call | solution.py:41
  28.5 0.7 copy.44
  29.2 4.4 %all-to-all-start.1 = ((bf16[40,128,256]{2,1,0:T(8,128)(2,1)}), bf16[40,128,256]{2,1,0:T(8,128)(2,1)}, u32[]{:S(2)}, u32[]{:S(2)}) async-start(bf16[40,128,256]{2,1,0:T(8,128)(2,1)} %choose_blocks.4), calls=%async_computation.1 | async-start | bytes 5242880 | tf_op jit(solution)/shard_map/all_to_all | solution.py:255
  33.7 0.6 reshape_squeeze.11.ids
  34.3 18.8 %collective-permute-done = s32[8,192]{1,0:T(8,128)S(1)} collective-permute-done((s32[8,192]{1,0:T(8,128)S(1)}, s32[8,192]{1,0:T(8,128)S(1)}, u32[]{:S(2)}, u32[]{:S(2)}) %collective-permute-start) | collective-permute-done | bytes 6176 | tf_op jit(solution)/shard_map/ppermute | solution.py:261
  53.1 0.3 compare_reduce_fusion.1
  53.4 0.2 select_reduce_fusion.1
  53.6 0.2 select_reduce_fusion.3
  53.8 0.7 copy.45.b
  54.5 1.3 either_ids.1
  55.8 1.3 reshape.286.ids
  57.1 1.3 collective-permute-start.3
  58.3 2.0 %collective-permute-start.4 = (bf16[32,128,256]{2,1,0:T(8,128)(2,1)}, bf16[32,128,256]{2,1,0:T(8,128)(2,1)}, u32[]{:S(2)}, u32[]{:S(2)}) collective-permute-start(bf16[32,128,256]{2,1,0:T(8,128)(2,1)} %collective-permute-done.2.refs_1_), channel_id=1, source_target_pairs={{8,16},{9,17},{10,18},{11,19},{12,20},{13,21},{14,22},{15,23},{16,... | collective-permute-start | bytes 6291464 | tf_op jit(solution)/shard_map/ppermute | solution.py:261
  60.3 5.5 %all-to-all-done.1.refs_1_ = bf16[40,128,256]{2,1,0:T(8,128)(2,1)} async-done(((bf16[40,128,256]{2,1,0:T(8,128)(2,1)}), bf16[40,128,256]{2,1,0:T(8,128)(2,1)}, u32[]{:S(2)}, u32[]{:S(2)}) %all-to-all-start.1) | async-done | bytes 2621472 | tf_op jit(solution)/shard_map/all_to_all | solution.py:255
  65.8 4.1 %choose_blocks.5 = bf16[40,128,256]{2,1,0:T(8,128)(2,1)} custom-call(s32[1]{0:T(128)} %bitcast.which, s32[40]{0:T(128)} %reshape.286.ids, bf16[32,128,256]{2,1,0:T(8,128)(2,1)} %bitcast.21, bf16[32,128,256]{2,1,0:T(8,128)(2,1)} %collective-permute-done.1.refs_1_.refs_0_), custom_call_target="tpu_custom_call" | custom-call | flops 10000000000 | bytes 5242880 | tf_op jit(solution)/shard_map/choose_blocks/pallas_call | solution.py:41
  69.9 4.4 %all-to-all-start.2 = ((bf16[40,128,256]{2,1,0:T(8,128)(2,1)}), bf16[40,128,256]{2,1,0:T(8,128)(2,1)}, u32[]{:S(2)}, u32[]{:S(2)}) async-start(bf16[40,128,256]{2,1,0:T(8,128)(2,1)} %choose_blocks.5), calls=%async_computation.2 | async-start | bytes 5242880 | tf_op jit(solution)/shard_map/all_to_all | solution.py:255
  74.4 4.2 %choose_blocks.7 = bf16[40,128,256]{2,1,0:T(8,128)(2,1)} custom-call(s32[1]{0:T(128)} %bitcast.6.which, s32[40]{0:T(128)} %reshape_squeeze.11.ids, bf16[32,128,256]{2,1,0:T(8,128)(2,1)} %collective-permute-done.1.refs_1_.refs_0_, bf16[32,128,256]{2,1,0:T(8,128)(2,1)} %collective-permute-done.2.refs_1_), custom_call_target="tpu_custom_call" | custom-call | flops 30000001024 | bytes 5242880 | tf_op jit(solution)/shard_map/choose_blocks/pallas_call | solution.py:41
  78.5 28.1 %all-to-all-done.2.refs_2_ = bf16[40,128,256]{2,1,0:T(8,128)(2,1)} async-done(((bf16[40,128,256]{2,1,0:T(8,128)(2,1)}), bf16[40,128,256]{2,1,0:T(8,128)(2,1)}, u32[]{:S(2)}, u32[]{:S(2)}) %all-to-all-start.2) | async-done | bytes 2621472 | tf_op jit(solution)/shard_map/all_to_all | solution.py:255
  106.6 4.4 %all-to-all-start.4 = ((bf16[40,128,256]{2,1,0:T(8,128)(2,1)}), bf16[40,128,256]{2,1,0:T(8,128)(2,1)}, u32[]{:S(2)}, u32[]{:S(2)}) async-start(bf16[40,128,256]{2,1,0:T(8,128)(2,1)} %choose_blocks.7), calls=%async_computation.4 | async-start | bytes 5242880 | tf_op jit(solution)/shard_map/all_to_all | solution.py:255
  111.2 0.1 and.140
  111.3 0.1 eq.209
  111.4 0.2 fusion.1
  111.6 0.2 convert_reduce_fusion
  111.9 0.7 convert_reduce_fusion.1
  112.6 0.2 reduce_window_sum.11
  112.9 0.7 reshape_squeeze.10.ids
  113.5 4.3 %collective-permute-start.5 = (bf16[40,128,256]{2,1,0:T(8,128)(2,1)}, bf16[40,128,256]{2,1,0:T(8,128)(2,1)}, u32[]{:S(2)}, u32[]{:S(2)}) collective-permute-start(bf16[40,128,256]{2,1,0:T(8,128)(2,1)} %all-to-all-done.2.refs_2_), channel_id=1, source_target_pairs={{0,24},{1,25},{2,26},{3,27},{4,28},{5,29},{6,30},{7,31},{24,0},{25... | collective-permute-start | bytes 7864328 | tf_op jit(solution)/shard_map/ppermute | solution.py:261
  117.8 4.2 %choose_blocks.6 = bf16[40,128,256]{2,1,0:T(8,128)(2,1)} custom-call(s32[1]{0:T(128)} %bitcast.5.which, s32[40]{0:T(128)} %reshape_squeeze.10.ids, bf16[32,128,256]{2,1,0:T(8,128)(2,1)} %collective-permute-done.3.refs_0_, bf16[32,128,256]{2,1,0:T(8,128)(2,1)} %collective-permute-done.4.refs_1_), custom_call_target="tpu_custom_call" | custom-call | flops 10000000000 | bytes 5242880 | tf_op jit(solution)/shard_map/choose_blocks/pallas_call | solution.py:41
  122.0 21.3 %all-to-all-done.4.refs_3_ = bf16[40,128,256]{2,1,0:T(8,128)(2,1)} async-done(((bf16[40,128,256]{2,1,0:T(8,128)(2,1)}), bf16[40,128,256]{2,1,0:T(8,128)(2,1)}, u32[]{:S(2)}, u32[]{:S(2)}) %all-to-all-start.4) | async-done | bytes 2621472 | tf_op jit(solution)/shard_map/all_to_all | solution.py:255
  143.3 4.4 %all-to-all-start.3 = ((bf16[40,128,256]{2,1,0:T(8,128)(2,1)}), bf16[40,128,256]{2,1,0:T(8,128)(2,1)}, u32[]{:S(2)}, u32[]{:S(2)}) async-start(bf16[40,128,256]{2,1,0:T(8,128)(2,1)} %choose_blocks.6), calls=%async_computation.3 | async-start | bytes 5242880 | tf_op jit(solution)/shard_map/all_to_all | solution.py:255
  148.1 0.6 reshape.287.late
  148.8 0.6 reshape.284.slots
  149.4 0.6 compare_select_fusion.slots
  150.0 15.0 %early_sums.1 = (f32[4096,256]{1,0:T(8,128)}, s8[32,128,512]{2,1,0:T(32,128)(4,1)}) custom-call(s32[192]{0:T(256)} %compare_select_fusion.slots, s32[128]{0:T(128)} %reshape.287.late, s32[32]{0:T(128)} %get-tuple-element.21.counts, bf16[32,128,256]{2,1,0:T(8,128)(2,1)} %bitcast.22, bf16[40,128,256]{2,1,0:T(8,128)(2,1)} %all-to-all-done.1.refs_1_, ...), custom_call_target="tpu_custom_call" | custom-call | flops 20000000000 | bytes 28901376 | tf_op jit(solution)/shard_map/early_sums/pallas_call | solution.py:123
  165.0 14.9 %all-to-all-done.3.refs_1_ = bf16[40,128,256]{2,1,0:T(8,128)(2,1)} async-done(((bf16[40,128,256]{2,1,0:T(8,128)(2,1)}), bf16[40,128,256]{2,1,0:T(8,128)(2,1)}, u32[]{:S(2)}, u32[]{:S(2)}) %all-to-all-start.3) | async-done | bytes 2621472 | tf_op jit(solution)/shard_map/all_to_all | solution.py:255
  180.0 13.2 %sage_layer.1 = bf16[4096,256]{1,0:T(8,128)(2,1)} custom-call(s32[128]{0:T(128)} %reshape.284.slots, s32[32]{0:T(128)} %get-tuple-element.21.counts, bf16[40,128,256]{2,1,0:T(8,128)(2,1)} %collective-permute-done.5.refs_0_, bf16[40,128,256]{2,1,0:T(8,128)(2,1)} %all-to-all-done.3.refs_1_, f32[4096,256]{1,0:T(8,128)} %get-tuple-element.15.refs_2_, ...), custom_call_target="tpu_custom_call" | custom-call | flops 2147483648 | bytes 10485760 | tf_op jit(solution)/shard_map/sage_layer/pallas_call | solution.py:208
  (33 shorter events, 1.2 us)
Async XLA Ops:
  0.0 53.1 %collective-permute-start.1 = (bf16[32,128,256]{2,1,0:T(8,128)(2,1)}, bf16[32,128,256]{2,1,0:T(8,128)(2,1)}, u32[]{:S(2)}, u32[]{:S(2)}) collective-permute-start(bf16[32,128,256]{2,1,0:T(8,128)(2,1)} %bitcast.18), channel_id=1, source_target_pairs={{8,0},{9,1},{10,2},{11,3},{12,4},{13,5},{14,6},{15,7},{16,8},{17,9... | collective-permute-start | bytes 6291464 | tf_op jit(solution)/shard_map/ppermute | solution.py:261
  1.3 51.8 %collective-permute-start.2 = (bf16[32,128,256]{2,1,0:T(8,128)(2,1)}, bf16[32,128,256]{2,1,0:T(8,128)(2,1)}, u32[]{:S(2)}, u32[]{:S(2)}) collective-permute-start(bf16[32,128,256]{2,1,0:T(8,128)(2,1)} %bitcast.19), channel_id=1, source_target_pairs={{0,8},{1,9},{2,10},{3,11},{4,12},{5,13},{6,14},{7,15},{8,16},{9,17... | collective-permute-start | bytes 6291464 | tf_op jit(solution)/shard_map/ppermute | solution.py:261
  9.7 8.9 %all-to-all-start = ((s32[8,1,192]{2,1,0:T(1,128)}), s32[8,1,192]{2,1,0:T(1,128)S(1)}, u32[]{:S(2)}, u32[]{:S(2)}) async-start(s32[8,1,192]{2,1,0:T(1,128)} %broadcast_in_dim.156), calls=%async_computation | async-start | bytes 16384 | tf_op jit(solution)/shard_map/all_to_all | solution.py:255
  18.5 34.6 %collective-permute-start = (s32[8,192]{1,0:T(8,128)S(1)}, s32[8,192]{1,0:T(8,128)S(1)}, u32[]{:S(2)}, u32[]{:S(2)}) collective-permute-start(s32[8,192]{1,0:T(8,128)S(1)} %bitcast.23), channel_id=1, source_target_pairs={{0,24},{1,25},{2,26},{3,27},{4,28},{5,29},{6,30},{7,31},{24,0},{25... | collective-permute-start | bytes 18440 | tf_op jit(solution)/shard_map/ppermute | solution.py:261
  29.2 36.7 %all-to-all-start.1 = ((bf16[40,128,256]{2,1,0:T(8,128)(2,1)}), bf16[40,128,256]{2,1,0:T(8,128)(2,1)}, u32[]{:S(2)}, u32[]{:S(2)}) async-start(bf16[40,128,256]{2,1,0:T(8,128)(2,1)} %choose_blocks.4), calls=%async_computation.1 | async-start | bytes 5242880 | tf_op jit(solution)/shard_map/all_to_all | solution.py:255
  57.1 56.5 %collective-permute-start.3 = (bf16[32,128,256]{2,1,0:T(8,128)(2,1)}, bf16[32,128,256]{2,1,0:T(8,128)(2,1)}, u32[]{:S(2)}, u32[]{:S(2)}) collective-permute-start(bf16[32,128,256]{2,1,0:T(8,128)(2,1)} %collective-permute-done.1.refs_1_.refs_0_), channel_id=1, source_target_pairs={{8,0},{9,1},{10,2},{11,3},{12,4},{13,5},{14,6},{15,7},{16,8},{17,9... | collective-permute-start | bytes 6291464 | tf_op jit(solution)/shard_map/ppermute | solution.py:261
  58.3 55.2 %collective-permute-start.4 = (bf16[32,128,256]{2,1,0:T(8,128)(2,1)}, bf16[32,128,256]{2,1,0:T(8,128)(2,1)}, u32[]{:S(2)}, u32[]{:S(2)}) collective-permute-start(bf16[32,128,256]{2,1,0:T(8,128)(2,1)} %collective-permute-done.2.refs_1_), channel_id=1, source_target_pairs={{8,16},{9,17},{10,18},{11,19},{12,20},{13,21},{14,22},{15,23},{16,... | collective-permute-start | bytes 6291464 | tf_op jit(solution)/shard_map/ppermute | solution.py:261
  69.9 36.7 %all-to-all-start.2 = ((bf16[40,128,256]{2,1,0:T(8,128)(2,1)}), bf16[40,128,256]{2,1,0:T(8,128)(2,1)}, u32[]{:S(2)}, u32[]{:S(2)}) async-start(bf16[40,128,256]{2,1,0:T(8,128)(2,1)} %choose_blocks.5), calls=%async_computation.2 | async-start | bytes 5242880 | tf_op jit(solution)/shard_map/all_to_all | solution.py:255
  106.6 36.7 %all-to-all-start.4 = ((bf16[40,128,256]{2,1,0:T(8,128)(2,1)}), bf16[40,128,256]{2,1,0:T(8,128)(2,1)}, u32[]{:S(2)}, u32[]{:S(2)}) async-start(bf16[40,128,256]{2,1,0:T(8,128)(2,1)} %choose_blocks.7), calls=%async_computation.4 | async-start | bytes 5242880 | tf_op jit(solution)/shard_map/all_to_all | solution.py:255
  113.5 66.4 %collective-permute-start.5 = (bf16[40,128,256]{2,1,0:T(8,128)(2,1)}, bf16[40,128,256]{2,1,0:T(8,128)(2,1)}, u32[]{:S(2)}, u32[]{:S(2)}) collective-permute-start(bf16[40,128,256]{2,1,0:T(8,128)(2,1)} %all-to-all-done.2.refs_2_), channel_id=1, source_target_pairs={{0,24},{1,25},{2,26},{3,27},{4,28},{5,29},{6,30},{7,31},{24,0},{25... | collective-permute-start | bytes 7864328 | tf_op jit(solution)/shard_map/ppermute | solution.py:261
  143.3 36.7 %all-to-all-start.3 = ((bf16[40,128,256]{2,1,0:T(8,128)(2,1)}), bf16[40,128,256]{2,1,0:T(8,128)(2,1)}, u32[]{:S(2)}, u32[]{:S(2)}) async-start(bf16[40,128,256]{2,1,0:T(8,128)(2,1)} %choose_blocks.6), calls=%async_computation.3 | async-start | bytes 5242880 | tf_op jit(solution)/shard_map/all_to_all | solution.py:255

commit v9 on v8

--- a/solution.py
+++ b/solution.py
@@ -21,13 +21,14 @@
 
 def choose_kernel(which, ids, *refs):
     *froms, out, held, in_sem, out_sem = refs
-    count = out.shape[0]
+    count, seats = out.shape[0], ids.shape[1]
     for j, source in enumerate(froms):
 
         @pl.when(which[0] == j)
         def _():
             for n in range(count):
-                pltpu.make_async_copy(source.at[ids[n]], held.at[n], in_sem).start()
+                block = source.at[ids[n // seats, n % seats]]
+                pltpu.make_async_copy(block, held.at[n], in_sem).start()
 
     pltpu.make_async_copy(out, held, in_sem).wait()
     leaving = pltpu.make_async_copy(held, out, out_sem)
@@ -36,7 +37,7 @@
 
 
 def choose(which, ids, froms, flops):
-    out = (ids.shape[0],) + froms[0].shape[1:]
+    out = (ids.shape[0] * ids.shape[1],) + froms[0].shape[1:]
     moved = out[0] * out[1] * out[2] * 2
     return pl.pallas_call(
         choose_kernel,
@@ -151,7 +152,7 @@
 
 
 def layer_kernel(slots, counts, *refs):
-    *froms, sums, left, degree, features, weight, out, table, totals, sems = refs
+    *froms, sums, left, degree, features, weight, out, table, totals, share, sems = refs
     step = pl.program_id(0)
     rows, tile = left.shape[:2]
     width = table.shape[2]
@@ -177,19 +178,26 @@
             def _():
                 totals[here, :] += added(r, first)
 
-    across = lax.broadcasted_iota(jnp.int32, (tile, tile), 1)
-    diagonal = lax.broadcasted_iota(jnp.int32, (tile, tile), 0) == across
-    ones = jnp.ones((2 * tile, tile), jnp.bfloat16)
+    column = lax.broadcasted_iota(jnp.int32, (tile, tile), 1)
+    diagonal = lax.broadcasted_iota(jnp.int32, (tile, tile), 0) == column
+    spread = []
     for r in range(rows):
-        here = pl.ds(r * tile, tile)
         count = degree[pl.ds(step * rows + r, 1), :]
         small = count & 7
         halves = [
             jnp.where(diagonal, part.astype(jnp.float32), 0.0).astype(jnp.bfloat16)
             for part in (count - small, small)
         ]
-        count = jnp.dot(jnp.concatenate(halves, axis=1), ones, preferred_element_type=jnp.float32)
-        part = jnp.concatenate([1.0 / count] * (width // tile), axis=1)
+        spread.append(jnp.concatenate(halves, axis=1))
+    ones = jnp.ones((2 * tile, tile), jnp.bfloat16)
+    share[...] = 1.0 / jnp.dot(
+        jnp.concatenate(spread, axis=0), ones, preferred_element_type=jnp.float32
+    )
+
+    many = min(rows, 4) * tile
+    for first in range(0, rows * tile, many):
+        here = pl.ds(first, many)
+        part = jnp.concatenate([share[here, :]] * (width // tile), axis=1)
         mean = (totals[here, :] * part).astype(jnp.bfloat16)
         joined = jnp.concatenate([features[here, :], mean], axis=1)
         hidden = jnp.dot(joined, weight[...], preferred_element_type=jnp.float32)
@@ -222,6 +230,7 @@
             scratch_shapes=[
                 pltpu.VMEM((blocks_in_table, tile, width), jnp.bfloat16),
                 pltpu.VMEM((items, width), jnp.float32),
+                pltpu.VMEM((items, tile), jnp.float32),
                 pltpu.SemaphoreType.DMA((len(froms),)),
             ],
         ),
@@ -280,7 +289,7 @@
         return jnp.sum(jnp.where(taken, blocks, 0), axis=3)
 
     near = seated(asked, wanted)
-    ids = [near[:, k, :].reshape(-1) for k in range(PLANES)]
+    ids = [near[:, k, :] for k in range(PLANES)]
 
     owners, within = columns // blocks_here, columns % blocks_here
     positions = jnp.arange(columns.shape[0], dtype=jnp.int32)
@@ -315,10 +324,10 @@
     got = [exchange(picked)]
     across, _, _ = lax.optimization_barrier((across, from_above, from_below))
     opposite = seated(across, wanted[:1])[:, 0, :]
-    ids[1] = either(end.astype(jnp.int32)[None], near[:, 1, :], opposite).reshape(-1)
-    ids[1], _ = lax.optimization_barrier((ids[1], got[0]))
+    ids[1] = either(end.astype(jnp.int32)[None], near[:, 1, :], opposite)
     picked = choose(inner, ids[1], [local, from_above], LIGHT)
-    got.append(exchange(picked))
+    leaving, _ = lax.optimization_barrier((picked, got[0]))
+    got.append(exchange(leaving))
     second_down = shift(from_above, down[:-1])
     second_up = shift(from_below, up[1:])
     leaving, _, _ = lax.optimization_barrier((got[1], second_down, second_up))

time: 195 us -> 192 us (0.985)
    ppermute x6, waiting for transfers between devices: 18.9 us -> 21.4 us  [shift(): return lax.ppermute(x, 'rows', pairs)]
    all_to_all x5, waiting for transfers between devices: 73.7 us -> 71.2 us  [exchange(): lax.all_to_all(x, 'rows', split_axis=0, concat_axis=0, axis_index_groups=...]
  transfers between devices with their start and end apart: 11 -> 11, of which waited for: 6 -> 7; matrix products, arithmetic and copies ran while one was open for 7% -> 6% of each run, Pallas kernels for 17% -> 17%
where the time goes in v9:
time: 192 us; the launch traced here: 191 us
  waiting for transfers between devices  92.7 us (48%)
  Pallas kernels  44.8 us (23%)
  starting transfers between devices  40.7 us (21%)
  local copies, waits for them, and re-layouts  6.89 us (4%)
  other arithmetic  5.35 us (3%)
    all_to_all x5, waiting for transfers between devices, exchange(): lax.all_to_all(x, 'rows', split_axis=0, concat_axis=0, axis_index_groups=...  71.2 us
    ppermute x6, waiting for transfers between devices, shift(): return lax.ppermute(x, 'rows', pairs)  21.4 us
    all_to_all x5, starting transfers between devices, exchange(): lax.all_to_all(x, 'rows', split_axis=0, concat_axis=0, axis_index_groups=...  21.3 us
    ppermute x6, starting transfers between devices, shift(): return lax.ppermute(x, 'rows', pairs)  19.3 us
    pallas_call x4, Pallas kernels, choose(): pl.pallas_call(choose_kernel, grid_spec=pltpu.PrefetchScalarGridSpec(num_...  16.7 us
    pallas_call x1, Pallas kernels, early(): pl.pallas_call(early_kernel, grid_spec=pltpu.PrefetchScalarGridSpec(num_s...  15 us
    pallas_call x1, Pallas kernels, layer(): pl.pallas_call(layer_kernel, grid_spec=pltpu.PrefetchScalarGridSpec(num_s...  11.8 us
  transfers between devices with their start and end apart: 11, of which 7 were waited for; matrix products, arithmetic and copies ran while one was open for 6% of the time, Pallas kernels for 17%

profile of v9, /device:TPU:0, one launch (start us, length us, event | category | flops | bytes accessed | tf_op | source)
XLA Modules:
  0.0 190.6 jit_solution(4066097547204608752)
XLA Ops:
  0.0 6.3 %collective-permute-start.2 = (bf16[32,128,256]{2,1,0:T(8,128)(2,1)}, bf16[32,128,256]{2,1,0:T(8,128)(2,1)}, u32[]{:S(2)}, u32[]{:S(2)}) collective-permute-start(bf16[32,128,256]{2,1,0:T(8,128)(2,1)} %bitcast.15), channel_id=1, source_target_pairs={{0,8},{1,9},{2,10},{3,11},{4,12},{5,13},{6,14},{7,15},{8,16},{9,17... | collective-permute-start | bytes 6291464 | tf_op jit(solution)/shard_map/ppermute | solution.py:270
  6.3 1.3 collective-permute-start.1
  7.6 0.8 copy.33
  8.4 0.6 broadcast_in_dim.156
  9.0 3.7 %all-to-all-start = ((s32[8,1,192]{2,1,0:T(1,128)}), s32[8,1,192]{2,1,0:T(1,128)S(1)}, u32[]{:S(2)}, u32[]{:S(2)}) async-start(s32[8,1,192]{2,1,0:T(1,128)} %broadcast_in_dim.156), calls=%async_computation | async-start | bytes 16384 | tf_op jit(solution)/shard_map/all_to_all | solution.py:264
  12.8 0.8 select_reduce_fusion.7
  13.7 3.8 %all-to-all-done = s32[8,1,192]{2,1,0:T(1,128)S(1)} async-done(((s32[8,1,192]{2,1,0:T(1,128)}), s32[8,1,192]{2,1,0:T(1,128)S(1)}, u32[]{:S(2)}, u32[]{:S(2)}) %all-to-all-start) | async-done | bytes 6176 | tf_op jit(solution)/shard_map/all_to_all | solution.py:264
  17.5 6.6 %collective-permute-start = (s32[8,192]{1,0:T(8,128)S(1)}, s32[8,192]{1,0:T(8,128)S(1)}, u32[]{:S(2)}, u32[]{:S(2)}) collective-permute-start(s32[8,192]{1,0:T(8,128)S(1)} %bitcast.20), channel_id=1, source_target_pairs={{0,24},{1,25},{2,26},{3,27},{4,28},{5,29},{6,30},{7,31},{24,0},{25... | collective-permute-start | bytes 18440 | tf_op jit(solution)/shard_map/ppermute | solution.py:270
  24.1 0.7 compare_reduce_fusion
  24.9 0.6 select_reduce_fusion
  25.5 0.4 select_reduce_fusion.2
  25.9 0.7 copy.46
  26.6 4.2 %choose_blocks.5 = bf16[40,128,256]{2,1,0:T(8,128)(2,1)} custom-call(s32[1]{0:T(128)} %constant.95.clone.1.which, s32[8,5]{1,0:T(8,128)} %bitcast.26, bf16[32,128,256]{2,1,0:T(8,128)(2,1)} %bitcast.17), custom_call_target="tpu_custom_call" | custom-call | flops 10000000000 | bytes 5242880 | tf_op jit(solution)/shard_map/choose_blocks/pallas_call | solution.py:42
  30.8 0.7 copy.49
  31.4 0.7 copy.44
  32.1 4.4 %all-to-all-start.1 = ((bf16[40,128,256]{2,1,0:T(8,128)(2,1)}), bf16[40,128,256]{2,1,0:T(8,128)(2,1)}, u32[]{:S(2)}, u32[]{:S(2)}) async-start(bf16[40,128,256]{2,1,0:T(8,128)(2,1)} %choose_blocks.5), calls=%async_computation.1 | async-start | bytes 5242880 | tf_op jit(solution)/shard_map/all_to_all | solution.py:264
  36.5 19.8 %collective-permute-done = s32[8,192]{1,0:T(8,128)S(1)} collective-permute-done((s32[8,192]{1,0:T(8,128)S(1)}, s32[8,192]{1,0:T(8,128)S(1)}, u32[]{:S(2)}, u32[]{:S(2)}) %collective-permute-start) | collective-permute-done | bytes 6176 | tf_op jit(solution)/shard_map/ppermute | solution.py:270
  56.3 0.3 compare_reduce_fusion.1
  56.6 0.2 select_reduce_fusion.1
  56.9 0.2 select_reduce_fusion.3
  57.0 0.7 copy.45.b
  57.7 1.3 either_ids.1.ids
  59.0 4.2 %choose_blocks.4 = bf16[40,128,256]{2,1,0:T(8,128)(2,1)} custom-call(s32[1]{0:T(128)} %bitcast.which, s32[8,5]{1,0:T(8,128)} %either_ids.1.ids, bf16[32,128,256]{2,1,0:T(8,128)(2,1)} %bitcast.18, bf16[32,128,256]{2,1,0:T(8,128)(2,1)} %collective-permute-done.1.refs_1_.refs_0_), custom_call_target="tpu_custom_call" | custom-call | flops 10000000000 | bytes 5242880 | tf_op jit(solution)/shard_map/choose_blocks/pallas_call | solution.py:42
  63.2 2.0 %collective-permute-start.4 = (bf16[32,128,256]{2,1,0:T(8,128)(2,1)}, bf16[32,128,256]{2,1,0:T(8,128)(2,1)}, u32[]{:S(2)}, u32[]{:S(2)}) collective-permute-start(bf16[32,128,256]{2,1,0:T(8,128)(2,1)} %collective-permute-done.2.refs_1_), channel_id=1, source_target_pairs={{8,16},{9,17},{10,18},{11,19},{12,20},{13,21},{14,22},{15,23},{16,... | collective-permute-start | bytes 6291464 | tf_op jit(solution)/shard_map/ppermute | solution.py:270
  65.2 1.3 collective-permute-start.3
  66.4 2.3 %all-to-all-done.1.refs_1_ = bf16[40,128,256]{2,1,0:T(8,128)(2,1)} async-done(((bf16[40,128,256]{2,1,0:T(8,128)(2,1)}), bf16[40,128,256]{2,1,0:T(8,128)(2,1)}, u32[]{:S(2)}, u32[]{:S(2)}) %all-to-all-start.1) | async-done | bytes 2621472 | tf_op jit(solution)/shard_map/all_to_all | solution.py:264
  68.8 4.4 %all-to-all-start.2 = ((bf16[40,128,256]{2,1,0:T(8,128)(2,1)}), bf16[40,128,256]{2,1,0:T(8,128)(2,1)}, u32[]{:S(2)}, u32[]{:S(2)}) async-start(bf16[40,128,256]{2,1,0:T(8,128)(2,1)} %choose_blocks.4), calls=%async_computation.2 | async-start | bytes 5242880 | tf_op jit(solution)/shard_map/all_to_all | solution.py:264
  73.2 4.2 %choose_blocks.7 = bf16[40,128,256]{2,1,0:T(8,128)(2,1)} custom-call(s32[1]{0:T(128)} %bitcast.8.which, s32[8,5]{1,0:T(8,128)} %bitcast.23, bf16[32,128,256]{2,1,0:T(8,128)(2,1)} %collective-permute-done.1.refs_1_.refs_0_, bf16[32,128,256]{2,1,0:T(8,128)(2,1)} %collective-permute-done.2.refs_1_), custom_call_target="tpu_custom_call" | custom-call | flops 30000001024 | bytes 5242880 | tf_op jit(solution)/shard_map/choose_blocks/pallas_call | solution.py:42
  77.4 28.0 %all-to-all-done.2.refs_2_ = bf16[40,128,256]{2,1,0:T(8,128)(2,1)} async-done(((bf16[40,128,256]{2,1,0:T(8,128)(2,1)}), bf16[40,128,256]{2,1,0:T(8,128)(2,1)}, u32[]{:S(2)}, u32[]{:S(2)}) %all-to-all-start.2) | async-done | bytes 2621472 | tf_op jit(solution)/shard_map/all_to_all | solution.py:264
  105.5 4.4 %all-to-all-start.4 = ((bf16[40,128,256]{2,1,0:T(8,128)(2,1)}), bf16[40,128,256]{2,1,0:T(8,128)(2,1)}, u32[]{:S(2)}, u32[]{:S(2)}) async-start(bf16[40,128,256]{2,1,0:T(8,128)(2,1)} %choose_blocks.7), calls=%async_computation.4 | async-start | bytes 5242880 | tf_op jit(solution)/shard_map/all_to_all | solution.py:264
  109.9 0.2 fusion.1
  110.2 0.1 and.140
  110.3 0.1 eq.209
  110.4 0.2 convert_reduce_fusion
  110.8 0.7 convert_reduce_fusion.1
  111.5 0.2 reduce_window_sum.11
  111.6 0.7 copy.47
  112.3 1.6 collective-permute-done.3.refs_0_
  113.9 1.9 %collective-permute-start.5 = (bf16[40,128,256]{2,1,0:T(8,128)(2,1)}, bf16[40,128,256]{2,1,0:T(8,128)(2,1)}, u32[]{:S(2)}, u32[]{:S(2)}) collective-permute-start(bf16[40,128,256]{2,1,0:T(8,128)(2,1)} %all-to-all-done.2.refs_2_), channel_id=1, source_target_pairs={{0,24},{1,25},{2,26},{3,27},{4,28},{5,29},{6,30},{7,31},{24,0},{25... | collective-permute-start | bytes 7864328 | tf_op jit(solution)/shard_map/ppermute | solution.py:270
  115.9 4.2 %choose_blocks.6 = bf16[40,128,256]{2,1,0:T(8,128)(2,1)} custom-call(s32[1]{0:T(128)} %bitcast.6.which, s32[8,5]{1,0:T(8,128)} %bitcast.25, bf16[32,128,256]{2,1,0:T(8,128)(2,1)} %collective-permute-done.3.refs_0_, bf16[32,128,256]{2,1,0:T(8,128)(2,1)} %collective-permute-done.4.refs_1_), custom_call_target="tpu_custom_call" | custom-call | flops 10000000000 | bytes 5242880 | tf_op jit(solution)/shard_map/choose_blocks/pallas_call | solution.py:42
  120.1 22.1 %all-to-all-done.4.refs_3_ = bf16[40,128,256]{2,1,0:T(8,128)(2,1)} async-done(((bf16[40,128,256]{2,1,0:T(8,128)(2,1)}), bf16[40,128,256]{2,1,0:T(8,128)(2,1)}, u32[]{:S(2)}, u32[]{:S(2)}) %all-to-all-start.4) | async-done | bytes 2621472 | tf_op jit(solution)/shard_map/all_to_all | solution.py:264
  142.2 4.4 %all-to-all-start.3 = ((bf16[40,128,256]{2,1,0:T(8,128)(2,1)}), bf16[40,128,256]{2,1,0:T(8,128)(2,1)}, u32[]{:S(2)}, u32[]{:S(2)}) async-start(bf16[40,128,256]{2,1,0:T(8,128)(2,1)} %choose_blocks.6), calls=%async_computation.3 | async-start | bytes 5242880 | tf_op jit(solution)/shard_map/all_to_all | solution.py:264
  146.9 0.6 reshape.283.late
  147.6 0.6 reshape.281.slots
  148.3 0.6 compare_select_fusion.slots
  148.9 15.0 %early_sums.1 = (f32[4096,256]{1,0:T(8,128)}, s8[32,128,512]{2,1,0:T(32,128)(4,1)}) custom-call(s32[192]{0:T(256)} %compare_select_fusion.slots, s32[128]{0:T(128)} %reshape.283.late, s32[32]{0:T(128)} %get-tuple-element.21.counts, bf16[32,128,256]{2,1,0:T(8,128)(2,1)} %bitcast.19, bf16[40,128,256]{2,1,0:T(8,128)(2,1)} %all-to-all-done.1.refs_1_, ...), custom_call_target="tpu_custom_call" | custom-call | flops 20000000000 | bytes 28901376 | tf_op jit(solution)/shard_map/early_sums/pallas_call | solution.py:124
  163.9 15.0 %all-to-all-done.3.refs_1_ = bf16[40,128,256]{2,1,0:T(8,128)(2,1)} async-done(((bf16[40,128,256]{2,1,0:T(8,128)(2,1)}), bf16[40,128,256]{2,1,0:T(8,128)(2,1)}, u32[]{:S(2)}, u32[]{:S(2)}) %all-to-all-start.3) | async-done | bytes 2621472 | tf_op jit(solution)/shard_map/all_to_all | solution.py:264
  178.8 11.8 %sage_layer.1 = bf16[4096,256]{1,0:T(8,128)(2,1)} custom-call(s32[128]{0:T(128)} %reshape.281.slots, s32[32]{0:T(128)} %get-tuple-element.21.counts, bf16[40,128,256]{2,1,0:T(8,128)(2,1)} %collective-permute-done.5.refs_0_, bf16[40,128,256]{2,1,0:T(8,128)(2,1)} %all-to-all-done.3.refs_1_, f32[4096,256]{1,0:T(8,128)} %get-tuple-element.15.refs_2_, ...), custom_call_target="tpu_custom_call" | custom-call | flops 2147483648 | bytes 10485760 | tf_op jit(solution)/shard_map/sage_layer/pallas_call | solution.py:216
  (29 shorter events, 0.9 us)
Async XLA Ops:
  0.0 56.3 %collective-permute-start.2 = (bf16[32,128,256]{2,1,0:T(8,128)(2,1)}, bf16[32,128,256]{2,1,0:T(8,128)(2,1)}, u32[]{:S(2)}, u32[]{:S(2)}) collective-permute-start(bf16[32,128,256]{2,1,0:T(8,128)(2,1)} %bitcast.15), channel_id=1, source_target_pairs={{0,8},{1,9},{2,10},{3,11},{4,12},{5,13},{6,14},{7,15},{8,16},{9,17... | collective-permute-start | bytes 6291464 | tf_op jit(solution)/shard_map/ppermute | solution.py:270
  6.3 50.1 %collective-permute-start.1 = (bf16[32,128,256]{2,1,0:T(8,128)(2,1)}, bf16[32,128,256]{2,1,0:T(8,128)(2,1)}, u32[]{:S(2)}, u32[]{:S(2)}) collective-permute-start(bf16[32,128,256]{2,1,0:T(8,128)(2,1)} %bitcast.16), channel_id=1, source_target_pairs={{8,0},{9,1},{10,2},{11,3},{12,4},{13,5},{14,6},{15,7},{16,8},{17,9... | collective-permute-start | bytes 6291464 | tf_op jit(solution)/shard_map/ppermute | solution.py:270
  9.0 8.4 %all-to-all-start = ((s32[8,1,192]{2,1,0:T(1,128)}), s32[8,1,192]{2,1,0:T(1,128)S(1)}, u32[]{:S(2)}, u32[]{:S(2)}) async-start(s32[8,1,192]{2,1,0:T(1,128)} %broadcast_in_dim.156), calls=%async_computation | async-start | bytes 16384 | tf_op jit(solution)/shard_map/all_to_all | solution.py:264
  17.5 38.9 %collective-permute-start = (s32[8,192]{1,0:T(8,128)S(1)}, s32[8,192]{1,0:T(8,128)S(1)}, u32[]{:S(2)}, u32[]{:S(2)}) collective-permute-start(s32[8,192]{1,0:T(8,128)S(1)} %bitcast.20), channel_id=1, source_target_pairs={{0,24},{1,25},{2,26},{3,27},{4,28},{5,29},{6,30},{7,31},{24,0},{25... | collective-permute-start | bytes 18440 | tf_op jit(solution)/shard_map/ppermute | solution.py:270
  32.1 36.7 %all-to-all-start.1 = ((bf16[40,128,256]{2,1,0:T(8,128)(2,1)}), bf16[40,128,256]{2,1,0:T(8,128)(2,1)}, u32[]{:S(2)}, u32[]{:S(2)}) async-start(bf16[40,128,256]{2,1,0:T(8,128)(2,1)} %choose_blocks.5), calls=%async_computation.1 | async-start | bytes 5242880 | tf_op jit(solution)/shard_map/all_to_all | solution.py:264
  63.2 49.1 %collective-permute-start.4 = (bf16[32,128,256]{2,1,0:T(8,128)(2,1)}, bf16[32,128,256]{2,1,0:T(8,128)(2,1)}, u32[]{:S(2)}, u32[]{:S(2)}) collective-permute-start(bf16[32,128,256]{2,1,0:T(8,128)(2,1)} %collective-permute-done.2.refs_1_), channel_id=1, source_target_pairs={{8,16},{9,17},{10,18},{11,19},{12,20},{13,21},{14,22},{15,23},{16,... | collective-permute-start | bytes 6291464 | tf_op jit(solution)/shard_map/ppermute | solution.py:270
  65.2 48.8 %collective-permute-start.3 = (bf16[32,128,256]{2,1,0:T(8,128)(2,1)}, bf16[32,128,256]{2,1,0:T(8,128)(2,1)}, u32[]{:S(2)}, u32[]{:S(2)}) collective-permute-start(bf16[32,128,256]{2,1,0:T(8,128)(2,1)} %collective-permute-done.1.refs_1_.refs_0_), channel_id=1, source_target_pairs={{8,0},{9,1},{10,2},{11,3},{12,4},{13,5},{14,6},{15,7},{16,8},{17,9... | collective-permute-start | bytes 6291464 | tf_op jit(solution)/shard_map/ppermute | solution.py:270
  68.8 36.7 %all-to-all-start.2 = ((bf16[40,128,256]{2,1,0:T(8,128)(2,1)}), bf16[40,128,256]{2,1,0:T(8,128)(2,1)}, u32[]{:S(2)}, u32[]{:S(2)}) async-start(bf16[40,128,256]{2,1,0:T(8,128)(2,1)} %choose_blocks.4), calls=%async_computation.2 | async-start | bytes 5242880 | tf_op jit(solution)/shard_map/all_to_all | solution.py:264
  105.5 36.7 %all-to-all-start.4 = ((bf16[40,128,256]{2,1,0:T(8,128)(2,1)}), bf16[40,128,256]{2,1,0:T(8,128)(2,1)}, u32[]{:S(2)}, u32[]{:S(2)}) async-start(bf16[40,128,256]{2,1,0:T(8,128)(2,1)} %choose_blocks.7), calls=%async_computation.4 | async-start | bytes 5242880 | tf_op jit(solution)/shard_map/all_to_all | solution.py:264
  113.9 64.9 %collective-permute-start.5 = (bf16[40,128,256]{2,1,0:T(8,128)(2,1)}, bf16[40,128,256]{2,1,0:T(8,128)(2,1)}, u32[]{:S(2)}, u32[]{:S(2)}) collective-permute-start(bf16[40,128,256]{2,1,0:T(8,128)(2,1)} %all-to-all-done.2.refs_2_), channel_id=1, source_target_pairs={{0,24},{1,25},{2,26},{3,27},{4,28},{5,29},{6,30},{7,31},{24,0},{25... | collective-permute-start | bytes 7864328 | tf_op jit(solution)/shard_map/ppermute | solution.py:270
  142.2 36.7 %all-to-all-start.3 = ((bf16[40,128,256]{2,1,0:T(8,128)(2,1)}), bf16[40,128,256]{2,1,0:T(8,128)(2,1)}, u32[]{:S(2)}, u32[]{:S(2)}) async-start(bf16[40,128,256]{2,1,0:T(8,128)(2,1)} %choose_blocks.6), calls=%async_computation.3 | async-start | bytes 5242880 | tf_op jit(solution)/shard_map/all_to_all | solution.py:264

commit v10 on v9

--- a/solution.py
+++ b/solution.py
@@ -19,15 +19,15 @@
     return jnp.sum(jnp.where(jnp.arange(table.shape[0])[:, None] == z, table, 0), axis=0)
 
 
-def choose_kernel(which, ids, *refs):
+def choose_kernel(which, ids, *refs, turn):
     *froms, out, held, in_sem, out_sem = refs
-    count, seats = out.shape[0], ids.shape[1]
+    count, seats = out.shape[0], ids.shape[2]
     for j, source in enumerate(froms):
 
         @pl.when(which[0] == j)
         def _():
             for n in range(count):
-                block = source.at[ids[n // seats, n % seats]]
+                block = source.at[ids[turn, n // seats, n % seats]]
                 pltpu.make_async_copy(block, held.at[n], in_sem).start()
 
     pltpu.make_async_copy(out, held, in_sem).wait()
@@ -36,11 +36,11 @@
     leaving.wait()
 
 
-def choose(which, ids, froms, flops):
-    out = (ids.shape[0] * ids.shape[1],) + froms[0].shape[1:]
+def choose(which, ids, turn, froms, flops):
+    out = (ids.shape[1] * ids.shape[2],) + froms[0].shape[1:]
     moved = out[0] * out[1] * out[2] * 2
     return pl.pallas_call(
-        choose_kernel,
+        functools.partial(choose_kernel, turn=turn),
         grid_spec=pltpu.PrefetchScalarGridSpec(
             num_scalar_prefetch=2,
             grid=(1,),
@@ -60,18 +60,23 @@
 
 
 def either_kernel(second, a, b, out):
-    out[...] = jnp.where(second[0] == 1, b[...], a[...])
+    out[...] = jnp.where(second[0] == 1, b[...], a[1:2])
 
 
 def either(second, a, b):
-    whole = pl.BlockSpec(a.shape, lambda i, s: (0, 0))
     return pl.pallas_call(
         either_kernel,
         grid_spec=pltpu.PrefetchScalarGridSpec(
-            num_scalar_prefetch=1, grid=(1,), in_specs=[whole, whole], out_specs=whole
-        ),
-        out_shape=jax.ShapeDtypeStruct(a.shape, a.dtype),
-        cost_estimate=pl.CostEstimate(flops=HEAVY, bytes_accessed=0, transcendentals=0),
+            num_scalar_prefetch=1,
+            grid=(1,),
+            in_specs=[
+                pl.BlockSpec(a.shape, lambda i, s: (0, 0, 0)),
+                pl.BlockSpec(b.shape, lambda i, s: (0, 0, 0)),
+            ],
+            out_specs=pl.BlockSpec(b.shape, lambda i, s: (0, 0, 0)),
+        ),
+        out_shape=jax.ShapeDtypeStruct(b.shape, b.dtype),
+        cost_estimate=pl.CostEstimate(flops=LIGHT // 2, bytes_accessed=0, transcendentals=0),
         name="either_ids",
     )(second, a, b)
 
@@ -89,11 +94,11 @@
 
 
 def early_kernel(slots, late, counts, *refs):
-    *froms, masks, sums, left, table, sems = refs
+    *froms, masks, sums, left, more, table, sems = refs
     step = pl.program_id(0)
     rows, per_block = masks.shape[:2]
     tile, width = table.shape[1:]
-    spare = left.shape[2] // tile
+    pair = left.shape[2] // tile
 
     @pl.when(step == 0)
     def _():
@@ -110,15 +115,17 @@
             [table[slots[row * per_block + t]] for t in range(per_block)], axis=0
         )
         sums[here, :] = jnp.dot(mask, picked, preferred_element_type=jnp.float32)
-        for t in range(spare):
-            kept = jnp.where(t < counts[row], masks[r, late[row * spare + t]], 0)
-            left[r, :, t * tile : (t + 1) * tile] = kept.astype(jnp.int8)
+        for t in range(2 * pair):
+            kept = masks[r, late[row * 2 * pair + t]].astype(jnp.float32)
+            kept = jnp.where(t < counts[row], kept, 0.0).astype(jnp.bfloat16)
+            into = left if t < pair else more
+            into[r, :, t % pair * tile : (t % pair + 1) * tile] = kept
 
 
 def early(slots, late, counts, froms, tile_masks):
     blocks_here, per_block, tile, _ = tile_masks.shape
     width = froms[0].shape[2]
-    spare = late.shape[0] // blocks_here
+    half = late.shape[0] // blocks_here // 2 * tile
     rows = 4 if blocks_here % 4 == 0 else 1
     blocks_in_table = sum(piece.shape[0] for piece in froms) + 1
     return pl.pallas_call(
@@ -130,7 +137,8 @@
             + [pl.BlockSpec((rows, per_block, tile, tile), lambda r, *_: (r, 0, 0, 0))],
             out_specs=[
                 pl.BlockSpec((rows * tile, width), lambda r, *_: (r, 0)),
-                pl.BlockSpec((rows, tile, spare * tile), lambda r, *_: (r, 0, 0)),
+                pl.BlockSpec((rows, tile, half), lambda r, *_: (r, 0, 0)),
+                pl.BlockSpec((rows, tile, half), lambda r, *_: (r, 0, 0)),
             ],
             scratch_shapes=[
                 pltpu.VMEM((blocks_in_table, tile, width), jnp.bfloat16),
@@ -139,7 +147,8 @@
         ),
         out_shape=[
             jax.ShapeDtypeStruct((blocks_here * tile, width), jnp.float32),
-            jax.ShapeDtypeStruct((blocks_here, tile, spare * tile), jnp.int8),
+            jax.ShapeDtypeStruct((blocks_here, tile, half), jnp.bfloat16),
+            jax.ShapeDtypeStruct((blocks_here, tile, half), jnp.bfloat16),
         ],
         compiler_params=pltpu.CompilerParams(vmem_limit_bytes=VMEM_LIMIT),
         cost_estimate=pl.CostEstimate(
@@ -152,31 +161,37 @@
 
 
 def layer_kernel(slots, counts, *refs):
-    *froms, sums, left, degree, features, weight, out, table, totals, share, sems = refs
+    *froms, more, sums, left, degree, features, weight, out, table, extra, totals, share, sems, extra_sems = refs
     step = pl.program_id(0)
     rows, tile = left.shape[:2]
+    pair = left.shape[2] // tile
     width = table.shape[2]
-    spare = left.shape[2] // tile
-    pair = min(2, spare)
-    pl.when(step == 0)(functools.partial(fill, froms, table, sems))
-
-    def added(r, first):
-        ends = min(first + pair, spare)
-        picked = [table[slots[(step * rows + r) * spare + t]] for t in range(first, ends)]
-        mask = left[r, :, first * tile : ends * tile].astype(jnp.int32)
-        mask = mask.astype(jnp.float32).astype(jnp.bfloat16)
+    blocks_here = more.shape[0]
+
+    def fetch(row):
+        return pltpu.make_async_copy(more.at[row], extra.at[row], extra_sems.at[row])
+
+    @pl.when(step == 0)
+    def _():
+        for row in range(blocks_here):
+            pl.when(counts[row] > pair)(fetch(row).start)
+        fill(froms, table, sems)
+
+    def added(row, first, mask):
+        picked = [table[slots[row * 2 * pair + t]] for t in range(first, first + pair)]
         return jnp.dot(mask, jnp.concatenate(picked, axis=0), preferred_element_type=jnp.float32)
 
     for r in range(rows):
         here = pl.ds(r * tile, tile)
-        totals[here, :] = sums[here, :] + added(r, 0)
+        totals[here, :] = sums[here, :] + added(step * rows + r, 0, left[r])
     for r in range(rows):
+        row = step * rows + r
         here = pl.ds(r * tile, tile)
-        for first in range(pair, spare, pair):
-
-            @pl.when(counts[step * rows + r] > first)
-            def _():
-                totals[here, :] += added(r, first)
+
+        @pl.when(counts[row] > pair)
+        def _():
+            fetch(row).wait()
+            totals[here, :] += added(row, pair, extra[row])
 
     column = lax.broadcasted_iota(jnp.int32, (tile, tile), 1)
     diagonal = lax.broadcasted_iota(jnp.int32, (tile, tile), 0) == column
@@ -194,7 +209,9 @@
         jnp.concatenate(spread, axis=0), ones, preferred_element_type=jnp.float32
     )
 
-    many = min(rows, 4) * tile
+    out_width = out.shape[1]
+    ones = jnp.ones((2 * out_width, tile), jnp.bfloat16)
+    many = min(rows, 2) * tile
     for first in range(0, rows * tile, many):
         here = pl.ds(first, many)
         part = jnp.concatenate([share[here, :]] * (width // tile), axis=1)
@@ -202,11 +219,17 @@
         joined = jnp.concatenate([features[here, :], mean], axis=1)
         hidden = jnp.dot(joined, weight[...], preferred_element_type=jnp.float32)
         hidden = jnp.maximum(hidden, 0.0)
-        scale = lax.rsqrt(jnp.sum(hidden * hidden, axis=1, keepdims=True) + 1e-06)
+        squares = hidden * hidden
+        high = squares.astype(jnp.bfloat16)
+        low = (squares - high.astype(jnp.float32)).astype(jnp.bfloat16)
+        total = jnp.dot(
+            jnp.concatenate([high, low], axis=1), ones, preferred_element_type=jnp.float32
+        )
+        scale = jnp.concatenate([lax.rsqrt(total + 1e-06)] * (out_width // tile), axis=1)
         out[here, :] = (hidden * scale).astype(jnp.bfloat16)
 
 
-def layer(slots, counts, froms, sums, left, degree, features, weight):
+def layer(slots, counts, froms, sums, left, more, degree, features, weight):
     blocks_here, tile, across = left.shape
     width = features.shape[1]
     out_width = weight.shape[1]
@@ -218,7 +241,7 @@
         grid_spec=pltpu.PrefetchScalarGridSpec(
             num_scalar_prefetch=2,
             grid=(blocks_here // rows,),
-            in_specs=[pl.BlockSpec(memory_space=pl.ANY)] * len(froms)
+            in_specs=[pl.BlockSpec(memory_space=pl.ANY)] * (len(froms) + 1)
             + [
                 pl.BlockSpec((items, width), lambda r, *_: (r, 0)),
                 pl.BlockSpec((rows, tile, across), lambda r, *_: (r, 0, 0)),
@@ -229,20 +252,22 @@
             out_specs=pl.BlockSpec((items, out_width), lambda r, *_: (r, 0)),
             scratch_shapes=[
                 pltpu.VMEM((blocks_in_table, tile, width), jnp.bfloat16),
+                pltpu.VMEM((blocks_here, tile, across), jnp.bfloat16),
                 pltpu.VMEM((items, width), jnp.float32),
                 pltpu.VMEM((items, tile), jnp.float32),
                 pltpu.SemaphoreType.DMA((len(froms),)),
+                pltpu.SemaphoreType.DMA((blocks_here,)),
             ],
         ),
         out_shape=jax.ShapeDtypeStruct((blocks_here * tile, out_width), jnp.bfloat16),
         compiler_params=pltpu.CompilerParams(vmem_limit_bytes=VMEM_LIMIT),
         cost_estimate=pl.CostEstimate(
             flops=2 * blocks_here * tile * (across + 2 * width) * out_width,
-            bytes_accessed=blocks_here * tile * (4 * width + across + 2 * width + 2 * out_width),
+            bytes_accessed=blocks_here * tile * (4 * width + 2 * across + 2 * width + 2 * out_width),
             transcendentals=blocks_here * tile,
         ),
         name="sage_layer",
-    )(slots, counts, *froms, sums, left, degree, features, weight)
+    )(slots, counts, *froms, more, sums, left, degree, features, weight)
 
 
 def on_device(features, tile_cols, tile_masks, degree, weight):
@@ -270,7 +295,6 @@
         return lax.ppermute(x, "rows", pairs)
 
     asked = exchange(jnp.broadcast_to(columns, (plane,) + columns.shape))
-    across = shift(asked, [(0, PLANES - 1), (PLANES - 1, 0)])
     down = [(a, a - 1) for a in range(1, PLANES)]
     up = [(a - 1, a) for a in range(1, PLANES)]
     from_above, from_below = shift(local, down), shift(local, up)
@@ -288,8 +312,7 @@
         taken = (need[:, :, None, :] == 1) & (place[:, :, None, :] == seat[:, None])
         return jnp.sum(jnp.where(taken, blocks, 0), axis=3)
 
-    near = seated(asked, wanted)
-    ids = [near[:, k, :] for k in range(PLANES)]
+    near = jnp.swapaxes(seated(asked, wanted), 0, 1)
 
     owners, within = columns // blocks_here, columns % blocks_here
     positions = jnp.arange(columns.shape[0], dtype=jnp.int32)
@@ -320,31 +343,34 @@
 
     always = jnp.zeros((1,), jnp.int32)
     inner = (~end).astype(jnp.int32)[None]
-    picked = choose(always, ids[0], [local], LIGHT)
+    picked = choose(always, near, 0, [local], LIGHT)
     got = [exchange(picked)]
+    asked, _ = lax.optimization_barrier((asked, picked))
+    across = shift(asked, [(0, PLANES - 1), (PLANES - 1, 0)])
     across, _, _ = lax.optimization_barrier((across, from_above, from_below))
-    opposite = seated(across, wanted[:1])[:, 0, :]
-    ids[1] = either(end.astype(jnp.int32)[None], near[:, 1, :], opposite)
-    picked = choose(inner, ids[1], [local, from_above], LIGHT)
+    opposite = jnp.swapaxes(seated(across, wanted[:1]), 0, 1)
+    middle = either(end.astype(jnp.int32)[None], near, opposite)
+    picked = choose(inner, middle, 0, [local, from_above], LIGHT)
     leaving, _ = lax.optimization_barrier((picked, got[0]))
     got.append(exchange(leaving))
     second_down = shift(from_above, down[:-1])
     second_up = shift(from_below, up[1:])
     leaving, _, _ = lax.optimization_barrier((got[1], second_down, second_up))
     crossed = shift(leaving, [(0, PLANES - 1), (PLANES - 1, 0)])
-    ids[2], _ = lax.optimization_barrier((ids[2], picked))
-    picked = choose((z > 0).astype(jnp.int32)[None], ids[2], [from_above, from_below], HEAVY)
-    got.append(exchange(picked))
+    near, _ = lax.optimization_barrier((near, picked))
+    below_or_above = (z > 0).astype(jnp.int32)[None]
+    got.append(exchange(choose(below_or_above, near, 2, [from_above, from_below], HEAVY)))
     beyond = (z >= PLANES // 2).astype(jnp.int32)[None]
-    got.append(exchange(choose(beyond, ids[3], [second_down, second_up], LIGHT)))
-
-    sums, left = early(slots, late.reshape(-1), counts, [local] + got[:3], tile_masks)
+    got.append(exchange(choose(beyond, near, 3, [second_down, second_up], LIGHT)))
+
+    sums, left, more = early(slots, late.reshape(-1), counts, [local] + got[:3], tile_masks)
     return layer(
         late_slots.reshape(-1),
         counts,
         [crossed, got[3]],
         sums,
         left,
+        more,
         degree.reshape(blocks_here, tile),
         features,
         weight,

time: 192 us -> 191 us (level); the launches traced: 191 us -> 188 us
  waiting for transfers between devices: 92.7 us -> 83.4 us
  starting transfers between devices: 40.7 us -> 45.1 us
  Pallas kernels: 44.8 us -> 48.6 us
    all_to_all x5, waiting for transfers between devices: 71.2 us -> 61.2 us  [exchange(): lax.all_to_all(x, 'rows', split_axis=0, concat_axis=0, axis_index_groups=...]
    ppermute x6, starting transfers between devices: 19.3 us -> 23.4 us  [shift(): return lax.ppermute(x, 'rows', pairs)]
    slice x5 -> x0, local copies, waits for them, and re-layouts: 2.7 us -> none  [the longest x4 2.03 us: on_device(): ids = [near[:, k, :] for k in range(PLANES)]]
    pallas_call x1, Pallas kernels: 11.8 us -> 14.2 us  [layer(): pl.pallas_call(layer_kernel, grid_spec=pltpu.PrefetchScalarGridSpec(num_s...]
  transfers between devices with their start and end apart: 11 -> 11, of which waited for: 7 -> 6; matrix products, arithmetic and copies ran while one was open for 6% -> 5% of each run, Pallas kernels for 17% -> 18%
where the time goes in v10:
time: 191 us; the launch traced here: 188 us
  waiting for transfers between devices  83.4 us (44%)
  Pallas kernels  48.6 us (25%)
  starting transfers between devices  45.1 us (24%)
  other arithmetic  5.29 us (3%)
  local copies, waits for them, and re-layouts  5.02 us (3%)
    all_to_all x5, waiting for transfers between devices, exchange(): lax.all_to_all(x, 'rows', split_axis=0, concat_axis=0, axis_index_groups=...  61.2 us
    ppermute x6, starting transfers between devices, shift(): return lax.ppermute(x, 'rows', pairs)  23.4 us
    ppermute x6, waiting for transfers between devices, shift(): return lax.ppermute(x, 'rows', pairs)  22.3 us
    all_to_all x5, starting transfers between devices, exchange(): lax.all_to_all(x, 'rows', split_axis=0, concat_axis=0, axis_index_groups=...  21.8 us
    pallas_call x4, Pallas kernels, choose(): pl.pallas_call(functools.partial(choose_kernel, turn=turn), grid_spec=plt...  17.4 us
    pallas_call x1, Pallas kernels, early(): pl.pallas_call(early_kernel, grid_spec=pltpu.PrefetchScalarGridSpec(num_s...  15.6 us
    pallas_call x1, Pallas kernels, layer(): pl.pallas_call(layer_kernel, grid_spec=pltpu.PrefetchScalarGridSpec(num_s...  14.2 us
  transfers between devices with their start and end apart: 11, of which 6 were waited for; matrix products, arithmetic and copies ran while one was open for 5% of the time, Pallas kernels for 18%

profile of v10, /device:TPU:0, one launch (start us, length us, event | category | flops | bytes accessed | tf_op | source)
XLA Modules:
  0.0 187.7 jit_solution(9149753116038086404)
XLA Ops:
  0.0 1.3 collective-permute-start.1
  1.3 6.9 %collective-permute-start.2 = (bf16[32,128,256]{2,1,0:T(8,128)(2,1)}, bf16[32,128,256]{2,1,0:T(8,128)(2,1)}, u32[]{:S(2)}, u32[]{:S(2)}) collective-permute-start(bf16[32,128,256]{2,1,0:T(8,128)(2,1)} %bitcast.14), channel_id=1, source_target_pairs={{0,8},{1,9},{2,10},{3,11},{4,12},{5,13},{6,14},{7,15},{8,16},{9,17... | collective-permute-start | bytes 6291464 | tf_op jit(solution)/shard_map/ppermute | solution.py:295
  8.2 0.8 copy.30
  9.0 0.1 reshape.280
  9.1 0.6 broadcast_in_dim.156
  9.7 4.2 %all-to-all-start = ((s32[8,1,192]{2,1,0:T(1,128)}), s32[8,1,192]{2,1,0:T(1,128)S(1)}, u32[]{:S(2)}, u32[]{:S(2)}) async-start(s32[8,1,192]{2,1,0:T(1,128)} %broadcast_in_dim.156), calls=%async_computation | async-start | bytes 16384 | tf_op jit(solution)/shard_map/all_to_all | solution.py:289
  13.9 0.8 select_reduce_fusion.7
  14.7 3.8 %all-to-all-done = s32[8,1,192]{2,1,0:T(1,128)S(1)} async-done(((s32[8,1,192]{2,1,0:T(1,128)}), s32[8,1,192]{2,1,0:T(1,128)S(1)}, u32[]{:S(2)}, u32[]{:S(2)}) %all-to-all-start) | async-done | bytes 6176 | tf_op jit(solution)/shard_map/all_to_all | solution.py:289
  18.5 0.7 compare_reduce_fusion
  19.3 0.6 select_reduce_fusion
  19.9 0.4 select_reduce_fusion.2
  20.3 0.7 copy.41
  21.1 4.5 %choose_blocks.4 = bf16[40,128,256]{2,1,0:T(8,128)(2,1)} custom-call(s32[1]{0:T(128)} %constant.95.clone.1.which, s32[4,8,5]{2,1,0:T(8,128)} %bitcast.20, bf16[32,128,256]{2,1,0:T(8,128)(2,1)} %bitcast.15), custom_call_target="tpu_custom_call" | custom-call | flops 10000000000 | bytes 5242880 | tf_op jit(solution)/shard_map/choose_blocks/pallas_call | solution.py:42
  25.5 4.4 %all-to-all-start.1 = ((bf16[40,128,256]{2,1,0:T(8,128)(2,1)}), bf16[40,128,256]{2,1,0:T(8,128)(2,1)}, u32[]{:S(2)}, u32[]{:S(2)}) async-start(bf16[40,128,256]{2,1,0:T(8,128)(2,1)} %choose_blocks.4), calls=%async_computation.1 | async-start | bytes 5242880 | tf_op jit(solution)/shard_map/all_to_all | solution.py:289
  29.9 3.2 %collective-permute-start = (s32[8,192]{1,0:T(8,128)S(1)}, s32[8,192]{1,0:T(8,128)S(1)}, u32[]{:S(2)}, u32[]{:S(2)}) collective-permute-start(s32[8,192]{1,0:T(8,128)S(1)} %bitcast.19), channel_id=1, source_target_pairs={{0,24},{1,25},{2,26},{3,27},{4,28},{5,29},{6,30},{7,31},{24,0},{25... | collective-permute-start | bytes 18440 | tf_op jit(solution)/shard_map/ppermute | solution.py:295
  33.2 19.9 %collective-permute-done = s32[8,192]{1,0:T(8,128)S(1)} collective-permute-done((s32[8,192]{1,0:T(8,128)S(1)}, s32[8,192]{1,0:T(8,128)S(1)}, u32[]{:S(2)}, u32[]{:S(2)}) %collective-permute-start) | collective-permute-done | bytes 6176 | tf_op jit(solution)/shard_map/ppermute | solution.py:295
  53.1 0.3 compare_reduce_fusion.1
  53.4 0.2 select_reduce_fusion.1
  53.6 0.2 select_reduce_fusion.3
  53.8 0.7 copy.42
  54.5 1.3 either_ids.1.ids
  55.8 4.3 %choose_blocks.5 = bf16[40,128,256]{2,1,0:T(8,128)(2,1)} custom-call(s32[1]{0:T(128)} %bitcast.which, s32[1,8,5]{2,1,0:T(8,128)} %either_ids.1.ids, bf16[32,128,256]{2,1,0:T(8,128)(2,1)} %bitcast.16, bf16[32,128,256]{2,1,0:T(8,128)(2,1)} %collective-permute-done.1.refs_1_.refs_0_), custom_call_target="tpu_custom_call" | custom-call | flops 10000000000 | bytes 5242880 | tf_op jit(solution)/shard_map/choose_blocks/pallas_call | solution.py:42
  60.1 1.3 collective-permute-start.3
  61.4 2.0 %collective-permute-start.4 = (bf16[32,128,256]{2,1,0:T(8,128)(2,1)}, bf16[32,128,256]{2,1,0:T(8,128)(2,1)}, u32[]{:S(2)}, u32[]{:S(2)}) collective-permute-start(bf16[32,128,256]{2,1,0:T(8,128)(2,1)} %collective-permute-done.2.refs_1_), channel_id=1, source_target_pairs={{8,16},{9,17},{10,18},{11,19},{12,20},{13,21},{14,22},{15,23},{16,... | collective-permute-start | bytes 6291464 | tf_op jit(solution)/shard_map/ppermute | solution.py:295
  63.4 4.4 %all-to-all-start.2 = ((bf16[40,128,256]{2,1,0:T(8,128)(2,1)}), bf16[40,128,256]{2,1,0:T(8,128)(2,1)}, u32[]{:S(2)}, u32[]{:S(2)}) async-start(bf16[40,128,256]{2,1,0:T(8,128)(2,1)} %choose_blocks.5), calls=%async_computation.2 | async-start | bytes 5242880 | tf_op jit(solution)/shard_map/all_to_all | solution.py:289
  67.8 4.4 %choose_blocks.7 = bf16[40,128,256]{2,1,0:T(8,128)(2,1)} custom-call(s32[1]{0:T(128)} %bitcast.7.which, s32[4,8,5]{2,1,0:T(8,128)} %bitcast.22, bf16[32,128,256]{2,1,0:T(8,128)(2,1)} %collective-permute-done.1.refs_1_.refs_0_, bf16[32,128,256]{2,1,0:T(8,128)(2,1)} %collective-permute-done.2.refs_1_), custom_call_target="tpu_custom_call" | custom-call | flops 30000001024 | bytes 5242880 | tf_op jit(solution)/shard_map/choose_blocks/pallas_call | solution.py:42
  72.2 27.8 %all-to-all-done.2.refs_2_ = bf16[40,128,256]{2,1,0:T(8,128)(2,1)} async-done(((bf16[40,128,256]{2,1,0:T(8,128)(2,1)}), bf16[40,128,256]{2,1,0:T(8,128)(2,1)}, u32[]{:S(2)}, u32[]{:S(2)}) %all-to-all-start.2) | async-done | bytes 2621472 | tf_op jit(solution)/shard_map/all_to_all | solution.py:289
  100.1 4.4 %all-to-all-start.4 = ((bf16[40,128,256]{2,1,0:T(8,128)(2,1)}), bf16[40,128,256]{2,1,0:T(8,128)(2,1)}, u32[]{:S(2)}, u32[]{:S(2)}) async-start(bf16[40,128,256]{2,1,0:T(8,128)(2,1)} %choose_blocks.7), calls=%async_computation.4 | async-start | bytes 5242880 | tf_op jit(solution)/shard_map/all_to_all | solution.py:289
  104.6 0.1 and.140
  104.7 0.1 eq.209
  104.8 0.2 fusion.1
  105.0 0.2 convert_reduce_fusion
  105.3 0.1 reduce_sum.104
  105.4 0.6 convert_reduce_fusion.1
  106.0 0.2 reduce_window_sum.11
  106.2 2.3 %collective-permute-done.3.refs_0_ = bf16[32,128,256]{2,1,0:T(8,128)(2,1)} collective-permute-done((bf16[32,128,256]{2,1,0:T(8,128)(2,1)}, bf16[32,128,256]{2,1,0:T(8,128)(2,1)}, u32[]{:S(2)}, u32[]{:S(2)}) %collective-permute-start.3) | collective-permute-done | bytes 2097184 | tf_op jit(solution)/shard_map/ppermute | solution.py:295
  108.5 8.7 %collective-permute-start.5 = (bf16[40,128,256]{2,1,0:T(8,128)(2,1)}, bf16[40,128,256]{2,1,0:T(8,128)(2,1)}, u32[]{:S(2)}, u32[]{:S(2)}) collective-permute-start(bf16[40,128,256]{2,1,0:T(8,128)(2,1)} %all-to-all-done.2.refs_2_), channel_id=1, source_target_pairs={{0,24},{1,25},{2,26},{3,27},{4,28},{5,29},{6,30},{7,31},{24,0},{25... | collective-permute-start | bytes 7864328 | tf_op jit(solution)/shard_map/ppermute | solution.py:295
  117.2 4.3 %choose_blocks.6 = bf16[40,128,256]{2,1,0:T(8,128)(2,1)} custom-call(s32[1]{0:T(128)} %bitcast.6.which, s32[4,8,5]{2,1,0:T(8,128)} %bitcast.23, bf16[32,128,256]{2,1,0:T(8,128)(2,1)} %collective-permute-done.3.refs_0_, bf16[32,128,256]{2,1,0:T(8,128)(2,1)} %collective-permute-done.4.refs_1_), custom_call_target="tpu_custom_call" | custom-call | flops 10000000000 | bytes 5242880 | tf_op jit(solution)/shard_map/choose_blocks/pallas_call | solution.py:42
  121.5 15.3 %all-to-all-done.4.refs_3_ = bf16[40,128,256]{2,1,0:T(8,128)(2,1)} async-done(((bf16[40,128,256]{2,1,0:T(8,128)(2,1)}), bf16[40,128,256]{2,1,0:T(8,128)(2,1)}, u32[]{:S(2)}, u32[]{:S(2)}) %all-to-all-start.4) | async-done | bytes 2621472 | tf_op jit(solution)/shard_map/all_to_all | solution.py:289
  136.8 4.4 %all-to-all-start.3 = ((bf16[40,128,256]{2,1,0:T(8,128)(2,1)}), bf16[40,128,256]{2,1,0:T(8,128)(2,1)}, u32[]{:S(2)}, u32[]{:S(2)}) async-start(bf16[40,128,256]{2,1,0:T(8,128)(2,1)} %choose_blocks.6), calls=%async_computation.3 | async-start | bytes 5242880 | tf_op jit(solution)/shard_map/all_to_all | solution.py:289
  141.2 0.1 copy.31
  141.5 0.1 copy.43
  141.5 0.7 reshape.283.late
  142.3 0.7 reshape.281.slots
  143.0 0.6 compare_select_fusion.slots
  143.6 15.6 %early_sums.1 = (f32[4096,256]{1,0:T(8,128)}, bf16[32,128,256]{2,1,0:T(8,128)(2,1)}, bf16[32,128,256]{2,1,0:T(8,128)(2,1)}) custom-call(s32[192]{0:T(256)} %compare_select_fusion.slots, s32[128]{0:T(128)} %reshape.283.late, s32[32]{0:T(128)} %get-tuple-element.25.counts, bf16[32,128,256]{2,1,0:T(8,128)(2,1)} %bitcast.17, ...), custom_call_target="tpu_custom_call" | custom-call | flops 20000000000 | bytes 28901376 | tf_op jit(solution)/shard_map/early_sums/pallas_call | solution.py:131
  159.2 14.2 %all-to-all-done.3.refs_1_ = bf16[40,128,256]{2,1,0:T(8,128)(2,1)} async-done(((bf16[40,128,256]{2,1,0:T(8,128)(2,1)}), bf16[40,128,256]{2,1,0:T(8,128)(2,1)}, u32[]{:S(2)}, u32[]{:S(2)}) %all-to-all-start.3) | async-done | bytes 2621472 | tf_op jit(solution)/shard_map/all_to_all | solution.py:289
  173.4 14.2 %sage_layer.1 = bf16[4096,256]{1,0:T(8,128)(2,1)} custom-call(s32[128]{0:T(128)} %reshape.281.slots, s32[32]{0:T(128)} %get-tuple-element.25.counts, bf16[40,128,256]{2,1,0:T(8,128)(2,1)} %collective-permute-done.5.refs_0_, bf16[40,128,256]{2,1,0:T(8,128)(2,1)} %all-to-all-done.3.refs_1_, bf16[32,128,256]{2,1,0:T(8,128)(2,1)} %get-tuple-element.18.refs_2_, ...), custom_call_target="tpu_custom_call" | custom-call | flops 1610612736 | bytes 10485760 | tf_op jit(solution)/shard_map/sage_layer/pallas_call | solution.py:239
  (25 shorter events, 0.5 us)
Async XLA Ops:
  0.0 53.1 %collective-permute-start.1 = (bf16[32,128,256]{2,1,0:T(8,128)(2,1)}, bf16[32,128,256]{2,1,0:T(8,128)(2,1)}, u32[]{:S(2)}, u32[]{:S(2)}) collective-permute-start(bf16[32,128,256]{2,1,0:T(8,128)(2,1)} %bitcast.13), channel_id=1, source_target_pairs={{8,0},{9,1},{10,2},{11,3},{12,4},{13,5},{14,6},{15,7},{16,8},{17,9... | collective-permute-start | bytes 6291464 | tf_op jit(solution)/shard_map/ppermute | solution.py:295
  1.3 51.8 %collective-permute-start.2 = (bf16[32,128,256]{2,1,0:T(8,128)(2,1)}, bf16[32,128,256]{2,1,0:T(8,128)(2,1)}, u32[]{:S(2)}, u32[]{:S(2)}) collective-permute-start(bf16[32,128,256]{2,1,0:T(8,128)(2,1)} %bitcast.14), channel_id=1, source_target_pairs={{0,8},{1,9},{2,10},{3,11},{4,12},{5,13},{6,14},{7,15},{8,16},{9,17... | collective-permute-start | bytes 6291464 | tf_op jit(solution)/shard_map/ppermute | solution.py:295
  9.7 8.9 %all-to-all-start = ((s32[8,1,192]{2,1,0:T(1,128)}), s32[8,1,192]{2,1,0:T(1,128)S(1)}, u32[]{:S(2)}, u32[]{:S(2)}) async-start(s32[8,1,192]{2,1,0:T(1,128)} %broadcast_in_dim.156), calls=%async_computation | async-start | bytes 16384 | tf_op jit(solution)/shard_map/all_to_all | solution.py:289
  25.5 37.9 %all-to-all-start.1 = ((bf16[40,128,256]{2,1,0:T(8,128)(2,1)}), bf16[40,128,256]{2,1,0:T(8,128)(2,1)}, u32[]{:S(2)}, u32[]{:S(2)}) async-start(bf16[40,128,256]{2,1,0:T(8,128)(2,1)} %choose_blocks.4), calls=%async_computation.1 | async-start | bytes 5242880 | tf_op jit(solution)/shard_map/all_to_all | solution.py:289
  29.9 23.2 %collective-permute-start = (s32[8,192]{1,0:T(8,128)S(1)}, s32[8,192]{1,0:T(8,128)S(1)}, u32[]{:S(2)}, u32[]{:S(2)}) collective-permute-start(s32[8,192]{1,0:T(8,128)S(1)} %bitcast.19), channel_id=1, source_target_pairs={{0,24},{1,25},{2,26},{3,27},{4,28},{5,29},{6,30},{7,31},{24,0},{25... | collective-permute-start | bytes 18440 | tf_op jit(solution)/shard_map/ppermute | solution.py:295
  60.1 48.4 %collective-permute-start.3 = (bf16[32,128,256]{2,1,0:T(8,128)(2,1)}, bf16[32,128,256]{2,1,0:T(8,128)(2,1)}, u32[]{:S(2)}, u32[]{:S(2)}) collective-permute-start(bf16[32,128,256]{2,1,0:T(8,128)(2,1)} %collective-permute-done.1.refs_1_.refs_0_), channel_id=1, source_target_pairs={{8,0},{9,1},{10,2},{11,3},{12,4},{13,5},{14,6},{15,7},{16,8},{17,9... | collective-permute-start | bytes 6291464 | tf_op jit(solution)/shard_map/ppermute | solution.py:295
  61.4 47.1 %collective-permute-start.4 = (bf16[32,128,256]{2,1,0:T(8,128)(2,1)}, bf16[32,128,256]{2,1,0:T(8,128)(2,1)}, u32[]{:S(2)}, u32[]{:S(2)}) collective-permute-start(bf16[32,128,256]{2,1,0:T(8,128)(2,1)} %collective-permute-done.2.refs_1_), channel_id=1, source_target_pairs={{8,16},{9,17},{10,18},{11,19},{12,20},{13,21},{14,22},{15,23},{16,... | collective-permute-start | bytes 6291464 | tf_op jit(solution)/shard_map/ppermute | solution.py:295
  63.4 36.7 %all-to-all-start.2 = ((bf16[40,128,256]{2,1,0:T(8,128)(2,1)}), bf16[40,128,256]{2,1,0:T(8,128)(2,1)}, u32[]{:S(2)}, u32[]{:S(2)}) async-start(bf16[40,128,256]{2,1,0:T(8,128)(2,1)} %choose_blocks.5), calls=%async_computation.2 | async-start | bytes 5242880 | tf_op jit(solution)/shard_map/all_to_all | solution.py:289
  100.1 36.7 %all-to-all-start.4 = ((bf16[40,128,256]{2,1,0:T(8,128)(2,1)}), bf16[40,128,256]{2,1,0:T(8,128)(2,1)}, u32[]{:S(2)}, u32[]{:S(2)}) async-start(bf16[40,128,256]{2,1,0:T(8,128)(2,1)} %choose_blocks.7), calls=%async_computation.4 | async-start | bytes 5242880 | tf_op jit(solution)/shard_map/all_to_all | solution.py:289
  108.5 64.9 %collective-permute-start.5 = (bf16[40,128,256]{2,1,0:T(8,128)(2,1)}, bf16[40,128,256]{2,1,0:T(8,128)(2,1)}, u32[]{:S(2)}, u32[]{:S(2)}) collective-permute-start(bf16[40,128,256]{2,1,0:T(8,128)(2,1)} %all-to-all-done.2.refs_2_), channel_id=1, source_target_pairs={{0,24},{1,25},{2,26},{3,27},{4,28},{5,29},{6,30},{7,31},{24,0},{25... | collective-permute-start | bytes 7864328 | tf_op jit(solution)/shard_map/ppermute | solution.py:295
  136.8 36.7 %all-to-all-start.3 = ((bf16[40,128,256]{2,1,0:T(8,128)(2,1)}), bf16[40,128,256]{2,1,0:T(8,128)(2,1)}, u32[]{:S(2)}, u32[]{:S(2)}) async-start(bf16[40,128,256]{2,1,0:T(8,128)(2,1)} %choose_blocks.6), calls=%async_computation.3 | async-start | bytes 5242880 | tf_op jit(solution)/shard_map/all_to_all | solution.py:289

commit v11 on v10

--- a/solution.py
+++ b/solution.py
@@ -19,66 +19,52 @@
     return jnp.sum(jnp.where(jnp.arange(table.shape[0])[:, None] == z, table, 0), axis=0)
 
 
-def choose_kernel(which, ids, *refs, turn):
-    *froms, out, held, in_sem, out_sem = refs
-    count, seats = out.shape[0], ids.shape[2]
+def choose_kernel(which, *refs, turns):
+    lists, (*froms, out, held, in_sems, out_sems) = refs[: len(turns)], refs[len(turns) :]
+    count, seats = out.shape[0], lists[0].shape[2]
+    groups = in_sems.shape[0]
+    size = count // groups
     for j, source in enumerate(froms):
+        ids, turn = lists[j % len(turns)], turns[j % len(turns)]
 
         @pl.when(which[0] == j)
         def _():
             for n in range(count):
                 block = source.at[ids[turn, n // seats, n % seats]]
-                pltpu.make_async_copy(block, held.at[n], in_sem).start()
-
-    pltpu.make_async_copy(out, held, in_sem).wait()
-    leaving = pltpu.make_async_copy(held, out, out_sem)
-    leaving.start()
-    leaving.wait()
-
-
-def choose(which, ids, turn, froms, flops):
-    out = (ids.shape[1] * ids.shape[2],) + froms[0].shape[1:]
+                pltpu.make_async_copy(block, held.at[n], in_sems.at[n // size]).start()
+
+    leaving = []
+    for g in range(groups):
+        here = pl.ds(g * size, size)
+        pltpu.make_async_copy(out.at[here], held.at[here], in_sems.at[g]).wait()
+        leaving.append(pltpu.make_async_copy(held.at[here], out.at[here], out_sems.at[g]))
+        leaving[-1].start()
+    for copy in leaving:
+        copy.wait()
+
+
+def choose(which, lists, turns, froms, flops):
+    out = (lists[0].shape[1] * lists[0].shape[2],) + froms[0].shape[1:]
     moved = out[0] * out[1] * out[2] * 2
+    groups = 4 if out[0] % 4 == 0 else 1
     return pl.pallas_call(
-        functools.partial(choose_kernel, turn=turn),
+        functools.partial(choose_kernel, turns=turns),
         grid_spec=pltpu.PrefetchScalarGridSpec(
-            num_scalar_prefetch=2,
+            num_scalar_prefetch=1 + len(lists),
             grid=(1,),
             in_specs=[pl.BlockSpec(memory_space=pltpu.HBM)] * len(froms),
             out_specs=pl.BlockSpec(memory_space=pltpu.HBM),
             scratch_shapes=[
                 pltpu.VMEM(out, froms[0].dtype),
-                pltpu.SemaphoreType.DMA,
-                pltpu.SemaphoreType.DMA,
+                pltpu.SemaphoreType.DMA((groups,)),
+                pltpu.SemaphoreType.DMA((groups,)),
             ],
         ),
         out_shape=jax.ShapeDtypeStruct(out, froms[0].dtype),
         compiler_params=pltpu.CompilerParams(vmem_limit_bytes=VMEM_LIMIT),
         cost_estimate=pl.CostEstimate(flops=flops, bytes_accessed=2 * moved, transcendentals=0),
         name="choose_blocks",
-    )(which, ids, *froms)
-
-
-def either_kernel(second, a, b, out):
-    out[...] = jnp.where(second[0] == 1, b[...], a[1:2])
-
-
-def either(second, a, b):
-    return pl.pallas_call(
-        either_kernel,
-        grid_spec=pltpu.PrefetchScalarGridSpec(
-            num_scalar_prefetch=1,
-            grid=(1,),
-            in_specs=[
-                pl.BlockSpec(a.shape, lambda i, s: (0, 0, 0)),
-                pl.BlockSpec(b.shape, lambda i, s: (0, 0, 0)),
-            ],
-            out_specs=pl.BlockSpec(b.shape, lambda i, s: (0, 0, 0)),
-        ),
-        out_shape=jax.ShapeDtypeStruct(b.shape, b.dtype),
-        cost_estimate=pl.CostEstimate(flops=LIGHT // 2, bytes_accessed=0, transcendentals=0),
-        name="either_ids",
-    )(second, a, b)
+    )(which, *lists, *froms)
 
 
 def fill(pieces, table, sems):
@@ -160,63 +146,93 @@
     )(slots, late, counts, *froms, tile_masks)
 
 
-def layer_kernel(slots, counts, *refs):
-    *froms, more, sums, left, degree, features, weight, out, table, extra, totals, share, sems, extra_sems = refs
-    step = pl.program_id(0)
-    rows, tile = left.shape[:2]
-    pair = left.shape[2] // tile
-    width = table.shape[2]
-    blocks_here = more.shape[0]
+def layer_kernel(slots, counts, *refs, many):
+    *froms, more, sums, left, features, degree, weight, out = refs[:-11]
+    table, extra, totals, masks, own, share, done, table_sems, extra_sems, in_sems, out_sems = refs[-11:]
+    blocks_here, tile, across = masks.shape
+    pair = across // tile
+    width, out_width = table.shape[2], done.shape[1]
+    chunks = blocks_here // many
+    items = many * tile
+
+    def table_copies():
+        at = 0
+        for n, piece in enumerate(froms):
+            cut = table_sems.shape[1]
+            size = piece.shape[0] // cut
+            for c in range(cut):
+                here = table.at[pl.ds(at + c * size, size)]
+                yield pltpu.make_async_copy(piece.at[pl.ds(c * size, size)], here, table_sems.at[n, c])
+            at += piece.shape[0]
+
+    def chunk_copies(c):
+        here, there = pl.ds(c * items, items), pl.ds(c * many, many)
+        return [
+            pltpu.make_async_copy(left.at[there], masks.at[there], in_sems.at[c, 0]),
+            pltpu.make_async_copy(sums.at[here], totals.at[here], in_sems.at[c, 1]),
+            pltpu.make_async_copy(features.at[here], own.at[here], in_sems.at[c, 2]),
+        ]
 
     def fetch(row):
         return pltpu.make_async_copy(more.at[row], extra.at[row], extra_sems.at[row])
 
-    @pl.when(step == 0)
-    def _():
-        for row in range(blocks_here):
+    def leave(c):
+        here = pl.ds(c * items, items)
+        return pltpu.make_async_copy(done.at[here], out.at[here], out_sems.at[c])
+
+    for copy in table_copies():
+        copy.start()
+    for c in range(chunks):
+        for copy in chunk_copies(c):
+            copy.start()
+        for row in range(c * many, (c + 1) * many):
             pl.when(counts[row] > pair)(fetch(row).start)
-        fill(froms, table, sems)
-
-    def added(row, first, mask):
-        picked = [table[slots[row * 2 * pair + t]] for t in range(first, first + pair)]
-        return jnp.dot(mask, jnp.concatenate(picked, axis=0), preferred_element_type=jnp.float32)
-
-    for r in range(rows):
-        here = pl.ds(r * tile, tile)
-        totals[here, :] = sums[here, :] + added(step * rows + r, 0, left[r])
-    for r in range(rows):
-        row = step * rows + r
-        here = pl.ds(r * tile, tile)
-
-        @pl.when(counts[row] > pair)
-        def _():
-            fetch(row).wait()
-            totals[here, :] += added(row, pair, extra[row])
 
     column = lax.broadcasted_iota(jnp.int32, (tile, tile), 1)
     diagonal = lax.broadcasted_iota(jnp.int32, (tile, tile), 0) == column
-    spread = []
-    for r in range(rows):
-        count = degree[pl.ds(step * rows + r, 1), :]
+    ones = jnp.ones((2 * tile, tile), jnp.bfloat16)
+    for row in range(blocks_here):
+        count = degree[row : row + 1, :]
         small = count & 7
         halves = [
             jnp.where(diagonal, part.astype(jnp.float32), 0.0).astype(jnp.bfloat16)
             for part in (count - small, small)
         ]
-        spread.append(jnp.concatenate(halves, axis=1))
-    ones = jnp.ones((2 * tile, tile), jnp.bfloat16)
-    share[...] = 1.0 / jnp.dot(
-        jnp.concatenate(spread, axis=0), ones, preferred_element_type=jnp.float32
-    )
-
-    out_width = out.shape[1]
+        spread = jnp.concatenate(halves, axis=1)
+        share[row * tile : (row + 1) * tile, :] = 1.0 / jnp.dot(
+            spread, ones, preferred_element_type=jnp.float32
+        )
+
+    for copy in table_copies():
+        copy.wait()
     ones = jnp.ones((2 * out_width, tile), jnp.bfloat16)
-    many = min(rows, 2) * tile
-    for first in range(0, rows * tile, many):
-        here = pl.ds(first, many)
+
+    def chunk(c, carry):
+        for copy in chunk_copies(c):
+            copy.wait()
+
+        def added(row, first, mask):
+            picked = [table[slots[row * 2 * pair + t]] for t in range(first, first + pair)]
+            return jnp.dot(mask, jnp.concatenate(picked, axis=0), preferred_element_type=jnp.float32)
+
+        def rows_of(row):
+            return pl.ds(pl.multiple_of(row * tile, tile), tile)
+
+        for r in range(many):
+            row = c * many + r
+            totals[rows_of(row), :] += added(row, 0, masks[row])
+        for r in range(many):
+            row = c * many + r
+
+            @pl.when(counts[row] > pair)
+            def _():
+                fetch(row).wait()
+                totals[rows_of(row), :] += added(row, pair, extra[row])
+
+        here = pl.ds(pl.multiple_of(c * items, items), items)
         part = jnp.concatenate([share[here, :]] * (width // tile), axis=1)
         mean = (totals[here, :] * part).astype(jnp.bfloat16)
-        joined = jnp.concatenate([features[here, :], mean], axis=1)
+        joined = jnp.concatenate([own[here, :], mean], axis=1)
         hidden = jnp.dot(joined, weight[...], preferred_element_type=jnp.float32)
         hidden = jnp.maximum(hidden, 0.0)
         squares = hidden * hidden
@@ -226,48 +242,57 @@
             jnp.concatenate([high, low], axis=1), ones, preferred_element_type=jnp.float32
         )
         scale = jnp.concatenate([lax.rsqrt(total + 1e-06)] * (out_width // tile), axis=1)
-        out[here, :] = (hidden * scale).astype(jnp.bfloat16)
+        done[here, :] = (hidden * scale).astype(jnp.bfloat16)
+        leave(c).start()
+        return carry
+
+    lax.fori_loop(0, chunks, chunk, 0)
+    for c in range(chunks):
+        leave(c).wait()
 
 
 def layer(slots, counts, froms, sums, left, more, degree, features, weight):
     blocks_here, tile, across = left.shape
-    width = features.shape[1]
+    items, width = features.shape
     out_width = weight.shape[1]
-    rows = 8 if blocks_here % 8 == 0 else 1
-    items = rows * tile
+    many = 4 if blocks_here % 4 == 0 else 1
+    chunks = blocks_here // many
     blocks_in_table = sum(piece.shape[0] for piece in froms)
+    cut = 4 if froms[0].shape[0] % 4 == 0 else 1
     return pl.pallas_call(
-        layer_kernel,
+        functools.partial(layer_kernel, many=many),
         grid_spec=pltpu.PrefetchScalarGridSpec(
             num_scalar_prefetch=2,
-            grid=(blocks_here // rows,),
-            in_specs=[pl.BlockSpec(memory_space=pl.ANY)] * (len(froms) + 1)
+            grid=(1,),
+            in_specs=[pl.BlockSpec(memory_space=pl.ANY)] * (len(froms) + 4)
             + [
-                pl.BlockSpec((items, width), lambda r, *_: (r, 0)),
-                pl.BlockSpec((rows, tile, across), lambda r, *_: (r, 0, 0)),
-                pl.BlockSpec((blocks_here, tile), lambda r, *_: (0, 0)),
-                pl.BlockSpec((items, width), lambda r, *_: (r, 0)),
-                pl.BlockSpec((2 * width, out_width), lambda r, *_: (0, 0)),
+                pl.BlockSpec((blocks_here, tile), lambda i, *_: (0, 0)),
+                pl.BlockSpec((2 * width, out_width), lambda i, *_: (0, 0)),
             ],
-            out_specs=pl.BlockSpec((items, out_width), lambda r, *_: (r, 0)),
+            out_specs=pl.BlockSpec(memory_space=pl.ANY),
             scratch_shapes=[
                 pltpu.VMEM((blocks_in_table, tile, width), jnp.bfloat16),
                 pltpu.VMEM((blocks_here, tile, across), jnp.bfloat16),
                 pltpu.VMEM((items, width), jnp.float32),
+                pltpu.VMEM((blocks_here, tile, across), jnp.bfloat16),
+                pltpu.VMEM((items, width), jnp.bfloat16),
                 pltpu.VMEM((items, tile), jnp.float32),
-                pltpu.SemaphoreType.DMA((len(froms),)),
+                pltpu.VMEM((items, out_width), jnp.bfloat16),
+                pltpu.SemaphoreType.DMA((len(froms), cut)),
                 pltpu.SemaphoreType.DMA((blocks_here,)),
+                pltpu.SemaphoreType.DMA((chunks, 3)),
+                pltpu.SemaphoreType.DMA((chunks,)),
             ],
         ),
-        out_shape=jax.ShapeDtypeStruct((blocks_here * tile, out_width), jnp.bfloat16),
+        out_shape=jax.ShapeDtypeStruct((items, out_width), jnp.bfloat16),
         compiler_params=pltpu.CompilerParams(vmem_limit_bytes=VMEM_LIMIT),
         cost_estimate=pl.CostEstimate(
-            flops=2 * blocks_here * tile * (across + 2 * width) * out_width,
-            bytes_accessed=blocks_here * tile * (4 * width + 2 * across + 2 * width + 2 * out_width),
-            transcendentals=blocks_here * tile,
+            flops=2 * items * (across + 2 * width) * out_width,
+            bytes_accessed=items * (4 * width + 2 * across + 2 * width + 2 * out_width),
+            transcendentals=items,
         ),
         name="sage_layer",
-    )(slots, counts, *froms, more, sums, left, degree, features, weight)
+    )(slots, counts, *froms, more, sums, left, features, degree, weight)
 
 
 def on_device(features, tile_cols, tile_masks, degree, weight):
@@ -300,7 +325,7 @@
     from_above, from_below = shift(local, down), shift(local, up)
 
     rounds = jnp.array([[0, 0, 1, 2], [1, 2, 0, 3], [2, 3, 1, 0], [3, 3, 2, 1]], jnp.int32)
-    line = pick_row(rounds, z) * plane + p
+    line = jnp.append(pick_row(rounds, z), PLANES - 1 - z) * plane + p
     blocks = jnp.arange(blocks_here, dtype=jnp.int32)
     wanted = line[:, None] * blocks_here + blocks[None, :]
     below = blocks[:, None] > blocks[None, :]
@@ -343,14 +368,12 @@
 
     always = jnp.zeros((1,), jnp.int32)
     inner = (~end).astype(jnp.int32)[None]
-    picked = choose(always, near, 0, [local], LIGHT)
+    picked = choose(always, [near], [0], [local], LIGHT)
     got = [exchange(picked)]
-    asked, _ = lax.optimization_barrier((asked, picked))
-    across = shift(asked, [(0, PLANES - 1), (PLANES - 1, 0)])
+    opposite, _ = lax.optimization_barrier((near[PLANES:], picked))
+    across = shift(opposite, [(0, PLANES - 1), (PLANES - 1, 0)])
     across, _, _ = lax.optimization_barrier((across, from_above, from_below))
-    opposite = jnp.swapaxes(seated(across, wanted[:1]), 0, 1)
-    middle = either(end.astype(jnp.int32)[None], near, opposite)
-    picked = choose(inner, middle, 0, [local, from_above], LIGHT)
+    picked = choose(inner, [across, near], [0, 1], [local, from_above], LIGHT)
     leaving, _ = lax.optimization_barrier((picked, got[0]))
     got.append(exchange(leaving))
     second_down = shift(from_above, down[:-1])
@@ -358,10 +381,10 @@
     leaving, _, _ = lax.optimization_barrier((got[1], second_down, second_up))
     crossed = shift(leaving, [(0, PLANES - 1), (PLANES - 1, 0)])
     near, _ = lax.optimization_barrier((near, picked))
-    below_or_above = (z > 0).astype(jnp.int32)[None]
-    got.append(exchange(choose(below_or_above, near, 2, [from_above, from_below], HEAVY)))
+    outer = (z > 0).astype(jnp.int32)[None]
+    got.append(exchange(choose(outer, [near], [2], [from_above, from_below], HEAVY)))
     beyond = (z >= PLANES // 2).astype(jnp.int32)[None]
-    got.append(exchange(choose(beyond, near, 3, [second_down, second_up], LIGHT)))
+    got.append(exchange(choose(beyond, [near], [3], [second_down, second_up], LIGHT)))
 
     sums, left, more = early(slots, late.reshape(-1), counts, [local] + got[:3], tile_masks)
     return layer(

time: 191 us -> 192 us (level); the launches traced: 188 us -> 191 us
  Pallas kernels: 48.6 us -> 51.4 us
    pallas_call x6 -> x5, Pallas kernels: 33 us -> 35.8 us  [the longest x1 18 us: layer(): pl.pallas_call(functools.partial(layer_kernel, many=many), grid_spec=pltp...]
    all_to_all x5, waiting for transfers between devices: 61.2 us -> 63.6 us  [exchange(): lax.all_to_all(x, 'rows', split_axis=0, concat_axis=0, axis_index_groups=...]
    ppermute x6, waiting for transfers between devices: 22.3 us -> 20 us  [shift(): return lax.ppermute(x, 'rows', pairs)]
  transfers between devices with their start and end apart: 11 -> 11, of which waited for: 6 -> 7; matrix products, arithmetic and copies ran while one was open for 5% -> 5% of each run, Pallas kernels for 18% -> 18%
where the time goes in v11:
time: 192 us; the launch traced here: 191 us
  waiting for transfers between devices  83.6 us (44%)
  Pallas kernels  51.4 us (27%)
  starting transfers between devices  44.8 us (23%)
  local copies, waits for them, and re-layouts  5.61 us (3%)
  other arithmetic  5.05 us (3%)
    all_to_all x5, waiting for transfers between devices, exchange(): lax.all_to_all(x, 'rows', split_axis=0, concat_axis=0, axis_index_groups=...  63.6 us
    ppermute x6, starting transfers between devices, shift(): return lax.ppermute(x, 'rows', pairs)  23 us
    all_to_all x5, starting transfers between devices, exchange(): lax.all_to_all(x, 'rows', split_axis=0, concat_axis=0, axis_index_groups=...  21.8 us
    ppermute x6, waiting for transfers between devices, shift(): return lax.ppermute(x, 'rows', pairs)  20 us
    pallas_call x1, Pallas kernels, layer(): pl.pallas_call(functools.partial(layer_kernel, many=many), grid_spec=pltp...  18 us
    pallas_call x4, Pallas kernels, choose(): pl.pallas_call(functools.partial(choose_kernel, turns=turns), grid_spec=p...  17.8 us
    pallas_call x1, Pallas kernels, early(): pl.pallas_call(early_kernel, grid_spec=pltpu.PrefetchScalarGridSpec(num_s...  15.6 us
  transfers between devices with their start and end apart: 11, of which 7 were waited for; matrix products, arithmetic and copies ran while one was open for 5% of the time, Pallas kernels for 18%

profile of v11, /device:TPU:0, one launch (start us, length us, event | category | flops | bytes accessed | tf_op | source)
XLA Modules:
  0.0 190.7 jit_solution(7645072214060500881)
XLA Ops:
  0.0 1.3 collective-permute-start.1
  1.3 6.9 %collective-permute-start.2 = (bf16[32,128,256]{2,1,0:T(8,128)(2,1)}, bf16[32,128,256]{2,1,0:T(8,128)(2,1)}, u32[]{:S(2)}, u32[]{:S(2)}) collective-permute-start(bf16[32,128,256]{2,1,0:T(8,128)(2,1)} %bitcast.11), channel_id=1, source_target_pairs={{0,8},{1,9},{2,10},{3,11},{4,12},{5,13},{6,14},{7,15},{8,16},{9,17... | collective-permute-start | bytes 6291464 | tf_op jit(solution)/shard_map/ppermute | solution.py:320
  8.2 0.8 copy.29
  9.0 0.1 reshape.236
  9.1 0.6 broadcast_in_dim.120
  9.7 4.2 %all-to-all-start = ((s32[8,1,192]{2,1,0:T(1,128)}), s32[8,1,192]{2,1,0:T(1,128)S(1)}, u32[]{:S(2)}, u32[]{:S(2)}) async-start(s32[8,1,192]{2,1,0:T(1,128)} %broadcast_in_dim.120), calls=%async_computation | async-start | bytes 16384 | tf_op jit(solution)/shard_map/all_to_all | solution.py:314
  13.9 0.8 select_reduce_fusion.5
  14.8 3.7 %all-to-all-done = s32[8,1,192]{2,1,0:T(1,128)S(1)} async-done(((s32[8,1,192]{2,1,0:T(1,128)}), s32[8,1,192]{2,1,0:T(1,128)S(1)}, u32[]{:S(2)}, u32[]{:S(2)}) %all-to-all-start) | async-done | bytes 6176 | tf_op jit(solution)/shard_map/all_to_all | solution.py:314
  18.5 0.9 compare_reduce_fusion
  19.4 0.7 select_reduce_fusion
  20.2 0.5 select_reduce_fusion.1
  20.7 0.7 copy.40
  21.4 4.5 %choose_blocks.4 = bf16[40,128,256]{2,1,0:T(8,128)(2,1)} custom-call(s32[1]{0:T(128)} %constant.94.clone.1.which, s32[5,8,5]{2,1,0:T(8,128)} %bitcast.16, bf16[32,128,256]{2,1,0:T(8,128)(2,1)} %bitcast.12), custom_call_target="tpu_custom_call" | custom-call | flops 10000000000 | bytes 5242880 | tf_op jit(solution)/shard_map/choose_blocks/pallas_call | solution.py:50
  26.0 4.4 %all-to-all-start.1 = ((bf16[40,128,256]{2,1,0:T(8,128)(2,1)}), bf16[40,128,256]{2,1,0:T(8,128)(2,1)}, u32[]{:S(2)}, u32[]{:S(2)}) async-start(bf16[40,128,256]{2,1,0:T(8,128)(2,1)} %choose_blocks.4), calls=%async_computation.1 | async-start | bytes 5242880 | tf_op jit(solution)/shard_map/all_to_all | solution.py:314
  30.4 0.7 slice.4
  31.1 3.2 %collective-permute-start = (s32[1,8,5]{2,1,0:T(8,128)S(1)}, s32[1,8,5]{2,1,0:T(8,128)S(1)}, u32[]{:S(2)}, u32[]{:S(2)}) collective-permute-start(s32[1,8,5]{2,1,0:T(8,128)S(1)} %slice.4), channel_id=1, source_target_pairs={{0,24},{1,25},{2,26},{3,27},{4,28},{5,29},{6,30},{7,31},{24,0},{25... | collective-permute-start | bytes 488 | tf_op jit(solution)/shard_map/ppermute | solution.py:320
  34.3 18.7 %collective-permute-done.refs_0_ = s32[1,8,5]{2,1,0:T(8,128)S(1)} collective-permute-done((s32[1,8,5]{2,1,0:T(8,128)S(1)}, s32[1,8,5]{2,1,0:T(8,128)S(1)}, u32[]{:S(2)}, u32[]{:S(2)}) %collective-permute-start) | collective-permute-done | bytes 192 | tf_op jit(solution)/shard_map/ppermute | solution.py:320
  53.0 0.6 copy-done
  53.6 4.5 %choose_blocks.5 = bf16[40,128,256]{2,1,0:T(8,128)(2,1)} custom-call(s32[1]{0:T(128)} %bitcast.which, s32[1,8,5]{2,1,0:T(8,128)} %copy-done, s32[5,8,5]{2,1,0:T(8,128)} %bitcast.18, bf16[32,128,256]{2,1,0:T(8,128)(2,1)} %bitcast.13, bf16[32,128,256]{2,1,0:T(8,128)(2,1)} %collective-permute-done.1.refs_3_.refs_1_), custom_call_target="tpu_custom_call" | custom-call | flops 10000000000 | bytes 5242880 | tf_op jit(solution)/shard_map/choose_blocks/pallas_call | solution.py:50
  58.1 1.3 collective-permute-start.3
  59.4 2.0 %collective-permute-start.4 = (bf16[32,128,256]{2,1,0:T(8,128)(2,1)}, bf16[32,128,256]{2,1,0:T(8,128)(2,1)}, u32[]{:S(2)}, u32[]{:S(2)}) collective-permute-start(bf16[32,128,256]{2,1,0:T(8,128)(2,1)} %collective-permute-done.2.refs_2_), channel_id=1, source_target_pairs={{8,16},{9,17},{10,18},{11,19},{12,20},{13,21},{14,22},{15,23},{16,... | collective-permute-start | bytes 6291464 | tf_op jit(solution)/shard_map/ppermute | solution.py:320
  61.4 1.3 all-to-all-done.1.refs_1_
  62.7 4.4 %all-to-all-start.2 = ((bf16[40,128,256]{2,1,0:T(8,128)(2,1)}), bf16[40,128,256]{2,1,0:T(8,128)(2,1)}, u32[]{:S(2)}, u32[]{:S(2)}) async-start(bf16[40,128,256]{2,1,0:T(8,128)(2,1)} %choose_blocks.5), calls=%async_computation.2 | async-start | bytes 5242880 | tf_op jit(solution)/shard_map/all_to_all | solution.py:314
  67.1 4.5 %choose_blocks.7 = bf16[40,128,256]{2,1,0:T(8,128)(2,1)} custom-call(s32[1]{0:T(128)} %bitcast.5.which, s32[5,8,5]{2,1,0:T(8,128)} %bitcast.19, bf16[32,128,256]{2,1,0:T(8,128)(2,1)} %collective-permute-done.1.refs_3_.refs_1_, bf16[32,128,256]{2,1,0:T(8,128)(2,1)} %collective-permute-done.2.refs_2_), custom_call_target="tpu_custom_call" | custom-call | flops 30000001024 | bytes 5242880 | tf_op jit(solution)/shard_map/choose_blocks/pallas_call | solution.py:50
  71.6 27.7 %all-to-all-done.2.refs_2_ = bf16[40,128,256]{2,1,0:T(8,128)(2,1)} async-done(((bf16[40,128,256]{2,1,0:T(8,128)(2,1)}), bf16[40,128,256]{2,1,0:T(8,128)(2,1)}, u32[]{:S(2)}, u32[]{:S(2)}) %all-to-all-start.2) | async-done | bytes 2621472 | tf_op jit(solution)/shard_map/all_to_all | solution.py:314
  99.4 4.4 %all-to-all-start.4 = ((bf16[40,128,256]{2,1,0:T(8,128)(2,1)}), bf16[40,128,256]{2,1,0:T(8,128)(2,1)}, u32[]{:S(2)}, u32[]{:S(2)}) async-start(bf16[40,128,256]{2,1,0:T(8,128)(2,1)} %choose_blocks.7), calls=%async_computation.4 | async-start | bytes 5242880 | tf_op jit(solution)/shard_map/all_to_all | solution.py:314
  103.8 0.1 select_reduce_fusion.4
  103.9 0.1 and.124
  104.0 0.1 eq.154
  104.1 0.2 fusion.1
  104.3 0.2 convert_reduce_fusion
  104.5 0.1 reduce_sum.86
  104.6 0.6 convert_reduce_fusion.1
  105.3 0.2 reduce_window_sum.11
  105.5 1.2 collective-permute-done.3.refs_1_
  106.7 8.4 %collective-permute-start.5 = (bf16[40,128,256]{2,1,0:T(8,128)(2,1)}, bf16[40,128,256]{2,1,0:T(8,128)(2,1)}, u32[]{:S(2)}, u32[]{:S(2)}) collective-permute-start(bf16[40,128,256]{2,1,0:T(8,128)(2,1)} %all-to-all-done.2.refs_2_), channel_id=1, source_target_pairs={{0,24},{1,25},{2,26},{3,27},{4,28},{5,29},{6,30},{7,31},{24,0},{25... | collective-permute-start | bytes 7864328 | tf_op jit(solution)/shard_map/ppermute | solution.py:320
  115.1 4.3 %choose_blocks.6 = bf16[40,128,256]{2,1,0:T(8,128)(2,1)} custom-call(s32[1]{0:T(128)} %bitcast.4.which, s32[5,8,5]{2,1,0:T(8,128)} %bitcast.20, bf16[32,128,256]{2,1,0:T(8,128)(2,1)} %collective-permute-done.3.refs_1_, bf16[32,128,256]{2,1,0:T(8,128)(2,1)} %collective-permute-done.4.refs_2_), custom_call_target="tpu_custom_call" | custom-call | flops 10000000000 | bytes 5242880 | tf_op jit(solution)/shard_map/choose_blocks/pallas_call | solution.py:50
  119.4 16.7 %all-to-all-done.4.refs_3_ = bf16[40,128,256]{2,1,0:T(8,128)(2,1)} async-done(((bf16[40,128,256]{2,1,0:T(8,128)(2,1)}), bf16[40,128,256]{2,1,0:T(8,128)(2,1)}, u32[]{:S(2)}, u32[]{:S(2)}) %all-to-all-start.4) | async-done | bytes 2621472 | tf_op jit(solution)/shard_map/all_to_all | solution.py:314
  136.0 4.4 %all-to-all-start.3 = ((bf16[40,128,256]{2,1,0:T(8,128)(2,1)}), bf16[40,128,256]{2,1,0:T(8,128)(2,1)}, u32[]{:S(2)}, u32[]{:S(2)}) async-start(bf16[40,128,256]{2,1,0:T(8,128)(2,1)} %choose_blocks.6), calls=%async_computation.3 | async-start | bytes 5242880 | tf_op jit(solution)/shard_map/all_to_all | solution.py:314
  140.4 0.1 copy.30
  140.7 0.1 copy.41
  140.8 0.7 reshape.239.late
  141.5 0.1 copy.37
  141.6 0.7 reshape.237.slots
  142.3 0.6 compare_select_fusion.slots
  142.9 15.6 %early_sums.1 = (f32[4096,256]{1,0:T(8,128)}, bf16[32,128,256]{2,1,0:T(8,128)(2,1)}, bf16[32,128,256]{2,1,0:T(8,128)(2,1)}) custom-call(s32[192]{0:T(256)} %compare_select_fusion.slots, s32[128]{0:T(128)} %reshape.239.late, s32[32]{0:T(128)} %get-tuple-element.25.counts, bf16[32,128,256]{2,1,0:T(8,128)(2,1)} %bitcast.14, ...), custom_call_target="tpu_custom_call" | custom-call | flops 20000000000 | bytes 28901376 | tf_op jit(solution)/shard_map/early_sums/pallas_call | solution.py:117
  158.5 14.2 %all-to-all-done.3.refs_1_ = bf16[40,128,256]{2,1,0:T(8,128)(2,1)} async-done(((bf16[40,128,256]{2,1,0:T(8,128)(2,1)}), bf16[40,128,256]{2,1,0:T(8,128)(2,1)}, u32[]{:S(2)}, u32[]{:S(2)}) %all-to-all-start.3) | async-done | bytes 2621472 | tf_op jit(solution)/shard_map/all_to_all | solution.py:314
  172.7 18.0 %sage_layer.1 = bf16[4096,256]{1,0:T(8,128)(2,1)} custom-call(s32[128]{0:T(128)} %reshape.237.slots, s32[32]{0:T(128)} %get-tuple-element.25.counts, bf16[40,128,256]{2,1,0:T(8,128)(2,1)} %collective-permute-done.5.refs_0_, bf16[40,128,256]{2,1,0:T(8,128)(2,1)} %all-to-all-done.3.refs_1_, bf16[32,128,256]{2,1,0:T(8,128)(2,1)} %get-tuple-element.18.refs_2_, ...), custom_call_target="tpu_custom_call" | custom-call | flops 1610612736 | bytes 10485760 | tf_op jit(solution)/shard_map/sage_layer/pallas_call | solution.py:262
  (21 shorter events, 0.4 us)
Async XLA Ops:
  0.0 53.0 %collective-permute-start.1 = (bf16[32,128,256]{2,1,0:T(8,128)(2,1)}, bf16[32,128,256]{2,1,0:T(8,128)(2,1)}, u32[]{:S(2)}, u32[]{:S(2)}) collective-permute-start(bf16[32,128,256]{2,1,0:T(8,128)(2,1)} %bitcast.10), channel_id=1, source_target_pairs={{8,0},{9,1},{10,2},{11,3},{12,4},{13,5},{14,6},{15,7},{16,8},{17,9... | collective-permute-start | bytes 6291464 | tf_op jit(solution)/shard_map/ppermute | solution.py:320
  1.3 51.7 %collective-permute-start.2 = (bf16[32,128,256]{2,1,0:T(8,128)(2,1)}, bf16[32,128,256]{2,1,0:T(8,128)(2,1)}, u32[]{:S(2)}, u32[]{:S(2)}) collective-permute-start(bf16[32,128,256]{2,1,0:T(8,128)(2,1)} %bitcast.11), channel_id=1, source_target_pairs={{0,8},{1,9},{2,10},{3,11},{4,12},{5,13},{6,14},{7,15},{8,16},{9,17... | collective-permute-start | bytes 6291464 | tf_op jit(solution)/shard_map/ppermute | solution.py:320
  9.7 8.9 %all-to-all-start = ((s32[8,1,192]{2,1,0:T(1,128)}), s32[8,1,192]{2,1,0:T(1,128)S(1)}, u32[]{:S(2)}, u32[]{:S(2)}) async-start(s32[8,1,192]{2,1,0:T(1,128)} %broadcast_in_dim.120), calls=%async_computation | async-start | bytes 16384 | tf_op jit(solution)/shard_map/all_to_all | solution.py:314
  26.0 36.7 %all-to-all-start.1 = ((bf16[40,128,256]{2,1,0:T(8,128)(2,1)}), bf16[40,128,256]{2,1,0:T(8,128)(2,1)}, u32[]{:S(2)}, u32[]{:S(2)}) async-start(bf16[40,128,256]{2,1,0:T(8,128)(2,1)} %choose_blocks.4), calls=%async_computation.1 | async-start | bytes 5242880 | tf_op jit(solution)/shard_map/all_to_all | solution.py:314
  31.1 21.9 %collective-permute-start = (s32[1,8,5]{2,1,0:T(8,128)S(1)}, s32[1,8,5]{2,1,0:T(8,128)S(1)}, u32[]{:S(2)}, u32[]{:S(2)}) collective-permute-start(s32[1,8,5]{2,1,0:T(8,128)S(1)} %slice.4), channel_id=1, source_target_pairs={{0,24},{1,25},{2,26},{3,27},{4,28},{5,29},{6,30},{7,31},{24,0},{25... | collective-permute-start | bytes 488 | tf_op jit(solution)/shard_map/ppermute | solution.py:320
  53.0 0.6 copy-start
  58.1 48.6 %collective-permute-start.3 = (bf16[32,128,256]{2,1,0:T(8,128)(2,1)}, bf16[32,128,256]{2,1,0:T(8,128)(2,1)}, u32[]{:S(2)}, u32[]{:S(2)}) collective-permute-start(bf16[32,128,256]{2,1,0:T(8,128)(2,1)} %collective-permute-done.1.refs_3_.refs_1_), channel_id=1, source_target_pairs={{8,0},{9,1},{10,2},{11,3},{12,4},{13,5},{14,6},{15,7},{16,8},{17,9... | collective-permute-start | bytes 6291464 | tf_op jit(solution)/shard_map/ppermute | solution.py:320
  59.4 47.3 %collective-permute-start.4 = (bf16[32,128,256]{2,1,0:T(8,128)(2,1)}, bf16[32,128,256]{2,1,0:T(8,128)(2,1)}, u32[]{:S(2)}, u32[]{:S(2)}) collective-permute-start(bf16[32,128,256]{2,1,0:T(8,128)(2,1)} %collective-permute-done.2.refs_2_), channel_id=1, source_target_pairs={{8,16},{9,17},{10,18},{11,19},{12,20},{13,21},{14,22},{15,23},{16,... | collective-permute-start | bytes 6291464 | tf_op jit(solution)/shard_map/ppermute | solution.py:320
  62.7 36.7 %all-to-all-start.2 = ((bf16[40,128,256]{2,1,0:T(8,128)(2,1)}), bf16[40,128,256]{2,1,0:T(8,128)(2,1)}, u32[]{:S(2)}, u32[]{:S(2)}) async-start(bf16[40,128,256]{2,1,0:T(8,128)(2,1)} %choose_blocks.5), calls=%async_computation.2 | async-start | bytes 5242880 | tf_op jit(solution)/shard_map/all_to_all | solution.py:314
  99.4 36.7 %all-to-all-start.4 = ((bf16[40,128,256]{2,1,0:T(8,128)(2,1)}), bf16[40,128,256]{2,1,0:T(8,128)(2,1)}, u32[]{:S(2)}, u32[]{:S(2)}) async-start(bf16[40,128,256]{2,1,0:T(8,128)(2,1)} %choose_blocks.7), calls=%async_computation.4 | async-start | bytes 5242880 | tf_op jit(solution)/shard_map/all_to_all | solution.py:314
  106.7 66.0 %collective-permute-start.5 = (bf16[40,128,256]{2,1,0:T(8,128)(2,1)}, bf16[40,128,256]{2,1,0:T(8,128)(2,1)}, u32[]{:S(2)}, u32[]{:S(2)}) collective-permute-start(bf16[40,128,256]{2,1,0:T(8,128)(2,1)} %all-to-all-done.2.refs_2_), channel_id=1, source_target_pairs={{0,24},{1,25},{2,26},{3,27},{4,28},{5,29},{6,30},{7,31},{24,0},{25... | collective-permute-start | bytes 7864328 | tf_op jit(solution)/shard_map/ppermute | solution.py:320
  136.0 36.7 %all-to-all-start.3 = ((bf16[40,128,256]{2,1,0:T(8,128)(2,1)}), bf16[40,128,256]{2,1,0:T(8,128)(2,1)}, u32[]{:S(2)}, u32[]{:S(2)}) async-start(bf16[40,128,256]{2,1,0:T(8,128)(2,1)} %choose_blocks.6), calls=%async_computation.3 | async-start | bytes 5242880 | tf_op jit(solution)/shard_map/all_to_all | solution.py:314

commit v12 on v9

--- a/solution.py
+++ b/solution.py
@@ -19,61 +19,52 @@
     return jnp.sum(jnp.where(jnp.arange(table.shape[0])[:, None] == z, table, 0), axis=0)
 
 
-def choose_kernel(which, ids, *refs):
-    *froms, out, held, in_sem, out_sem = refs
-    count, seats = out.shape[0], ids.shape[1]
+def choose_kernel(which, *refs, turns):
+    lists, (*froms, out, held, in_sems, out_sems) = refs[: len(turns)], refs[len(turns) :]
+    count, seats = out.shape[0], lists[0].shape[2]
+    groups = in_sems.shape[0]
+    size = count // groups
     for j, source in enumerate(froms):
+        ids, turn = lists[j % len(turns)], turns[j % len(turns)]
 
         @pl.when(which[0] == j)
         def _():
             for n in range(count):
-                block = source.at[ids[n // seats, n % seats]]
-                pltpu.make_async_copy(block, held.at[n], in_sem).start()
-
-    pltpu.make_async_copy(out, held, in_sem).wait()
-    leaving = pltpu.make_async_copy(held, out, out_sem)
-    leaving.start()
-    leaving.wait()
-
-
-def choose(which, ids, froms, flops):
-    out = (ids.shape[0] * ids.shape[1],) + froms[0].shape[1:]
+                block = source.at[ids[turn, n // seats, n % seats]]
+                pltpu.make_async_copy(block, held.at[n], in_sems.at[n // size]).start()
+
+    leaving = []
+    for g in range(groups):
+        here = pl.ds(g * size, size)
+        pltpu.make_async_copy(out.at[here], held.at[here], in_sems.at[g]).wait()
+        leaving.append(pltpu.make_async_copy(held.at[here], out.at[here], out_sems.at[g]))
+        leaving[-1].start()
+    for copy in leaving:
+        copy.wait()
+
+
+def choose(which, lists, turns, froms, flops):
+    out = (lists[0].shape[1] * lists[0].shape[2],) + froms[0].shape[1:]
     moved = out[0] * out[1] * out[2] * 2
+    groups = 4 if out[0] % 4 == 0 else 1
     return pl.pallas_call(
-        choose_kernel,
+        functools.partial(choose_kernel, turns=turns),
         grid_spec=pltpu.PrefetchScalarGridSpec(
-            num_scalar_prefetch=2,
+            num_scalar_prefetch=1 + len(lists),
             grid=(1,),
             in_specs=[pl.BlockSpec(memory_space=pltpu.HBM)] * len(froms),
             out_specs=pl.BlockSpec(memory_space=pltpu.HBM),
             scratch_shapes=[
                 pltpu.VMEM(out, froms[0].dtype),
-                pltpu.SemaphoreType.DMA,
-                pltpu.SemaphoreType.DMA,
+                pltpu.SemaphoreType.DMA((groups,)),
+                pltpu.SemaphoreType.DMA((groups,)),
             ],
         ),
         out_shape=jax.ShapeDtypeStruct(out, froms[0].dtype),
         compiler_params=pltpu.CompilerParams(vmem_limit_bytes=VMEM_LIMIT),
         cost_estimate=pl.CostEstimate(flops=flops, bytes_accessed=2 * moved, transcendentals=0),
         name="choose_blocks",
-    )(which, ids, *froms)
-
-
-def either_kernel(second, a, b, out):
-    out[...] = jnp.where(second[0] == 1, b[...], a[...])
-
-
-def either(second, a, b):
-    whole = pl.BlockSpec(a.shape, lambda i, s: (0, 0))
-    return pl.pallas_call(
-        either_kernel,
-        grid_spec=pltpu.PrefetchScalarGridSpec(
-            num_scalar_prefetch=1, grid=(1,), in_specs=[whole, whole], out_specs=whole
-        ),
-        out_shape=jax.ShapeDtypeStruct(a.shape, a.dtype),
-        cost_estimate=pl.CostEstimate(flops=HEAVY, bytes_accessed=0, transcendentals=0),
-        name="either_ids",
-    )(second, a, b)
+    )(which, *lists, *froms)
 
 
 def fill(pieces, table, sems):
@@ -84,8 +75,7 @@
         at += piece.shape[0]
     for copy in copies:
         copy.start()
-    for copy in copies:
-        copy.wait()
+    return copies
 
 
 def early_kernel(slots, late, counts, *refs):
@@ -98,7 +88,8 @@
     @pl.when(step == 0)
     def _():
         table[table.shape[0] - 1] = jnp.zeros((tile, width), table.dtype)
-        fill(froms, table, sems)
+        for copy in fill(froms, table, sems):
+            copy.wait()
 
     for r in range(rows):
         row = step * rows + r
@@ -158,7 +149,29 @@
     width = table.shape[2]
     spare = left.shape[2] // tile
     pair = min(2, spare)
-    pl.when(step == 0)(functools.partial(fill, froms, table, sems))
+
+    @pl.when(step == 0)
+    def _():
+        copies = fill(froms, table, sems)
+        column = lax.broadcasted_iota(jnp.int32, (tile, tile), 1)
+        diagonal = lax.broadcasted_iota(jnp.int32, (tile, tile), 0) == column
+        ones = jnp.ones((2 * tile, tile), jnp.bfloat16)
+        for first in range(0, degree.shape[0], rows):
+            spread = []
+            for row in range(first, first + rows):
+                count = degree[row : row + 1, :]
+                small = count & 7
+                halves = [
+                    jnp.where(diagonal, part.astype(jnp.float32), 0.0).astype(jnp.bfloat16)
+                    for part in (count - small, small)
+                ]
+                spread.append(jnp.concatenate(halves, axis=1))
+            share[first * tile : (first + rows) * tile, :] = 1.0 / jnp.dot(
+                jnp.concatenate(spread, axis=0), ones, preferred_element_type=jnp.float32
+            )
+        for copy in copies:
+            copy.wait()
+
 
     def added(r, first):
         ends = min(first + pair, spare)
@@ -178,26 +191,11 @@
             def _():
                 totals[here, :] += added(r, first)
 
-    column = lax.broadcasted_iota(jnp.int32, (tile, tile), 1)
-    diagonal = lax.broadcasted_iota(jnp.int32, (tile, tile), 0) == column
-    spread = []
-    for r in range(rows):
-        count = degree[pl.ds(step * rows + r, 1), :]
-        small = count & 7
-        halves = [
-            jnp.where(diagonal, part.astype(jnp.float32), 0.0).astype(jnp.bfloat16)
-            for part in (count - small, small)
-        ]
-        spread.append(jnp.concatenate(halves, axis=1))
-    ones = jnp.ones((2 * tile, tile), jnp.bfloat16)
-    share[...] = 1.0 / jnp.dot(
-        jnp.concatenate(spread, axis=0), ones, preferred_element_type=jnp.float32
-    )
-
     many = min(rows, 4) * tile
     for first in range(0, rows * tile, many):
         here = pl.ds(first, many)
-        part = jnp.concatenate([share[here, :]] * (width // tile), axis=1)
+        there = pl.ds(pl.multiple_of(step * rows * tile + first, tile), many)
+        part = jnp.concatenate([share[there, :]] * (width // tile), axis=1)
         mean = (totals[here, :] * part).astype(jnp.bfloat16)
         joined = jnp.concatenate([features[here, :], mean], axis=1)
         hidden = jnp.dot(joined, weight[...], preferred_element_type=jnp.float32)
@@ -230,7 +228,7 @@
             scratch_shapes=[
                 pltpu.VMEM((blocks_in_table, tile, width), jnp.bfloat16),
                 pltpu.VMEM((items, width), jnp.float32),
-                pltpu.VMEM((items, tile), jnp.float32),
+                pltpu.VMEM((blocks_here * tile, tile), jnp.float32),
                 pltpu.SemaphoreType.DMA((len(froms),)),
             ],
         ),
@@ -270,13 +268,11 @@
         return lax.ppermute(x, "rows", pairs)
 
     asked = exchange(jnp.broadcast_to(columns, (plane,) + columns.shape))
-    across = shift(asked, [(0, PLANES - 1), (PLANES - 1, 0)])
-    down = [(a, a - 1) for a in range(1, PLANES)]
-    up = [(a - 1, a) for a in range(1, PLANES)]
-    from_above, from_below = shift(local, down), shift(local, up)
-
-    rounds = jnp.array([[0, 0, 1, 2], [1, 2, 0, 3], [2, 3, 1, 0], [3, 3, 2, 1]], jnp.int32)
-    line = pick_row(rounds, z) * plane + p
+    swap, outward, inward = [(1, 2), (2, 1)], [(1, 0), (2, 3)], [(0, 1), (3, 2)]
+    beyond, near_out, near_in = shift(local, swap), shift(local, outward), shift(local, inward)
+
+    rounds = jnp.array([[0, 0, 1, 2], [1, 2, 0, 3], [2, 1, 3, 0], [3, 3, 2, 1]], jnp.int32)
+    line = jnp.append(pick_row(rounds, z), PLANES - 1 - z) * plane + p
     blocks = jnp.arange(blocks_here, dtype=jnp.int32)
     wanted = line[:, None] * blocks_here + blocks[None, :]
     below = blocks[:, None] > blocks[None, :]
@@ -288,8 +284,7 @@
         taken = (need[:, :, None, :] == 1) & (place[:, :, None, :] == seat[:, None])
         return jnp.sum(jnp.where(taken, blocks, 0), axis=3)
 
-    near = seated(asked, wanted)
-    ids = [near[:, k, :] for k in range(PLANES)]
+    near = jnp.swapaxes(seated(asked, wanted), 0, 1)
 
     owners, within = columns // blocks_here, columns % blocks_here
     positions = jnp.arange(columns.shape[0], dtype=jnp.int32)
@@ -297,7 +292,7 @@
     repeated = jnp.any(same & (positions[None, :] < positions[:, None]), axis=1)
     ahead = (owners[:, None] == owners[None, :]) & (columns[None, :] < columns[:, None])
     ranks = jnp.sum(ahead & ~repeated[None, :], axis=1, dtype=jnp.int32)
-    rounds_of = jnp.array([[0, 2, 3, 1], [2, 0, 1, 3], [3, 2, 0, 1], [1, 3, 2, 0]], jnp.int32)
+    rounds_of = jnp.array([[0, 2, 3, 1], [2, 0, 1, 3], [3, 1, 0, 2], [1, 3, 2, 0]], jnp.int32)
     their_plane = owners // plane
     among = their_plane[:, None] == jnp.arange(PLANES)
     turn = jnp.sum(jnp.where(among, pick_row(rounds_of, z)[None, :], 0), axis=1)
@@ -320,23 +315,20 @@
 
     always = jnp.zeros((1,), jnp.int32)
     inner = (~end).astype(jnp.int32)[None]
-    picked = choose(always, ids[0], [local], LIGHT)
+    picked = choose(always, [near], [0], [local], LIGHT)
     got = [exchange(picked)]
-    across, _, _ = lax.optimization_barrier((across, from_above, from_below))
-    opposite = seated(across, wanted[:1])[:, 0, :]
-    ids[1] = either(end.astype(jnp.int32)[None], near[:, 1, :], opposite)
-    picked = choose(inner, ids[1], [local, from_above], LIGHT)
+    opposite, _ = lax.optimization_barrier((near[PLANES:], picked))
+    across = shift(opposite, [(0, PLANES - 1), (PLANES - 1, 0)])
+    across, _, _, _ = lax.optimization_barrier((across, beyond, near_out, near_in))
+    picked = choose(inner, [across, near], [0, 1], [local, beyond], LIGHT)
     leaving, _ = lax.optimization_barrier((picked, got[0]))
     got.append(exchange(leaving))
-    second_down = shift(from_above, down[:-1])
-    second_up = shift(from_below, up[1:])
-    leaving, _, _ = lax.optimization_barrier((got[1], second_down, second_up))
+    far_out, far_in = shift(beyond, outward), shift(near_in, swap)
+    leaving, _, _ = lax.optimization_barrier((got[1], far_out, far_in))
     crossed = shift(leaving, [(0, PLANES - 1), (PLANES - 1, 0)])
-    ids[2], _ = lax.optimization_barrier((ids[2], picked))
-    picked = choose((z > 0).astype(jnp.int32)[None], ids[2], [from_above, from_below], HEAVY)
-    got.append(exchange(picked))
-    beyond = (z >= PLANES // 2).astype(jnp.int32)[None]
-    got.append(exchange(choose(beyond, ids[3], [second_down, second_up], LIGHT)))
+    near, _ = lax.optimization_barrier((near, picked))
+    got.append(exchange(choose(inner, [near], [2], [near_out, near_in], HEAVY)))
+    got.append(exchange(choose(inner, [near], [3], [far_out, far_in], LIGHT)))
 
     sums, left = early(slots, late.reshape(-1), counts, [local] + got[:3], tile_masks)
     return layer(

time: 192 us -> 191 us (level)
  the two profiles are of different devices: /device:TPU:0 before, /device:TPU:8 now
where the time goes in v12:
time: 191 us; the launch traced here: 189 us
  waiting for transfers between devices  92.7 us (49%)
  Pallas kernels  43.6 us (23%)
  starting transfers between devices  42.4 us (22%)
  other arithmetic  5.07 us (3%)
  local copies, waits for them, and re-layouts  4.99 us (3%)
    all_to_all x5, waiting for transfers between devices, exchange(): lax.all_to_all(x, 'rows', split_axis=0, concat_axis=0, axis_index_groups=...  70.4 us
    ppermute x7, waiting for transfers between devices, shift(): return lax.ppermute(x, 'rows', pairs)  22.3 us
    all_to_all x5, starting transfers between devices, exchange(): lax.all_to_all(x, 'rows', split_axis=0, concat_axis=0, axis_index_groups=...  21.3 us
    ppermute x7, starting transfers between devices, shift(): return lax.ppermute(x, 'rows', pairs)  21.1 us
    pallas_call x4, Pallas kernels, choose(): pl.pallas_call(functools.partial(choose_kernel, turns=turns), grid_spec=p...  17.9 us
    pallas_call x1, Pallas kernels, early(): pl.pallas_call(early_kernel, grid_spec=pltpu.PrefetchScalarGridSpec(num_s...  15 us
    pallas_call x1, Pallas kernels, layer(): pl.pallas_call(layer_kernel, grid_spec=pltpu.PrefetchScalarGridSpec(num_s...  10.7 us
  transfers between devices with their start and end apart: 12, of which 7 were waited for; matrix products, arithmetic and copies ran while one was open for 5% of the time, Pallas kernels for 17%

profile of v12, /device:TPU:8, one launch (start us, length us, event | category | flops | bytes accessed | tf_op | source)
XLA Modules:
  0.0 189.0 jit_solution(1745263551548142628)
XLA Ops:
  0.0 1.3 collective-permute-start.3
  1.3 7.3 %collective-permute-start.2 = (bf16[32,128,256]{2,1,0:T(8,128)(2,1)}, bf16[32,128,256]{2,1,0:T(8,128)(2,1)}, u32[]{:S(2)}, u32[]{:S(2)}) collective-permute-start(bf16[32,128,256]{2,1,0:T(8,128)(2,1)} %bitcast.9), channel_id=1, source_target_pairs={{8,0},{9,1},{10,2},{11,3},{12,4},{13,5},{14,6},{15,7},{16,24},{17,... | collective-permute-start | bytes 6291464 | tf_op jit(solution)/shard_map/ppermute | solution.py:268
  8.6 3.5 %collective-permute-start.1 = (bf16[32,128,256]{2,1,0:T(8,128)(2,1)}, bf16[32,128,256]{2,1,0:T(8,128)(2,1)}, u32[]{:S(2)}, u32[]{:S(2)}) collective-permute-start(bf16[32,128,256]{2,1,0:T(8,128)(2,1)} %bitcast.10), channel_id=1, source_target_pairs={{8,16},{9,17},{10,18},{11,19},{12,20},{13,21},{14,22},{15,23},{16,... | collective-permute-start | bytes 6291464 | tf_op jit(solution)/shard_map/ppermute | solution.py:268
  12.0 0.8 copy.29
  12.8 0.1 reshape.236
  12.9 0.6 broadcast_in_dim.110
  13.5 3.7 %all-to-all-start = ((s32[8,1,192]{2,1,0:T(1,128)}), s32[8,1,192]{2,1,0:T(1,128)S(1)}, u32[]{:S(2)}, u32[]{:S(2)}) async-start(s32[8,1,192]{2,1,0:T(1,128)} %broadcast_in_dim.110), calls=%async_computation | async-start | bytes 16384 | tf_op jit(solution)/shard_map/all_to_all | solution.py:262
  17.3 0.8 select_reduce_fusion.5
  18.2 3.7 %all-to-all-done = s32[8,1,192]{2,1,0:T(1,128)S(1)} async-done(((s32[8,1,192]{2,1,0:T(1,128)}), s32[8,1,192]{2,1,0:T(1,128)S(1)}, u32[]{:S(2)}, u32[]{:S(2)}) %all-to-all-start) | async-done | bytes 6176 | tf_op jit(solution)/shard_map/all_to_all | solution.py:262
  22.0 0.9 compare_reduce_fusion
  22.9 0.7 select_reduce_fusion
  23.6 0.5 select_reduce_fusion.1
  24.1 0.7 copy.40
  24.9 4.7 %choose_blocks.4 = bf16[40,128,256]{2,1,0:T(8,128)(2,1)} custom-call(s32[1]{0:T(128)} %constant.93.clone.1.which, s32[5,8,5]{2,1,0:T(8,128)} %bitcast.15, bf16[32,128,256]{2,1,0:T(8,128)(2,1)} %bitcast.11), custom_call_target="tpu_custom_call" | custom-call | flops 10000000000 | bytes 5242880 | tf_op jit(solution)/shard_map/choose_blocks/pallas_call | solution.py:50
  29.5 4.4 %all-to-all-start.1 = ((bf16[40,128,256]{2,1,0:T(8,128)(2,1)}), bf16[40,128,256]{2,1,0:T(8,128)(2,1)}, u32[]{:S(2)}, u32[]{:S(2)}) async-start(bf16[40,128,256]{2,1,0:T(8,128)(2,1)} %choose_blocks.4), calls=%async_computation.1 | async-start | bytes 5242880 | tf_op jit(solution)/shard_map/all_to_all | solution.py:262
  34.0 0.7 slice.4
  34.6 0.6 collective-permute-start
  35.3 14.3 %collective-permute-done.3.refs_2_ = bf16[32,128,256]{2,1,0:T(8,128)(2,1)} collective-permute-done((bf16[32,128,256]{2,1,0:T(8,128)(2,1)}, bf16[32,128,256]{2,1,0:T(8,128)(2,1)}, u32[]{:S(2)}, u32[]{:S(2)}) %collective-permute-start.3) | collective-permute-done | bytes 2097184 | tf_op jit(solution)/shard_map/ppermute | solution.py:268
  49.6 2.5 %collective-permute-done.2.refs_1_ = bf16[32,128,256]{2,1,0:T(8,128)(2,1)} collective-permute-done((bf16[32,128,256]{2,1,0:T(8,128)(2,1)}, bf16[32,128,256]{2,1,0:T(8,128)(2,1)}, u32[]{:S(2)}, u32[]{:S(2)}) %collective-permute-start.2) | collective-permute-done | bytes 2097184 | tf_op jit(solution)/shard_map/ppermute | solution.py:268
  52.2 5.5 %collective-permute-done.1.refs_3_ = bf16[32,128,256]{2,1,0:T(8,128)(2,1)} collective-permute-done((bf16[32,128,256]{2,1,0:T(8,128)(2,1)}, bf16[32,128,256]{2,1,0:T(8,128)(2,1)}, u32[]{:S(2)}, u32[]{:S(2)}) %collective-permute-start.1) | collective-permute-done | bytes 2097184 | tf_op jit(solution)/shard_map/ppermute | solution.py:268
  57.7 4.3 %choose_blocks.5 = bf16[40,128,256]{2,1,0:T(8,128)(2,1)} custom-call(s32[1]{0:T(128)} %bitcast.which, s32[1,8,5]{2,1,0:T(8,128)} %copy-done, s32[5,8,5]{2,1,0:T(8,128)} %bitcast.17, bf16[32,128,256]{2,1,0:T(8,128)(2,1)} %bitcast.12, bf16[32,128,256]{2,1,0:T(8,128)(2,1)} %collective-permute-done.1.refs_3_), custom_call_target="tpu_custom_call" | custom-call | flops 10000000000 | bytes 5242880 | tf_op jit(solution)/shard_map/choose_blocks/pallas_call | solution.py:50
  62.0 3.7 %collective-permute-start.5 = (bf16[32,128,256]{2,1,0:T(8,128)(2,1)}, bf16[32,128,256]{2,1,0:T(8,128)(2,1)}, u32[]{:S(2)}, u32[]{:S(2)}) collective-permute-start(bf16[32,128,256]{2,1,0:T(8,128)(2,1)} %collective-permute-done.3.refs_2_), channel_id=1, source_target_pairs={{8,16},{9,17},{10,18},{11,19},{12,20},{13,21},{14,22},{15,23},{16,... | collective-permute-start | bytes 6291464 | tf_op jit(solution)/shard_map/ppermute | solution.py:268
  65.6 2.6 %collective-permute-start.4 = (bf16[32,128,256]{2,1,0:T(8,128)(2,1)}, bf16[32,128,256]{2,1,0:T(8,128)(2,1)}, u32[]{:S(2)}, u32[]{:S(2)}) collective-permute-start(bf16[32,128,256]{2,1,0:T(8,128)(2,1)} %collective-permute-done.1.refs_3_), channel_id=1, source_target_pairs={{8,0},{9,1},{10,2},{11,3},{12,4},{13,5},{14,6},{15,7},{16,24},{17,... | collective-permute-start | bytes 6291464 | tf_op jit(solution)/shard_map/ppermute | solution.py:268
  68.2 4.4 %all-to-all-start.2 = ((bf16[40,128,256]{2,1,0:T(8,128)(2,1)}), bf16[40,128,256]{2,1,0:T(8,128)(2,1)}, u32[]{:S(2)}, u32[]{:S(2)}) async-start(bf16[40,128,256]{2,1,0:T(8,128)(2,1)} %choose_blocks.5), calls=%async_computation.2 | async-start | bytes 5242880 | tf_op jit(solution)/shard_map/all_to_all | solution.py:262
  72.6 4.5 %choose_blocks.7 = bf16[40,128,256]{2,1,0:T(8,128)(2,1)} custom-call(s32[1]{0:T(128)} %bitcast.which, s32[5,8,5]{2,1,0:T(8,128)} %bitcast.18, bf16[32,128,256]{2,1,0:T(8,128)(2,1)} %collective-permute-done.2.refs_1_, bf16[32,128,256]{2,1,0:T(8,128)(2,1)} %collective-permute-done.3.refs_2_), custom_call_target="tpu_custom_call" | custom-call | flops 30000001024 | bytes 5242880 | tf_op jit(solution)/shard_map/choose_blocks/pallas_call | solution.py:50
  77.2 27.7 %all-to-all-done.2.refs_2_ = bf16[40,128,256]{2,1,0:T(8,128)(2,1)} async-done(((bf16[40,128,256]{2,1,0:T(8,128)(2,1)}), bf16[40,128,256]{2,1,0:T(8,128)(2,1)}, u32[]{:S(2)}, u32[]{:S(2)}) %all-to-all-start.2) | async-done | bytes 2621472 | tf_op jit(solution)/shard_map/all_to_all | solution.py:262
  104.9 4.4 %all-to-all-start.4 = ((bf16[40,128,256]{2,1,0:T(8,128)(2,1)}), bf16[40,128,256]{2,1,0:T(8,128)(2,1)}, u32[]{:S(2)}, u32[]{:S(2)}) async-start(bf16[40,128,256]{2,1,0:T(8,128)(2,1)} %choose_blocks.7), calls=%async_computation.4 | async-start | bytes 5242880 | tf_op jit(solution)/shard_map/all_to_all | solution.py:262
  109.3 0.2 fusion.1
  109.5 0.1 select_reduce_fusion.4
  109.6 0.1 and.124
  109.7 0.1 eq.154
  109.9 0.2 convert_reduce_fusion
  110.1 0.1 reduce_sum.86
  110.2 0.7 convert_reduce_fusion.1
  110.9 0.2 reduce_window_sum.11
  111.0 2.1 %collective-permute-start.6 = (bf16[40,128,256]{2,1,0:T(8,128)(2,1)}, bf16[40,128,256]{2,1,0:T(8,128)(2,1)}, u32[]{:S(2)}, u32[]{:S(2)}) collective-permute-start(bf16[40,128,256]{2,1,0:T(8,128)(2,1)} %all-to-all-done.2.refs_2_), channel_id=1, source_target_pairs={{0,24},{1,25},{2,26},{3,27},{4,28},{5,29},{6,30},{7,31},{24,0},{25... | collective-permute-start | bytes 7864328 | tf_op jit(solution)/shard_map/ppermute | solution.py:268
  113.2 4.4 %choose_blocks.6 = bf16[40,128,256]{2,1,0:T(8,128)(2,1)} custom-call(s32[1]{0:T(128)} %bitcast.which, s32[5,8,5]{2,1,0:T(8,128)} %bitcast.19, bf16[32,128,256]{2,1,0:T(8,128)(2,1)} %collective-permute-done.4.refs_1_, bf16[32,128,256]{2,1,0:T(8,128)(2,1)} %collective-permute-done.5.refs_2_), custom_call_target="tpu_custom_call" | custom-call | flops 10000000000 | bytes 5242880 | tf_op jit(solution)/shard_map/choose_blocks/pallas_call | solution.py:50
  117.6 24.0 %all-to-all-done.4.refs_3_ = bf16[40,128,256]{2,1,0:T(8,128)(2,1)} async-done(((bf16[40,128,256]{2,1,0:T(8,128)(2,1)}), bf16[40,128,256]{2,1,0:T(8,128)(2,1)}, u32[]{:S(2)}, u32[]{:S(2)}) %all-to-all-start.4) | async-done | bytes 2621472 | tf_op jit(solution)/shard_map/all_to_all | solution.py:262
  141.6 4.4 %all-to-all-start.3 = ((bf16[40,128,256]{2,1,0:T(8,128)(2,1)}), bf16[40,128,256]{2,1,0:T(8,128)(2,1)}, u32[]{:S(2)}, u32[]{:S(2)}) async-start(bf16[40,128,256]{2,1,0:T(8,128)(2,1)} %choose_blocks.6), calls=%async_computation.3 | async-start | bytes 5242880 | tf_op jit(solution)/shard_map/all_to_all | solution.py:262
  146.0 0.1 copy.30
  146.3 0.1 copy.41
  146.4 0.6 reshape.239.late
  147.0 0.1 copy.37
  147.1 0.7 reshape.237.slots
  147.8 0.6 compare_select_fusion.slots
  148.4 15.0 %early_sums.1 = (f32[4096,256]{1,0:T(8,128)}, s8[32,128,512]{2,1,0:T(32,128)(4,1)}) custom-call(s32[192]{0:T(256)} %compare_select_fusion.slots, s32[128]{0:T(128)} %reshape.239.late, s32[32]{0:T(128)} %get-tuple-element.23.counts, bf16[32,128,256]{2,1,0:T(8,128)(2,1)} %bitcast.13, bf16[40,128,256]{2,1,0:T(8,128)(2,1)} %all-to-all-done.1.refs_1_, ...), custom_call_target="tpu_custom_call" | custom-call | flops 20000000000 | bytes 28901376 | tf_op jit(solution)/shard_map/early_sums/pallas_call | solution.py:115
  163.4 14.9 %all-to-all-done.3.refs_1_ = bf16[40,128,256]{2,1,0:T(8,128)(2,1)} async-done(((bf16[40,128,256]{2,1,0:T(8,128)(2,1)}), bf16[40,128,256]{2,1,0:T(8,128)(2,1)}, u32[]{:S(2)}, u32[]{:S(2)}) %all-to-all-start.3) | async-done | bytes 2621472 | tf_op jit(solution)/shard_map/all_to_all | solution.py:262
  178.3 10.7 %sage_layer.1 = bf16[4096,256]{1,0:T(8,128)(2,1)} custom-call(s32[128]{0:T(128)} %reshape.237.slots, s32[32]{0:T(128)} %get-tuple-element.23.counts, bf16[40,128,256]{2,1,0:T(8,128)(2,1)} %collective-permute-done.6.refs_0_, bf16[40,128,256]{2,1,0:T(8,128)(2,1)} %all-to-all-done.3.refs_1_, f32[4096,256]{1,0:T(8,128)} %get-tuple-element.17.refs_2_, ...), custom_call_target="tpu_custom_call" | custom-call | flops 2147483648 | bytes 10485760 | tf_op jit(solution)/shard_map/sage_layer/pallas_call | solution.py:214
  (23 shorter events, 0.4 us)
Async XLA Ops:
  0.0 49.6 %collective-permute-start.3 = (bf16[32,128,256]{2,1,0:T(8,128)(2,1)}, bf16[32,128,256]{2,1,0:T(8,128)(2,1)}, u32[]{:S(2)}, u32[]{:S(2)}) collective-permute-start(bf16[32,128,256]{2,1,0:T(8,128)(2,1)} %bitcast.8), channel_id=1, source_target_pairs={{0,8},{1,9},{2,10},{3,11},{4,12},{5,13},{6,14},{7,15},{24,16},{25,... | collective-permute-start | bytes 6291464 | tf_op jit(solution)/shard_map/ppermute | solution.py:268
  1.3 50.9 %collective-permute-start.2 = (bf16[32,128,256]{2,1,0:T(8,128)(2,1)}, bf16[32,128,256]{2,1,0:T(8,128)(2,1)}, u32[]{:S(2)}, u32[]{:S(2)}) collective-permute-start(bf16[32,128,256]{2,1,0:T(8,128)(2,1)} %bitcast.9), channel_id=1, source_target_pairs={{8,0},{9,1},{10,2},{11,3},{12,4},{13,5},{14,6},{15,7},{16,24},{17,... | collective-permute-start | bytes 6291464 | tf_op jit(solution)/shard_map/ppermute | solution.py:268
  8.6 49.1 %collective-permute-start.1 = (bf16[32,128,256]{2,1,0:T(8,128)(2,1)}, bf16[32,128,256]{2,1,0:T(8,128)(2,1)}, u32[]{:S(2)}, u32[]{:S(2)}) collective-permute-start(bf16[32,128,256]{2,1,0:T(8,128)(2,1)} %bitcast.10), channel_id=1, source_target_pairs={{8,16},{9,17},{10,18},{11,19},{12,20},{13,21},{14,22},{15,23},{16,... | collective-permute-start | bytes 6291464 | tf_op jit(solution)/shard_map/ppermute | solution.py:268
  13.5 8.4 %all-to-all-start = ((s32[8,1,192]{2,1,0:T(1,128)}), s32[8,1,192]{2,1,0:T(1,128)S(1)}, u32[]{:S(2)}, u32[]{:S(2)}) async-start(s32[8,1,192]{2,1,0:T(1,128)} %broadcast_in_dim.110), calls=%async_computation | async-start | bytes 16384 | tf_op jit(solution)/shard_map/all_to_all | solution.py:262
  29.5 38.7 %all-to-all-start.1 = ((bf16[40,128,256]{2,1,0:T(8,128)(2,1)}), bf16[40,128,256]{2,1,0:T(8,128)(2,1)}, u32[]{:S(2)}, u32[]{:S(2)}) async-start(bf16[40,128,256]{2,1,0:T(8,128)(2,1)} %choose_blocks.4), calls=%async_computation.1 | async-start | bytes 5242880 | tf_op jit(solution)/shard_map/all_to_all | solution.py:262
  34.6 0.7 collective-permute-start
  35.3 22.3 %copy-start = (s32[1,8,5]{2,1,0:T(8,128)}, s32[1,8,5]{2,1,0:T(8,128)S(1)}, u32[]{:S(2)}) copy-start(s32[1,8,5]{2,1,0:T(8,128)S(1)} %collective-permute-done.refs_0_) | copy-start | bytes 484
  62.0 49.1 %collective-permute-start.5 = (bf16[32,128,256]{2,1,0:T(8,128)(2,1)}, bf16[32,128,256]{2,1,0:T(8,128)(2,1)}, u32[]{:S(2)}, u32[]{:S(2)}) collective-permute-start(bf16[32,128,256]{2,1,0:T(8,128)(2,1)} %collective-permute-done.3.refs_2_), channel_id=1, source_target_pairs={{8,16},{9,17},{10,18},{11,19},{12,20},{13,21},{14,22},{15,23},{16,... | collective-permute-start | bytes 6291464 | tf_op jit(solution)/shard_map/ppermute | solution.py:268
  65.6 45.4 %collective-permute-start.4 = (bf16[32,128,256]{2,1,0:T(8,128)(2,1)}, bf16[32,128,256]{2,1,0:T(8,128)(2,1)}, u32[]{:S(2)}, u32[]{:S(2)}) collective-permute-start(bf16[32,128,256]{2,1,0:T(8,128)(2,1)} %collective-permute-done.1.refs_3_), channel_id=1, source_target_pairs={{8,0},{9,1},{10,2},{11,3},{12,4},{13,5},{14,6},{15,7},{16,24},{17,... | collective-permute-start | bytes 6291464 | tf_op jit(solution)/shard_map/ppermute | solution.py:268
  68.2 36.7 %all-to-all-start.2 = ((bf16[40,128,256]{2,1,0:T(8,128)(2,1)}), bf16[40,128,256]{2,1,0:T(8,128)(2,1)}, u32[]{:S(2)}, u32[]{:S(2)}) async-start(bf16[40,128,256]{2,1,0:T(8,128)(2,1)} %choose_blocks.5), calls=%async_computation.2 | async-start | bytes 5242880 | tf_op jit(solution)/shard_map/all_to_all | solution.py:262
  104.9 36.7 %all-to-all-start.4 = ((bf16[40,128,256]{2,1,0:T(8,128)(2,1)}), bf16[40,128,256]{2,1,0:T(8,128)(2,1)}, u32[]{:S(2)}, u32[]{:S(2)}) async-start(bf16[40,128,256]{2,1,0:T(8,128)(2,1)} %choose_blocks.7), calls=%async_computation.4 | async-start | bytes 5242880 | tf_op jit(solution)/shard_map/all_to_all | solution.py:262
  111.0 67.2 %collective-permute-start.6 = (bf16[40,128,256]{2,1,0:T(8,128)(2,1)}, bf16[40,128,256]{2,1,0:T(8,128)(2,1)}, u32[]{:S(2)}, u32[]{:S(2)}) collective-permute-start(bf16[40,128,256]{2,1,0:T(8,128)(2,1)} %all-to-all-done.2.refs_2_), channel_id=1, source_target_pairs={{0,24},{1,25},{2,26},{3,27},{4,28},{5,29},{6,30},{7,31},{24,0},{25... | collective-permute-start | bytes 7864328 | tf_op jit(solution)/shard_map/ppermute | solution.py:268
  141.6 36.7 %all-to-all-start.3 = ((bf16[40,128,256]{2,1,0:T(8,128)(2,1)}), bf16[40,128,256]{2,1,0:T(8,128)(2,1)}, u32[]{:S(2)}, u32[]{:S(2)}) async-start(bf16[40,128,256]{2,1,0:T(8,128)(2,1)} %choose_blocks.6), calls=%async_computation.3 | async-start | bytes 5242880 | tf_op jit(solution)/shard_map/all_to_all | solution.py:262

commit v13 on v12

--- a/solution.py
+++ b/solution.py
@@ -268,8 +268,8 @@
         return lax.ppermute(x, "rows", pairs)
 
     asked = exchange(jnp.broadcast_to(columns, (plane,) + columns.shape))
-    swap, outward, inward = [(1, 2), (2, 1)], [(1, 0), (2, 3)], [(0, 1), (3, 2)]
-    beyond, near_out, near_in = shift(local, swap), shift(local, outward), shift(local, inward)
+    swap, outward, beside = [(1, 2), (2, 1)], [(1, 0), (2, 3)], [(0, 1), (1, 0), (2, 3), (3, 2)]
+    near_by, beyond = shift(local, beside), shift(local, swap)
 
     rounds = jnp.array([[0, 0, 1, 2], [1, 2, 0, 3], [2, 1, 3, 0], [3, 3, 2, 1]], jnp.int32)
     line = jnp.append(pick_row(rounds, z), PLANES - 1 - z) * plane + p
@@ -319,15 +319,15 @@
     got = [exchange(picked)]
     opposite, _ = lax.optimization_barrier((near[PLANES:], picked))
     across = shift(opposite, [(0, PLANES - 1), (PLANES - 1, 0)])
-    across, _, _, _ = lax.optimization_barrier((across, beyond, near_out, near_in))
+    across, _, _ = lax.optimization_barrier((across, beyond, near_by))
     picked = choose(inner, [across, near], [0, 1], [local, beyond], LIGHT)
     leaving, _ = lax.optimization_barrier((picked, got[0]))
     got.append(exchange(leaving))
-    far_out, far_in = shift(beyond, outward), shift(near_in, swap)
+    far_out, far_in = shift(beyond, outward), shift(near_by, swap)
     leaving, _, _ = lax.optimization_barrier((got[1], far_out, far_in))
     crossed = shift(leaving, [(0, PLANES - 1), (PLANES - 1, 0)])
     near, _ = lax.optimization_barrier((near, picked))
-    got.append(exchange(choose(inner, [near], [2], [near_out, near_in], HEAVY)))
+    got.append(exchange(choose(always, [near], [2], [near_by], HEAVY)))
     got.append(exchange(choose(inner, [near], [3], [far_out, far_in], LIGHT)))
 
     sums, left = early(slots, late.reshape(-1), counts, [local] + got[:3], tile_masks)

time: 191 us -> 184 us (0.963)
  the two profiles are of different devices: /device:TPU:8 before, /device:TPU:0 now
where the time goes in v13:
time: 184 us; the launch traced here: 181 us
  waiting for transfers between devices  88.6 us (48%)
  Pallas kernels  43.9 us (24%)
  starting transfers between devices  37.7 us (20%)
  local copies, waits for them, and re-layouts  5.56 us (3%)
  other arithmetic  5.07 us (3%)
    all_to_all x5, waiting for transfers between devices, exchange(): lax.all_to_all(x, 'rows', split_axis=0, concat_axis=0, axis_index_groups=...  63.8 us
    ppermute x6, waiting for transfers between devices, shift(): return lax.ppermute(x, 'rows', pairs)  24.8 us
    all_to_all x5, starting transfers between devices, exchange(): lax.all_to_all(x, 'rows', split_axis=0, concat_axis=0, axis_index_groups=...  21.3 us
    pallas_call x4, Pallas kernels, choose(): pl.pallas_call(functools.partial(choose_kernel, turns=turns), grid_spec=p...  17.4 us
    ppermute x6, starting transfers between devices, shift(): return lax.ppermute(x, 'rows', pairs)  16.3 us
    pallas_call x1, Pallas kernels, early(): pl.pallas_call(early_kernel, grid_spec=pltpu.PrefetchScalarGridSpec(num_s...  15 us
    pallas_call x1, Pallas kernels, layer(): pl.pallas_call(layer_kernel, grid_spec=pltpu.PrefetchScalarGridSpec(num_s...  11.5 us
  transfers between devices with their start and end apart: 11, of which 6 were waited for; matrix products, arithmetic and copies ran while one was open for 6% of the time, Pallas kernels for 18%

profile of v13, /device:TPU:0, one launch (start us, length us, event | category | flops | bytes accessed | tf_op | source)
XLA Modules:
  0.0 181.1 jit_solution(131235216126398703)
XLA Ops:
  0.0 3.0 %collective-permute-start.2 = (bf16[32,128,256]{2,1,0:T(8,128)(2,1)}, bf16[32,128,256]{2,1,0:T(8,128)(2,1)}, u32[]{:S(2)}, u32[]{:S(2)}) collective-permute-start(bf16[32,128,256]{2,1,0:T(8,128)(2,1)} %bitcast.8), channel_id=1, source_target_pairs={{0,8},{1,9},{2,10},{3,11},{4,12},{5,13},{6,14},{7,15},{8,0},{9,1},... | collective-permute-start | bytes 6291464 | tf_op jit(solution)/shard_map/ppermute | solution.py:268
  3.0 2.0 %collective-permute-start.1 = (bf16[32,128,256]{2,1,0:T(8,128)(2,1)}, bf16[32,128,256]{2,1,0:T(8,128)(2,1)}, u32[]{:S(2)}, u32[]{:S(2)}) collective-permute-start(bf16[32,128,256]{2,1,0:T(8,128)(2,1)} %bitcast.9), channel_id=1, source_target_pairs={{8,16},{9,17},{10,18},{11,19},{12,20},{13,21},{14,22},{15,23},{16,... | collective-permute-start | bytes 6291464 | tf_op jit(solution)/shard_map/ppermute | solution.py:268
  5.0 0.8 copy.29
  5.8 0.1 reshape.236
  5.9 0.6 broadcast_in_dim.110
  6.5 3.7 %all-to-all-start = ((s32[8,1,192]{2,1,0:T(1,128)}), s32[8,1,192]{2,1,0:T(1,128)S(1)}, u32[]{:S(2)}, u32[]{:S(2)}) async-start(s32[8,1,192]{2,1,0:T(1,128)} %broadcast_in_dim.110), calls=%async_computation | async-start | bytes 16384 | tf_op jit(solution)/shard_map/all_to_all | solution.py:262
  10.2 0.8 select_reduce_fusion.5
  11.0 0.1 fusion.13
  11.2 3.7 %all-to-all-done = s32[8,1,192]{2,1,0:T(1,128)S(1)} async-done(((s32[8,1,192]{2,1,0:T(1,128)}), s32[8,1,192]{2,1,0:T(1,128)S(1)}, u32[]{:S(2)}, u32[]{:S(2)}) %all-to-all-start) | async-done | bytes 6176 | tf_op jit(solution)/shard_map/all_to_all | solution.py:262
  14.9 0.9 compare_reduce_fusion
  15.8 0.7 select_reduce_fusion
  16.6 0.5 select_reduce_fusion.1
  17.1 0.7 copy.40
  17.8 4.3 %choose_blocks.4 = bf16[40,128,256]{2,1,0:T(8,128)(2,1)} custom-call(s32[1]{0:T(128)} %constant.93.clone.1.which, s32[5,8,5]{2,1,0:T(8,128)} %bitcast.14, bf16[32,128,256]{2,1,0:T(8,128)(2,1)} %bitcast.10), custom_call_target="tpu_custom_call" | custom-call | flops 10000000000 | bytes 5242880 | tf_op jit(solution)/shard_map/choose_blocks/pallas_call | solution.py:50
  22.1 4.4 %all-to-all-start.1 = ((bf16[40,128,256]{2,1,0:T(8,128)(2,1)}), bf16[40,128,256]{2,1,0:T(8,128)(2,1)}, u32[]{:S(2)}, u32[]{:S(2)}) async-start(bf16[40,128,256]{2,1,0:T(8,128)(2,1)} %choose_blocks.4), calls=%async_computation.1 | async-start | bytes 5242880 | tf_op jit(solution)/shard_map/all_to_all | solution.py:262
  26.5 0.7 slice.4
  27.2 4.4 %collective-permute-start = (s32[1,8,5]{2,1,0:T(8,128)S(1)}, s32[1,8,5]{2,1,0:T(8,128)S(1)}, u32[]{:S(2)}, u32[]{:S(2)}) collective-permute-start(s32[1,8,5]{2,1,0:T(8,128)S(1)} %slice.4), channel_id=1, source_target_pairs={{0,24},{1,25},{2,26},{3,27},{4,28},{5,29},{6,30},{7,31},{24,0},{25... | collective-permute-start | bytes 488 | tf_op jit(solution)/shard_map/ppermute | solution.py:268
  31.7 19.6 %collective-permute-done.refs_0_ = s32[1,8,5]{2,1,0:T(8,128)S(1)} collective-permute-done((s32[1,8,5]{2,1,0:T(8,128)S(1)}, s32[1,8,5]{2,1,0:T(8,128)S(1)}, u32[]{:S(2)}, u32[]{:S(2)}) %collective-permute-start) | collective-permute-done | bytes 192 | tf_op jit(solution)/shard_map/ppermute | solution.py:268
  51.3 0.6 copy-done
  51.8 4.4 %choose_blocks.5 = bf16[40,128,256]{2,1,0:T(8,128)(2,1)} custom-call(s32[1]{0:T(128)} %bitcast.which, s32[1,8,5]{2,1,0:T(8,128)} %copy-done, s32[5,8,5]{2,1,0:T(8,128)} %bitcast.16, bf16[32,128,256]{2,1,0:T(8,128)(2,1)} %bitcast.11, bf16[32,128,256]{2,1,0:T(8,128)(2,1)} %collective-permute-done.1.refs_3_), custom_call_target="tpu_custom_call" | custom-call | flops 10000000000 | bytes 5242880 | tf_op jit(solution)/shard_map/choose_blocks/pallas_call | solution.py:50
  56.2 2.0 %collective-permute-start.4 = (bf16[32,128,256]{2,1,0:T(8,128)(2,1)}, bf16[32,128,256]{2,1,0:T(8,128)(2,1)}, u32[]{:S(2)}, u32[]{:S(2)}) collective-permute-start(bf16[32,128,256]{2,1,0:T(8,128)(2,1)} %collective-permute-done.2.refs_1_), channel_id=1, source_target_pairs={{8,16},{9,17},{10,18},{11,19},{12,20},{13,21},{14,22},{15,23},{16,... | collective-permute-start | bytes 6291464 | tf_op jit(solution)/shard_map/ppermute | solution.py:268
  58.2 1.3 collective-permute-start.3
  59.5 4.4 %all-to-all-start.2 = ((bf16[40,128,256]{2,1,0:T(8,128)(2,1)}), bf16[40,128,256]{2,1,0:T(8,128)(2,1)}, u32[]{:S(2)}, u32[]{:S(2)}) async-start(bf16[40,128,256]{2,1,0:T(8,128)(2,1)} %choose_blocks.5), calls=%async_computation.2 | async-start | bytes 5242880 | tf_op jit(solution)/shard_map/all_to_all | solution.py:262
  63.9 4.3 %choose_blocks.7 = bf16[40,128,256]{2,1,0:T(8,128)(2,1)} custom-call(s32[1]{0:T(128)} %constant.93.clone.1.which, s32[5,8,5]{2,1,0:T(8,128)} %bitcast.17, bf16[32,128,256]{2,1,0:T(8,128)(2,1)} %collective-permute-done.2.refs_1_), custom_call_target="tpu_custom_call" | custom-call | flops 30000001024 | bytes 5242880 | tf_op jit(solution)/shard_map/choose_blocks/pallas_call | solution.py:50
  68.2 28.0 %all-to-all-done.2.refs_2_ = bf16[40,128,256]{2,1,0:T(8,128)(2,1)} async-done(((bf16[40,128,256]{2,1,0:T(8,128)(2,1)}), bf16[40,128,256]{2,1,0:T(8,128)(2,1)}, u32[]{:S(2)}, u32[]{:S(2)}) %all-to-all-start.2) | async-done | bytes 2621472 | tf_op jit(solution)/shard_map/all_to_all | solution.py:262
  96.2 4.4 %all-to-all-start.4 = ((bf16[40,128,256]{2,1,0:T(8,128)(2,1)}), bf16[40,128,256]{2,1,0:T(8,128)(2,1)}, u32[]{:S(2)}, u32[]{:S(2)}) async-start(bf16[40,128,256]{2,1,0:T(8,128)(2,1)} %choose_blocks.7), calls=%async_computation.4 | async-start | bytes 5242880 | tf_op jit(solution)/shard_map/all_to_all | solution.py:262
  100.6 0.2 fusion.1
  100.8 0.1 select_reduce_fusion.4
  100.9 0.1 and.124
  101.0 0.1 eq.154
  101.2 0.2 convert_reduce_fusion
  101.4 0.1 reduce_sum.86
  101.5 0.7 convert_reduce_fusion.1
  102.2 0.2 reduce_window_sum.11
  102.3 5.3 %collective-permute-done.3.refs_1_ = bf16[32,128,256]{2,1,0:T(8,128)(2,1)} collective-permute-done((bf16[32,128,256]{2,1,0:T(8,128)(2,1)}, bf16[32,128,256]{2,1,0:T(8,128)(2,1)}, u32[]{:S(2)}, u32[]{:S(2)}) %collective-permute-start.3) | collective-permute-done | bytes 2097184 | tf_op jit(solution)/shard_map/ppermute | solution.py:268
  107.6 3.6 %collective-permute-start.5 = (bf16[40,128,256]{2,1,0:T(8,128)(2,1)}, bf16[40,128,256]{2,1,0:T(8,128)(2,1)}, u32[]{:S(2)}, u32[]{:S(2)}) collective-permute-start(bf16[40,128,256]{2,1,0:T(8,128)(2,1)} %all-to-all-done.2.refs_2_), channel_id=1, source_target_pairs={{0,24},{1,25},{2,26},{3,27},{4,28},{5,29},{6,30},{7,31},{24,0},{25... | collective-permute-start | bytes 7864328 | tf_op jit(solution)/shard_map/ppermute | solution.py:268
  111.2 4.4 %choose_blocks.6 = bf16[40,128,256]{2,1,0:T(8,128)(2,1)} custom-call(s32[1]{0:T(128)} %bitcast.which, s32[5,8,5]{2,1,0:T(8,128)} %bitcast.18, bf16[32,128,256]{2,1,0:T(8,128)(2,1)} %collective-permute-done.3.refs_1_, bf16[32,128,256]{2,1,0:T(8,128)(2,1)} %collective-permute-done.4.refs_2_), custom_call_target="tpu_custom_call" | custom-call | flops 10000000000 | bytes 5242880 | tf_op jit(solution)/shard_map/choose_blocks/pallas_call | solution.py:50
  115.6 17.2 %all-to-all-done.4.refs_3_ = bf16[40,128,256]{2,1,0:T(8,128)(2,1)} async-done(((bf16[40,128,256]{2,1,0:T(8,128)(2,1)}), bf16[40,128,256]{2,1,0:T(8,128)(2,1)}, u32[]{:S(2)}, u32[]{:S(2)}) %all-to-all-start.4) | async-done | bytes 2621472 | tf_op jit(solution)/shard_map/all_to_all | solution.py:262
  132.9 4.4 %all-to-all-start.3 = ((bf16[40,128,256]{2,1,0:T(8,128)(2,1)}), bf16[40,128,256]{2,1,0:T(8,128)(2,1)}, u32[]{:S(2)}, u32[]{:S(2)}) async-start(bf16[40,128,256]{2,1,0:T(8,128)(2,1)} %choose_blocks.6), calls=%async_computation.3 | async-start | bytes 5242880 | tf_op jit(solution)/shard_map/all_to_all | solution.py:262
  137.3 0.1 copy.30
  137.6 0.1 copy.41
  137.7 0.6 reshape.239.late
  138.3 0.1 copy.37
  138.4 0.7 reshape.237.slots
  139.1 0.6 compare_select_fusion.slots
  139.7 15.0 %early_sums.1 = (f32[4096,256]{1,0:T(8,128)}, s8[32,128,512]{2,1,0:T(32,128)(4,1)}) custom-call(s32[192]{0:T(256)} %compare_select_fusion.slots, s32[128]{0:T(128)} %reshape.239.late, s32[32]{0:T(128)} %get-tuple-element.23.counts, bf16[32,128,256]{2,1,0:T(8,128)(2,1)} %bitcast.12, bf16[40,128,256]{2,1,0:T(8,128)(2,1)} %all-to-all-done.1.refs_1_, ...), custom_call_target="tpu_custom_call" | custom-call | flops 20000000000 | bytes 28901376 | tf_op jit(solution)/shard_map/early_sums/pallas_call | solution.py:115
  154.7 14.9 %all-to-all-done.3.refs_1_ = bf16[40,128,256]{2,1,0:T(8,128)(2,1)} async-done(((bf16[40,128,256]{2,1,0:T(8,128)(2,1)}), bf16[40,128,256]{2,1,0:T(8,128)(2,1)}, u32[]{:S(2)}, u32[]{:S(2)}) %all-to-all-start.3) | async-done | bytes 2621472 | tf_op jit(solution)/shard_map/all_to_all | solution.py:262
  169.6 11.5 %sage_layer.1 = bf16[4096,256]{1,0:T(8,128)(2,1)} custom-call(s32[128]{0:T(128)} %reshape.237.slots, s32[32]{0:T(128)} %get-tuple-element.23.counts, bf16[40,128,256]{2,1,0:T(8,128)(2,1)} %collective-permute-done.5.refs_0_, bf16[40,128,256]{2,1,0:T(8,128)(2,1)} %all-to-all-done.3.refs_1_, f32[4096,256]{1,0:T(8,128)} %get-tuple-element.17.refs_2_, ...), custom_call_target="tpu_custom_call" | custom-call | flops 2147483648 | bytes 10485760 | tf_op jit(solution)/shard_map/sage_layer/pallas_call | solution.py:214
  (21 shorter events, 0.4 us)
Async XLA Ops:
  0.0 51.2 %collective-permute-start.2 = (bf16[32,128,256]{2,1,0:T(8,128)(2,1)}, bf16[32,128,256]{2,1,0:T(8,128)(2,1)}, u32[]{:S(2)}, u32[]{:S(2)}) collective-permute-start(bf16[32,128,256]{2,1,0:T(8,128)(2,1)} %bitcast.8), channel_id=1, source_target_pairs={{0,8},{1,9},{2,10},{3,11},{4,12},{5,13},{6,14},{7,15},{8,0},{9,1},... | collective-permute-start | bytes 6291464 | tf_op jit(solution)/shard_map/ppermute | solution.py:268
  3.0 48.2 %collective-permute-start.1 = (bf16[32,128,256]{2,1,0:T(8,128)(2,1)}, bf16[32,128,256]{2,1,0:T(8,128)(2,1)}, u32[]{:S(2)}, u32[]{:S(2)}) collective-permute-start(bf16[32,128,256]{2,1,0:T(8,128)(2,1)} %bitcast.9), channel_id=1, source_target_pairs={{8,16},{9,17},{10,18},{11,19},{12,20},{13,21},{14,22},{15,23},{16,... | collective-permute-start | bytes 6291464 | tf_op jit(solution)/shard_map/ppermute | solution.py:268
  6.5 8.4 %all-to-all-start = ((s32[8,1,192]{2,1,0:T(1,128)}), s32[8,1,192]{2,1,0:T(1,128)S(1)}, u32[]{:S(2)}, u32[]{:S(2)}) async-start(s32[8,1,192]{2,1,0:T(1,128)} %broadcast_in_dim.110), calls=%async_computation | async-start | bytes 16384 | tf_op jit(solution)/shard_map/all_to_all | solution.py:262
  22.1 37.4 %all-to-all-start.1 = ((bf16[40,128,256]{2,1,0:T(8,128)(2,1)}), bf16[40,128,256]{2,1,0:T(8,128)(2,1)}, u32[]{:S(2)}, u32[]{:S(2)}) async-start(bf16[40,128,256]{2,1,0:T(8,128)(2,1)} %choose_blocks.4), calls=%async_computation.1 | async-start | bytes 5242880 | tf_op jit(solution)/shard_map/all_to_all | solution.py:262
  27.2 24.0 %collective-permute-start = (s32[1,8,5]{2,1,0:T(8,128)S(1)}, s32[1,8,5]{2,1,0:T(8,128)S(1)}, u32[]{:S(2)}, u32[]{:S(2)}) collective-permute-start(s32[1,8,5]{2,1,0:T(8,128)S(1)} %slice.4), channel_id=1, source_target_pairs={{0,24},{1,25},{2,26},{3,27},{4,28},{5,29},{6,30},{7,31},{24,0},{25... | collective-permute-start | bytes 488 | tf_op jit(solution)/shard_map/ppermute | solution.py:268
  51.2 0.6 copy-start
  56.2 46.1 %collective-permute-start.4 = (bf16[32,128,256]{2,1,0:T(8,128)(2,1)}, bf16[32,128,256]{2,1,0:T(8,128)(2,1)}, u32[]{:S(2)}, u32[]{:S(2)}) collective-permute-start(bf16[32,128,256]{2,1,0:T(8,128)(2,1)} %collective-permute-done.2.refs_1_), channel_id=1, source_target_pairs={{8,16},{9,17},{10,18},{11,19},{12,20},{13,21},{14,22},{15,23},{16,... | collective-permute-start | bytes 6291464 | tf_op jit(solution)/shard_map/ppermute | solution.py:268
  58.2 49.4 %collective-permute-start.3 = (bf16[32,128,256]{2,1,0:T(8,128)(2,1)}, bf16[32,128,256]{2,1,0:T(8,128)(2,1)}, u32[]{:S(2)}, u32[]{:S(2)}) collective-permute-start(bf16[32,128,256]{2,1,0:T(8,128)(2,1)} %collective-permute-done.1.refs_3_), channel_id=1, source_target_pairs={{8,0},{9,1},{10,2},{11,3},{12,4},{13,5},{14,6},{15,7},{16,24},{17,... | collective-permute-start | bytes 6291464 | tf_op jit(solution)/shard_map/ppermute | solution.py:268
  59.5 36.7 %all-to-all-start.2 = ((bf16[40,128,256]{2,1,0:T(8,128)(2,1)}), bf16[40,128,256]{2,1,0:T(8,128)(2,1)}, u32[]{:S(2)}, u32[]{:S(2)}) async-start(bf16[40,128,256]{2,1,0:T(8,128)(2,1)} %choose_blocks.5), calls=%async_computation.2 | async-start | bytes 5242880 | tf_op jit(solution)/shard_map/all_to_all | solution.py:262
  96.2 36.7 %all-to-all-start.4 = ((bf16[40,128,256]{2,1,0:T(8,128)(2,1)}), bf16[40,128,256]{2,1,0:T(8,128)(2,1)}, u32[]{:S(2)}, u32[]{:S(2)}) async-start(bf16[40,128,256]{2,1,0:T(8,128)(2,1)} %choose_blocks.7), calls=%async_computation.4 | async-start | bytes 5242880 | tf_op jit(solution)/shard_map/all_to_all | solution.py:262
  107.6 62.0 %collective-permute-start.5 = (bf16[40,128,256]{2,1,0:T(8,128)(2,1)}, bf16[40,128,256]{2,1,0:T(8,128)(2,1)}, u32[]{:S(2)}, u32[]{:S(2)}) collective-permute-start(bf16[40,128,256]{2,1,0:T(8,128)(2,1)} %all-to-all-done.2.refs_2_), channel_id=1, source_target_pairs={{0,24},{1,25},{2,26},{3,27},{4,28},{5,29},{6,30},{7,31},{24,0},{25... | collective-permute-start | bytes 7864328 | tf_op jit(solution)/shard_map/ppermute | solution.py:268
  132.9 36.7 %all-to-all-start.3 = ((bf16[40,128,256]{2,1,0:T(8,128)(2,1)}), bf16[40,128,256]{2,1,0:T(8,128)(2,1)}, u32[]{:S(2)}, u32[]{:S(2)}) async-start(bf16[40,128,256]{2,1,0:T(8,128)(2,1)} %choose_blocks.6), calls=%async_computation.3 | async-start | bytes 5242880 | tf_op jit(solution)/shard_map/all_to_all | solution.py:262

commit v14 on v13

--- a/solution.py
+++ b/solution.py
@@ -11,6 +11,7 @@
 PLANES = 4
 HEAVY = 3 * 10**10
 LIGHT = 10**10
+CUT = 4
 
 VMEM_LIMIT = 62 * 1024 * 1024
 
@@ -67,11 +68,13 @@
     )(which, *lists, *froms)
 
 
-def fill(pieces, table, sems):
-    copies, at = [], 0
+def fill(pieces, table, sems, at=0):
+    copies, cut = [], sems.shape[1]
     for n, piece in enumerate(pieces):
-        here = table.at[pl.ds(at, piece.shape[0])]
-        copies.append(pltpu.make_async_copy(piece, here, sems.at[n]))
+        size = piece.shape[0] // cut
+        for c in range(cut):
+            here = table.at[pl.ds(at + c * size, size)]
+            copies.append(pltpu.make_async_copy(piece.at[pl.ds(c * size, size)], here, sems.at[n, c]))
         at += piece.shape[0]
     for copy in copies:
         copy.start()
@@ -125,7 +128,7 @@
             ],
             scratch_shapes=[
                 pltpu.VMEM((blocks_in_table, tile, width), jnp.bfloat16),
-                pltpu.SemaphoreType.DMA((len(froms),)),
+                pltpu.SemaphoreType.DMA((len(froms), CUT)),
             ],
         ),
         out_shape=[
@@ -142,8 +145,8 @@
     )(slots, late, counts, *froms, tile_masks)
 
 
-def layer_kernel(slots, counts, *refs):
-    *froms, sums, left, degree, features, weight, out, table, totals, share, sems = refs
+def layer_kernel(slots, counts, end, crossed, last, *refs):
+    sums, left, degree, features, weight, out, table, totals, share, sems, far_sems = refs
     step = pl.program_id(0)
     rows, tile = left.shape[:2]
     width = table.shape[2]
@@ -152,7 +155,17 @@
 
     @pl.when(step == 0)
     def _():
-        copies = fill(froms, table, sems)
+        size = crossed.shape[0]
+        copies = fill([last], table, sems, size)
+
+        @pl.when(end[0] == 1)
+        def _():
+            fill([crossed], table, far_sems)
+
+        @pl.when(end[0] == 0)
+        def _():
+            table[0] = jnp.zeros((tile, width), table.dtype)
+
         column = lax.broadcasted_iota(jnp.int32, (tile, tile), 1)
         diagonal = lax.broadcasted_iota(jnp.int32, (tile, tile), 0) == column
         ones = jnp.ones((2 * tile, tile), jnp.bfloat16)
@@ -172,6 +185,11 @@
         for copy in copies:
             copy.wait()
 
+        @pl.when(end[0] == 1)
+        def _():
+            for c in range(CUT):
+                here = pl.ds(c * (size // CUT), size // CUT)
+                pltpu.make_async_copy(crossed.at[here], table.at[here], far_sems.at[0, c]).wait()
 
     def added(r, first):
         ends = min(first + pair, spare)
@@ -191,7 +209,7 @@
             def _():
                 totals[here, :] += added(r, first)
 
-    many = min(rows, 4) * tile
+    many = rows * tile
     for first in range(0, rows * tile, many):
         here = pl.ds(first, many)
         there = pl.ds(pl.multiple_of(step * rows * tile + first, tile), many)
@@ -204,7 +222,7 @@
         out[here, :] = (hidden * scale).astype(jnp.bfloat16)
 
 
-def layer(slots, counts, froms, sums, left, degree, features, weight):
+def layer(slots, counts, end, froms, sums, left, degree, features, weight):
     blocks_here, tile, across = left.shape
     width = features.shape[1]
     out_width = weight.shape[1]
@@ -214,7 +232,7 @@
     return pl.pallas_call(
         layer_kernel,
         grid_spec=pltpu.PrefetchScalarGridSpec(
-            num_scalar_prefetch=2,
+            num_scalar_prefetch=3,
             grid=(blocks_here // rows,),
             in_specs=[pl.BlockSpec(memory_space=pl.ANY)] * len(froms)
             + [
@@ -229,7 +247,8 @@
                 pltpu.VMEM((blocks_in_table, tile, width), jnp.bfloat16),
                 pltpu.VMEM((items, width), jnp.float32),
                 pltpu.VMEM((blocks_here * tile, tile), jnp.float32),
-                pltpu.SemaphoreType.DMA((len(froms),)),
+                pltpu.SemaphoreType.DMA((1, CUT)),
+                pltpu.SemaphoreType.DMA((1, CUT)),
             ],
         ),
         out_shape=jax.ShapeDtypeStruct((blocks_here * tile, out_width), jnp.bfloat16),
@@ -240,7 +259,7 @@
             transcendentals=blocks_here * tile,
         ),
         name="sage_layer",
-    )(slots, counts, *froms, sums, left, degree, features, weight)
+    )(slots, counts, end, *froms, sums, left, degree, features, weight)
 
 
 def on_device(features, tile_cols, tile_masks, degree, weight):
@@ -334,6 +353,7 @@
     return layer(
         late_slots.reshape(-1),
         counts,
+        end.astype(jnp.int32)[None],
         [crossed, got[3]],
         sums,
         left,

time: 184 us -> 183 us (level)
  no operation moved by 1% of the time
where the time goes in v14:
time: 183 us; the launch traced here: 181 us
  waiting for transfers between devices  88.5 us (48%)
  Pallas kernels  44.2 us (24%)
  starting transfers between devices  37.6 us (21%)
  local copies, waits for them, and re-layouts  5.48 us (3%)
  other arithmetic  5.07 us (3%)
    all_to_all x5, waiting for transfers between devices, exchange(): lax.all_to_all(x, 'rows', split_axis=0, concat_axis=0, axis_index_groups=...  63.8 us
    ppermute x6, waiting for transfers between devices, shift(): return lax.ppermute(x, 'rows', pairs)  24.7 us
    all_to_all x5, starting transfers between devices, exchange(): lax.all_to_all(x, 'rows', split_axis=0, concat_axis=0, axis_index_groups=...  21.3 us
    pallas_call x4, Pallas kernels, choose(): pl.pallas_call(functools.partial(choose_kernel, turns=turns), grid_spec=p...  17.6 us
    ppermute x6, starting transfers between devices, shift(): return lax.ppermute(x, 'rows', pairs)  16.3 us
    pallas_call x1, Pallas kernels, early(): pl.pallas_call(early_kernel, grid_spec=pltpu.PrefetchScalarGridSpec(num_s...  15 us
    pallas_call x1, Pallas kernels, layer(): pl.pallas_call(layer_kernel, grid_spec=pltpu.PrefetchScalarGridSpec(num_s...  11.6 us
  transfers between devices with their start and end apart: 11, of which 6 were waited for; matrix products, arithmetic and copies ran while one was open for 6% of the time, Pallas kernels for 18%

profile of v14, /device:TPU:0, one launch (start us, length us, event | category | flops | bytes accessed | tf_op | source)
XLA Modules:
  0.0 181.2 jit_solution(14330267194887041568)
XLA Ops:
  0.0 3.0 %collective-permute-start.2 = (bf16[32,128,256]{2,1,0:T(8,128)(2,1)}, bf16[32,128,256]{2,1,0:T(8,128)(2,1)}, u32[]{:S(2)}, u32[]{:S(2)}) collective-permute-start(bf16[32,128,256]{2,1,0:T(8,128)(2,1)} %bitcast.9), channel_id=1, source_target_pairs={{0,8},{1,9},{2,10},{3,11},{4,12},{5,13},{6,14},{7,15},{8,0},{9,1},... | collective-permute-start | bytes 6291464 | tf_op jit(solution)/shard_map/ppermute | solution.py:287
  3.0 2.0 %collective-permute-start.1 = (bf16[32,128,256]{2,1,0:T(8,128)(2,1)}, bf16[32,128,256]{2,1,0:T(8,128)(2,1)}, u32[]{:S(2)}, u32[]{:S(2)}) collective-permute-start(bf16[32,128,256]{2,1,0:T(8,128)(2,1)} %bitcast.10), channel_id=1, source_target_pairs={{8,16},{9,17},{10,18},{11,19},{12,20},{13,21},{14,22},{15,23},{16,... | collective-permute-start | bytes 6291464 | tf_op jit(solution)/shard_map/ppermute | solution.py:287
  5.0 0.8 copy.29
  5.8 0.1 reshape.236
  5.9 0.6 broadcast_in_dim.117
  6.5 3.7 %all-to-all-start = ((s32[8,1,192]{2,1,0:T(1,128)}), s32[8,1,192]{2,1,0:T(1,128)S(1)}, u32[]{:S(2)}, u32[]{:S(2)}) async-start(s32[8,1,192]{2,1,0:T(1,128)} %broadcast_in_dim.117), calls=%async_computation | async-start | bytes 16384 | tf_op jit(solution)/shard_map/all_to_all | solution.py:281
  10.2 0.8 select_reduce_fusion.5
  11.0 0.1 fusion.13
  11.2 3.7 %all-to-all-done = s32[8,1,192]{2,1,0:T(1,128)S(1)} async-done(((s32[8,1,192]{2,1,0:T(1,128)}), s32[8,1,192]{2,1,0:T(1,128)S(1)}, u32[]{:S(2)}, u32[]{:S(2)}) %all-to-all-start) | async-done | bytes 6176 | tf_op jit(solution)/shard_map/all_to_all | solution.py:281
  14.9 0.9 compare_reduce_fusion
  15.8 0.7 select_reduce_fusion
  16.6 0.5 select_reduce_fusion.1
  17.1 0.7 copy.40
  17.8 4.2 %choose_blocks.4 = bf16[40,128,256]{2,1,0:T(8,128)(2,1)} custom-call(s32[1]{0:T(128)} %constant.93.clone.1.which, s32[5,8,5]{2,1,0:T(8,128)} %bitcast.15, bf16[32,128,256]{2,1,0:T(8,128)(2,1)} %bitcast.11), custom_call_target="tpu_custom_call" | custom-call | flops 10000000000 | bytes 5242880 | tf_op jit(solution)/shard_map/choose_blocks/pallas_call | solution.py:51
  22.1 4.4 %all-to-all-start.1 = ((bf16[40,128,256]{2,1,0:T(8,128)(2,1)}), bf16[40,128,256]{2,1,0:T(8,128)(2,1)}, u32[]{:S(2)}, u32[]{:S(2)}) async-start(bf16[40,128,256]{2,1,0:T(8,128)(2,1)} %choose_blocks.4), calls=%async_computation.1 | async-start | bytes 5242880 | tf_op jit(solution)/shard_map/all_to_all | solution.py:281
  26.5 0.7 slice.4
  27.2 4.8 %collective-permute-start = (s32[1,8,5]{2,1,0:T(8,128)S(1)}, s32[1,8,5]{2,1,0:T(8,128)S(1)}, u32[]{:S(2)}, u32[]{:S(2)}) collective-permute-start(s32[1,8,5]{2,1,0:T(8,128)S(1)} %slice.4), channel_id=1, source_target_pairs={{0,24},{1,25},{2,26},{3,27},{4,28},{5,29},{6,30},{7,31},{24,0},{25... | collective-permute-start | bytes 488 | tf_op jit(solution)/shard_map/ppermute | solution.py:287
  32.0 19.3 %collective-permute-done.refs_0_ = s32[1,8,5]{2,1,0:T(8,128)S(1)} collective-permute-done((s32[1,8,5]{2,1,0:T(8,128)S(1)}, s32[1,8,5]{2,1,0:T(8,128)S(1)}, u32[]{:S(2)}, u32[]{:S(2)}) %collective-permute-start) | collective-permute-done | bytes 192 | tf_op jit(solution)/shard_map/ppermute | solution.py:287
  51.3 0.6 copy-done
  51.8 4.4 %choose_blocks.5 = bf16[40,128,256]{2,1,0:T(8,128)(2,1)} custom-call(s32[1]{0:T(128)} %bitcast.1.which, s32[1,8,5]{2,1,0:T(8,128)} %copy-done, s32[5,8,5]{2,1,0:T(8,128)} %bitcast.17, bf16[32,128,256]{2,1,0:T(8,128)(2,1)} %bitcast.12, bf16[32,128,256]{2,1,0:T(8,128)(2,1)} %collective-permute-done.1.refs_3_), custom_call_target="tpu_custom_call" | custom-call | flops 10000000000 | bytes 5242880 | tf_op jit(solution)/shard_map/choose_blocks/pallas_call | solution.py:51
  56.2 2.0 %collective-permute-start.4 = (bf16[32,128,256]{2,1,0:T(8,128)(2,1)}, bf16[32,128,256]{2,1,0:T(8,128)(2,1)}, u32[]{:S(2)}, u32[]{:S(2)}) collective-permute-start(bf16[32,128,256]{2,1,0:T(8,128)(2,1)} %collective-permute-done.2.refs_1_), channel_id=1, source_target_pairs={{8,16},{9,17},{10,18},{11,19},{12,20},{13,21},{14,22},{15,23},{16,... | collective-permute-start | bytes 6291464 | tf_op jit(solution)/shard_map/ppermute | solution.py:287
  58.2 1.3 collective-permute-start.3
  59.5 4.4 %all-to-all-start.2 = ((bf16[40,128,256]{2,1,0:T(8,128)(2,1)}), bf16[40,128,256]{2,1,0:T(8,128)(2,1)}, u32[]{:S(2)}, u32[]{:S(2)}) async-start(bf16[40,128,256]{2,1,0:T(8,128)(2,1)} %choose_blocks.5), calls=%async_computation.2 | async-start | bytes 5242880 | tf_op jit(solution)/shard_map/all_to_all | solution.py:281
  64.0 4.4 %choose_blocks.7 = bf16[40,128,256]{2,1,0:T(8,128)(2,1)} custom-call(s32[1]{0:T(128)} %constant.93.clone.1.which, s32[5,8,5]{2,1,0:T(8,128)} %bitcast.18, bf16[32,128,256]{2,1,0:T(8,128)(2,1)} %collective-permute-done.2.refs_1_), custom_call_target="tpu_custom_call" | custom-call | flops 30000001024 | bytes 5242880 | tf_op jit(solution)/shard_map/choose_blocks/pallas_call | solution.py:51
  68.4 27.8 %all-to-all-done.2.refs_2_ = bf16[40,128,256]{2,1,0:T(8,128)(2,1)} async-done(((bf16[40,128,256]{2,1,0:T(8,128)(2,1)}), bf16[40,128,256]{2,1,0:T(8,128)(2,1)}, u32[]{:S(2)}, u32[]{:S(2)}) %all-to-all-start.2) | async-done | bytes 2621472 | tf_op jit(solution)/shard_map/all_to_all | solution.py:281
  96.2 4.4 %all-to-all-start.4 = ((bf16[40,128,256]{2,1,0:T(8,128)(2,1)}), bf16[40,128,256]{2,1,0:T(8,128)(2,1)}, u32[]{:S(2)}, u32[]{:S(2)}) async-start(bf16[40,128,256]{2,1,0:T(8,128)(2,1)} %choose_blocks.7), calls=%async_computation.4 | async-start | bytes 5242880 | tf_op jit(solution)/shard_map/all_to_all | solution.py:281
  100.6 0.2 fusion.1
  100.9 0.1 select_reduce_fusion.4
  101.0 0.1 and.124
  101.1 0.1 eq.154
  101.2 0.2 convert_reduce_fusion
  101.4 0.1 reduce_sum.86
  101.5 0.7 convert_reduce_fusion.1
  102.2 0.2 reduce_window_sum.11
  102.4 5.4 %collective-permute-done.3.refs_1_ = bf16[32,128,256]{2,1,0:T(8,128)(2,1)} collective-permute-done((bf16[32,128,256]{2,1,0:T(8,128)(2,1)}, bf16[32,128,256]{2,1,0:T(8,128)(2,1)}, u32[]{:S(2)}, u32[]{:S(2)}) %collective-permute-start.3) | collective-permute-done | bytes 2097184 | tf_op jit(solution)/shard_map/ppermute | solution.py:287
  107.7 3.3 %collective-permute-start.5 = (bf16[40,128,256]{2,1,0:T(8,128)(2,1)}, bf16[40,128,256]{2,1,0:T(8,128)(2,1)}, u32[]{:S(2)}, u32[]{:S(2)}) collective-permute-start(bf16[40,128,256]{2,1,0:T(8,128)(2,1)} %all-to-all-done.2.refs_2_), channel_id=1, source_target_pairs={{0,24},{1,25},{2,26},{3,27},{4,28},{5,29},{6,30},{7,31},{24,0},{25... | collective-permute-start | bytes 7864328 | tf_op jit(solution)/shard_map/ppermute | solution.py:287
  111.0 4.5 %choose_blocks.6 = bf16[40,128,256]{2,1,0:T(8,128)(2,1)} custom-call(s32[1]{0:T(128)} %bitcast.1.which, s32[5,8,5]{2,1,0:T(8,128)} %bitcast.19, bf16[32,128,256]{2,1,0:T(8,128)(2,1)} %collective-permute-done.3.refs_1_, bf16[32,128,256]{2,1,0:T(8,128)(2,1)} %collective-permute-done.4.refs_2_), custom_call_target="tpu_custom_call" | custom-call | flops 10000000000 | bytes 5242880 | tf_op jit(solution)/shard_map/choose_blocks/pallas_call | solution.py:51
  115.6 17.4 %all-to-all-done.4.refs_3_ = bf16[40,128,256]{2,1,0:T(8,128)(2,1)} async-done(((bf16[40,128,256]{2,1,0:T(8,128)(2,1)}), bf16[40,128,256]{2,1,0:T(8,128)(2,1)}, u32[]{:S(2)}, u32[]{:S(2)}) %all-to-all-start.4) | async-done | bytes 2621472 | tf_op jit(solution)/shard_map/all_to_all | solution.py:281
  132.9 4.4 %all-to-all-start.3 = ((bf16[40,128,256]{2,1,0:T(8,128)(2,1)}), bf16[40,128,256]{2,1,0:T(8,128)(2,1)}, u32[]{:S(2)}, u32[]{:S(2)}) async-start(bf16[40,128,256]{2,1,0:T(8,128)(2,1)} %choose_blocks.6), calls=%async_computation.3 | async-start | bytes 5242880 | tf_op jit(solution)/shard_map/all_to_all | solution.py:281
  137.3 0.1 copy.30
  137.6 0.1 copy.41
  137.7 0.6 reshape.239.late
  138.3 0.1 copy.37
  138.4 0.6 reshape.237.slots
  139.0 0.6 compare_select_fusion.slots
  139.6 15.0 %early_sums.1 = (f32[4096,256]{1,0:T(8,128)}, s8[32,128,512]{2,1,0:T(32,128)(4,1)}) custom-call(s32[192]{0:T(256)} %compare_select_fusion.slots, s32[128]{0:T(128)} %reshape.239.late, s32[32]{0:T(128)} %get-tuple-element.23.counts, bf16[32,128,256]{2,1,0:T(8,128)(2,1)} %bitcast.13, bf16[40,128,256]{2,1,0:T(8,128)(2,1)} %all-to-all-done.1.refs_1_, ...), custom_call_target="tpu_custom_call" | custom-call | flops 20000000000 | bytes 28901376 | tf_op jit(solution)/shard_map/early_sums/pallas_call | solution.py:118
  154.7 14.9 %all-to-all-done.3.last = bf16[40,128,256]{2,1,0:T(8,128)(2,1)} async-done(((bf16[40,128,256]{2,1,0:T(8,128)(2,1)}), bf16[40,128,256]{2,1,0:T(8,128)(2,1)}, u32[]{:S(2)}, u32[]{:S(2)}) %all-to-all-start.3) | async-done | bytes 2621472 | tf_op jit(solution)/shard_map/all_to_all | solution.py:281
  169.6 11.6 %sage_layer.1 = bf16[4096,256]{1,0:T(8,128)(2,1)} custom-call(s32[128]{0:T(128)} %reshape.237.slots, s32[32]{0:T(128)} %get-tuple-element.23.counts, s32[1]{0:T(128)} %bitcast.end, bf16[40,128,256]{2,1,0:T(8,128)(2,1)} %collective-permute-done.5.crossed, bf16[40,128,256]{2,1,0:T(8,128)(2,1)} %all-to-all-done.3.last, f32[4096,256]{1,0:T(8,128)} %get-tuple-element.17.refs_0_, ...), custom_call_target="tpu_custom_call" | custom-call | flops 2147483648 | bytes 10485760 | tf_op jit(solution)/shard_map/sage_layer/pallas_call | solution.py:232
  (21 shorter events, 0.4 us)
Async XLA Ops:
  0.0 51.2 %collective-permute-start.2 = (bf16[32,128,256]{2,1,0:T(8,128)(2,1)}, bf16[32,128,256]{2,1,0:T(8,128)(2,1)}, u32[]{:S(2)}, u32[]{:S(2)}) collective-permute-start(bf16[32,128,256]{2,1,0:T(8,128)(2,1)} %bitcast.9), channel_id=1, source_target_pairs={{0,8},{1,9},{2,10},{3,11},{4,12},{5,13},{6,14},{7,15},{8,0},{9,1},... | collective-permute-start | bytes 6291464 | tf_op jit(solution)/shard_map/ppermute | solution.py:287
  3.0 48.2 %collective-permute-start.1 = (bf16[32,128,256]{2,1,0:T(8,128)(2,1)}, bf16[32,128,256]{2,1,0:T(8,128)(2,1)}, u32[]{:S(2)}, u32[]{:S(2)}) collective-permute-start(bf16[32,128,256]{2,1,0:T(8,128)(2,1)} %bitcast.10), channel_id=1, source_target_pairs={{8,16},{9,17},{10,18},{11,19},{12,20},{13,21},{14,22},{15,23},{16,... | collective-permute-start | bytes 6291464 | tf_op jit(solution)/shard_map/ppermute | solution.py:287
  6.5 8.4 %all-to-all-start = ((s32[8,1,192]{2,1,0:T(1,128)}), s32[8,1,192]{2,1,0:T(1,128)S(1)}, u32[]{:S(2)}, u32[]{:S(2)}) async-start(s32[8,1,192]{2,1,0:T(1,128)} %broadcast_in_dim.117), calls=%async_computation | async-start | bytes 16384 | tf_op jit(solution)/shard_map/all_to_all | solution.py:281
  22.1 37.5 %all-to-all-start.1 = ((bf16[40,128,256]{2,1,0:T(8,128)(2,1)}), bf16[40,128,256]{2,1,0:T(8,128)(2,1)}, u32[]{:S(2)}, u32[]{:S(2)}) async-start(bf16[40,128,256]{2,1,0:T(8,128)(2,1)} %choose_blocks.4), calls=%async_computation.1 | async-start | bytes 5242880 | tf_op jit(solution)/shard_map/all_to_all | solution.py:281
  27.2 24.1 %collective-permute-start = (s32[1,8,5]{2,1,0:T(8,128)S(1)}, s32[1,8,5]{2,1,0:T(8,128)S(1)}, u32[]{:S(2)}, u32[]{:S(2)}) collective-permute-start(s32[1,8,5]{2,1,0:T(8,128)S(1)} %slice.4), channel_id=1, source_target_pairs={{0,24},{1,25},{2,26},{3,27},{4,28},{5,29},{6,30},{7,31},{24,0},{25... | collective-permute-start | bytes 488 | tf_op jit(solution)/shard_map/ppermute | solution.py:287
  51.2 0.6 copy-start
  56.2 46.1 %collective-permute-start.4 = (bf16[32,128,256]{2,1,0:T(8,128)(2,1)}, bf16[32,128,256]{2,1,0:T(8,128)(2,1)}, u32[]{:S(2)}, u32[]{:S(2)}) collective-permute-start(bf16[32,128,256]{2,1,0:T(8,128)(2,1)} %collective-permute-done.2.refs_1_), channel_id=1, source_target_pairs={{8,16},{9,17},{10,18},{11,19},{12,20},{13,21},{14,22},{15,23},{16,... | collective-permute-start | bytes 6291464 | tf_op jit(solution)/shard_map/ppermute | solution.py:287
  58.2 49.5 %collective-permute-start.3 = (bf16[32,128,256]{2,1,0:T(8,128)(2,1)}, bf16[32,128,256]{2,1,0:T(8,128)(2,1)}, u32[]{:S(2)}, u32[]{:S(2)}) collective-permute-start(bf16[32,128,256]{2,1,0:T(8,128)(2,1)} %collective-permute-done.1.refs_3_), channel_id=1, source_target_pairs={{8,0},{9,1},{10,2},{11,3},{12,4},{13,5},{14,6},{15,7},{16,24},{17,... | collective-permute-start | bytes 6291464 | tf_op jit(solution)/shard_map/ppermute | solution.py:287
  59.5 36.7 %all-to-all-start.2 = ((bf16[40,128,256]{2,1,0:T(8,128)(2,1)}), bf16[40,128,256]{2,1,0:T(8,128)(2,1)}, u32[]{:S(2)}, u32[]{:S(2)}) async-start(bf16[40,128,256]{2,1,0:T(8,128)(2,1)} %choose_blocks.5), calls=%async_computation.2 | async-start | bytes 5242880 | tf_op jit(solution)/shard_map/all_to_all | solution.py:281
  96.2 36.7 %all-to-all-start.4 = ((bf16[40,128,256]{2,1,0:T(8,128)(2,1)}), bf16[40,128,256]{2,1,0:T(8,128)(2,1)}, u32[]{:S(2)}, u32[]{:S(2)}) async-start(bf16[40,128,256]{2,1,0:T(8,128)(2,1)} %choose_blocks.7), calls=%async_computation.4 | async-start | bytes 5242880 | tf_op jit(solution)/shard_map/all_to_all | solution.py:281
  107.7 61.9 %collective-permute-start.5 = (bf16[40,128,256]{2,1,0:T(8,128)(2,1)}, bf16[40,128,256]{2,1,0:T(8,128)(2,1)}, u32[]{:S(2)}, u32[]{:S(2)}) collective-permute-start(bf16[40,128,256]{2,1,0:T(8,128)(2,1)} %all-to-all-done.2.refs_2_), channel_id=1, source_target_pairs={{0,24},{1,25},{2,26},{3,27},{4,28},{5,29},{6,30},{7,31},{24,0},{25... | collective-permute-start | bytes 7864328 | tf_op jit(solution)/shard_map/ppermute | solution.py:287
  132.9 36.7 %all-to-all-start.3 = ((bf16[40,128,256]{2,1,0:T(8,128)(2,1)}), bf16[40,128,256]{2,1,0:T(8,128)(2,1)}, u32[]{:S(2)}, u32[]{:S(2)}) async-start(bf16[40,128,256]{2,1,0:T(8,128)(2,1)} %choose_blocks.6), calls=%async_computation.3 | async-start | bytes 5242880 | tf_op jit(solution)/shard_map/all_to_all | solution.py:281

commit v15 on v14

--- a/solution.py
+++ b/solution.py
@@ -105,8 +105,9 @@
         )
         sums[here, :] = jnp.dot(mask, picked, preferred_element_type=jnp.float32)
         for t in range(spare):
-            kept = jnp.where(t < counts[row], masks[r, late[row * spare + t]], 0)
-            left[r, :, t * tile : (t + 1) * tile] = kept.astype(jnp.int8)
+            kept = masks[r, late[row * spare + t]].astype(jnp.float32)
+            kept = jnp.where(t < counts[row], kept, 0.0).astype(jnp.bfloat16)
+            left[r, :, t * tile : (t + 1) * tile] = kept
 
 
 def early(slots, late, counts, froms, tile_masks):
@@ -133,7 +134,7 @@
         ),
         out_shape=[
             jax.ShapeDtypeStruct((blocks_here * tile, width), jnp.float32),
-            jax.ShapeDtypeStruct((blocks_here, tile, spare * tile), jnp.int8),
+            jax.ShapeDtypeStruct((blocks_here, tile, spare * tile), jnp.bfloat16),
         ],
         compiler_params=pltpu.CompilerParams(vmem_limit_bytes=VMEM_LIMIT),
         cost_estimate=pl.CostEstimate(
@@ -194,8 +195,7 @@
     def added(r, first):
         ends = min(first + pair, spare)
         picked = [table[slots[(step * rows + r) * spare + t]] for t in range(first, ends)]
-        mask = left[r, :, first * tile : ends * tile].astype(jnp.int32)
-        mask = mask.astype(jnp.float32).astype(jnp.bfloat16)
+        mask = left[r, :, first * tile : ends * tile]
         return jnp.dot(mask, jnp.concatenate(picked, axis=0), preferred_element_type=jnp.float32)
 
     for r in range(rows):
@@ -255,7 +255,7 @@
         compiler_params=pltpu.CompilerParams(vmem_limit_bytes=VMEM_LIMIT),
         cost_estimate=pl.CostEstimate(
             flops=2 * blocks_here * tile * (across + 2 * width) * out_width,
-            bytes_accessed=blocks_here * tile * (4 * width + across + 2 * width + 2 * out_width),
+            bytes_accessed=blocks_here * tile * (4 * width + 2 * across + 2 * width + 2 * out_width),
             transcendentals=blocks_here * tile,
         ),
         name="sage_layer",

time: 183 us -> 186 us (1.016)
    ppermute x6, waiting for transfers between devices: 24.7 us -> 22.5 us  [shift(): return lax.ppermute(x, 'rows', pairs)]
where the time goes in v15:
time: 186 us; the launch traced here: 184 us
  waiting for transfers between devices  87.5 us (47%)
  Pallas kernels  46 us (25%)
  starting transfers between devices  39.3 us (21%)
  local copies, waits for them, and re-layouts  5.62 us (3%)
  other arithmetic  5.09 us (3%)
    all_to_all x5, waiting for transfers between devices, exchange(): lax.all_to_all(x, 'rows', split_axis=0, concat_axis=0, axis_index_groups=...  65.1 us
    ppermute x6, waiting for transfers between devices, shift(): return lax.ppermute(x, 'rows', pairs)  22.5 us
    all_to_all x5, starting transfers between devices, exchange(): lax.all_to_all(x, 'rows', split_axis=0, concat_axis=0, axis_index_groups=...  21.4 us
    pallas_call x4, Pallas kernels, choose(): pl.pallas_call(functools.partial(choose_kernel, turns=turns), grid_spec=p...  18.4 us
    ppermute x6, starting transfers between devices, shift(): return lax.ppermute(x, 'rows', pairs)  18 us
    pallas_call x1, Pallas kernels, early(): pl.pallas_call(early_kernel, grid_spec=pltpu.PrefetchScalarGridSpec(num_s...  15.6 us
    pallas_call x1, Pallas kernels, layer(): pl.pallas_call(layer_kernel, grid_spec=pltpu.PrefetchScalarGridSpec(num_s...  12.1 us
  transfers between devices with their start and end apart: 11, of which 6 were waited for; matrix products, arithmetic and copies ran while one was open for 6% of the time, Pallas kernels for 18%

profile of v15, /device:TPU:0, one launch (start us, length us, event | category | flops | bytes accessed | tf_op | source)
XLA Modules:
  0.0 183.8 jit_solution(15839116486971068756)
XLA Ops:
  0.0 2.0 %collective-permute-start.1 = (bf16[32,128,256]{2,1,0:T(8,128)(2,1)}, bf16[32,128,256]{2,1,0:T(8,128)(2,1)}, u32[]{:S(2)}, u32[]{:S(2)}) collective-permute-start(bf16[32,128,256]{2,1,0:T(8,128)(2,1)} %bitcast.9), channel_id=1, source_target_pairs={{8,16},{9,17},{10,18},{11,19},{12,20},{13,21},{14,22},{15,23},{16,... | collective-permute-start | bytes 6291464 | tf_op jit(solution)/shard_map/ppermute | solution.py:287
  2.0 4.6 %collective-permute-start.2 = (bf16[32,128,256]{2,1,0:T(8,128)(2,1)}, bf16[32,128,256]{2,1,0:T(8,128)(2,1)}, u32[]{:S(2)}, u32[]{:S(2)}) collective-permute-start(bf16[32,128,256]{2,1,0:T(8,128)(2,1)} %bitcast.10), channel_id=1, source_target_pairs={{0,8},{1,9},{2,10},{3,11},{4,12},{5,13},{6,14},{7,15},{8,0},{9,1},... | collective-permute-start | bytes 6291464 | tf_op jit(solution)/shard_map/ppermute | solution.py:287
  6.6 0.8 copy.29
  7.3 0.1 reshape.236
  7.4 0.6 broadcast_in_dim.117
  8.1 3.7 %all-to-all-start = ((s32[8,1,192]{2,1,0:T(1,128)}), s32[8,1,192]{2,1,0:T(1,128)S(1)}, u32[]{:S(2)}, u32[]{:S(2)}) async-start(s32[8,1,192]{2,1,0:T(1,128)} %broadcast_in_dim.117), calls=%async_computation | async-start | bytes 16384 | tf_op jit(solution)/shard_map/all_to_all | solution.py:281
  11.8 0.8 select_reduce_fusion.5
  12.6 0.1 fusion.13
  12.8 3.7 %all-to-all-done = s32[8,1,192]{2,1,0:T(1,128)S(1)} async-done(((s32[8,1,192]{2,1,0:T(1,128)}), s32[8,1,192]{2,1,0:T(1,128)S(1)}, u32[]{:S(2)}, u32[]{:S(2)}) %all-to-all-start) | async-done | bytes 6176 | tf_op jit(solution)/shard_map/all_to_all | solution.py:281
  16.5 0.9 compare_reduce_fusion
  17.4 0.7 select_reduce_fusion
  18.2 0.5 select_reduce_fusion.1
  18.7 0.7 copy.40
  19.4 4.7 %choose_blocks.4 = bf16[40,128,256]{2,1,0:T(8,128)(2,1)} custom-call(s32[1]{0:T(128)} %constant.93.clone.1.which, s32[5,8,5]{2,1,0:T(8,128)} %bitcast.15, bf16[32,128,256]{2,1,0:T(8,128)(2,1)} %bitcast.11), custom_call_target="tpu_custom_call" | custom-call | flops 10000000000 | bytes 5242880 | tf_op jit(solution)/shard_map/choose_blocks/pallas_call | solution.py:51
  24.1 4.4 %all-to-all-start.1 = ((bf16[40,128,256]{2,1,0:T(8,128)(2,1)}), bf16[40,128,256]{2,1,0:T(8,128)(2,1)}, u32[]{:S(2)}, u32[]{:S(2)}) async-start(bf16[40,128,256]{2,1,0:T(8,128)(2,1)} %choose_blocks.4), calls=%async_computation.1 | async-start | bytes 5242880 | tf_op jit(solution)/shard_map/all_to_all | solution.py:281
  28.5 0.7 slice.4
  29.2 3.4 %collective-permute-start = (s32[1,8,5]{2,1,0:T(8,128)S(1)}, s32[1,8,5]{2,1,0:T(8,128)S(1)}, u32[]{:S(2)}, u32[]{:S(2)}) collective-permute-start(s32[1,8,5]{2,1,0:T(8,128)S(1)} %slice.4), channel_id=1, source_target_pairs={{0,24},{1,25},{2,26},{3,27},{4,28},{5,29},{6,30},{7,31},{24,0},{25... | collective-permute-start | bytes 488 | tf_op jit(solution)/shard_map/ppermute | solution.py:287
  32.6 20.7 %collective-permute-done.refs_0_ = s32[1,8,5]{2,1,0:T(8,128)S(1)} collective-permute-done((s32[1,8,5]{2,1,0:T(8,128)S(1)}, s32[1,8,5]{2,1,0:T(8,128)S(1)}, u32[]{:S(2)}, u32[]{:S(2)}) %collective-permute-start) | collective-permute-done | bytes 192 | tf_op jit(solution)/shard_map/ppermute | solution.py:287
  53.3 0.6 copy-done
  53.9 4.5 %choose_blocks.5 = bf16[40,128,256]{2,1,0:T(8,128)(2,1)} custom-call(s32[1]{0:T(128)} %bitcast.1.which, s32[1,8,5]{2,1,0:T(8,128)} %copy-done, s32[5,8,5]{2,1,0:T(8,128)} %bitcast.17, bf16[32,128,256]{2,1,0:T(8,128)(2,1)} %bitcast.12, bf16[32,128,256]{2,1,0:T(8,128)(2,1)} %collective-permute-done.1.refs_3_), custom_call_target="tpu_custom_call" | custom-call | flops 10000000000 | bytes 5242880 | tf_op jit(solution)/shard_map/choose_blocks/pallas_call | solution.py:51
  58.4 1.3 collective-permute-start.3
  59.7 2.1 %collective-permute-start.4 = (bf16[32,128,256]{2,1,0:T(8,128)(2,1)}, bf16[32,128,256]{2,1,0:T(8,128)(2,1)}, u32[]{:S(2)}, u32[]{:S(2)}) collective-permute-start(bf16[32,128,256]{2,1,0:T(8,128)(2,1)} %collective-permute-done.2.refs_1_), channel_id=1, source_target_pairs={{8,16},{9,17},{10,18},{11,19},{12,20},{13,21},{14,22},{15,23},{16,... | collective-permute-start | bytes 6291464 | tf_op jit(solution)/shard_map/ppermute | solution.py:287
  61.7 4.4 %all-to-all-start.2 = ((bf16[40,128,256]{2,1,0:T(8,128)(2,1)}), bf16[40,128,256]{2,1,0:T(8,128)(2,1)}, u32[]{:S(2)}, u32[]{:S(2)}) async-start(bf16[40,128,256]{2,1,0:T(8,128)(2,1)} %choose_blocks.5), calls=%async_computation.2 | async-start | bytes 5242880 | tf_op jit(solution)/shard_map/all_to_all | solution.py:281
  66.2 4.5 %choose_blocks.7 = bf16[40,128,256]{2,1,0:T(8,128)(2,1)} custom-call(s32[1]{0:T(128)} %constant.93.clone.1.which, s32[5,8,5]{2,1,0:T(8,128)} %bitcast.18, bf16[32,128,256]{2,1,0:T(8,128)(2,1)} %collective-permute-done.2.refs_1_), custom_call_target="tpu_custom_call" | custom-call | flops 30000001024 | bytes 5242880 | tf_op jit(solution)/shard_map/choose_blocks/pallas_call | solution.py:51
  70.6 27.8 %all-to-all-done.2.refs_2_ = bf16[40,128,256]{2,1,0:T(8,128)(2,1)} async-done(((bf16[40,128,256]{2,1,0:T(8,128)(2,1)}), bf16[40,128,256]{2,1,0:T(8,128)(2,1)}, u32[]{:S(2)}, u32[]{:S(2)}) %all-to-all-start.2) | async-done | bytes 2621472 | tf_op jit(solution)/shard_map/all_to_all | solution.py:281
  98.4 4.4 %all-to-all-start.4 = ((bf16[40,128,256]{2,1,0:T(8,128)(2,1)}), bf16[40,128,256]{2,1,0:T(8,128)(2,1)}, u32[]{:S(2)}, u32[]{:S(2)}) async-start(bf16[40,128,256]{2,1,0:T(8,128)(2,1)} %choose_blocks.7), calls=%async_computation.4 | async-start | bytes 5242880 | tf_op jit(solution)/shard_map/all_to_all | solution.py:281
  102.9 0.1 select_reduce_fusion.4
  103.0 0.1 and.124
  103.1 0.1 eq.154
  103.2 0.2 fusion.1
  103.4 0.2 convert_reduce_fusion
  103.6 0.1 reduce_sum.86
  103.7 0.7 convert_reduce_fusion.1
  104.4 0.2 reduce_window_sum.11
  104.6 1.8 collective-permute-done.3.refs_1_
  106.4 4.7 %collective-permute-start.5 = (bf16[40,128,256]{2,1,0:T(8,128)(2,1)}, bf16[40,128,256]{2,1,0:T(8,128)(2,1)}, u32[]{:S(2)}, u32[]{:S(2)}) collective-permute-start(bf16[40,128,256]{2,1,0:T(8,128)(2,1)} %all-to-all-done.2.refs_2_), channel_id=1, source_target_pairs={{0,24},{1,25},{2,26},{3,27},{4,28},{5,29},{6,30},{7,31},{24,0},{25... | collective-permute-start | bytes 7864328 | tf_op jit(solution)/shard_map/ppermute | solution.py:287
  111.1 4.8 %choose_blocks.6 = bf16[40,128,256]{2,1,0:T(8,128)(2,1)} custom-call(s32[1]{0:T(128)} %bitcast.1.which, s32[5,8,5]{2,1,0:T(8,128)} %bitcast.19, bf16[32,128,256]{2,1,0:T(8,128)(2,1)} %collective-permute-done.3.refs_1_, bf16[32,128,256]{2,1,0:T(8,128)(2,1)} %collective-permute-done.4.refs_2_), custom_call_target="tpu_custom_call" | custom-call | flops 10000000000 | bytes 5242880 | tf_op jit(solution)/shard_map/choose_blocks/pallas_call | solution.py:51
  115.8 19.3 %all-to-all-done.4.refs_3_ = bf16[40,128,256]{2,1,0:T(8,128)(2,1)} async-done(((bf16[40,128,256]{2,1,0:T(8,128)(2,1)}), bf16[40,128,256]{2,1,0:T(8,128)(2,1)}, u32[]{:S(2)}, u32[]{:S(2)}) %all-to-all-start.4) | async-done | bytes 2621472 | tf_op jit(solution)/shard_map/all_to_all | solution.py:281
  135.1 4.4 %all-to-all-start.3 = ((bf16[40,128,256]{2,1,0:T(8,128)(2,1)}), bf16[40,128,256]{2,1,0:T(8,128)(2,1)}, u32[]{:S(2)}, u32[]{:S(2)}) async-start(bf16[40,128,256]{2,1,0:T(8,128)(2,1)} %choose_blocks.6), calls=%async_computation.3 | async-start | bytes 5242880 | tf_op jit(solution)/shard_map/all_to_all | solution.py:281
  139.5 0.1 copy.30
  139.8 0.1 copy.41
  139.9 0.7 reshape.239.late
  140.6 0.1 copy.37
  140.7 0.7 reshape.237.slots
  141.4 0.6 compare_select_fusion.slots
  142.0 15.6 %early_sums.1 = (f32[4096,256]{1,0:T(8,128)}, bf16[32,128,512]{2,1,0:T(8,128)(2,1)}) custom-call(s32[192]{0:T(256)} %compare_select_fusion.slots, s32[128]{0:T(128)} %reshape.239.late, s32[32]{0:T(128)} %get-tuple-element.23.counts, bf16[32,128,256]{2,1,0:T(8,128)(2,1)} %bitcast.13, bf16[40,128,256]{2,1,0:T(8,128)(2,1)} %all-to-all-done.1.refs_1_, ...), custom_call_target="tpu_custom_call" | custom-call | flops 20000000000 | bytes 28901376 | tf_op jit(solution)/shard_map/early_sums/pallas_call | solution.py:119
  157.6 14.2 %all-to-all-done.3.last = bf16[40,128,256]{2,1,0:T(8,128)(2,1)} async-done(((bf16[40,128,256]{2,1,0:T(8,128)(2,1)}), bf16[40,128,256]{2,1,0:T(8,128)(2,1)}, u32[]{:S(2)}, u32[]{:S(2)}) %all-to-all-start.3) | async-done | bytes 2621472 | tf_op jit(solution)/shard_map/all_to_all | solution.py:281
  171.8 12.1 %sage_layer.1 = bf16[4096,256]{1,0:T(8,128)(2,1)} custom-call(s32[128]{0:T(128)} %reshape.237.slots, s32[32]{0:T(128)} %get-tuple-element.23.counts, s32[1]{0:T(128)} %bitcast.end, bf16[40,128,256]{2,1,0:T(8,128)(2,1)} %collective-permute-done.5.crossed, bf16[40,128,256]{2,1,0:T(8,128)(2,1)} %all-to-all-done.3.last, f32[4096,256]{1,0:T(8,128)} %get-tuple-element.17.refs_0_, ...), custom_call_target="tpu_custom_call" | custom-call | flops 2147483648 | bytes 12582912 | tf_op jit(solution)/shard_map/sage_layer/pallas_call | solution.py:232
  (21 shorter events, 0.4 us)
Async XLA Ops:
  0.0 53.3 %collective-permute-start.1 = (bf16[32,128,256]{2,1,0:T(8,128)(2,1)}, bf16[32,128,256]{2,1,0:T(8,128)(2,1)}, u32[]{:S(2)}, u32[]{:S(2)}) collective-permute-start(bf16[32,128,256]{2,1,0:T(8,128)(2,1)} %bitcast.9), channel_id=1, source_target_pairs={{8,16},{9,17},{10,18},{11,19},{12,20},{13,21},{14,22},{15,23},{16,... | collective-permute-start | bytes 6291464 | tf_op jit(solution)/shard_map/ppermute | solution.py:287
  2.0 51.3 %collective-permute-start.2 = (bf16[32,128,256]{2,1,0:T(8,128)(2,1)}, bf16[32,128,256]{2,1,0:T(8,128)(2,1)}, u32[]{:S(2)}, u32[]{:S(2)}) collective-permute-start(bf16[32,128,256]{2,1,0:T(8,128)(2,1)} %bitcast.10), channel_id=1, source_target_pairs={{0,8},{1,9},{2,10},{3,11},{4,12},{5,13},{6,14},{7,15},{8,0},{9,1},... | collective-permute-start | bytes 6291464 | tf_op jit(solution)/shard_map/ppermute | solution.py:287
  8.1 8.4 %all-to-all-start = ((s32[8,1,192]{2,1,0:T(1,128)}), s32[8,1,192]{2,1,0:T(1,128)S(1)}, u32[]{:S(2)}, u32[]{:S(2)}) async-start(s32[8,1,192]{2,1,0:T(1,128)} %broadcast_in_dim.117), calls=%async_computation | async-start | bytes 16384 | tf_op jit(solution)/shard_map/all_to_all | solution.py:281
  24.1 37.7 %all-to-all-start.1 = ((bf16[40,128,256]{2,1,0:T(8,128)(2,1)}), bf16[40,128,256]{2,1,0:T(8,128)(2,1)}, u32[]{:S(2)}, u32[]{:S(2)}) async-start(bf16[40,128,256]{2,1,0:T(8,128)(2,1)} %choose_blocks.4), calls=%async_computation.1 | async-start | bytes 5242880 | tf_op jit(solution)/shard_map/all_to_all | solution.py:281
  29.2 24.1 %collective-permute-start = (s32[1,8,5]{2,1,0:T(8,128)S(1)}, s32[1,8,5]{2,1,0:T(8,128)S(1)}, u32[]{:S(2)}, u32[]{:S(2)}) collective-permute-start(s32[1,8,5]{2,1,0:T(8,128)S(1)} %slice.4), channel_id=1, source_target_pairs={{0,24},{1,25},{2,26},{3,27},{4,28},{5,29},{6,30},{7,31},{24,0},{25... | collective-permute-start | bytes 488 | tf_op jit(solution)/shard_map/ppermute | solution.py:287
  53.3 0.6 copy-start
  58.4 48.0 %collective-permute-start.3 = (bf16[32,128,256]{2,1,0:T(8,128)(2,1)}, bf16[32,128,256]{2,1,0:T(8,128)(2,1)}, u32[]{:S(2)}, u32[]{:S(2)}) collective-permute-start(bf16[32,128,256]{2,1,0:T(8,128)(2,1)} %collective-permute-done.1.refs_3_), channel_id=1, source_target_pairs={{8,0},{9,1},{10,2},{11,3},{12,4},{13,5},{14,6},{15,7},{16,24},{17,... | collective-permute-start | bytes 6291464 | tf_op jit(solution)/shard_map/ppermute | solution.py:287
  59.7 46.7 %collective-permute-start.4 = (bf16[32,128,256]{2,1,0:T(8,128)(2,1)}, bf16[32,128,256]{2,1,0:T(8,128)(2,1)}, u32[]{:S(2)}, u32[]{:S(2)}) collective-permute-start(bf16[32,128,256]{2,1,0:T(8,128)(2,1)} %collective-permute-done.2.refs_1_), channel_id=1, source_target_pairs={{8,16},{9,17},{10,18},{11,19},{12,20},{13,21},{14,22},{15,23},{16,... | collective-permute-start | bytes 6291464 | tf_op jit(solution)/shard_map/ppermute | solution.py:287
  61.7 36.7 %all-to-all-start.2 = ((bf16[40,128,256]{2,1,0:T(8,128)(2,1)}), bf16[40,128,256]{2,1,0:T(8,128)(2,1)}, u32[]{:S(2)}, u32[]{:S(2)}) async-start(bf16[40,128,256]{2,1,0:T(8,128)(2,1)} %choose_blocks.5), calls=%async_computation.2 | async-start | bytes 5242880 | tf_op jit(solution)/shard_map/all_to_all | solution.py:281
  98.4 36.7 %all-to-all-start.4 = ((bf16[40,128,256]{2,1,0:T(8,128)(2,1)}), bf16[40,128,256]{2,1,0:T(8,128)(2,1)}, u32[]{:S(2)}, u32[]{:S(2)}) async-start(bf16[40,128,256]{2,1,0:T(8,128)(2,1)} %choose_blocks.7), calls=%async_computation.4 | async-start | bytes 5242880 | tf_op jit(solution)/shard_map/all_to_all | solution.py:281
  106.4 65.4 %collective-permute-start.5 = (bf16[40,128,256]{2,1,0:T(8,128)(2,1)}, bf16[40,128,256]{2,1,0:T(8,128)(2,1)}, u32[]{:S(2)}, u32[]{:S(2)}) collective-permute-start(bf16[40,128,256]{2,1,0:T(8,128)(2,1)} %all-to-all-done.2.refs_2_), channel_id=1, source_target_pairs={{0,24},{1,25},{2,26},{3,27},{4,28},{5,29},{6,30},{7,31},{24,0},{25... | collective-permute-start | bytes 7864328 | tf_op jit(solution)/shard_map/ppermute | solution.py:287
  135.1 36.7 %all-to-all-start.3 = ((bf16[40,128,256]{2,1,0:T(8,128)(2,1)}), bf16[40,128,256]{2,1,0:T(8,128)(2,1)}, u32[]{:S(2)}, u32[]{:S(2)}) async-start(bf16[40,128,256]{2,1,0:T(8,128)(2,1)} %choose_blocks.6), calls=%async_computation.3 | async-start | bytes 5242880 | tf_op jit(solution)/shard_map/all_to_all | solution.py:281

commit v16 on v14

--- a/solution.py
+++ b/solution.py
@@ -342,7 +342,8 @@
     picked = choose(inner, [across, near], [0, 1], [local, beyond], LIGHT)
     leaving, _ = lax.optimization_barrier((picked, got[0]))
     got.append(exchange(leaving))
-    far_out, far_in = shift(beyond, outward), shift(near_by, swap)
+    second, _ = lax.optimization_barrier((near_by, got[0]))
+    far_out, far_in = shift(beyond, outward), shift(second, swap)
     leaving, _, _ = lax.optimization_barrier((got[1], far_out, far_in))
     crossed = shift(leaving, [(0, PLANES - 1), (PLANES - 1, 0)])
     near, _ = lax.optimization_barrier((near, picked))

time: 183 us -> 225 us (1.23)
  the two profiles are of different devices: /device:TPU:0 before, /device:TPU:8 now
where the time goes in v16:
time: 225 us; the launch traced here: 223 us
  waiting for transfers between devices  135 us (60%)
  Pallas kernels  43.2 us (19%)
  starting transfers between devices  35.1 us (16%)
  other arithmetic  5.06 us (2%)
  local copies, waits for them, and re-layouts  4.96 us (2%)
    ppermute x6, waiting for transfers between devices, shift(): return lax.ppermute(x, 'rows', pairs)  90.4 us
    all_to_all x5, waiting for transfers between devices, exchange(): lax.all_to_all(x, 'rows', split_axis=0, concat_axis=0, axis_index_groups=...  44.3 us
    all_to_all x5, starting transfers between devices, exchange(): lax.all_to_all(x, 'rows', split_axis=0, concat_axis=0, axis_index_groups=...  21.3 us
    pallas_call x4, Pallas kernels, choose(): pl.pallas_call(functools.partial(choose_kernel, turns=turns), grid_spec=p...  18.3 us
    pallas_call x1, Pallas kernels, early(): pl.pallas_call(early_kernel, grid_spec=pltpu.PrefetchScalarGridSpec(num_s...  15 us
    ppermute x6, starting transfers between devices, shift(): return lax.ppermute(x, 'rows', pairs)  13.7 us
    pallas_call x1, Pallas kernels, layer(): pl.pallas_call(layer_kernel, grid_spec=pltpu.PrefetchScalarGridSpec(num_s...  9.86 us
  transfers between devices with their start and end apart: 11, of which 7 were waited for; matrix products, arithmetic and copies ran while one was open for 4% of the time, Pallas kernels for 15%

profile of v16, /device:TPU:8, one launch (start us, length us, event | category | flops | bytes accessed | tf_op | source)
XLA Modules:
  0.0 223.3 jit_solution(11453082842092237903)
XLA Ops:
  0.0 5.0 %collective-permute-start.1 = (bf16[32,128,256]{2,1,0:T(8,128)(2,1)}, bf16[32,128,256]{2,1,0:T(8,128)(2,1)}, u32[]{:S(2)}, u32[]{:S(2)}) collective-permute-start(bf16[32,128,256]{2,1,0:T(8,128)(2,1)} %bitcast.10), channel_id=1, source_target_pairs={{8,16},{9,17},{10,18},{11,19},{12,20},{13,21},{14,22},{15,23},{16,... | collective-permute-start | bytes 6291464 | tf_op jit(solution)/shard_map/ppermute | solution.py:287
  5.1 0.8 copy.29
  5.8 0.1 reshape.236
  5.9 0.6 broadcast_in_dim.117
  6.5 3.7 %all-to-all-start = ((s32[8,1,192]{2,1,0:T(1,128)}), s32[8,1,192]{2,1,0:T(1,128)S(1)}, u32[]{:S(2)}, u32[]{:S(2)}) async-start(s32[8,1,192]{2,1,0:T(1,128)} %broadcast_in_dim.117), calls=%async_computation | async-start | bytes 16384 | tf_op jit(solution)/shard_map/all_to_all | solution.py:281
  10.3 0.8 select_reduce_fusion.5
  11.1 0.1 fusion.13
  11.2 3.7 %all-to-all-done = s32[8,1,192]{2,1,0:T(1,128)S(1)} async-done(((s32[8,1,192]{2,1,0:T(1,128)}), s32[8,1,192]{2,1,0:T(1,128)S(1)}, u32[]{:S(2)}, u32[]{:S(2)}) %all-to-all-start) | async-done | bytes 6176 | tf_op jit(solution)/shard_map/all_to_all | solution.py:281
  15.0 0.9 compare_reduce_fusion
  15.9 0.7 select_reduce_fusion
  16.6 0.5 select_reduce_fusion.1
  17.2 0.7 copy.40
  17.9 4.6 %choose_blocks.4 = bf16[40,128,256]{2,1,0:T(8,128)(2,1)} custom-call(s32[1]{0:T(128)} %constant.93.clone.1.which, s32[5,8,5]{2,1,0:T(8,128)} %bitcast.15, bf16[32,128,256]{2,1,0:T(8,128)(2,1)} %bitcast.11), custom_call_target="tpu_custom_call" | custom-call | flops 10000000000 | bytes 5242880 | tf_op jit(solution)/shard_map/choose_blocks/pallas_call | solution.py:51
  22.5 4.4 %all-to-all-start.1 = ((bf16[40,128,256]{2,1,0:T(8,128)(2,1)}), bf16[40,128,256]{2,1,0:T(8,128)(2,1)}, u32[]{:S(2)}, u32[]{:S(2)}) async-start(bf16[40,128,256]{2,1,0:T(8,128)(2,1)} %choose_blocks.4), calls=%async_computation.1 | async-start | bytes 5242880 | tf_op jit(solution)/shard_map/all_to_all | solution.py:281
  26.9 0.7 slice.4
  27.6 0.6 collective-permute-start
  28.2 19.5 %collective-permute-done.2.refs_1_ = bf16[32,128,256]{2,1,0:T(8,128)(2,1)} collective-permute-done((bf16[32,128,256]{2,1,0:T(8,128)(2,1)}, bf16[32,128,256]{2,1,0:T(8,128)(2,1)}, u32[]{:S(2)}, u32[]{:S(2)}) %collective-permute-start.2) | collective-permute-done | bytes 2097184 | tf_op jit(solution)/shard_map/ppermute | solution.py:287
  47.7 3.1 %collective-permute-done.1.refs_3_ = bf16[32,128,256]{2,1,0:T(8,128)(2,1)} collective-permute-done((bf16[32,128,256]{2,1,0:T(8,128)(2,1)}, bf16[32,128,256]{2,1,0:T(8,128)(2,1)}, u32[]{:S(2)}, u32[]{:S(2)}) %collective-permute-start.1) | collective-permute-done | bytes 2097184 | tf_op jit(solution)/shard_map/ppermute | solution.py:287
  50.8 4.4 %choose_blocks.5 = bf16[40,128,256]{2,1,0:T(8,128)(2,1)} custom-call(s32[1]{0:T(128)} %bitcast.1.which, s32[1,8,5]{2,1,0:T(8,128)} %copy-done, s32[5,8,5]{2,1,0:T(8,128)} %bitcast.17, bf16[32,128,256]{2,1,0:T(8,128)(2,1)} %bitcast.12, bf16[32,128,256]{2,1,0:T(8,128)(2,1)} %collective-permute-done.1.refs_3_), custom_call_target="tpu_custom_call" | custom-call | flops 10000000000 | bytes 5242880 | tf_op jit(solution)/shard_map/choose_blocks/pallas_call | solution.py:51
  55.2 3.4 %collective-permute-start.3 = (bf16[32,128,256]{2,1,0:T(8,128)(2,1)}, bf16[32,128,256]{2,1,0:T(8,128)(2,1)}, u32[]{:S(2)}, u32[]{:S(2)}) collective-permute-start(bf16[32,128,256]{2,1,0:T(8,128)(2,1)} %collective-permute-done.1.refs_3_), channel_id=1, source_target_pairs={{8,0},{9,1},{10,2},{11,3},{12,4},{13,5},{14,6},{15,7},{16,24},{17,... | collective-permute-start | bytes 6291464 | tf_op jit(solution)/shard_map/ppermute | solution.py:287
  58.6 0.5 all-to-all-done.1.refs_1_
  59.1 4.4 %all-to-all-start.2 = ((bf16[40,128,256]{2,1,0:T(8,128)(2,1)}), bf16[40,128,256]{2,1,0:T(8,128)(2,1)}, u32[]{:S(2)}, u32[]{:S(2)}) async-start(bf16[40,128,256]{2,1,0:T(8,128)(2,1)} %choose_blocks.5), calls=%async_computation.2 | async-start | bytes 5242880 | tf_op jit(solution)/shard_map/all_to_all | solution.py:281
  63.5 2.5 %collective-permute-start.4 = (bf16[32,128,256]{2,1,0:T(8,128)(2,1)}, bf16[32,128,256]{2,1,0:T(8,128)(2,1)}, u32[]{:S(2)}, u32[]{:S(2)}) collective-permute-start(bf16[32,128,256]{2,1,0:T(8,128)(2,1)} %collective-permute-done.2.refs_1_), channel_id=1, source_target_pairs={{8,16},{9,17},{10,18},{11,19},{12,20},{13,21},{14,22},{15,23},{16,... | collective-permute-start | bytes 6291464 | tf_op jit(solution)/shard_map/ppermute | solution.py:287
  66.0 4.7 %choose_blocks.7 = bf16[40,128,256]{2,1,0:T(8,128)(2,1)} custom-call(s32[1]{0:T(128)} %constant.93.clone.1.which, s32[5,8,5]{2,1,0:T(8,128)} %bitcast.18, bf16[32,128,256]{2,1,0:T(8,128)(2,1)} %collective-permute-done.2.refs_1_), custom_call_target="tpu_custom_call" | custom-call | flops 30000001024 | bytes 5242880 | tf_op jit(solution)/shard_map/choose_blocks/pallas_call | solution.py:51
  70.7 25.1 %all-to-all-done.2.refs_2_ = bf16[40,128,256]{2,1,0:T(8,128)(2,1)} async-done(((bf16[40,128,256]{2,1,0:T(8,128)(2,1)}), bf16[40,128,256]{2,1,0:T(8,128)(2,1)}, u32[]{:S(2)}, u32[]{:S(2)}) %all-to-all-start.2) | async-done | bytes 2621472 | tf_op jit(solution)/shard_map/all_to_all | solution.py:281
  95.8 4.4 %all-to-all-start.4 = ((bf16[40,128,256]{2,1,0:T(8,128)(2,1)}), bf16[40,128,256]{2,1,0:T(8,128)(2,1)}, u32[]{:S(2)}, u32[]{:S(2)}) async-start(bf16[40,128,256]{2,1,0:T(8,128)(2,1)} %choose_blocks.7), calls=%async_computation.4 | async-start | bytes 5242880 | tf_op jit(solution)/shard_map/all_to_all | solution.py:281
  100.2 0.2 fusion.1
  100.4 0.1 select_reduce_fusion.4
  100.5 0.1 and.124
  100.6 0.1 eq.154
  100.8 0.2 convert_reduce_fusion
  101.0 0.1 reduce_sum.86
  101.1 0.7 convert_reduce_fusion.1
  101.8 0.2 reduce_window_sum.11
  101.9 67.9 %collective-permute-done.4.refs_2_ = bf16[32,128,256]{2,1,0:T(8,128)(2,1)} collective-permute-done((bf16[32,128,256]{2,1,0:T(8,128)(2,1)}, bf16[32,128,256]{2,1,0:T(8,128)(2,1)}, u32[]{:S(2)}, u32[]{:S(2)}) %collective-permute-start.4) | collective-permute-done | bytes 2097184 | tf_op jit(solution)/shard_map/ppermute | solution.py:287
  169.8 2.2 collective-permute-start.5
  172.0 4.7 %choose_blocks.6 = bf16[40,128,256]{2,1,0:T(8,128)(2,1)} custom-call(s32[1]{0:T(128)} %bitcast.1.which, s32[5,8,5]{2,1,0:T(8,128)} %bitcast.19, bf16[32,128,256]{2,1,0:T(8,128)(2,1)} %collective-permute-done.3.refs_1_, bf16[32,128,256]{2,1,0:T(8,128)(2,1)} %collective-permute-done.4.refs_2_), custom_call_target="tpu_custom_call" | custom-call | flops 10000000000 | bytes 5242880 | tf_op jit(solution)/shard_map/choose_blocks/pallas_call | solution.py:51
  176.7 4.4 %all-to-all-start.3 = ((bf16[40,128,256]{2,1,0:T(8,128)(2,1)}), bf16[40,128,256]{2,1,0:T(8,128)(2,1)}, u32[]{:S(2)}, u32[]{:S(2)}) async-start(bf16[40,128,256]{2,1,0:T(8,128)(2,1)} %choose_blocks.6), calls=%async_computation.3 | async-start | bytes 5242880 | tf_op jit(solution)/shard_map/all_to_all | solution.py:281
  181.1 0.1 copy.30
  181.2 0.1 copy.36
  181.4 0.1 copy.41
  181.5 0.7 reshape.239.late
  182.2 0.1 copy.37
  182.3 0.6 reshape.237.slots
  182.9 0.6 compare_select_fusion.slots
  183.5 15.0 %early_sums.1 = (f32[4096,256]{1,0:T(8,128)}, s8[32,128,512]{2,1,0:T(32,128)(4,1)}) custom-call(s32[192]{0:T(256)} %compare_select_fusion.slots, s32[128]{0:T(128)} %reshape.239.late, s32[32]{0:T(128)} %get-tuple-element.25.counts, bf16[32,128,256]{2,1,0:T(8,128)(2,1)} %bitcast.13, bf16[40,128,256]{2,1,0:T(8,128)(2,1)} %all-to-all-done.1.refs_1_, ...), custom_call_target="tpu_custom_call" | custom-call | flops 20000000000 | bytes 28901376 | tf_op jit(solution)/shard_map/early_sums/pallas_call | solution.py:118
  198.5 14.9 %all-to-all-done.3.last = bf16[40,128,256]{2,1,0:T(8,128)(2,1)} async-done(((bf16[40,128,256]{2,1,0:T(8,128)(2,1)}), bf16[40,128,256]{2,1,0:T(8,128)(2,1)}, u32[]{:S(2)}, u32[]{:S(2)}) %all-to-all-start.3) | async-done | bytes 2621472 | tf_op jit(solution)/shard_map/all_to_all | solution.py:281
  213.4 9.9 %sage_layer.1 = bf16[4096,256]{1,0:T(8,128)(2,1)} custom-call(s32[128]{0:T(128)} %reshape.237.slots, s32[32]{0:T(128)} %get-tuple-element.25.counts, s32[1]{0:T(128)} %bitcast.end, bf16[40,128,256]{2,1,0:T(8,128)(2,1)} %collective-permute-done.5.crossed, bf16[40,128,256]{2,1,0:T(8,128)(2,1)} %all-to-all-done.3.last, f32[4096,256]{1,0:T(8,128)} %get-tuple-element.19.refs_0_, ...), custom_call_target="tpu_custom_call" | custom-call | flops 2147483648 | bytes 10485760 | tf_op jit(solution)/shard_map/sage_layer/pallas_call | solution.py:232
  (21 shorter events, 0.3 us)
Async XLA Ops:
  0.0 47.7 %collective-permute-start.2 = (bf16[32,128,256]{2,1,0:T(8,128)(2,1)}, bf16[32,128,256]{2,1,0:T(8,128)(2,1)}, u32[]{:S(2)}, u32[]{:S(2)}) collective-permute-start(bf16[32,128,256]{2,1,0:T(8,128)(2,1)} %bitcast.9), channel_id=1, source_target_pairs={{0,8},{1,9},{2,10},{3,11},{4,12},{5,13},{6,14},{7,15},{8,0},{9,1},... | collective-permute-start | bytes 6291464 | tf_op jit(solution)/shard_map/ppermute | solution.py:287
  0.0 50.8 %collective-permute-start.1 = (bf16[32,128,256]{2,1,0:T(8,128)(2,1)}, bf16[32,128,256]{2,1,0:T(8,128)(2,1)}, u32[]{:S(2)}, u32[]{:S(2)}) collective-permute-start(bf16[32,128,256]{2,1,0:T(8,128)(2,1)} %bitcast.10), channel_id=1, source_target_pairs={{8,16},{9,17},{10,18},{11,19},{12,20},{13,21},{14,22},{15,23},{16,... | collective-permute-start | bytes 6291464 | tf_op jit(solution)/shard_map/ppermute | solution.py:287
  6.5 8.4 %all-to-all-start = ((s32[8,1,192]{2,1,0:T(1,128)}), s32[8,1,192]{2,1,0:T(1,128)S(1)}, u32[]{:S(2)}, u32[]{:S(2)}) async-start(s32[8,1,192]{2,1,0:T(1,128)} %broadcast_in_dim.117), calls=%async_computation | async-start | bytes 16384 | tf_op jit(solution)/shard_map/all_to_all | solution.py:281
  22.5 36.7 %all-to-all-start.1 = ((bf16[40,128,256]{2,1,0:T(8,128)(2,1)}), bf16[40,128,256]{2,1,0:T(8,128)(2,1)}, u32[]{:S(2)}, u32[]{:S(2)}) async-start(bf16[40,128,256]{2,1,0:T(8,128)(2,1)} %choose_blocks.4), calls=%async_computation.1 | async-start | bytes 5242880 | tf_op jit(solution)/shard_map/all_to_all | solution.py:281
  27.6 0.7 collective-permute-start
  28.2 22.6 %copy-start = (s32[1,8,5]{2,1,0:T(8,128)}, s32[1,8,5]{2,1,0:T(8,128)S(1)}, u32[]{:S(2)}) copy-start(s32[1,8,5]{2,1,0:T(8,128)S(1)} %collective-permute-done.refs_0_) | copy-start | bytes 484
  55.2 46.7 %collective-permute-start.3 = (bf16[32,128,256]{2,1,0:T(8,128)(2,1)}, bf16[32,128,256]{2,1,0:T(8,128)(2,1)}, u32[]{:S(2)}, u32[]{:S(2)}) collective-permute-start(bf16[32,128,256]{2,1,0:T(8,128)(2,1)} %collective-permute-done.1.refs_3_), channel_id=1, source_target_pairs={{8,0},{9,1},{10,2},{11,3},{12,4},{13,5},{14,6},{15,7},{16,24},{17,... | collective-permute-start | bytes 6291464 | tf_op jit(solution)/shard_map/ppermute | solution.py:287
  59.1 36.7 %all-to-all-start.2 = ((bf16[40,128,256]{2,1,0:T(8,128)(2,1)}), bf16[40,128,256]{2,1,0:T(8,128)(2,1)}, u32[]{:S(2)}, u32[]{:S(2)}) async-start(bf16[40,128,256]{2,1,0:T(8,128)(2,1)} %choose_blocks.5), calls=%async_computation.2 | async-start | bytes 5242880 | tf_op jit(solution)/shard_map/all_to_all | solution.py:281
  63.5 106.3 %collective-permute-start.4 = (bf16[32,128,256]{2,1,0:T(8,128)(2,1)}, bf16[32,128,256]{2,1,0:T(8,128)(2,1)}, u32[]{:S(2)}, u32[]{:S(2)}) collective-permute-start(bf16[32,128,256]{2,1,0:T(8,128)(2,1)} %collective-permute-done.2.refs_1_), channel_id=1, source_target_pairs={{8,16},{9,17},{10,18},{11,19},{12,20},{13,21},{14,22},{15,23},{16,... | collective-permute-start | bytes 6291464 | tf_op jit(solution)/shard_map/ppermute | solution.py:287
  95.8 80.9 %all-to-all-start.4 = ((bf16[40,128,256]{2,1,0:T(8,128)(2,1)}), bf16[40,128,256]{2,1,0:T(8,128)(2,1)}, u32[]{:S(2)}, u32[]{:S(2)}) async-start(bf16[40,128,256]{2,1,0:T(8,128)(2,1)} %choose_blocks.7), calls=%async_computation.4 | async-start | bytes 5242880 | tf_op jit(solution)/shard_map/all_to_all | solution.py:281
  169.8 43.6 %collective-permute-start.5 = (bf16[40,128,256]{2,1,0:T(8,128)(2,1)}, bf16[40,128,256]{2,1,0:T(8,128)(2,1)}, u32[]{:S(2)}, u32[]{:S(2)}) collective-permute-start(bf16[40,128,256]{2,1,0:T(8,128)(2,1)} %all-to-all-done.2.refs_2_), channel_id=1, source_target_pairs={{0,24},{1,25},{2,26},{3,27},{4,28},{5,29},{6,30},{7,31},{24,0},{25... | collective-permute-start | bytes 7864328 | tf_op jit(solution)/shard_map/ppermute | solution.py:287
  176.7 36.7 %all-to-all-start.3 = ((bf16[40,128,256]{2,1,0:T(8,128)(2,1)}), bf16[40,128,256]{2,1,0:T(8,128)(2,1)}, u32[]{:S(2)}, u32[]{:S(2)}) async-start(bf16[40,128,256]{2,1,0:T(8,128)(2,1)} %choose_blocks.6), calls=%async_computation.3 | async-start | bytes 5242880 | tf_op jit(solution)/shard_map/all_to_all | solution.py:281

commit v17 on v14

--- a/solution.py
+++ b/solution.py
@@ -47,7 +47,7 @@
 def choose(which, lists, turns, froms, flops):
     out = (lists[0].shape[1] * lists[0].shape[2],) + froms[0].shape[1:]
     moved = out[0] * out[1] * out[2] * 2
-    groups = 4 if out[0] % 4 == 0 else 1
+    groups = 1
     return pl.pallas_call(
         functools.partial(choose_kernel, turns=turns),
         grid_spec=pltpu.PrefetchScalarGridSpec(

time: 183 us -> 183 us (level)
  no operation moved by 1% of the time
where the time goes in v17:
time: 183 us; the launch traced here: 181 us
  waiting for transfers between devices  88.6 us (48%)
  Pallas kernels  44.2 us (24%)
  starting transfers between devices  37.4 us (20%)
  local copies, waits for them, and re-layouts  5.48 us (3%)
  other arithmetic  5.07 us (3%)
    all_to_all x5, waiting for transfers between devices, exchange(): lax.all_to_all(x, 'rows', split_axis=0, concat_axis=0, axis_index_groups=...  63.6 us
    ppermute x6, waiting for transfers between devices, shift(): return lax.ppermute(x, 'rows', pairs)  25 us
    all_to_all x5, starting transfers between devices, exchange(): lax.all_to_all(x, 'rows', split_axis=0, concat_axis=0, axis_index_groups=...  21.3 us
    pallas_call x4, Pallas kernels, choose(): pl.pallas_call(functools.partial(choose_kernel, turns=turns), grid_spec=p...  17.8 us
    ppermute x6, starting transfers between devices, shift(): return lax.ppermute(x, 'rows', pairs)  16.1 us
    pallas_call x1, Pallas kernels, early(): pl.pallas_call(early_kernel, grid_spec=pltpu.PrefetchScalarGridSpec(num_s...  15 us
    pallas_call x1, Pallas kernels, layer(): pl.pallas_call(layer_kernel, grid_spec=pltpu.PrefetchScalarGridSpec(num_s...  11.3 us
  transfers between devices with their start and end apart: 11, of which 6 were waited for; matrix products, arithmetic and copies ran while one was open for 6% of the time, Pallas kernels for 18%

profile of v17, /device:TPU:0, one launch (start us, length us, event | category | flops | bytes accessed | tf_op | source)
XLA Modules:
  0.0 180.9 jit_solution(12717917788214768363)
XLA Ops:
  0.0 3.0 %collective-permute-start.2 = (bf16[32,128,256]{2,1,0:T(8,128)(2,1)}, bf16[32,128,256]{2,1,0:T(8,128)(2,1)}, u32[]{:S(2)}, u32[]{:S(2)}) collective-permute-start(bf16[32,128,256]{2,1,0:T(8,128)(2,1)} %bitcast.9), channel_id=1, source_target_pairs={{0,8},{1,9},{2,10},{3,11},{4,12},{5,13},{6,14},{7,15},{8,0},{9,1},... | collective-permute-start | bytes 6291464 | tf_op jit(solution)/shard_map/ppermute | solution.py:287
  3.0 2.0 %collective-permute-start.1 = (bf16[32,128,256]{2,1,0:T(8,128)(2,1)}, bf16[32,128,256]{2,1,0:T(8,128)(2,1)}, u32[]{:S(2)}, u32[]{:S(2)}) collective-permute-start(bf16[32,128,256]{2,1,0:T(8,128)(2,1)} %bitcast.10), channel_id=1, source_target_pairs={{8,16},{9,17},{10,18},{11,19},{12,20},{13,21},{14,22},{15,23},{16,... | collective-permute-start | bytes 6291464 | tf_op jit(solution)/shard_map/ppermute | solution.py:287
  5.0 0.8 copy.29
  5.8 0.1 reshape.236
  5.9 0.6 broadcast_in_dim.117
  6.5 3.7 %all-to-all-start = ((s32[8,1,192]{2,1,0:T(1,128)}), s32[8,1,192]{2,1,0:T(1,128)S(1)}, u32[]{:S(2)}, u32[]{:S(2)}) async-start(s32[8,1,192]{2,1,0:T(1,128)} %broadcast_in_dim.117), calls=%async_computation | async-start | bytes 16384 | tf_op jit(solution)/shard_map/all_to_all | solution.py:281
  10.2 0.8 select_reduce_fusion.5
  11.0 0.1 fusion.13
  11.2 3.7 %all-to-all-done = s32[8,1,192]{2,1,0:T(1,128)S(1)} async-done(((s32[8,1,192]{2,1,0:T(1,128)}), s32[8,1,192]{2,1,0:T(1,128)S(1)}, u32[]{:S(2)}, u32[]{:S(2)}) %all-to-all-start) | async-done | bytes 6176 | tf_op jit(solution)/shard_map/all_to_all | solution.py:281
  14.9 0.9 compare_reduce_fusion
  15.8 0.7 select_reduce_fusion
  16.6 0.5 select_reduce_fusion.1
  17.1 0.7 copy.40
  17.8 4.4 %choose_blocks.4 = bf16[40,128,256]{2,1,0:T(8,128)(2,1)} custom-call(s32[1]{0:T(128)} %constant.93.clone.1.which, s32[5,8,5]{2,1,0:T(8,128)} %bitcast.15, bf16[32,128,256]{2,1,0:T(8,128)(2,1)} %bitcast.11), custom_call_target="tpu_custom_call" | custom-call | flops 10000000000 | bytes 5242880 | tf_op jit(solution)/shard_map/choose_blocks/pallas_call | solution.py:51
  22.3 4.4 %all-to-all-start.1 = ((bf16[40,128,256]{2,1,0:T(8,128)(2,1)}), bf16[40,128,256]{2,1,0:T(8,128)(2,1)}, u32[]{:S(2)}, u32[]{:S(2)}) async-start(bf16[40,128,256]{2,1,0:T(8,128)(2,1)} %choose_blocks.4), calls=%async_computation.1 | async-start | bytes 5242880 | tf_op jit(solution)/shard_map/all_to_all | solution.py:281
  26.7 0.7 slice.4
  27.4 4.4 %collective-permute-start = (s32[1,8,5]{2,1,0:T(8,128)S(1)}, s32[1,8,5]{2,1,0:T(8,128)S(1)}, u32[]{:S(2)}, u32[]{:S(2)}) collective-permute-start(s32[1,8,5]{2,1,0:T(8,128)S(1)} %slice.4), channel_id=1, source_target_pairs={{0,24},{1,25},{2,26},{3,27},{4,28},{5,29},{6,30},{7,31},{24,0},{25... | collective-permute-start | bytes 488 | tf_op jit(solution)/shard_map/ppermute | solution.py:287
  31.8 19.5 %collective-permute-done.refs_0_ = s32[1,8,5]{2,1,0:T(8,128)S(1)} collective-permute-done((s32[1,8,5]{2,1,0:T(8,128)S(1)}, s32[1,8,5]{2,1,0:T(8,128)S(1)}, u32[]{:S(2)}, u32[]{:S(2)}) %collective-permute-start) | collective-permute-done | bytes 192 | tf_op jit(solution)/shard_map/ppermute | solution.py:287
  51.3 0.6 copy-done
  51.8 4.4 %choose_blocks.5 = bf16[40,128,256]{2,1,0:T(8,128)(2,1)} custom-call(s32[1]{0:T(128)} %bitcast.1.which, s32[1,8,5]{2,1,0:T(8,128)} %copy-done, s32[5,8,5]{2,1,0:T(8,128)} %bitcast.17, bf16[32,128,256]{2,1,0:T(8,128)(2,1)} %bitcast.12, bf16[32,128,256]{2,1,0:T(8,128)(2,1)} %collective-permute-done.1.refs_3_), custom_call_target="tpu_custom_call" | custom-call | flops 10000000000 | bytes 5242880 | tf_op jit(solution)/shard_map/choose_blocks/pallas_call | solution.py:51
  56.3 2.0 %collective-permute-start.4 = (bf16[32,128,256]{2,1,0:T(8,128)(2,1)}, bf16[32,128,256]{2,1,0:T(8,128)(2,1)}, u32[]{:S(2)}, u32[]{:S(2)}) collective-permute-start(bf16[32,128,256]{2,1,0:T(8,128)(2,1)} %collective-permute-done.2.refs_1_), channel_id=1, source_target_pairs={{8,16},{9,17},{10,18},{11,19},{12,20},{13,21},{14,22},{15,23},{16,... | collective-permute-start | bytes 6291464 | tf_op jit(solution)/shard_map/ppermute | solution.py:287
  58.3 1.3 collective-permute-start.3
  59.6 4.4 %all-to-all-start.2 = ((bf16[40,128,256]{2,1,0:T(8,128)(2,1)}), bf16[40,128,256]{2,1,0:T(8,128)(2,1)}, u32[]{:S(2)}, u32[]{:S(2)}) async-start(bf16[40,128,256]{2,1,0:T(8,128)(2,1)} %choose_blocks.5), calls=%async_computation.2 | async-start | bytes 5242880 | tf_op jit(solution)/shard_map/all_to_all | solution.py:281
  64.0 4.4 %choose_blocks.7 = bf16[40,128,256]{2,1,0:T(8,128)(2,1)} custom-call(s32[1]{0:T(128)} %constant.93.clone.1.which, s32[5,8,5]{2,1,0:T(8,128)} %bitcast.18, bf16[32,128,256]{2,1,0:T(8,128)(2,1)} %collective-permute-done.2.refs_1_), custom_call_target="tpu_custom_call" | custom-call | flops 30000001024 | bytes 5242880 | tf_op jit(solution)/shard_map/choose_blocks/pallas_call | solution.py:51
  68.4 27.9 %all-to-all-done.2.refs_2_ = bf16[40,128,256]{2,1,0:T(8,128)(2,1)} async-done(((bf16[40,128,256]{2,1,0:T(8,128)(2,1)}), bf16[40,128,256]{2,1,0:T(8,128)(2,1)}, u32[]{:S(2)}, u32[]{:S(2)}) %all-to-all-start.2) | async-done | bytes 2621472 | tf_op jit(solution)/shard_map/all_to_all | solution.py:281
  96.3 4.4 %all-to-all-start.4 = ((bf16[40,128,256]{2,1,0:T(8,128)(2,1)}), bf16[40,128,256]{2,1,0:T(8,128)(2,1)}, u32[]{:S(2)}, u32[]{:S(2)}) async-start(bf16[40,128,256]{2,1,0:T(8,128)(2,1)} %choose_blocks.7), calls=%async_computation.4 | async-start | bytes 5242880 | tf_op jit(solution)/shard_map/all_to_all | solution.py:281
  100.7 0.2 fusion.1
  100.9 0.1 select_reduce_fusion.4
  101.0 0.1 and.124
  101.1 0.1 eq.154
  101.2 0.2 convert_reduce_fusion
  101.5 0.1 reduce_sum.86
  101.6 0.7 convert_reduce_fusion.1
  102.2 0.2 reduce_window_sum.11
  102.4 5.5 %collective-permute-done.3.refs_1_ = bf16[32,128,256]{2,1,0:T(8,128)(2,1)} collective-permute-done((bf16[32,128,256]{2,1,0:T(8,128)(2,1)}, bf16[32,128,256]{2,1,0:T(8,128)(2,1)}, u32[]{:S(2)}, u32[]{:S(2)}) %collective-permute-start.3) | collective-permute-done | bytes 2097184 | tf_op jit(solution)/shard_map/ppermute | solution.py:287
  107.9 3.4 %collective-permute-start.5 = (bf16[40,128,256]{2,1,0:T(8,128)(2,1)}, bf16[40,128,256]{2,1,0:T(8,128)(2,1)}, u32[]{:S(2)}, u32[]{:S(2)}) collective-permute-start(bf16[40,128,256]{2,1,0:T(8,128)(2,1)} %all-to-all-done.2.refs_2_), channel_id=1, source_target_pairs={{0,24},{1,25},{2,26},{3,27},{4,28},{5,29},{6,30},{7,31},{24,0},{25... | collective-permute-start | bytes 7864328 | tf_op jit(solution)/shard_map/ppermute | solution.py:287
  111.3 4.6 %choose_blocks.6 = bf16[40,128,256]{2,1,0:T(8,128)(2,1)} custom-call(s32[1]{0:T(128)} %bitcast.1.which, s32[5,8,5]{2,1,0:T(8,128)} %bitcast.19, bf16[32,128,256]{2,1,0:T(8,128)(2,1)} %collective-permute-done.3.refs_1_, bf16[32,128,256]{2,1,0:T(8,128)(2,1)} %collective-permute-done.4.refs_2_), custom_call_target="tpu_custom_call" | custom-call | flops 10000000000 | bytes 5242880 | tf_op jit(solution)/shard_map/choose_blocks/pallas_call | solution.py:51
  115.9 17.1 %all-to-all-done.4.refs_3_ = bf16[40,128,256]{2,1,0:T(8,128)(2,1)} async-done(((bf16[40,128,256]{2,1,0:T(8,128)(2,1)}), bf16[40,128,256]{2,1,0:T(8,128)(2,1)}, u32[]{:S(2)}, u32[]{:S(2)}) %all-to-all-start.4) | async-done | bytes 2621472 | tf_op jit(solution)/shard_map/all_to_all | solution.py:281
  132.9 4.4 %all-to-all-start.3 = ((bf16[40,128,256]{2,1,0:T(8,128)(2,1)}), bf16[40,128,256]{2,1,0:T(8,128)(2,1)}, u32[]{:S(2)}, u32[]{:S(2)}) async-start(bf16[40,128,256]{2,1,0:T(8,128)(2,1)} %choose_blocks.6), calls=%async_computation.3 | async-start | bytes 5242880 | tf_op jit(solution)/shard_map/all_to_all | solution.py:281
  137.4 0.1 copy.30
  137.6 0.1 copy.41
  137.7 0.6 reshape.239.late
  138.3 0.1 copy.37
  138.4 0.6 reshape.237.slots
  139.1 0.6 compare_select_fusion.slots
  139.7 15.0 %early_sums.1 = (f32[4096,256]{1,0:T(8,128)}, s8[32,128,512]{2,1,0:T(32,128)(4,1)}) custom-call(s32[192]{0:T(256)} %compare_select_fusion.slots, s32[128]{0:T(128)} %reshape.239.late, s32[32]{0:T(128)} %get-tuple-element.23.counts, bf16[32,128,256]{2,1,0:T(8,128)(2,1)} %bitcast.13, bf16[40,128,256]{2,1,0:T(8,128)(2,1)} %all-to-all-done.1.refs_1_, ...), custom_call_target="tpu_custom_call" | custom-call | flops 20000000000 | bytes 28901376 | tf_op jit(solution)/shard_map/early_sums/pallas_call | solution.py:118
  154.7 14.9 %all-to-all-done.3.last = bf16[40,128,256]{2,1,0:T(8,128)(2,1)} async-done(((bf16[40,128,256]{2,1,0:T(8,128)(2,1)}), bf16[40,128,256]{2,1,0:T(8,128)(2,1)}, u32[]{:S(2)}, u32[]{:S(2)}) %all-to-all-start.3) | async-done | bytes 2621472 | tf_op jit(solution)/shard_map/all_to_all | solution.py:281
  169.6 11.3 %sage_layer.1 = bf16[4096,256]{1,0:T(8,128)(2,1)} custom-call(s32[128]{0:T(128)} %reshape.237.slots, s32[32]{0:T(128)} %get-tuple-element.23.counts, s32[1]{0:T(128)} %bitcast.end, bf16[40,128,256]{2,1,0:T(8,128)(2,1)} %collective-permute-done.5.crossed, bf16[40,128,256]{2,1,0:T(8,128)(2,1)} %all-to-all-done.3.last, f32[4096,256]{1,0:T(8,128)} %get-tuple-element.17.refs_0_, ...), custom_call_target="tpu_custom_call" | custom-call | flops 2147483648 | bytes 10485760 | tf_op jit(solution)/shard_map/sage_layer/pallas_call | solution.py:232
  (21 shorter events, 0.4 us)
Async XLA Ops:
  0.0 51.2 %collective-permute-start.2 = (bf16[32,128,256]{2,1,0:T(8,128)(2,1)}, bf16[32,128,256]{2,1,0:T(8,128)(2,1)}, u32[]{:S(2)}, u32[]{:S(2)}) collective-permute-start(bf16[32,128,256]{2,1,0:T(8,128)(2,1)} %bitcast.9), channel_id=1, source_target_pairs={{0,8},{1,9},{2,10},{3,11},{4,12},{5,13},{6,14},{7,15},{8,0},{9,1},... | collective-permute-start | bytes 6291464 | tf_op jit(solution)/shard_map/ppermute | solution.py:287
  3.0 48.2 %collective-permute-start.1 = (bf16[32,128,256]{2,1,0:T(8,128)(2,1)}, bf16[32,128,256]{2,1,0:T(8,128)(2,1)}, u32[]{:S(2)}, u32[]{:S(2)}) collective-permute-start(bf16[32,128,256]{2,1,0:T(8,128)(2,1)} %bitcast.10), channel_id=1, source_target_pairs={{8,16},{9,17},{10,18},{11,19},{12,20},{13,21},{14,22},{15,23},{16,... | collective-permute-start | bytes 6291464 | tf_op jit(solution)/shard_map/ppermute | solution.py:287
  6.5 8.4 %all-to-all-start = ((s32[8,1,192]{2,1,0:T(1,128)}), s32[8,1,192]{2,1,0:T(1,128)S(1)}, u32[]{:S(2)}, u32[]{:S(2)}) async-start(s32[8,1,192]{2,1,0:T(1,128)} %broadcast_in_dim.117), calls=%async_computation | async-start | bytes 16384 | tf_op jit(solution)/shard_map/all_to_all | solution.py:281
  22.3 37.3 %all-to-all-start.1 = ((bf16[40,128,256]{2,1,0:T(8,128)(2,1)}), bf16[40,128,256]{2,1,0:T(8,128)(2,1)}, u32[]{:S(2)}, u32[]{:S(2)}) async-start(bf16[40,128,256]{2,1,0:T(8,128)(2,1)} %choose_blocks.4), calls=%async_computation.1 | async-start | bytes 5242880 | tf_op jit(solution)/shard_map/all_to_all | solution.py:281
  27.4 23.9 %collective-permute-start = (s32[1,8,5]{2,1,0:T(8,128)S(1)}, s32[1,8,5]{2,1,0:T(8,128)S(1)}, u32[]{:S(2)}, u32[]{:S(2)}) collective-permute-start(s32[1,8,5]{2,1,0:T(8,128)S(1)} %slice.4), channel_id=1, source_target_pairs={{0,24},{1,25},{2,26},{3,27},{4,28},{5,29},{6,30},{7,31},{24,0},{25... | collective-permute-start | bytes 488 | tf_op jit(solution)/shard_map/ppermute | solution.py:287
  51.2 0.6 copy-start
  56.3 46.1 %collective-permute-start.4 = (bf16[32,128,256]{2,1,0:T(8,128)(2,1)}, bf16[32,128,256]{2,1,0:T(8,128)(2,1)}, u32[]{:S(2)}, u32[]{:S(2)}) collective-permute-start(bf16[32,128,256]{2,1,0:T(8,128)(2,1)} %collective-permute-done.2.refs_1_), channel_id=1, source_target_pairs={{8,16},{9,17},{10,18},{11,19},{12,20},{13,21},{14,22},{15,23},{16,... | collective-permute-start | bytes 6291464 | tf_op jit(solution)/shard_map/ppermute | solution.py:287
  58.3 49.6 %collective-permute-start.3 = (bf16[32,128,256]{2,1,0:T(8,128)(2,1)}, bf16[32,128,256]{2,1,0:T(8,128)(2,1)}, u32[]{:S(2)}, u32[]{:S(2)}) collective-permute-start(bf16[32,128,256]{2,1,0:T(8,128)(2,1)} %collective-permute-done.1.refs_3_), channel_id=1, source_target_pairs={{8,0},{9,1},{10,2},{11,3},{12,4},{13,5},{14,6},{15,7},{16,24},{17,... | collective-permute-start | bytes 6291464 | tf_op jit(solution)/shard_map/ppermute | solution.py:287
  59.6 36.7 %all-to-all-start.2 = ((bf16[40,128,256]{2,1,0:T(8,128)(2,1)}), bf16[40,128,256]{2,1,0:T(8,128)(2,1)}, u32[]{:S(2)}, u32[]{:S(2)}) async-start(bf16[40,128,256]{2,1,0:T(8,128)(2,1)} %choose_blocks.5), calls=%async_computation.2 | async-start | bytes 5242880 | tf_op jit(solution)/shard_map/all_to_all | solution.py:281
  96.3 36.7 %all-to-all-start.4 = ((bf16[40,128,256]{2,1,0:T(8,128)(2,1)}), bf16[40,128,256]{2,1,0:T(8,128)(2,1)}, u32[]{:S(2)}, u32[]{:S(2)}) async-start(bf16[40,128,256]{2,1,0:T(8,128)(2,1)} %choose_blocks.7), calls=%async_computation.4 | async-start | bytes 5242880 | tf_op jit(solution)/shard_map/all_to_all | solution.py:281
  107.9 61.8 %collective-permute-start.5 = (bf16[40,128,256]{2,1,0:T(8,128)(2,1)}, bf16[40,128,256]{2,1,0:T(8,128)(2,1)}, u32[]{:S(2)}, u32[]{:S(2)}) collective-permute-start(bf16[40,128,256]{2,1,0:T(8,128)(2,1)} %all-to-all-done.2.refs_2_), channel_id=1, source_target_pairs={{0,24},{1,25},{2,26},{3,27},{4,28},{5,29},{6,30},{7,31},{24,0},{25... | collective-permute-start | bytes 7864328 | tf_op jit(solution)/shard_map/ppermute | solution.py:287
  132.9 36.7 %all-to-all-start.3 = ((bf16[40,128,256]{2,1,0:T(8,128)(2,1)}), bf16[40,128,256]{2,1,0:T(8,128)(2,1)}, u32[]{:S(2)}, u32[]{:S(2)}) async-start(bf16[40,128,256]{2,1,0:T(8,128)(2,1)} %choose_blocks.6), calls=%async_computation.3 | async-start | bytes 5242880 | tf_op jit(solution)/shard_map/all_to_all | solution.py:281
